TPU v7x, 32 devices: a whole 2x2x4 slice. The times are simulated.
32 devices in a mesh: ctx: 4 (over z), fsdp: 8 (over y, x, core).
Axes of the slice: x: 2, y: 2, z: 4, core: 2. Of those that a mesh axis runs over, the one named last changes fastest.
Arguments:
- tokens: bfloat16 [8, 1024, 2048], P('fsdp', 'ctx'), may hold values from -6 to 6
- routes: int32 [8, 1024, 6], P('fsdp', 'ctx'), may hold values from 0 to 15, all different within a row; in each aligned block of 256 rows (0 to 255, 256 to 511, ..., all dimensions but the last counted through in order) at most 128 rows name the same one
- gate_values: float32 [8, 1024, 6], P('fsdp', 'ctx'), may hold values from 1 to 2
- cotangent: bfloat16 [8, 1024, 2048], P('fsdp', 'ctx'), may hold values from -6 to 6
- attention_gain: bfloat16 [2048], P(('ctx', 'fsdp')), may hold values from 0.5 to 1.5
- query_weight: bfloat16 [2048, 3072], P(('ctx', 'fsdp')), may hold values from -0.125 to 0.125
- latent_weight: bfloat16 [2048, 576], P(('ctx', 'fsdp')), may hold values from -0.125 to 0.125
- latent_gain: bfloat16 [512], P(('ctx', 'fsdp')), may hold values from 0.5 to 1.5
- expand_weight: bfloat16 [512, 4096], P(('ctx', 'fsdp')), may hold values from -0.25 to 0.25
- output_weight: bfloat16 [2048, 2048], P(('ctx', 'fsdp')), may hold values from -2 to 2
- feedforward_gain: bfloat16 [2048], P(('ctx', 'fsdp')), may hold values from 0.5 to 1.5
- shared_gate: bfloat16 [2048, 2816], P(('ctx', 'fsdp')), may hold values from -0.125 to 0.125
- shared_up: bfloat16 [2048, 2816], P(('ctx', 'fsdp')), may hold values from -0.125 to 0.125
- shared_down: bfloat16 [2816, 2048], P(('ctx', 'fsdp')), may hold values from -0.109375 to 0.109375
- expert_gate: bfloat16 [16, 2048, 1408], P('fsdp', 'ctx'), may hold values from -0.125 to 0.125
- expert_up: bfloat16 [16, 2048, 1408], P('fsdp', 'ctx'), may hold values from -0.125 to 0.125
- expert_down: bfloat16 [16, 1408, 2048], P('fsdp', None, 'ctx'), may hold values from -0.3125 to 0.3125
Outputs:
- layer_out: bfloat16 [8, 1024, 2048], P('fsdp', 'ctx')
- tokens_grad: float32 [8, 1024, 2048], P('fsdp', 'ctx')
- attention_gain_grad: float32 [2048], P(('ctx', 'fsdp'))
- query_weight_grad: float32 [2048, 3072], P(('ctx', 'fsdp'))
- latent_weight_grad: float32 [2048, 576], P(('ctx', 'fsdp'))
- latent_gain_grad: float32 [512], P(('ctx', 'fsdp'))
- expand_weight_grad: float32 [512, 4096], P(('ctx', 'fsdp'))
- output_weight_grad: float32 [2048, 2048], P(('ctx', 'fsdp'))
- feedforward_gain_grad: float32 [2048], P(('ctx', 'fsdp'))
- shared_gate_grad: float32 [2048, 2816], P(('ctx', 'fsdp'))
- shared_up_grad: float32 [2048, 2816], P(('ctx', 'fsdp'))
- shared_down_grad: float32 [2816, 2048], P(('ctx', 'fsdp'))
- expert_gate_grad: float32 [16, 2048, 1408], P('fsdp', 'ctx')
- expert_up_grad: float32 [16, 2048, 1408], P('fsdp', 'ctx')
- expert_down_grad: float32 [16, 1408, 2048], P('fsdp', None, 'ctx')
Inputs may be any that keep to these rules, and one draw needn't show every extreme that they name: `routes`: each row names 6 different experts. Among the 256 rows of one device no expert is named by more than 128 rows, and in some device some expert is named by exactly 128.
All inputs are finite; a program needn't handle non-finite values.
Results may differ from a plain program's by a relative error of at most 0.025.
Values may be sent and summed in bfloat16 or wider, within the bound.
A program may use at most 448 MiB of HBM per device.

v0:
```python
import jax
import jax.numpy as jnp
from jax import lax
from jax.sharding import PartitionSpec as P

HEADS = 16
NOPE = 128
ROPE = 64
LATENT = 512
VDIM = 128
TOP = 6
EXP_DEV = 2


epsilon = 1e-06
rope_base = 10000.0
masked_score = -1e30


def stored_positions(row_index, per_device, block_count):
    device = row_index // per_device
    within = row_index % per_device
    half_block = per_device // 2
    return jnp.where(
        within >= half_block,
        (block_count - 1 - device) * half_block + within - half_block,
        device * half_block + within,
    )


def rotary(values, positions, direction):
    half_rope = values.shape[-1] // 2
    frequency = rope_base ** (-jnp.arange(half_rope, dtype=jnp.float32) / half_rope)
    angles = positions.astype(jnp.float32)[:, None] * frequency[None, :]
    cosine_table = jnp.cos(angles)
    sine_table = direction * jnp.sin(angles)
    if values.ndim == 3:
        cosine_table = cosine_table[:, None, :]
        sine_table = sine_table[:, None, :]
    front_half = values[..., :half_rope]
    back_half = values[..., half_rope:]
    return jnp.concatenate(
        [
            front_half * cosine_table - back_half * sine_table,
            back_half * cosine_table + front_half * sine_table,
        ],
        axis=-1,
    )


def norm_forward(values):
    inverse = lax.rsqrt(jnp.mean(values * values, axis=-1, keepdims=True) + epsilon)
    return (values * inverse, inverse)


def norm_backward(normed_grad, plain, inverse, gain):
    gain_grad = jnp.sum(normed_grad * plain, axis=0)
    scaled = normed_grad * gain
    return (
        inverse * (scaled - plain * jnp.mean(scaled * plain, axis=-1, keepdims=True)),
        gain_grad,
    )


def silu_slope(values):
    sigma = jax.nn.sigmoid(values)
    return (values * sigma, sigma * (1.0 + values * (1.0 - sigma)))


def score_block(query_latent, query_rope, all_latent, all_keys, allowed, score_scale):
    raw_scores = jnp.einsum(
        "thc,kc->htk", query_latent, all_latent, preferred_element_type=jnp.float32
    ) + jnp.einsum("thd,kd->htk", query_rope, all_keys, preferred_element_type=jnp.float32)
    return jnp.where(allowed[None], raw_scores * score_scale, masked_score)


def local(
    tokens,
    routes,
    gate_values,
    cotangent,
    attention_gain,
    query_weight,
    latent_weight,
    latent_gain,
    expand_weight,
    output_weight,
    feedforward_gain,
    shared_gate,
    shared_up,
    shared_down,
    expert_gate,
    expert_up,
    expert_down,
):
    row_count = tokens.shape[1]
    model_width = tokens.shape[2]
    ctx_count = lax.axis_size("ctx")
    fsdp_count = lax.axis_size("fsdp")
    experts_total = EXP_DEV * fsdp_count
    capacity = row_count * TOP * 4 // (3 * experts_total)
    slot_total = experts_total * capacity
    score_scale = (NOPE + ROPE) ** (-0.5)
    source = tokens[0].astype(jnp.float32)
    cot_low = cotangent[0]
    cot_full = cot_low.astype(jnp.float32)
    local_routes = routes[0]
    local_gates = gate_values[0]
    positions = stored_positions(
        lax.axis_index("ctx") * row_count + jnp.arange(row_count, dtype=jnp.int32),
        row_count,
        2 * ctx_count,
    )
    key_positions = stored_positions(
        jnp.arange(row_count * ctx_count, dtype=jnp.int32), row_count, 2 * ctx_count
    )
    allowed = positions[:, None] >= key_positions[None, :]
    attention_set = (
        lax.all_gather(attention_gain, ("ctx", "fsdp"), axis=0, tiled=True),
        lax.all_gather(feedforward_gain, ("ctx", "fsdp"), axis=0, tiled=True),
        lax.all_gather(query_weight, ("ctx", "fsdp"), axis=0, tiled=True),
        lax.all_gather(latent_weight, ("ctx", "fsdp"), axis=0, tiled=True),
        lax.all_gather(latent_gain, ("ctx", "fsdp"), axis=0, tiled=True),
        lax.all_gather(expand_weight, ("ctx", "fsdp"), axis=0, tiled=True),
        lax.all_gather(output_weight, ("ctx", "fsdp"), axis=0, tiled=True),
    )
    gain_one, gain_two, full_query, full_latent, gain_latent, full_expand, full_output = (
        attention_set
    )
    gain_one = gain_one.astype(jnp.float32)
    gain_two = gain_two.astype(jnp.float32)
    gain_latent = gain_latent.astype(jnp.float32)
    plain_one, inverse_one = norm_forward(source)
    normed = (plain_one * gain_one).astype(jnp.bfloat16)
    query_raw = jnp.dot(normed, full_query, preferred_element_type=jnp.float32).reshape(
        row_count, HEADS, NOPE + ROPE
    )
    query_nope = query_raw[:, :, :NOPE].astype(jnp.bfloat16)
    query_rope = rotary(query_raw[:, :, NOPE:], positions, 1.0).astype(jnp.bfloat16)
    latent_raw = jnp.dot(normed, full_latent, preferred_element_type=jnp.float32)
    plain_latent, inverse_latent = norm_forward(latent_raw[:, :LATENT])
    latent_norm = (plain_latent * gain_latent).astype(jnp.bfloat16)
    key_rope = rotary(latent_raw[:, LATENT:], positions, 1.0).astype(jnp.bfloat16)
    all_latent, all_keys = (
        lax.all_gather(latent_norm, "ctx", axis=0, tiled=True),
        lax.all_gather(key_rope, "ctx", axis=0, tiled=True),
    )
    expand = full_expand.reshape(LATENT, HEADS, NOPE + VDIM)
    expand_key = expand[:, :, :NOPE]
    expand_value = expand[:, :, NOPE:]
    query_latent = jnp.einsum(
        "thd,chd->thc", query_nope, expand_key, preferred_element_type=jnp.float32
    ).astype(jnp.bfloat16)
    scores = score_block(query_latent, query_rope, all_latent, all_keys, allowed, score_scale)
    row_max = jnp.max(scores, axis=-1, keepdims=True)
    row_sum = jnp.sum(jnp.exp(scores - row_max), axis=-1, keepdims=True)
    log_total = row_max + jnp.log(row_sum)
    soft_weights = jnp.exp(scores - log_total)
    latent_out = jnp.einsum(
        "htk,kc->thc",
        soft_weights.astype(jnp.bfloat16),
        all_latent,
        preferred_element_type=jnp.float32,
    ).astype(jnp.bfloat16)
    values_out = (
        jnp.einsum("thc,chv->thv", latent_out, expand_value, preferred_element_type=jnp.float32)
        .astype(jnp.bfloat16)
        .reshape(row_count, HEADS * VDIM)
    )
    middle = source + jnp.dot(values_out, full_output, preferred_element_type=jnp.float32)
    expert_set = (
        lax.all_gather(expert_gate, "ctx", axis=1, tiled=True),
        lax.all_gather(expert_up, "ctx", axis=1, tiled=True),
        lax.all_gather(expert_down, "ctx", axis=2, tiled=True),
    )
    gate_all, up_all, down_all = expert_set
    plain_two, inverse_two = norm_forward(middle)
    second = (plain_two * gain_two).astype(jnp.bfloat16)
    full_sgate, full_sup, full_sdown = (
        lax.all_gather(shared_gate, ("ctx", "fsdp"), axis=0, tiled=True),
        lax.all_gather(shared_up, ("ctx", "fsdp"), axis=0, tiled=True),
        lax.all_gather(shared_down, ("ctx", "fsdp"), axis=0, tiled=True),
    )
    shared_g = jnp.dot(second, full_sgate, preferred_element_type=jnp.float32)
    shared_u = jnp.dot(second, full_sup, preferred_element_type=jnp.float32)
    shared_silu, shared_slope = silu_slope(shared_g)
    shared_hidden = (shared_silu * shared_u).astype(jnp.bfloat16)
    shared_out = jnp.dot(shared_hidden, full_sdown, preferred_element_type=jnp.float32)
    expert_index = jnp.arange(experts_total, dtype=jnp.int32)
    member = (local_routes[:, :, None] == expert_index[None, None, :]).astype(jnp.float32)
    counts = jnp.sum(member, axis=1)
    before = jnp.cumsum(counts, axis=0) - counts
    slot_within = jnp.sum(member * before[:, None, :], axis=-1).astype(jnp.int32)
    flat_slot = local_routes * capacity + slot_within
    slot_index = jnp.arange(slot_total, dtype=jnp.int32)
    slot_picks = (flat_slot[:, :, None] == slot_index[None, None, :]).astype(jnp.float32)
    chooser = jnp.sum(slot_picks, axis=1).astype(jnp.bfloat16)
    slot_gate = jnp.sum(slot_picks * local_gates[:, :, None], axis=(0, 1))
    flat_pick = flat_slot.reshape(-1)
    outgoing = (
        jnp.einsum("ts,td->sd", chooser, second, preferred_element_type=jnp.float32)
        .astype(jnp.bfloat16)
        .reshape(fsdp_count, EXP_DEV, capacity, model_width)
    )
    arrived_rows = lax.all_to_all(outgoing, "fsdp", split_axis=0, concat_axis=0, tiled=True)
    gate_pre = jnp.einsum(
        "secd,edf->secf", arrived_rows, gate_all, preferred_element_type=jnp.float32
    )
    up_pre = jnp.einsum("secd,edf->secf", arrived_rows, up_all, preferred_element_type=jnp.float32)
    hidden_act = (jax.nn.silu(gate_pre) * up_pre).astype(jnp.bfloat16)
    result = jnp.einsum(
        "secf,efd->secd", hidden_act, down_all, preferred_element_type=jnp.float32
    ).astype(jnp.bfloat16)
    came_back = lax.all_to_all(result, "fsdp", split_axis=0, concat_axis=0, tiled=True)
    back_rows = (
        jnp.take(came_back.reshape(slot_total, model_width), flat_pick, axis=0)
        .reshape(row_count, TOP, model_width)
        .astype(jnp.float32)
    )
    routed = jnp.sum(back_rows * local_gates[:, :, None], axis=1)
    final_sum = middle + (shared_out + routed)
    layer_out = final_sum.astype(jnp.bfloat16)[None]
    slot_cot = jnp.einsum("ts,td->sd", chooser, cot_low, preferred_element_type=jnp.float32)
    outgoing_grad = (
        (slot_cot * slot_gate[:, None])
        .astype(jnp.bfloat16)
        .reshape(fsdp_count, EXP_DEV, capacity, model_width)
    )
    arrived_grad = lax.all_to_all(outgoing_grad, "fsdp", split_axis=0, concat_axis=0, tiled=True)
    gate_pre = jnp.einsum(
        "secd,edf->secf", arrived_rows, gate_all, preferred_element_type=jnp.float32
    )
    up_pre = jnp.einsum("secd,edf->secf", arrived_rows, up_all, preferred_element_type=jnp.float32)
    gate_silu, gate_slope = silu_slope(gate_pre)
    hidden_act = (gate_silu * up_pre).astype(jnp.bfloat16)
    hidden_grad = jnp.einsum(
        "secd,efd->secf", arrived_grad, down_all, preferred_element_type=jnp.float32
    )
    down_grad = jnp.einsum(
        "secf,secd->efd", hidden_act, arrived_grad, preferred_element_type=jnp.float32
    )
    up_back = (hidden_grad * gate_silu).astype(jnp.bfloat16)
    gate_back = (hidden_grad * up_pre * gate_slope).astype(jnp.bfloat16)
    gate_grad = jnp.einsum(
        "secd,secf->edf", arrived_rows, gate_back, preferred_element_type=jnp.float32
    )
    up_grad = jnp.einsum(
        "secd,secf->edf", arrived_rows, up_back, preferred_element_type=jnp.float32
    )
    arrived_back = (
        jnp.einsum("secf,edf->secd", gate_back, gate_all, preferred_element_type=jnp.float32)
        + jnp.einsum("secf,edf->secd", up_back, up_all, preferred_element_type=jnp.float32)
    ).astype(jnp.bfloat16)
    returned_grad = lax.all_to_all(arrived_back, "fsdp", split_axis=0, concat_axis=0, tiled=True)
    expert_grads = (
        lax.psum_scatter(gate_grad, "ctx", scatter_dimension=1, tiled=True),
        lax.psum_scatter(up_grad, "ctx", scatter_dimension=1, tiled=True),
        lax.psum_scatter(down_grad, "ctx", scatter_dimension=2, tiled=True),
    )
    routed_back = jnp.sum(
        jnp.take(returned_grad.reshape(slot_total, model_width), flat_pick, axis=0)
        .reshape(row_count, TOP, model_width)
        .astype(jnp.float32),
        axis=1,
    )
    shared_hidden_grad = jnp.einsum(
        "td,fd->tf", cot_low, full_sdown, preferred_element_type=jnp.float32
    )
    sdown_grad = jnp.einsum("tf,td->fd", shared_hidden, cot_low, preferred_element_type=jnp.float32)
    sup_back = (shared_hidden_grad * shared_silu).astype(jnp.bfloat16)
    sgate_back = (shared_hidden_grad * shared_u * shared_slope).astype(jnp.bfloat16)
    sgate_grad = jnp.einsum("td,tf->df", second, sgate_back, preferred_element_type=jnp.float32)
    sup_grad = jnp.einsum("td,tf->df", second, sup_back, preferred_element_type=jnp.float32)
    shared_second_grad = jnp.einsum(
        "tf,df->td", sgate_back, full_sgate, preferred_element_type=jnp.float32
    ) + jnp.einsum("tf,df->td", sup_back, full_sup, preferred_element_type=jnp.float32)
    shared_grads = (
        lax.psum_scatter(sgate_grad, ("ctx", "fsdp"), scatter_dimension=0, tiled=True),
        lax.psum_scatter(sup_grad, ("ctx", "fsdp"), scatter_dimension=0, tiled=True),
        lax.psum_scatter(sdown_grad, ("ctx", "fsdp"), scatter_dimension=0, tiled=True),
    )
    second_grad = shared_second_grad + routed_back
    middle_part, gain_two_grad = norm_backward(second_grad, plain_two, inverse_two, gain_two)
    middle_grad = cot_full + middle_part
    attended_grad = middle_grad.astype(jnp.bfloat16)
    output_weight_grad = jnp.einsum(
        "tv,td->vd", values_out, attended_grad, preferred_element_type=jnp.float32
    )
    values_grad = (
        jnp.einsum("td,vd->tv", attended_grad, full_output, preferred_element_type=jnp.float32)
        .astype(jnp.bfloat16)
        .reshape(row_count, HEADS, VDIM)
    )
    latent_out_grad = jnp.einsum(
        "thv,chv->thc", values_grad, expand_value, preferred_element_type=jnp.float32
    ).astype(jnp.bfloat16)
    expand_value_grad = jnp.einsum(
        "thc,thv->chv", latent_out, values_grad, preferred_element_type=jnp.float32
    )
    scores = score_block(query_latent, query_rope, all_latent, all_keys, allowed, score_scale)
    soft_weights = jnp.exp(scores - log_total)
    soft_grad = jnp.einsum(
        "thc,kc->htk", latent_out_grad, all_latent, preferred_element_type=jnp.float32
    )
    all_latent_grad = jnp.einsum(
        "htk,thc->kc",
        soft_weights.astype(jnp.bfloat16),
        latent_out_grad,
        preferred_element_type=jnp.float32,
    )
    row_inner = jnp.sum(soft_weights * soft_grad, axis=-1, keepdims=True)
    score_grad = (soft_weights * (soft_grad - row_inner) * score_scale).astype(jnp.bfloat16)
    query_latent_grad = jnp.einsum(
        "htk,kc->thc", score_grad, all_latent, preferred_element_type=jnp.float32
    ).astype(jnp.bfloat16)
    all_latent_grad = all_latent_grad + jnp.einsum(
        "htk,thc->kc", score_grad, query_latent, preferred_element_type=jnp.float32
    )
    query_rope_grad = jnp.einsum(
        "htk,kd->thd", score_grad, all_keys, preferred_element_type=jnp.float32
    )
    all_keys_grad = jnp.einsum(
        "htk,thd->kd", score_grad, query_rope, preferred_element_type=jnp.float32
    )
    latent_grad, keys_grad = (
        lax.psum_scatter(all_latent_grad, "ctx", scatter_dimension=0, tiled=True),
        lax.psum_scatter(all_keys_grad, "ctx", scatter_dimension=0, tiled=True),
    )
    query_nope_grad = jnp.einsum(
        "thc,chd->thd", query_latent_grad, expand_key, preferred_element_type=jnp.float32
    )
    expand_key_grad = jnp.einsum(
        "thd,thc->chd", query_nope, query_latent_grad, preferred_element_type=jnp.float32
    )
    expand_grad = jnp.concatenate([expand_key_grad, expand_value_grad], axis=-1).reshape(
        LATENT, HEADS * (NOPE + VDIM)
    )
    query_grad = (
        jnp.concatenate([query_nope_grad, rotary(query_rope_grad, positions, -1.0)], axis=-1)
        .astype(jnp.bfloat16)
        .reshape(row_count, HEADS * (NOPE + ROPE))
    )
    latent_part_grad, gain_latent_grad = norm_backward(
        latent_grad, plain_latent, inverse_latent, gain_latent
    )
    latent_raw_grad = jnp.concatenate(
        [latent_part_grad, rotary(keys_grad, positions, -1.0)], axis=-1
    ).astype(jnp.bfloat16)
    query_weight_grad = jnp.einsum(
        "td,tq->dq", normed, query_grad, preferred_element_type=jnp.float32
    )
    latent_weight_grad = jnp.einsum(
        "td,tq->dq", normed, latent_raw_grad, preferred_element_type=jnp.float32
    )
    normed_grad = jnp.einsum(
        "tq,dq->td", query_grad, full_query, preferred_element_type=jnp.float32
    ) + jnp.einsum("tq,dq->td", latent_raw_grad, full_latent, preferred_element_type=jnp.float32)
    source_part, gain_one_grad = norm_backward(normed_grad, plain_one, inverse_one, gain_one)
    tokens_grad = (middle_grad + source_part)[None]
    attention_grads = (
        lax.psum_scatter(gain_one_grad, ("ctx", "fsdp"), scatter_dimension=0, tiled=True),
        lax.psum_scatter(gain_two_grad, ("ctx", "fsdp"), scatter_dimension=0, tiled=True),
        lax.psum_scatter(query_weight_grad, ("ctx", "fsdp"), scatter_dimension=0, tiled=True),
        lax.psum_scatter(latent_weight_grad, ("ctx", "fsdp"), scatter_dimension=0, tiled=True),
        lax.psum_scatter(gain_latent_grad, ("ctx", "fsdp"), scatter_dimension=0, tiled=True),
        lax.psum_scatter(expand_grad, ("ctx", "fsdp"), scatter_dimension=0, tiled=True),
        lax.psum_scatter(output_weight_grad, ("ctx", "fsdp"), scatter_dimension=0, tiled=True),
    )
    return (
        layer_out,
        tokens_grad,
        attention_grads[0],
        attention_grads[2],
        attention_grads[3],
        attention_grads[4],
        attention_grads[5],
        attention_grads[6],
        attention_grads[1],
        shared_grads[0],
        shared_grads[1],
        shared_grads[2],
        expert_grads[0],
        expert_grads[1],
        expert_grads[2],
    )


def solution(mesh):
    in_specs = (
        P("fsdp", "ctx", None),
        P("fsdp", "ctx", None),
        P("fsdp", "ctx", None),
        P("fsdp", "ctx", None),
        P(("ctx", "fsdp")),
        P(("ctx", "fsdp"), None),
        P(("ctx", "fsdp"), None),
        P(("ctx", "fsdp")),
        P(("ctx", "fsdp"), None),
        P(("ctx", "fsdp"), None),
        P(("ctx", "fsdp")),
        P(("ctx", "fsdp"), None),
        P(("ctx", "fsdp"), None),
        P(("ctx", "fsdp"), None),
        P("fsdp", "ctx", None),
        P("fsdp", "ctx", None),
        P("fsdp", None, "ctx"),
    )
    out_specs = (
        P("fsdp", "ctx", None),
        P("fsdp", "ctx", None),
        P(("ctx", "fsdp")),
        P(("ctx", "fsdp"), None),
        P(("ctx", "fsdp"), None),
        P(("ctx", "fsdp")),
        P(("ctx", "fsdp"), None),
        P(("ctx", "fsdp"), None),
        P(("ctx", "fsdp")),
        P(("ctx", "fsdp"), None),
        P(("ctx", "fsdp"), None),
        P(("ctx", "fsdp"), None),
        P("fsdp", "ctx", None),
        P("fsdp", "ctx", None),
        P("fsdp", None, "ctx"),
    )
    return jax.shard_map(local, mesh=mesh, in_specs=in_specs, out_specs=out_specs, check_vma=False)
```

profile of v0, /device:TPU:1, one launch (start us, length us, event | category | flops | bytes accessed | tf_op | source)
XLA Modules:
  0.0 4176.7 jit_solution(18238658566704240962)
XLA Ops:
  12.0 40.9 all-reduce.7
  103.6 31.6 all-gather.18.cloned.1.call-done
  141.6 90.9 %all-gather.16.cloned.1.call-done = bf16[2048,3072]{1,0:T(8,128)(2,1)} async-done(((bf16[64,3072]{1,0:T(8,128)(2,1)}), bf16[2048,3072]{1,0:T(8,128)(2,1)}) %all-gather.16.cloned.1.call-update) | async-done | bytes 12582928 | tf_op jit(solution)/shard_map/all_gather | solution.py:121
  298.9 42.6 %all-gather.20.cloned.1.call-done = bf16[2048,2048]{1,0:T(8,128)(2,1)} async-done(((bf16[64,2048]{1,0:T(8,128)(2,1)}), bf16[2048,2048]{1,0:T(8,128)(2,1)}) %all-gather.20.cloned.1.call-update) | async-done | bytes 8388624 | tf_op jit(solution)/shard_map/all_gather | solution.py:125
  366.0 84.8 %all-to-all-done = bf16[8,2,128,2048]{3,2,1,0:T(8,128)(2,1)} async-done(((bf16[8,2,128,2048]{3,2,1,0:T(8,128)(2,1)}), bf16[8,2,128,2048]{3,2,1,0:T(8,128)(2,1)}, u32[]{:S(2)}, u32[]{:S(2)}) %all-to-all-start) | async-done | bytes 8388640 | tf_op jit(solution)/shard_map/all_to_all | solution.py:205
  460.0 82.4 %all-gather.30.cloned.1.call-done = bf16[2,2048,1408]{2,1,0:T(8,128)(2,1)} async-done(((bf16[2,512,1408]{2,1,0:T(8,128)(2,1)}), bf16[2,2048,1408]{2,1,0:T(8,128)(2,1)}) %all-gather.30.cloned.1.call-update) | async-done | bytes 11534352 | tf_op jit(solution)/shard_map/all_gather | solution.py:173
  542.4 20.1 fusion.7
  562.5 180.8 %all-gather.28.cloned.1.call-done = bf16[2,2048,1408]{2,1,0:T(8,128)(2,1)} async-done(((bf16[2,512,1408]{2,1,0:T(8,128)(2,1)}), bf16[2,2048,1408]{2,1,0:T(8,128)(2,1)}) %all-gather.28.cloned.1.call-update) | async-done | bytes 11534352 | tf_op jit(solution)/shard_map/all_gather | solution.py:172
  763.1 181.0 %all-gather.32.cloned.1.call-done = bf16[2,1408,2048]{2,1,0:T(8,128)(2,1)} async-done(((bf16[2,1408,512]{2,1,0:T(8,128)(2,1)}), bf16[2,1408,2048]{2,1,0:T(8,128)(2,1)}) %all-gather.32.cloned.1.call-update) | async-done | bytes 11534352 | tf_op jit(solution)/shard_map/all_gather | solution.py:174
  944.1 28.1 fusion.14
  972.2 21.5 fusion.5
  993.7 20.6 fusion.26
  1028.1 20.1 convert_bitcast_fusion
  1056.5 82.0 %all-to-all-done.3 = bf16[8,2,128,2048]{3,2,1,0:T(8,128)(2,1)} async-done(((bf16[8,2,128,2048]{3,2,1,0:T(8,128)(2,1)}), bf16[8,2,128,2048]{3,2,1,0:T(8,128)(2,1)}, u32[]{:S(2)}, u32[]{:S(2)}) %all-to-all-start.3) | async-done | bytes 8388640 | tf_op jit(solution)/shard_map/all_to_all | solution.py:254
  1185.3 107.7 %all-gather.26.cloned.1.call-done = bf16[2816,2048]{1,0:T(8,128)(2,1)} async-done(((bf16[88,2048]{1,0:T(8,128)(2,1)}), bf16[2816,2048]{1,0:T(8,128)(2,1)}) %all-gather.26.cloned.1.call-update) | async-done | bytes 11534352 | tf_op jit(solution)/shard_map/all_gather | solution.py:182
  1429.2 22.9 convolution_bitcast_fusion.6
  1452.3 26.3 bitcast_add_fusion
  1480.3 39.5 reduce-scatter.13.cloned.1.call-done
  1532.7 25.4 convolution_convert_fusion.1
  1621.7 22.9 convolution_bitcast_fusion.5
  1660.3 21.6 convolution_bitcast_fusion.2
  1682.0 21.9 convolution_bitcast_fusion.1
  1704.0 20.7 convolution_bitcast_fusion
  1768.2 41.9 %all-reduce.6 = (f32[2048]{0:T(1024)S(1)}, f32[512]{0:T(512)S(1)}, f32[2048]{0:T(1024)S(1)}) all-reduce(f32[2048]{0:T(1024)S(1)} %get-tuple-element.18, f32[512]{0:T(512)S(1)} %copy-done.69, f32[2048]{0:T(1024)S(1)} %copy-done.70), channel_id=4, replica_groups=mesh['ctx'=4,'fsdp'=8] {'ctx','fsdp'}, use_global_device_ids=true, to_apply=%region_20.22.clone | all-reduce | flops 4608 | bytes 36864
  1815.3 249.9 %reduce-scatter.25.cloned.1.call-done = f32[64,2816]{1,0:T(8,128)} async-done(((f32[2048,2816]{1,0:T(8,128)}), f32[64,2816]{1,0:T(8,128)}) %reduce-scatter.25.cloned.1.call-update) | async-done | bytes 720912 | tf_op jit(solution)/shard_map/reduce_scatter | solution.py:278
  2065.2 254.2 %reduce-scatter.27.cloned.1.call-done = f32[64,2816]{1,0:T(8,128)} async-done(((f32[2048,2816]{1,0:T(8,128)}), f32[64,2816]{1,0:T(8,128)}) %reduce-scatter.27.cloned.1.call-update) | async-done | bytes 720912 | tf_op jit(solution)/shard_map/reduce_scatter | solution.py:279
  2319.4 254.2 %reduce-scatter.29.cloned.1.call-done = f32[88,2048]{1,0:T(8,128)} async-done(((f32[2816,2048]{1,0:T(8,128)}), f32[88,2048]{1,0:T(8,128)}) %reduce-scatter.29.cloned.1.call-update) | async-done | bytes 720912 | tf_op jit(solution)/shard_map/reduce_scatter | solution.py:280
  2573.5 188.7 %reduce-scatter.23.cloned.1.call-done = f32[64,2048]{1,0:T(8,128)} async-done(((f32[2048,2048]{1,0:T(8,128)}), f32[64,2048]{1,0:T(8,128)}) %reduce-scatter.23.cloned.1.call-update) | async-done | bytes 524304 | tf_op jit(solution)/shard_map/reduce_scatter | solution.py:367
  2762.2 253.4 %reduce-scatter.17.cloned.1.call-done = f32[64,3072]{1,0:T(8,128)} async-done(((f32[2048,3072]{1,0:T(8,128)}), f32[64,3072]{1,0:T(8,128)}) %reduce-scatter.17.cloned.1.call-update) | async-done | bytes 786448 | tf_op jit(solution)/shard_map/reduce_scatter | solution.py:363
  3015.7 383.4 %reduce-scatter.31.cloned.1.call-done = f32[2,512,1408]{2,1,0:T(8,128)} async-done(((f32[2,2048,1408]{2,1,0:T(8,128)}), f32[2,512,1408]{2,1,0:T(8,128)}) %reduce-scatter.31.cloned.1.call-update) | async-done | bytes 5767184 | tf_op jit(solution)/shard_map/reduce_scatter | solution.py:256
  3399.1 385.4 %reduce-scatter.33.cloned.1.call-done = f32[2,512,1408]{2,1,0:T(8,128)} async-done(((f32[2,2048,1408]{2,1,0:T(8,128)}), f32[2,512,1408]{2,1,0:T(8,128)}) %reduce-scatter.33.cloned.1.call-update) | async-done | bytes 5767184 | tf_op jit(solution)/shard_map/reduce_scatter | solution.py:257
  3784.4 385.5 %reduce-scatter.35.cloned.1.call-done = f32[2,1408,512]{2,1,0:T(8,128)} async-done(((f32[2,1408,2048]{2,1,0:T(8,128)}), f32[2,1408,512]{2,1,0:T(8,128)}) %reduce-scatter.35.cloned.1.call-update) | async-done | bytes 5767184 | tf_op jit(solution)/shard_map/reduce_scatter | solution.py:258
  (320 shorter events, 528.5 us)
Async XLA Ops:
  7.2 64.1 %all-gather.12.cloned.1.call-start = ((), (), s32[]{:S(2)}) async-start(), calls=%async_computation.16 | async-start | bytes 2703360 | tf_op jit(solution)/shard_map/all_gather | solution.py:122
  7.9 127.3 %all-gather.18.cloned.1.call-start = ((), (), s32[]{:S(2)}) async-start(), calls=%async_computation.19 | async-start | bytes 4325376 | tf_op jit(solution)/shard_map/all_gather | solution.py:124
  8.7 223.9 %all-gather.16.cloned.1.call-start = ((), (), s32[]{:S(2)}) async-start(), calls=%async_computation.18 | async-start | bytes 12976128 | tf_op jit(solution)/shard_map/all_gather | solution.py:121
  9.4 251.9 %all-gather.14.cloned.1.call-start = ((), (), s32[]{:S(2)}) async-start(), calls=%async_computation.17 | async-start | bytes 1310720 | tf_op jit(solution)/shard_map/all_gather | solution.py:145
  52.9 196.5 %copy-start.41 = (f32[2048]{0:T(1024)}, f32[2048]{0:T(1024)S(1)}, u32[]{:S(2)}) copy-start(f32[2048]{0:T(1024)S(1)} %convert_element_type.178) | copy-start | bytes 24580
  54.4 195.0 %copy-start.57 = (f32[256]{0:T(256)}, f32[256]{0:T(256)S(1)}, u32[]{:S(2)}) copy-start(f32[256]{0:T(256)S(1)} %add_rsqrt_fusion.2) | copy-start | bytes 3076
  75.6 265.9 %all-gather.20.cloned.1.call-start = ((), (), s32[]{:S(2)}) async-start(), calls=%async_computation.20 | async-start | bytes 8650752 | tf_op jit(solution)/shard_map/all_gather | solution.py:125
  76.2 466.2 %all-gather.30.cloned.1.call-start = ((), (), s32[]{:S(2)}) async-start(), calls=%async_computation.25 | async-start | bytes 14417920 | tf_op jit(solution)/shard_map/all_gather | solution.py:173
  76.7 666.5 %all-gather.28.cloned.1.call-start = ((), (), s32[]{:S(2)}) async-start(), calls=%async_computation.24 | async-start | bytes 14417920 | tf_op jit(solution)/shard_map/all_gather | solution.py:172
  77.5 866.6 %all-gather.32.cloned.1.call-start = ((), (), s32[]{:S(2)}) async-start(), calls=%async_computation.26 | async-start | bytes 14417920 | tf_op jit(solution)/shard_map/all_gather | solution.py:174
  78.2 1070.3 %all-gather.22.cloned.1.call-start = ((), (), s32[]{:S(2)}) async-start(), calls=%async_computation.21 | async-start | bytes 11894784 | tf_op jit(solution)/shard_map/all_gather | solution.py:180
  79.0 1097.4 %all-gather.24.cloned.1.call-start = ((), (), s32[]{:S(2)}) async-start(), calls=%async_computation.22 | async-start | bytes 11894784 | tf_op jit(solution)/shard_map/all_gather | solution.py:181
  79.6 267.8 %copy-start.51 = (f32[2048]{0:T(1024)}, f32[2048]{0:T(1024)S(1)}, u32[]{:S(2)}) copy-start(f32[2048]{0:T(1024)S(1)} %convert_element_type.192) | copy-start | bytes 24580
  80.9 168.4 %copy-start.72 = (f32[256]{0:T(256)}, f32[256]{0:T(256)S(1)}, u32[]{:S(2)}) copy-start(f32[256]{0:T(256)S(1)} %fusion.141) | copy-start | bytes 3076
  103.6 164.4 %copy-start.39 = (bf16[1024,64]{0,1:T(8,128)(2,1)}, bf16[1024,64]{0,1:T(8,128)(2,1)S(1)}, u32[]{:S(2)}) copy-start(bf16[1024,64]{0,1:T(8,128)(2,1)S(1)} %all_gather.51) | copy-start | bytes 393220
  355.0 95.8 %all-to-all-start = ((bf16[8,2,128,2048]{3,2,1,0:T(8,128)(2,1)}), bf16[8,2,128,2048]{3,2,1,0:T(8,128)(2,1)}, u32[]{:S(2)}, u32[]{:S(2)}) async-start(bf16[8,2,128,2048]{3,2,1,0:T(8,128)(2,1)} %bitcast.301), calls=%async_computation | async-start | bytes 16777216 | tf_op jit(solution)/shard_map/all_to_all | solution.py:205
  450.8 312.3 %all-to-all-start.2 = ((bf16[8,2,128,2048]{3,2,1,0:T(8,128)(2,1)}), bf16[8,2,128,2048]{3,2,1,0:T(8,128)(2,1)}, u32[]{:S(2)}, u32[]{:S(2)}) async-start(bf16[8,2,128,2048]{3,2,1,0:T(8,128)(2,1)} %bitcast.313), calls=%async_computation.2 | async-start | bytes 16777216 | tf_op jit(solution)/shard_map/all_to_all | solution.py:229
  459.3 833.7 %all-gather.26.cloned.1.call-start = ((), (), s32[]{:S(2)}) async-start(), calls=%async_computation.23 | async-start | bytes 11894784 | tf_op jit(solution)/shard_map/all_gather | solution.py:182
  1022.6 116.0 %all-to-all-start.3 = ((bf16[8,2,128,2048]{3,2,1,0:T(8,128)(2,1)}), bf16[8,2,128,2048]{3,2,1,0:T(8,128)(2,1)}, u32[]{:S(2)}, u32[]{:S(2)}) async-start(bf16[8,2,128,2048]{3,2,1,0:T(8,128)(2,1)} %copy.137), calls=%async_computation.3 | async-start | bytes 16777216 | tf_op jit(solution)/shard_map/all_to_all | solution.py:254
  1138.6 195.4 %all-to-all-start.1 = ((bf16[8,2,128,2048]{3,2,1,0:T(8,128)(2,1)}), bf16[8,2,128,2048]{3,2,1,0:T(8,128)(2,1)}, u32[]{:S(2)}, u32[]{:S(2)}) async-start(bf16[8,2,128,2048]{3,2,1,0:T(8,128)(2,1)} %copy.134), calls=%async_computation.1 | async-start | bytes 16777216 | tf_op jit(solution)/shard_map/all_to_all | solution.py:214
  1147.7 331.0 %reduce-scatter.15.cloned.1.call-start = ((), (), s32[]{:S(2)}) async-start(), calls=%async_computation.28 | async-start | bytes 327680 | tf_op jit(solution)/shard_map/reduce_scatter | solution.py:327
  1452.2 67.5 %reduce-scatter.13.cloned.1.call-start = ((), (), s32[]{:S(2)}) async-start(), calls=%async_computation.27 | async-start | bytes 2621440 | tf_op jit(solution)/shard_map/reduce_scatter | solution.py:326
  1478.6 336.7 %reduce-scatter.19.cloned.1.call-start = ((), (), s32[]{:S(2)}) async-start(), calls=%async_computation.30 | async-start | bytes 5406720 | tf_op jit(solution)/shard_map/reduce_scatter | solution.py:364
  1527.0 288.3 %reduce-scatter.21.cloned.1.call-start = ((), (), s32[]{:S(2)}) async-start(), calls=%async_computation.31 | async-start | bytes 8650752 | tf_op jit(solution)/shard_map/reduce_scatter | solution.py:366
  1576.6 488.6 %reduce-scatter.25.cloned.1.call-start = ((), (), s32[]{:S(2)}) async-start(), calls=%async_computation.33 | async-start | bytes 23789568 | tf_op jit(solution)/shard_map/reduce_scatter | solution.py:278
  1587.9 731.5 %reduce-scatter.27.cloned.1.call-start = ((), (), s32[]{:S(2)}) async-start(), calls=%async_computation.34 | async-start | bytes 23789568 | tf_op jit(solution)/shard_map/reduce_scatter | solution.py:279
  1598.7 974.8 %reduce-scatter.29.cloned.1.call-start = ((), (), s32[]{:S(2)}) async-start(), calls=%async_computation.35 | async-start | bytes 23789568 | tf_op jit(solution)/shard_map/reduce_scatter | solution.py:280
  1609.8 1152.4 %reduce-scatter.23.cloned.1.call-start = ((), (), s32[]{:S(2)}) async-start(), calls=%async_computation.32 | async-start | bytes 17301504 | tf_op jit(solution)/shard_map/reduce_scatter | solution.py:367
  1620.8 1394.9 %reduce-scatter.17.cloned.1.call-start = ((), (), s32[]{:S(2)}) async-start(), calls=%async_computation.29 | async-start | bytes 25952256 | tf_op jit(solution)/shard_map/reduce_scatter | solution.py:363
  1660.2 1738.8 %reduce-scatter.31.cloned.1.call-start = ((), (), s32[]{:S(2)}) async-start(), calls=%async_computation.36 | async-start | bytes 28835840 | tf_op jit(solution)/shard_map/reduce_scatter | solution.py:256
  1681.9 2102.5 %reduce-scatter.33.cloned.1.call-start = ((), (), s32[]{:S(2)}) async-start(), calls=%async_computation.37 | async-start | bytes 28835840 | tf_op jit(solution)/shard_map/reduce_scatter | solution.py:257
  1704.0 2466.0 %reduce-scatter.35.cloned.1.call-start = ((), (), s32[]{:S(2)}) async-start(), calls=%async_computation.38 | async-start | bytes 28835840 | tf_op jit(solution)/shard_map/reduce_scatter | solution.py:258
  (72 other events, 1728.7 us)
Sparse Core Ops, SparseCore 0:
  10.8 60.4 all-gather.11
  74.2 60.9 all-gather.17
  138.0 94.4 all-gather.15
  234.5 26.6 all-gather.13
  264.0 77.4 all-gather.19
  342.9 199.4 all-gather.29
  544.0 199.2 all-gather.27
  744.8 199.2 all-gather.31
  947.0 89.5 all-gather.21
  1039.3 137.0 all-gather.23
  1179.2 113.6 all-gather.25
  1452.3 15.3 reduce-scatter.14
  1478.7 41.0 reduce-scatter.12
  1527.1 137.0 reduce-scatter.18
  1666.9 145.2 reduce-scatter.20
  1814.9 250.2 reduce-scatter.24
  2067.9 251.4 reduce-scatter.26
  2322.1 251.4 reduce-scatter.28
  2576.4 185.7 reduce-scatter.22
  2769.1 246.5 reduce-scatter.16
  3018.8 380.2 reduce-scatter.30
  3402.0 382.4 reduce-scatter.32
  3787.5 382.3 reduce-scatter.34
where the time goes:
time: 4190 us; the launch traced here: 4180 us
  waiting for transfers between devices  3320 us (79%)
  matrix products  513 us (12%)
  local copies, waits for them, and re-layouts  135 us (3%)
  blocking collectives  93.9 us (2%)
  other arithmetic  69.4 us (2%)
    reduce_scatter x1, waiting for transfers between devices, local(): lax.psum_scatter(down_grad, 'ctx', scatter_dimension=2, tiled=True)  386 us
    reduce_scatter x1, waiting for transfers between devices, local(): lax.psum_scatter(up_grad, 'ctx', scatter_dimension=1, tiled=True)  385 us
    reduce_scatter x1, waiting for transfers between devices, local(): lax.psum_scatter(gate_grad, 'ctx', scatter_dimension=1, tiled=True)  383 us
    reduce_scatter x1, waiting for transfers between devices, local(): lax.psum_scatter(sdown_grad, ('ctx', 'fsdp'), scatter_dimension=0, tiled=...  254 us
    reduce_scatter x1, waiting for transfers between devices, local(): lax.psum_scatter(sup_grad, ('ctx', 'fsdp'), scatter_dimension=0, tiled=True)  254 us
    reduce_scatter x1, waiting for transfers between devices, local(): lax.psum_scatter(query_weight_grad, ('ctx', 'fsdp'), scatter_dimension=0,...  253 us
    reduce_scatter x1, waiting for transfers between devices, local(): lax.psum_scatter(sgate_grad, ('ctx', 'fsdp'), scatter_dimension=0, tiled=...  250 us
    reduce_scatter x1, waiting for transfers between devices, local(): lax.psum_scatter(output_weight_grad, ('ctx', 'fsdp'), scatter_dimension=0...  189 us
  transfers between devices with their start and end apart: 27, of which 20 were waited for; matrix products, arithmetic and copies ran while one was open for 14% of the time, Pallas kernels for 0%

commit v1 on v0

v1 whole, which is shorter than its diff:
```python
import functools

import jax
import jax.numpy as jnp
from jax import lax
from jax.experimental import pallas as pl
from jax.experimental.pallas import tpu as pltpu
from jax.sharding import PartitionSpec as P

HEADS = 16
NOPE = 128
ROPE = 64
LATENT = 512
VDIM = 128
TOP = 6
EXP_DEV = 2


epsilon = 1e-06
rope_base = 10000.0
masked_score = -1e30


def stored_positions(row_index, per_device, block_count):
    device = row_index // per_device
    within = row_index % per_device
    half_block = per_device // 2
    return jnp.where(
        within >= half_block,
        (block_count - 1 - device) * half_block + within - half_block,
        device * half_block + within,
    )


def rotary(values, positions, direction):
    half_rope = values.shape[-1] // 2
    frequency = rope_base ** (-jnp.arange(half_rope, dtype=jnp.float32) / half_rope)
    angles = positions.astype(jnp.float32)[:, None] * frequency[None, :]
    cosine_table = jnp.cos(angles)
    sine_table = direction * jnp.sin(angles)
    if values.ndim == 3:
        cosine_table = cosine_table[:, None, :]
        sine_table = sine_table[:, None, :]
    front_half = values[..., :half_rope]
    back_half = values[..., half_rope:]
    return jnp.concatenate(
        [
            front_half * cosine_table - back_half * sine_table,
            back_half * cosine_table + front_half * sine_table,
        ],
        axis=-1,
    )


def norm_forward(values):
    inverse = lax.rsqrt(jnp.mean(values * values, axis=-1, keepdims=True) + epsilon)
    return (values * inverse, inverse)


def norm_backward(normed_grad, plain, inverse, gain):
    gain_grad = jnp.sum(normed_grad * plain, axis=0)
    scaled = normed_grad * gain
    return (
        inverse * (scaled - plain * jnp.mean(scaled * plain, axis=-1, keepdims=True)),
        gain_grad,
    )


def silu_slope(values):
    sigma = jax.nn.sigmoid(values)
    return (values * sigma, sigma * (1.0 + values * (1.0 - sigma)))


def score_block(query_latent, query_rope, all_latent, all_keys, allowed, score_scale):
    raw_scores = jnp.einsum(
        "thc,kc->htk", query_latent, all_latent, preferred_element_type=jnp.float32
    ) + jnp.einsum("thd,kd->htk", query_rope, all_keys, preferred_element_type=jnp.float32)
    return jnp.where(allowed[None], raw_scores * score_scale, masked_score)


LOW = jnp.bfloat16
FULL = jnp.float32


MESH_ID = pl.DeviceIdType.MESH
BIG_VMEM = 60 * 1024 * 1024


def flip(index, bit):
    return index + bit - 2 * bit * lax.rem(lax.div(index, bit), 2)


def toggled(index, mask):
    for bit in (1, 2, 4):
        if mask & bit:
            index = flip(index, bit)
    return index


def nearest(z, step):
    upper = lax.div(z, 2)
    if step == 0:
        return z
    if step == 1:
        return z + 1 - 2 * upper
    if step == 2:
        return 2 - 2 * lax.rem(z, 2) + upper
    return 3 - 3 * upper


def remote(source, target, send, receive, z, f):
    return pltpu.make_async_remote_copy(
        src_ref=source,
        dst_ref=target,
        send_sem=send,
        recv_sem=receive,
        device_id={"ctx": z, "fsdp": f},
        device_id_type=MESH_ID,
    )


def greet(z, f, masks, ctx_count):
    barrier = pltpu.get_barrier_semaphore()
    for mask in masks:
        pl.semaphore_signal(
            barrier,
            inc=1,
            device_id={"ctx": z, "fsdp": toggled(f, mask)},
            device_id_type=MESH_ID,
        )

    @pl.when(z > 0)
    def _():
        pl.semaphore_signal(
            barrier, inc=1, device_id={"ctx": z - 1, "fsdp": f}, device_id_type=MESH_ID
        )

    @pl.when(z < ctx_count - 1)
    def _():
        pl.semaphore_signal(
            barrier, inc=1, device_id={"ctx": z + 1, "fsdp": f}, device_id_type=MESH_ID
        )

    along = lax.div(z + ctx_count - 1, ctx_count) + lax.div(2 * ctx_count - 2 - z, ctx_count)
    pl.semaphore_wait(barrier, len(masks) + along)


def both_ways(z, block, ctx_count, act):
    @pl.when((block <= z) & (z < ctx_count - 1))
    def _():
        act(0, z + 1)

    @pl.when((block >= z) & (z > 0))
    def _():
        act(1, z - 1)


def gather_kernel(
    ctx_count, shard_ref, out_ref, own_sem, z_send, z_recv, p_send, p_recv, c_send, c_recv
):
    z, f = lax.axis_index("ctx"), lax.axis_index("fsdp")
    core, x_near, y_near = flip(f, 1), flip(f, 2), flip(f, 4)
    far = flip(x_near, 4)
    half = shard_ref.shape[0] // 2
    upper, lower = pl.ds(0, half), pl.ds(half, half)
    greet(z, f, (1, 2, 4), ctx_count)
    own = pltpu.make_async_copy(shard_ref, out_ref.at[z, f], own_sem)
    own.start()
    own.wait()

    def z_copy(block, way, target):
        at = out_ref.at[block, f]
        return remote(at, at, z_send.at[block, way], z_recv.at[block], target, f)

    def p_copy(block, which):
        at = (
            out_ref.at[block, f],
            out_ref.at[block, f],
            out_ref.at[block, x_near, upper],
            out_ref.at[block, y_near, lower],
        )[which]
        to = (x_near, y_near, y_near, x_near)[which]
        return remote(at, at, p_send.at[block, which], p_recv.at[block, which], z, to)

    def p_arrived(block, which):
        at = (
            out_ref.at[block, x_near],
            out_ref.at[block, y_near],
            out_ref.at[block, far, upper],
            out_ref.at[block, far, lower],
        )[which]
        remote(at, at, p_send.at[block, which], p_recv.at[block, which], z, x_near).wait_recv()

    def c_copy(block, which):
        at = out_ref.at[block, (f, x_near, y_near, far)[which]]
        return remote(at, at, c_send.at[block, which], c_recv.at[block, which], z, core)

    def c_arrived(block, which):
        at = out_ref.at[block, flip((f, x_near, y_near, far)[which], 1)]
        remote(at, at, c_send.at[block, which], c_recv.at[block, which], z, core).wait_recv()

    def first(step):
        block = nearest(z, step)
        if step > 0:
            at = out_ref.at[block, f]
            remote(at, at, z_send.at[block, 0], z_recv.at[block], z, core).wait_recv()
        both_ways(z, block, ctx_count, lambda way, to: z_copy(block, way, to).start())
        p_copy(block, 0).start()
        p_copy(block, 1).start()
        c_copy(block, 0).start()

    def second(step):
        block = nearest(z, step)
        for which in (0, 1):
            p_arrived(block, which)
            p_copy(block, which + 2).start()
            c_copy(block, which + 1).start()

    def third(step):
        block = nearest(z, step)
        p_arrived(block, 2)
        p_arrived(block, 3)
        c_copy(block, 3).start()

    for step in range(ctx_count + 2):
        if step < ctx_count:
            first(step)
        if 0 <= step - 1 < ctx_count:
            second(step - 1)
        if 0 <= step - 2 < ctx_count:
            third(step - 2)
    for step in range(ctx_count):
        block = nearest(z, step)
        for which in range(4):
            c_arrived(block, which)
    for step in range(ctx_count):
        block = nearest(z, step)
        both_ways(z, block, ctx_count, lambda way, to: z_copy(block, way, to).wait_send())
        for which in range(4):
            p_copy(block, which).wait_send()
            c_copy(block, which).wait_send()


def gather_dense(shard, ctx_count, fsdp_count):
    rows, width = shard.shape
    dma = pltpu.SemaphoreType.DMA
    out = pl.pallas_call(
        functools.partial(gather_kernel, ctx_count),
        out_shape=jax.ShapeDtypeStruct((ctx_count, fsdp_count, rows, width), shard.dtype),
        in_specs=[pl.BlockSpec(memory_space=pl.ANY)],
        out_specs=pl.BlockSpec(memory_space=pl.ANY),
        scratch_shapes=[
            dma,
            dma((ctx_count, 2)),
            dma((ctx_count,)),
            dma((ctx_count, 4)),
            dma((ctx_count, 4)),
            dma((ctx_count, 4)),
            dma((ctx_count, 4)),
        ],
        compiler_params=pltpu.CompilerParams(collective_id=0, has_side_effects=True),
        cost_estimate=pl.CostEstimate(flops=0, bytes_accessed=400_000_000, transcendentals=0),
    )(shard)
    return out.reshape(ctx_count * fsdp_count * rows, width)


def add_rows(target, rows, *terms):
    @pl.loop(0, rows, step=16)
    def _(start):
        part = pl.ds(pl.multiple_of(start, 16), 16)
        total = terms[0][part, :].astype(FULL)
        for term in terms[1:]:
            total = total + term[part, :].astype(FULL)
        target[part, :] = total.astype(target.dtype)


def scatter_kernel(
    ctx_count,
    grad_ref,
    out_ref,
    mine,
    from_core,
    from_x,
    from_y,
    half_x,
    half_y,
    from_z,
    load_sem,
    c_send,
    c_recv,
    p_send,
    p_recv,
    z_send,
    z_recv,
):
    z, f = lax.axis_index("ctx"), lax.axis_index("fsdp")
    side = lax.rem(f, 2)
    chip = lax.div(f, 2)
    core, x_near, y_near = flip(f, 1), flip(f, 2), flip(f, 4)
    x_chip, y_chip = flip(chip, 1), flip(chip, 2)
    far_chip = flip(x_chip, 2)
    rows = out_ref.shape[0]
    half = rows // 2
    upper, lower = pl.ds(0, half), pl.ds(half, half)
    greet(z, f, (1, 2, 4), ctx_count)

    def load(block):
        return pltpu.make_async_copy(
            grad_ref.at[block, :, side], mine.at[block], load_sem.at[block]
        )

    def c_copy(block):
        return remote(
            grad_ref.at[block, :, 1 - side],
            from_core.at[block],
            c_send.at[block],
            c_recv.at[block],
            z,
            core,
        )

    def p_copy(block, which):
        source, target, to = (
            (mine.at[block, far_chip, upper], half_y.at[block], y_near),
            (mine.at[block, far_chip, lower], half_x.at[block], x_near),
            (mine.at[block, x_chip], from_x.at[block], x_near),
            (mine.at[block, y_chip], from_y.at[block], y_near),
        )[which]
        return remote(source, target, p_send.at[block, which], p_recv.at[block, which], z, to)

    def z_copy(block, way, target):
        return remote(
            mine.at[block, chip],
            from_z.at[way, block],
            z_send.at[block],
            z_recv.at[way, block],
            target,
            f,
        )

    def z_arrived(block, way):
        at = from_z.at[way, block]
        remote(at, at, z_send.at[block], z_recv.at[way, block], z, core).wait_recv()

    order = [nearest(z, ctx_count - 1 - step) for step in range(ctx_count)]

    def first(step):
        block = order[step]
        load(block).wait()
        c_copy(block).wait_recv()
        add_rows(
            mine.at[block, far_chip], rows, mine.at[block, far_chip], from_core.at[block, far_chip]
        )
        p_copy(block, 0).start()
        p_copy(block, 1).start()

    def second(step):
        block = order[step]
        add_rows(
            mine.at[block, x_chip], rows, mine.at[block, x_chip], from_core.at[block, x_chip]
        )
        add_rows(
            mine.at[block, y_chip], rows, mine.at[block, y_chip], from_core.at[block, y_chip]
        )
        p_copy(block, 0).wait_recv()
        x_upper = mine.at[block, x_chip, upper]
        add_rows(x_upper, half, x_upper, half_y.at[block])
        p_copy(block, 2).start()
        p_copy(block, 1).wait_recv()
        y_lower = mine.at[block, y_chip, lower]
        add_rows(y_lower, half, y_lower, half_x.at[block])
        p_copy(block, 3).start()

    def third(step):
        block = order[step]
        p_copy(block, 2).wait_recv()
        p_copy(block, 3).wait_recv()
        own = mine.at[block, chip]
        terms = (own, from_core.at[block, chip], from_x.at[block], from_y.at[block])
        if step == ctx_count - 1:

            @pl.when(z > 0)
            def _():
                z_arrived(block, 0)

            @pl.when(z < ctx_count - 1)
            def _():
                z_arrived(block, 1)

            @pl.when(z == 0)
            def _():
                add_rows(out_ref, rows, *terms, from_z.at[1, block])

            @pl.when(z == ctx_count - 1)
            def _():
                add_rows(out_ref, rows, *terms, from_z.at[0, block])

            @pl.when((z > 0) & (z < ctx_count - 1))
            def _():
                add_rows(out_ref, rows, *terms, from_z.at[0, block], from_z.at[1, block])

            return

        for way, above in ((1, True), (0, False)):
            heading = (block < z) if above else (block > z)
            has_more = (z < ctx_count - 1) if above else (z > 0)

            @pl.when(heading & has_more)
            def _():
                z_arrived(block, way)
                add_rows(own, rows, *terms, from_z.at[way, block])

            @pl.when(heading & jnp.logical_not(has_more))
            def _():
                add_rows(own, rows, *terms)

            @pl.when(heading)
            def _():
                z_copy(block, way, z - 1 if above else z + 1).start()

    for step in range(ctx_count):
        c_copy(order[step]).start()
        load(order[step]).start()
    for step in range(ctx_count + 2):
        if step < ctx_count:
            first(step)
        if 0 <= step - 1 < ctx_count:
            second(step - 1)
        if 0 <= step - 2 < ctx_count:
            third(step - 2)
    for step in range(ctx_count):
        block = order[step]
        c_copy(block).wait_send()
        for which in range(4):
            p_copy(block, which).wait_send()
        if step < ctx_count - 1:
            z_copy(block, 0, z).wait_send()


def scatter_dense(grad, ctx_count, fsdp_count):
    width = grad.shape[1]
    rows = grad.shape[0] // (ctx_count * fsdp_count)
    dma = pltpu.SemaphoreType.DMA
    chips = fsdp_count // 2
    vmem = lambda *shape: pltpu.VMEM(shape + (width,), LOW)
    return pl.pallas_call(
        functools.partial(scatter_kernel, ctx_count),
        out_shape=jax.ShapeDtypeStruct((rows, width), FULL),
        in_specs=[pl.BlockSpec(memory_space=pl.ANY)],
        out_specs=pl.BlockSpec(memory_space=pltpu.VMEM),
        scratch_shapes=[
            vmem(ctx_count, chips, rows),
            vmem(ctx_count, chips, rows),
            vmem(ctx_count, rows),
            vmem(ctx_count, rows),
            vmem(ctx_count, rows // 2),
            vmem(ctx_count, rows // 2),
            vmem(2, ctx_count, rows),
            dma((ctx_count,)),
            dma((ctx_count,)),
            dma((ctx_count,)),
            dma((ctx_count, 4)),
            dma((ctx_count, 4)),
            dma((ctx_count,)),
            dma((2, ctx_count)),
        ],
        compiler_params=pltpu.CompilerParams(
            collective_id=1, has_side_effects=True, vmem_limit_bytes=BIG_VMEM
        ),
        cost_estimate=pl.CostEstimate(flops=0, bytes_accessed=500_000_000, transcendentals=0),
    )(grad.reshape(ctx_count, chips, 2, rows, width))


PEERS = (6, 7, 2, 4, 3, 5, 1)


def dispatch_kernel(
    ctx_count,
    rows_ref,
    choose_ref,
    all_ref,
    out_ref,
    blocks,
    chosen,
    own_sem,
    all_sem,
    keep_sem,
    z_send,
    z_recv,
    p_send,
    p_recv,
):
    z, f = lax.axis_index("ctx"), lax.axis_index("fsdp")
    width = rows_ref.shape[1]
    groups, share = chosen.shape[1], chosen.shape[2]
    greet(z, f, PEERS, ctx_count)
    own = pltpu.make_async_copy(rows_ref, blocks.at[z], own_sem)
    own.start()
    own.wait()

    def z_copy(block, way, target):
        at = blocks.at[block]
        return remote(at, at, z_send.at[block, way], z_recv.at[block], target, f)

    def p_copy(block, place):
        to = toggled(f, PEERS[place])
        return remote(
            chosen.at[block, to],
            out_ref.at[block, f],
            p_send.at[block, place],
            p_recv.at[block, place],
            z,
            to,
        )

    def p_arrived(block, place):
        at = out_ref.at[block, toggled(f, PEERS[place])]
        remote(at, at, p_send.at[block, place], p_recv.at[block, place], z, flip(f, 1)).wait_recv()

    def keep(block):
        return pltpu.make_async_copy(
            chosen.at[block, f], out_ref.at[block, f], keep_sem.at[block]
        )

    def store(block):
        return pltpu.make_async_copy(blocks.at[block], all_ref.at[block], all_sem.at[block])

    for step in range(ctx_count):
        block = nearest(z, step)
        if step > 0:
            at = blocks.at[block]
            remote(at, at, z_send.at[block, 0], z_recv.at[block], z, flip(f, 1)).wait_recv()
        both_ways(z, block, ctx_count, lambda way, to: z_copy(block, way, to).start())
        store(block).start()

        @pl.loop(0, width, step=256)
        def _(start):
            part = pl.ds(pl.multiple_of(start, 256), 256)
            tile = jnp.dot(
                choose_ref[block], blocks[block, :, part], preferred_element_type=FULL
            ).astype(LOW)
            chosen[block, :, :, part] = tile.reshape(groups, share, 256)

        for place in range(len(PEERS)):
            p_copy(block, place).start()
        keep(block).start()
    for step in range(ctx_count):
        block = nearest(z, step)
        store(block).wait()
        keep(block).wait()
        for place in range(len(PEERS)):
            p_arrived(block, place)
    for step in range(ctx_count):
        block = nearest(z, step)
        both_ways(z, block, ctx_count, lambda way, to: z_copy(block, way, to).wait_send())
        for place in range(len(PEERS)):
            p_copy(block, place).wait_send()


def dispatch_rows(rows, chooser, ctx_count, fsdp_count):
    count, width = rows.shape
    share = chooser.shape[1] // fsdp_count
    dma = pltpu.SemaphoreType.DMA
    return pl.pallas_call(
        functools.partial(dispatch_kernel, ctx_count),
        out_shape=(
            jax.ShapeDtypeStruct((ctx_count, count, width), LOW),
            jax.ShapeDtypeStruct((ctx_count, fsdp_count, share, width), LOW),
        ),
        in_specs=[pl.BlockSpec(memory_space=pl.ANY), pl.BlockSpec(memory_space=pltpu.VMEM)],
        out_specs=(pl.BlockSpec(memory_space=pl.ANY), pl.BlockSpec(memory_space=pl.ANY)),
        scratch_shapes=[
            pltpu.VMEM((ctx_count, count, width), LOW),
            pltpu.VMEM((ctx_count, fsdp_count, share, width), LOW),
            dma,
            dma((ctx_count,)),
            dma((ctx_count,)),
            dma((ctx_count, 2)),
            dma((ctx_count,)),
            dma((ctx_count, len(PEERS))),
            dma((ctx_count, len(PEERS))),
        ],
        compiler_params=pltpu.CompilerParams(
            collective_id=2, has_side_effects=True, vmem_limit_bytes=BIG_VMEM
        ),
        cost_estimate=pl.CostEstimate(
            flops=2_000_000_000, bytes_accessed=300_000_000, transcendentals=0
        ),
    )(rows, chooser)


def combine_kernel(
    ctx_count,
    slots_ref,
    mix_ref,
    extra_ref,
    out_ref,
    arrived,
    extra,
    parts,
    from_z,
    keep_sem,
    extra_sem,
    p_send,
    p_recv,
    z_send,
    z_recv,
):
    z, f = lax.axis_index("ctx"), lax.axis_index("fsdp")
    count, width = out_ref.shape
    slots = mix_ref.shape[2]
    greet(z, f, PEERS, ctx_count)

    def p_copy(block, place):
        to = toggled(f, PEERS[place])
        return remote(
            slots_ref.at[block, to],
            arrived.at[block, f],
            p_send.at[block, place],
            p_recv.at[block, place],
            z,
            to,
        )

    def p_arrived(block, place):
        at = arrived.at[block, toggled(f, PEERS[place])]
        remote(at, at, p_send.at[block, place], p_recv.at[block, place], z, flip(f, 1)).wait_recv()

    def keep(block):
        return pltpu.make_async_copy(
            slots_ref.at[block, f], arrived.at[block, f], keep_sem.at[block]
        )

    def load(block):
        return pltpu.make_async_copy(extra_ref.at[block], extra.at[block], extra_sem.at[block])

    def z_copy(block, way, target):
        return remote(
            parts.at[block],
            from_z.at[way, block],
            z_send.at[block],
            z_recv.at[way, block],
            target,
            f,
        )

    def z_arrived(block, way):
        at = from_z.at[way, block]
        remote(at, at, z_send.at[block], z_recv.at[way, block], z, flip(f, 1)).wait_recv()

    def mix(block, target, *ways):
        @pl.loop(0, width, step=256)
        def _(start):
            part = pl.ds(pl.multiple_of(start, 256), 256)
            total = jnp.dot(
                mix_ref[block],
                arrived[block, :, :, part].reshape(slots, 256),
                preferred_element_type=FULL,
            ) + extra[block, :, part].astype(FULL)
            for way in ways:
                total = total + from_z[way, block, :, part].astype(FULL)
            target[:, part] = total.astype(target.dtype)

    order = [nearest(z, ctx_count - 1 - step) for step in range(ctx_count)]
    for block in order:
        for place in range(len(PEERS)):
            p_copy(block, place).start()
        keep(block).start()
        load(block).start()
    for step in range(ctx_count):
        block = order[step]
        keep(block).wait()
        load(block).wait()
        for place in range(len(PEERS)):
            p_arrived(block, place)
        if step < ctx_count - 1:
            for way, above in ((1, True), (0, False)):
                heading = (block < z) if above else (block > z)
                has_more = (z < ctx_count - 1) if above else (z > 0)

                @pl.when(heading & has_more)
                def _():
                    z_arrived(block, way)
                    mix(block, parts.at[block], way)

                @pl.when(heading & jnp.logical_not(has_more))
                def _():
                    mix(block, parts.at[block])

                @pl.when(heading)
                def _():
                    z_copy(block, way, z - 1 if above else z + 1).start()

        else:

            @pl.when(z > 0)
            def _():
                z_arrived(block, 0)

            @pl.when(z < ctx_count - 1)
            def _():
                z_arrived(block, 1)

            @pl.when(z == 0)
            def _():
                mix(block, out_ref, 1)

            @pl.when(z == ctx_count - 1)
            def _():
                mix(block, out_ref, 0)

            @pl.when((z > 0) & (z < ctx_count - 1))
            def _():
                mix(block, out_ref, 0, 1)

    for step in range(ctx_count):
        block = order[step]
        for place in range(len(PEERS)):
            p_copy(block, place).wait_send()
        if step < ctx_count - 1:
            z_copy(block, 0, z).wait_send()


def combine_rows(slots, mixer, extra, ctx_count, fsdp_count):
    share, width = slots.shape[2:]
    count = mixer.shape[1]
    dma = pltpu.SemaphoreType.DMA
    return pl.pallas_call(
        functools.partial(combine_kernel, ctx_count),
        out_shape=jax.ShapeDtypeStruct((count, width), FULL),
        in_specs=[
            pl.BlockSpec(memory_space=pl.ANY),
            pl.BlockSpec(memory_space=pltpu.VMEM),
            pl.BlockSpec(memory_space=pl.ANY),
        ],
        out_specs=pl.BlockSpec(memory_space=pltpu.VMEM),
        scratch_shapes=[
            pltpu.VMEM((ctx_count, fsdp_count, share, width), LOW),
            pltpu.VMEM((ctx_count, count, width), LOW),
            pltpu.VMEM((ctx_count, count, width), LOW),
            pltpu.VMEM((2, ctx_count, count, width), LOW),
            dma((ctx_count,)),
            dma((ctx_count,)),
            dma((ctx_count, len(PEERS))),
            dma((ctx_count, len(PEERS))),
            dma((ctx_count,)),
            dma((2, ctx_count)),
        ],
        compiler_params=pltpu.CompilerParams(
            collective_id=3, has_side_effects=True, vmem_limit_bytes=BIG_VMEM
        ),
        cost_estimate=pl.CostEstimate(
            flops=2_000_000_000, bytes_accessed=300_000_000, transcendentals=0
        ),
    )(slots, mixer, extra)


def mm(subscripts, left, right):
    return jnp.einsum(subscripts, left, right, preferred_element_type=FULL)


def member_pairs(fsdp_count, members, step):
    return [
        (f, f // members * members + (f % members + step) % members) for f in range(fsdp_count)
    ]


def by_member(own, others, member, members):
    if members == 2:
        first = member == 0
        return jnp.stack([jnp.where(first, own, others[0]), jnp.where(first, others[0], own)])
    stack = jnp.stack([own] + others)
    return jnp.take(stack, (member - jnp.arange(members)) % members, axis=0)


def part_of(array, member, step, members):
    return lax.dynamic_index_in_dim(array, (member + step) % members, 0, keepdims=False)


def swap_parts(array, members, fsdp_count):
    member = lax.axis_index("fsdp") % members
    others = [
        lax.ppermute(
            part_of(array, member, step, members), "fsdp", member_pairs(fsdp_count, members, step)
        )
        for step in range(1, members)
    ]
    return by_member(part_of(array, member, 0, members), others, member, members)


def share_parts(array, members, fsdp_count):
    member = lax.axis_index("fsdp") % members
    others = [
        lax.ppermute(array, "fsdp", member_pairs(fsdp_count, members, step))
        for step in range(1, members)
    ]
    return by_member(array, others, member, members)


def sum_parts(array, members, fsdp_count):
    member = lax.axis_index("fsdp") % members
    total = part_of(array, member, 0, members).astype(FULL)
    for step in range(1, members):
        total = total + lax.ppermute(
            part_of(array, member, step, members), "fsdp", member_pairs(fsdp_count, members, step)
        ).astype(FULL)
    return total.astype(LOW)


def along_line(array):
    return lax.all_to_all(array, "ctx", split_axis=0, concat_axis=0, tiled=True)


def bring_expert(pieces, members, fsdp_count):
    swapped = swap_parts(pieces, members, fsdp_count)
    moved = along_line(swapped.reshape((-1,) + swapped.shape[2:]))
    return share_parts(moved, members, fsdp_count).swapaxes(0, 1)


def return_expert(grad, members, fsdp_count):
    moved = along_line(sum_parts(grad, members, fsdp_count))
    moved = moved.reshape((members, EXP_DEV) + moved.shape[1:])
    return swap_parts(moved, members, fsdp_count).swapaxes(0, 1)


def gather_rows(rows, chooser, ctx_count, fsdp_count):
    if (ctx_count, fsdp_count) == (4, 8):
        return dispatch_rows(rows, chooser, ctx_count, fsdp_count)
    every = lax.all_gather(rows, "ctx", axis=0)
    chosen = mm("bst,btd->bsd", chooser, every).astype(LOW)
    chosen = chosen.reshape(ctx_count, fsdp_count, -1, rows.shape[1])
    return every, lax.all_to_all(chosen, "fsdp", split_axis=1, concat_axis=1, tiled=True)


def return_rows(slots, mixer, extra, ctx_count, fsdp_count, urgent):
    if urgent and (ctx_count, fsdp_count) == (4, 8):
        return combine_rows(slots, mixer, extra.astype(LOW), ctx_count, fsdp_count)
    back = lax.all_to_all(slots, "fsdp", split_axis=1, concat_axis=1, tiled=True)
    back = back.reshape(ctx_count, mixer.shape[2], -1)
    total = (mm("bts,bsd->btd", mixer, back) + extra).astype(LOW)
    return lax.psum_scatter(total, "ctx", scatter_dimension=0, tiled=False).astype(FULL)


def gather_shards(shard, ctx_count, fsdp_count):
    if (ctx_count, fsdp_count) == (4, 8):
        return gather_dense(shard, ctx_count, fsdp_count)
    return lax.all_gather(shard, ("ctx", "fsdp"), axis=0, tiled=True)


def scatter_shards(grad, ctx_count, fsdp_count):
    if (ctx_count, fsdp_count) == (4, 8):
        return scatter_dense(grad, ctx_count, fsdp_count)
    return lax.psum_scatter(grad, ("ctx", "fsdp"), scatter_dimension=0, tiled=True).astype(FULL)


def local(
    tokens,
    routes,
    gate_values,
    cotangent,
    attention_gain,
    query_weight,
    latent_weight,
    latent_gain,
    expand_weight,
    output_weight,
    feedforward_gain,
    shared_gate,
    shared_up,
    shared_down,
    expert_gate,
    expert_up,
    expert_down,
):
    row_count = tokens.shape[1]
    model_width = tokens.shape[2]
    ctx_count = lax.axis_size("ctx")
    fsdp_count = lax.axis_size("fsdp")
    device_count = ctx_count * fsdp_count
    experts_total = EXP_DEV * fsdp_count
    capacity = row_count * TOP * 4 // (3 * experts_total)
    members = ctx_count // EXP_DEV
    plane_experts = experts_total // ctx_count
    plane_slots = plane_experts * capacity
    share = capacity // members
    sequence = ctx_count * row_count
    z = lax.axis_index("ctx")
    score_scale = (NOPE + ROPE) ** (-0.5)
    source = tokens[0].astype(FULL)
    cot_low = cotangent[0]
    cot_full = cot_low.astype(FULL)
    positions = stored_positions(
        z * row_count + jnp.arange(row_count, dtype=jnp.int32), row_count, 2 * ctx_count
    )
    key_positions = stored_positions(
        jnp.arange(sequence, dtype=jnp.int32), row_count, 2 * ctx_count
    )
    allowed = positions[:, None] >= key_positions[None, :]

    dense_rows = latent_weight.shape[0]
    gain_rows = latent_gain.shape[0]
    rotary_end = LATENT + ROPE
    query_end = query_weight.shape[1]
    packed = jnp.concatenate(
        [
            query_weight,
            output_weight,
            expand_weight.reshape(dense_rows, -1),
            latent_weight,
            attention_gain[:, None],
            feedforward_gain[:, None],
            jnp.pad(latent_gain, (0, dense_rows - gain_rows))[:, None],
            jnp.zeros((dense_rows, 61), LOW),
        ],
        axis=1,
    )
    packed = gather_shards(packed, ctx_count, fsdp_count)
    full_query = packed[:, :query_end]
    output_end = query_end + output_weight.shape[1]
    full_output = packed[:, query_end:output_end]
    expand_end = output_end + expand_weight.shape[1] * gain_rows // dense_rows
    full_expand = packed[:, output_end:expand_end].reshape(LATENT, -1)
    tail = packed[:, expand_end:]
    full_latent = tail[:, :rotary_end]
    gain_one = tail[:, rotary_end].astype(FULL)
    gain_two = tail[:, rotary_end + 1].astype(FULL)
    gain_latent = (
        tail[:, rotary_end + 2].reshape(device_count, dense_rows)[:, :gain_rows].reshape(LATENT)
    ).astype(FULL)

    all_routes = lax.all_gather(routes[0], "ctx", axis=0)
    all_gates = lax.all_gather(gate_values[0], "ctx", axis=0)
    expert_index = jnp.arange(experts_total, dtype=jnp.int32)
    member_of = (all_routes[..., None] == expert_index).astype(FULL)
    counts = jnp.sum(member_of, axis=2)
    before = jnp.cumsum(counts, axis=1) - counts
    within = jnp.sum(member_of * before[:, :, None, :], axis=-1).astype(jnp.int32)
    slot = jnp.where(
        all_routes % ctx_count == z, all_routes // ctx_count * capacity + within, -1
    )
    hits = slot[..., None] == jnp.arange(plane_slots, dtype=jnp.int32)
    chooser = jnp.sum(hits.astype(FULL), axis=2).astype(LOW)
    mixer = jnp.sum(jnp.where(hits, all_gates[..., None], 0.0), axis=2)
    mixer = mixer.astype(LOW)

    all_cot, arrived_grad = gather_rows(
        cot_low, mixer.swapaxes(1, 2), ctx_count, fsdp_count
    )
    all_cot = all_cot.reshape(sequence, model_width)
    arrived_grad = arrived_grad.reshape(-1, model_width)

    hidden_units = expert_gate.shape[2]

    def parts(weight):
        return weight.reshape(
            (EXP_DEV, members, weight.shape[1] // members) + weight.shape[2:]
        ).swapaxes(0, 1)

    gate_all = bring_expert(parts(expert_gate), members, fsdp_count).reshape(
        model_width, hidden_units
    )
    up_all = bring_expert(parts(expert_up), members, fsdp_count).reshape(model_width, hidden_units)
    down_all = (
        bring_expert(parts(expert_down), members, fsdp_count)
        .transpose(1, 2, 0, 3)
        .reshape(hidden_units, model_width)
    )

    pair = jnp.stack([shared_gate, shared_up])
    pair = lax.all_to_all(pair, "ctx", split_axis=2, concat_axis=1, tiled=True)
    shared_units = pair.shape[2]
    pair = lax.all_gather(pair, "fsdp", axis=0)
    pair = (
        pair.reshape(fsdp_count, 2, ctx_count, dense_rows, shared_units)
        .transpose(1, 2, 0, 3, 4)
        .reshape(2, model_width, shared_units)
    )
    full_sgate, full_sup = (pair[0], pair[1])
    full_sdown = lax.all_gather(shared_down, "fsdp", axis=0, tiled=True)

    plain_one, inverse_one = norm_forward(source)
    normed = (plain_one * gain_one).astype(LOW)
    query_raw = jnp.dot(normed, full_query, preferred_element_type=FULL).reshape(
        row_count, HEADS, NOPE + ROPE
    )
    query_nope = query_raw[:, :, :NOPE].astype(LOW)
    query_rope = rotary(query_raw[:, :, NOPE:], positions, 1.0).astype(LOW)
    latent_raw = jnp.dot(normed, full_latent, preferred_element_type=FULL)
    plain_latent, inverse_latent = norm_forward(latent_raw[:, :LATENT])
    latent_norm = (plain_latent * gain_latent).astype(LOW)
    key_rope = rotary(latent_raw[:, LATENT:], positions, 1.0).astype(LOW)
    keys = lax.all_gather(
        jnp.concatenate([latent_norm, key_rope], axis=1), "ctx", axis=0, tiled=True
    )
    all_latent, all_keys = (keys[:, :LATENT], keys[:, LATENT:])
    expand = full_expand.reshape(LATENT, HEADS, NOPE + VDIM)
    expand_key = expand[:, :, :NOPE]
    expand_value = expand[:, :, NOPE:]
    query_latent = mm("thd,chd->thc", query_nope, expand_key).astype(LOW)
    scores = score_block(query_latent, query_rope, all_latent, all_keys, allowed, score_scale)
    row_max = jnp.max(scores, axis=-1, keepdims=True)
    row_sum = jnp.sum(jnp.exp(scores - row_max), axis=-1, keepdims=True)
    log_total = row_max + jnp.log(row_sum)
    soft_weights = jnp.exp(scores - log_total)
    latent_out = mm("htk,kc->thc", soft_weights.astype(LOW), all_latent).astype(LOW)
    values_out = (
        mm("thc,chv->thv", latent_out, expand_value).astype(LOW).reshape(row_count, HEADS * VDIM)
    )
    middle = source + jnp.dot(values_out, full_output, preferred_element_type=FULL)
    plain_two, inverse_two = norm_forward(middle)
    second = (plain_two * gain_two).astype(LOW)

    all_second, arrived_rows = gather_rows(
        second, chooser.swapaxes(1, 2), ctx_count, fsdp_count
    )
    all_second = all_second.reshape(sequence, model_width)
    arrived_rows = arrived_rows.reshape(-1, model_width)
    gate_pre = jnp.dot(arrived_rows, gate_all, preferred_element_type=FULL)
    up_pre = jnp.dot(arrived_rows, up_all, preferred_element_type=FULL)
    gate_silu, gate_slope = silu_slope(gate_pre)
    hidden_act = (gate_silu * up_pre).astype(LOW)
    hidden_grad = mm("sd,fd->sf", arrived_grad, down_all)
    up_back = (hidden_grad * gate_silu).astype(LOW)
    gate_back = (hidden_grad * up_pre * gate_slope).astype(LOW)
    arrived_back = (mm("sf,df->sd", gate_back, gate_all) + mm("sf,df->sd", up_back, up_all)).astype(
        LOW
    )
    result = jnp.dot(hidden_act, down_all, preferred_element_type=FULL).astype(LOW)

    shared_g = jnp.dot(all_second, full_sgate, preferred_element_type=FULL)
    shared_u = jnp.dot(all_second, full_sup, preferred_element_type=FULL)
    shared_silu, shared_slope = silu_slope(shared_g)
    shared_hidden = (shared_silu * shared_u).astype(LOW)
    shared_hidden_grad = mm("td,fd->tf", all_cot, full_sdown)
    sup_back = (shared_hidden_grad * shared_silu).astype(LOW)
    sgate_back = (shared_hidden_grad * shared_u * shared_slope).astype(LOW)
    shared_second_grad = mm("tf,df->td", sgate_back, full_sgate) + mm(
        "tf,df->td", sup_back, full_sup
    )
    slots_shape = (ctx_count, fsdp_count, share, model_width)
    rows_shape = (ctx_count, row_count, model_width)
    second_grad = return_rows(
        arrived_back.reshape(slots_shape),
        chooser,
        shared_second_grad.reshape(rows_shape),
        ctx_count,
        fsdp_count,
        True,
    )
    shared_out = jnp.dot(shared_hidden, full_sdown, preferred_element_type=FULL)
    out_sum = return_rows(
        result.reshape(slots_shape),
        mixer,
        shared_out.reshape(rows_shape),
        ctx_count,
        fsdp_count,
        False,
    )
    layer_out = (middle + out_sum).astype(LOW)[None]

    gate_grad = mm("sd,sf->df", arrived_rows, gate_back).astype(LOW)
    up_grad = mm("sd,sf->df", arrived_rows, up_back).astype(LOW)
    down_grad = mm("sf,sd->fd", hidden_act, arrived_grad).astype(LOW)

    def give_back(grad, like):
        return return_expert(grad, members, fsdp_count).reshape(like.shape).astype(FULL)

    part_rows = model_width // ctx_count // members
    line_shape = (ctx_count, members, part_rows, hidden_units)
    expert_grads = (
        give_back(gate_grad.reshape(line_shape).swapaxes(0, 1), expert_gate),
        give_back(up_grad.reshape(line_shape).swapaxes(0, 1), expert_up),
        give_back(
            down_grad.reshape(members, hidden_units // members, ctx_count, -1).swapaxes(1, 2),
            expert_down,
        ),
    )
    pair_grad = jnp.stack(
        [mm("td,tf->df", all_second, sgate_back), mm("td,tf->df", all_second, sup_back)]
    ).astype(LOW)
    pair_grad = (
        pair_grad.reshape(2, ctx_count, fsdp_count, dense_rows, shared_units)
        .transpose(2, 0, 1, 3, 4)
        .reshape(fsdp_count, 2, ctx_count * dense_rows, shared_units)
    )
    pair_grad = lax.psum_scatter(pair_grad, "fsdp", scatter_dimension=0, tiled=False)
    pair_grad = lax.all_to_all(
        pair_grad, "ctx", split_axis=1, concat_axis=2, tiled=True
    ).astype(FULL)
    sdown_grad = mm("tf,td->fd", shared_hidden, all_cot).astype(LOW)
    sdown_grad = lax.psum_scatter(sdown_grad, "fsdp", scatter_dimension=0, tiled=True).astype(FULL)

    middle_part, gain_two_grad = norm_backward(second_grad, plain_two, inverse_two, gain_two)
    middle_grad = cot_full + middle_part
    attended_grad = middle_grad.astype(LOW)
    output_weight_grad = mm("tv,td->vd", values_out, attended_grad)
    values_grad = (
        mm("td,vd->tv", attended_grad, full_output).astype(LOW).reshape(row_count, HEADS, VDIM)
    )
    latent_out_grad = mm("thv,chv->thc", values_grad, expand_value).astype(LOW)
    expand_value_grad = mm("thc,thv->chv", latent_out, values_grad)
    scores = score_block(query_latent, query_rope, all_latent, all_keys, allowed, score_scale)
    soft_weights = jnp.exp(scores - log_total)
    soft_grad = mm("thc,kc->htk", latent_out_grad, all_latent)
    all_latent_grad = mm("htk,thc->kc", soft_weights.astype(LOW), latent_out_grad)
    row_inner = jnp.sum(soft_weights * soft_grad, axis=-1, keepdims=True)
    score_grad = (soft_weights * (soft_grad - row_inner) * score_scale).astype(LOW)
    query_latent_grad = mm("htk,kc->thc", score_grad, all_latent).astype(LOW)
    all_latent_grad = all_latent_grad + mm("htk,thc->kc", score_grad, query_latent)
    query_rope_grad = mm("htk,kd->thd", score_grad, all_keys)
    all_keys_grad = mm("htk,thd->kd", score_grad, query_rope)
    keys_part = lax.psum_scatter(
        jnp.concatenate([all_latent_grad, all_keys_grad], axis=1),
        "ctx",
        scatter_dimension=0,
        tiled=True,
    )
    latent_grad, keys_grad = (keys_part[:, :LATENT], keys_part[:, LATENT:])
    query_nope_grad = mm("thc,chd->thd", query_latent_grad, expand_key)
    expand_key_grad = mm("thd,thc->chd", query_nope, query_latent_grad)
    expand_grad = jnp.concatenate([expand_key_grad, expand_value_grad], axis=-1).reshape(
        LATENT, HEADS * (NOPE + VDIM)
    )
    query_grad = (
        jnp.concatenate([query_nope_grad, rotary(query_rope_grad, positions, -1.0)], axis=-1)
        .astype(LOW)
        .reshape(row_count, HEADS * (NOPE + ROPE))
    )
    latent_part_grad, gain_latent_grad = norm_backward(
        latent_grad, plain_latent, inverse_latent, gain_latent
    )
    latent_raw_grad = jnp.concatenate(
        [latent_part_grad, rotary(keys_grad, positions, -1.0)], axis=-1
    ).astype(LOW)
    query_weight_grad = mm("td,tq->dq", normed, query_grad)
    latent_weight_grad = mm("td,tq->dq", normed, latent_raw_grad)
    normed_grad = mm("tq,dq->td", query_grad, full_query) + mm(
        "tq,dq->td", latent_raw_grad, full_latent
    )
    source_part, gain_one_grad = norm_backward(normed_grad, plain_one, inverse_one, gain_one)
    tokens_grad = (middle_grad + source_part)[None]

    gain_latent_column = jnp.pad(
        gain_latent_grad.reshape(device_count, gain_rows), ((0, 0), (0, dense_rows - gain_rows))
    ).reshape(model_width)
    packed_grad = scatter_shards(
        jnp.concatenate(
            [
                query_weight_grad.astype(LOW),
                output_weight_grad.astype(LOW),
                expand_grad.astype(LOW).reshape(model_width, -1),
                latent_weight_grad.astype(LOW),
                gain_one_grad[:, None].astype(LOW),
                gain_two_grad[:, None].astype(LOW),
                gain_latent_column[:, None].astype(LOW),
                jnp.zeros((model_width, 61), LOW),
            ],
            axis=1,
        ),
        ctx_count,
        fsdp_count,
    )
    tail_grad = packed_grad[:, expand_end:]
    return (
        layer_out,
        tokens_grad,
        tail_grad[:, rotary_end],
        packed_grad[:, :query_end],
        tail_grad[:, :rotary_end],
        tail_grad[:gain_rows, rotary_end + 2],
        packed_grad[:, output_end:expand_end].reshape(expand_weight.shape),
        packed_grad[:, query_end:output_end],
        tail_grad[:, rotary_end + 1],
        pair_grad[0],
        pair_grad[1],
        sdown_grad,
        expert_grads[0],
        expert_grads[1],
        expert_grads[2],
    )


def solution(mesh):
    in_specs = (
        P("fsdp", "ctx", None),
        P("fsdp", "ctx", None),
        P("fsdp", "ctx", None),
        P("fsdp", "ctx", None),
        P(("ctx", "fsdp")),
        P(("ctx", "fsdp"), None),
        P(("ctx", "fsdp"), None),
        P(("ctx", "fsdp")),
        P(("ctx", "fsdp"), None),
        P(("ctx", "fsdp"), None),
        P(("ctx", "fsdp")),
        P(("ctx", "fsdp"), None),
        P(("ctx", "fsdp"), None),
        P(("ctx", "fsdp"), None),
        P("fsdp", "ctx", None),
        P("fsdp", "ctx", None),
        P("fsdp", None, "ctx"),
    )
    out_specs = (
        P("fsdp", "ctx", None),
        P("fsdp", "ctx", None),
        P(("ctx", "fsdp")),
        P(("ctx", "fsdp"), None),
        P(("ctx", "fsdp"), None),
        P(("ctx", "fsdp")),
        P(("ctx", "fsdp"), None),
        P(("ctx", "fsdp"), None),
        P(("ctx", "fsdp")),
        P(("ctx", "fsdp"), None),
        P(("ctx", "fsdp"), None),
        P(("ctx", "fsdp"), None),
        P("fsdp", "ctx", None),
        P("fsdp", "ctx", None),
        P("fsdp", None, "ctx"),
    )
    return jax.shard_map(local, mesh=mesh, in_specs=in_specs, out_specs=out_specs, check_vma=False)
```

time: 4190 us -> 1800 us (0.43)
  waiting for transfers between devices: 3320 us -> 128 us
  Pallas kernels: 0 us -> 682 us
  local copies, waits for them, and re-layouts: 135 us -> 266 us
    reduce_scatter x12 -> x4, waiting for transfers between devices: 2390 us -> 0.01 us  [the longest x1 0.01 us: local(): lax.psum_scatter(sdown_grad, 'fsdp', scatter_dimension=0, tiled=True)]
    all_gather x11 -> x3, waiting for transfers between devices: 753 us -> 0.01 us  [the longest x1 0.01 us: local(): lax.all_gather(jnp.concatenate([latent_norm, key_rope], axis=1), 'ctx', a...]
    pallas_call x0 -> x5, Pallas kernels: none -> 682 us  [the longest x2 290 us: dispatch_rows(): pl.pallas_call(functools.partial(dispatch_kernel, ctx_count), out_shape=(...]
    unnamed x2 -> x0, blocking collectives: 82.7 us -> none
    concatenate x0 -> x3, local copies, waits for them, and re-layouts: none -> 53.3 us  [the longest x1 43.3 us: local(): jnp.concatenate([query_weight_grad.astype(LOW), output_weight_grad.astype...]
    dot_general x42 -> x41, matrix products: 499 us -> 452 us  [the longest x32 350 us: mm(): return jnp.einsum(subscripts, left, right, preferred_element_type=FULL)]
    all_to_all x4 -> x8, waiting for transfers between devices: 167 us -> 127 us  [the longest x1 63.7 us: return_rows(): lax.all_to_all(slots, 'fsdp', split_axis=1, concat_axis=1, tiled=True)]
  transfers between devices with their start and end apart: 27 -> 27, of which waited for: 20 -> 3; matrix products, arithmetic and copies ran while one was open for 14% -> 40% of each run, Pallas kernels for 0% -> 23%
where the time goes in v1:
time: 1800 us; the launch traced here: 1780 us
  Pallas kernels  682 us (38%)
  matrix products  476 us (26%)
  local copies, waits for them, and re-layouts  266 us (15%)
  waiting for transfers between devices  128 us (7%)
  other arithmetic  88.5 us (5%)
  blocking collectives  77.2 us (4%)
  starting transfers between devices  50.3 us (3%)
    dot_general x32, matrix products, mm(): return jnp.einsum(subscripts, left, right, preferred_element_type=FULL)  350 us
    pallas_call x2, Pallas kernels, dispatch_rows(): pl.pallas_call(functools.partial(dispatch_kernel, ctx_count), out_shape=(...  290 us
    pallas_call x1, Pallas kernels, gather_dense(): pl.pallas_call(functools.partial(gather_kernel, ctx_count), out_shape=jax...  149 us
    pallas_call x1, Pallas kernels, scatter_dense(): pl.pallas_call(functools.partial(scatter_kernel, ctx_count), out_shape=ja...  125 us
    pallas_call x1, Pallas kernels, combine_rows(): pl.pallas_call(functools.partial(combine_kernel, ctx_count), out_shape=ja...  117 us
    all_to_all x1, waiting for transfers between devices, return_rows(): lax.all_to_all(slots, 'fsdp', split_axis=1, concat_axis=1, tiled=True)  63.7 us
    all_to_all x6, waiting for transfers between devices, along_line(): return lax.all_to_all(array, 'ctx', split_axis=0, concat_axis=0, tiled=True)  63.7 us
    concatenate x1, local copies, waits for them, and re-layouts, local(): jnp.concatenate([query_weight_grad.astype(LOW), output_weight_grad.astype...  43.3 us
  transfers between devices with their start and end apart: 27, of which 3 were waited for; matrix products, arithmetic and copies ran while one was open for 40% of the time, Pallas kernels for 23%

profile of v1, /device:TPU:1, one launch (start us, length us, event | category | flops | bytes accessed | tf_op | source)
XLA Modules:
  0.0 1783.2 jit_solution(4009050749012836892)
XLA Ops:
  12.6 149.1 %shard_map.280 = bf16[4,8,64,6784]{3,2,1,0:T(8,128)(2,1)} custom-call(bf16[64,6784]{1,0:T(8,128)(2,1)} %concatenate.39.shard_ref), custom_call_target="tpu_custom_call" | custom-call | bytes 400000000 | tf_op jit(solution)/shard_map/pallas_call | solution.py:247
  177.6 37.2 %all_to_all.59 = bf16[4,2,45056]{2,1,0:T(2,128)(2,1)} all-to-all(bf16[4,2,45056]{2,1,0:T(2,128)(2,1)} %reshape.603), channel_id=1, replica_groups=mesh['ctx'=4,'fsdp'=8] {'ctx'}, dimensions={0} | all-to-all | bytes 1441792 | tf_op jit(solution)/shard_map/all_to_all | solution.py:970
  238.6 11.0 slice_bitcast_fusion
  254.2 15.8 copy.302
  277.6 29.5 %all_gather.19 = s32[4,256,6]{1,2,0:T(8,128)S(1)} all-gather(s32[1,256,6]{1,2,0:T(8,128)S(1)} %copy.307), channel_id=1, replica_groups=mesh['ctx'=4,'fsdp'=8] {'ctx'}, dimensions={0}, use_global_device_ids=true | all-gather | bytes 30720 | tf_op jit(solution)/shard_map/all_gather | solution.py:931
  309.7 10.5 all_gather.20
  359.0 158.2 %shard_map.282 = (bf16[4,256,2048]{2,1,0:T(8,128)(2,1)}, bf16[4,8,64,2048]{3,2,1,0:T(8,128)(2,1)}) custom-call(bf16[256,2048]{1,0:T(8,128)(2,1)} %bitcast.488, bf16[4,512,256]{2,1,0:T(8,128)(2,1)} %bitcast.475), custom_call_target="tpu_custom_call" | custom-call | flops 2000000000 | bytes 300000000 | tf_op jit(solution)/shard_map/pallas_call | solution.py:564
  528.4 12.9 fusion.22
  541.2 11.0 fusion.133
  565.9 10.6 convolution_convert_fusion.10
  587.3 132.3 %shard_map.281 = (bf16[4,256,2048]{2,1,0:T(8,128)(2,1)}, bf16[4,8,64,2048]{3,2,1,0:T(8,128)(2,1)}) custom-call(bf16[256,2048]{1,0:T(8,128)(2,1)} %multiply_convert_fusion.6.rows_ref, bf16[4,512,256]{2,1,0:T(8,128)(2,1)} %copy.315.choose_ref), custom_call_target="tpu_custom_call" | custom-call | flops 2000000000 | bytes 300000000 | tf_op jit(solution)/shard_map/pallas_call | solution.py:564
  748.7 18.7 %fusion.134 = f32[2048,1408]{1,0:T(8,128)} fusion(bf16[2048,2048]{1,0:T(8,128)(2,1)} %bitcast.504, bf16[2048,1408]{1,0:T(8,128)(2,1)S(1)} %bitcast.457), kind=kOutput, calls=%fused_computation.275 | convolution fusion | flops 11811160064 | bytes 25690112 | tf_op jit(solution)/shard_map/dot_general | solution.py:1019
  774.6 15.8 fusion.138
  790.4 30.3 %multiply_convert_fusion = (bf16[2048,1408]{1,0:T(8,128)(2,1)}, bf16[2048,1408]{1,0:T(8,128)(2,1)}, bf16[2048,1408]{1,0:T(8,128)(2,1)}) fusion(f32[2048,1408]{1,0:T(8,128)} %fusion.138, f32[2048,1408]{1,0:T(8,128)} %fusion.134, bf16[2048,2048]{1,0:T(8,128)(2,1)} %bitcast.505, bf16[2048,1408]{1,0:T(8,128)(2,1)} %bitcast.459), kind=kOutput, calls=%fused_computation.14 | convolution fusion | flops 11854413824 | bytes 54525952 | tf_op jit(solution)/shard_map/dot_general | solution.py:1018
  820.7 17.9 %convolution_convert_fusion.3 = bf16[1408,2048]{1,0:T(8,128)(2,1)} fusion(bf16[2048,1408]{1,0:T(8,128)(2,1)} %get-tuple-element.38, bf16[2048,2048]{1,0:T(8,128)(2,1)} %bitcast.508), kind=kOutput, calls=%fused_computation.28 | convolution fusion | flops 11814043648 | bytes 19922944 | tf_op jit(solution)/shard_map/sf,sd->fd/dot_general | solution.py:759
  838.6 10.7 reshape.575
  882.8 10.9 multiply_convert_fusion.3
  909.4 18.4 %convolution_convert_fusion.2 = bf16[2048,2048]{1,0:T(8,128)(2,1)} fusion(bf16[2048,1408]{1,0:T(8,128)(2,1)} %get-tuple-element.38, bf16[1408,2048]{1,0:T(8,128)(2,1)} %bitcast.462), kind=kOutput, calls=%fused_computation.27 | convolution fusion | flops 11815354368 | bytes 19922944 | tf_op jit(solution)/shard_map/dot_general | solution.py:1028
  943.6 23.1 %all-to-all-done.8 = bf16[4,704,512]{2,1,0:T(8,128)(2,1)S(1)} async-done(((bf16[4,704,512]{2,1,0:T(8,128)(2,1)}), bf16[4,704,512]{2,1,0:T(8,128)(2,1)S(1)}, u32[]{:S(2)}, u32[]{:S(2)}) %all-to-all-start.8) | async-done | bytes 2883616 | tf_op jit(solution)/shard_map/all_to_all | solution.py:811
  982.6 17.2 convolution_convert_fusion.4
  1000.3 17.2 convolution_convert_fusion.5
  1024.5 63.7 %all-to-all-done.3 = bf16[4,8,64,2048]{3,2,0,1:T(8,128)(2,1)} async-done(((bf16[4,8,64,2048]{3,2,0,1:T(8,128)(2,1)}), bf16[4,8,64,2048]{3,2,0,1:T(8,128)(2,1)}, u32[]{:S(2)}, u32[]{:S(2)}) %all-to-all-start.3) | async-done | bytes 8388640 | tf_op jit(solution)/shard_map/all_to_all | solution.py:838
  1093.1 19.5 %fusion.139 = f32[2048,2048]{1,0:T(8,128)} fusion(bf16[2048,1408]{1,0:T(8,128)(2,1)} %get-tuple-element.37, bf16[2048,1408]{1,0:T(8,128)(2,1)} %bitcast.460), kind=kOutput, calls=%fused_computation.280 | convolution fusion | flops 11811160064 | bytes 28311552 | tf_op jit(solution)/shard_map/sf,df->sd/dot_general | solution.py:759
  1142.1 40.5 %all-to-all-done.7 = bf16[4,256,1408]{2,1,0:T(8,128)(2,1)} async-done(((bf16[4,256,1408]{2,1,0:T(8,128)(2,1)}), bf16[4,256,1408]{2,1,0:T(8,128)(2,1)}, u32[]{:S(2)}, u32[]{:S(2)}) %all-to-all-start.7) | async-done | bytes 2883616 | tf_op jit(solution)/shard_map/all_to_all | solution.py:811
  1187.6 21.6 %add_convert_fusion = bf16[2048,2048]{1,0:T(8,128)(2,1)} fusion(f32[2048,2048]{1,0:T(8,128)} %fusion.139, bf16[2048,1408]{1,0:T(8,128)(2,1)} %get-tuple-element.36, bf16[2048,1408]{1,0:T(8,128)(2,1)} %bitcast.454), kind=kOutput, calls=%fused_computation.7 | convolution fusion | flops 11819548672 | bytes 36700160 | tf_op jit(solution)/shard_map/sf,df->sd/dot_general | solution.py:759
  1230.1 117.3 %shard_map.283 = f32[256,2048]{1,0:T(8,128)} custom-call(bf16[4,8,64,2048]{3,2,1,0:T(8,128)(2,1)} %bitcast.447, bf16[4,256,512]{2,1,0:T(8,128)(2,1)} %get-tuple-element.32.mix_ref, bf16[4,256,2048]{2,1,0:T(8,128)(2,1)} %bitcast.474), custom_call_target="tpu_custom_call" | custom-call | flops 2000000000 | bytes 300000000 | tf_op jit(solution)/shard_map/pallas_call | solution.py:728
  1408.6 22.2 %convolution_bitcast_fusion.1 = f32[1024,64]{0,1:T(8,128)S(1)} fusion(bf16[256,16,32]{0,2,1:T(8,128)(2,1)S(1)} %copy-done.33, bf16[256,16,32]{0,2,1:T(8,128)(2,1)S(1)} %copy-done.31, f32[1024,256,16]{1,0,2:T(8,128)} %fusion.18, f32[16,256,1024]{1,2,0:T(8,128)} %get-tuple-element.84, f32[16,256]{1,0:T(8,128)S(1)} %copy-done.51), kind=kOutput, calls=%fused_computation.158 | convolution fusion | flops 567284736 | bytes 34357248 | tf_op jit(solution)/shard_map/htk,thd->kd/dot_general | solution.py:759
  1430.9 26.7 %bitcast_add_fusion.1 = f32[1024,512]{0,1:T(8,128)S(1)} fusion(f32[1024,512,1]{0,1,2:T(8,128)} %fusion.16, bf16[16,512,256]{2,1,0:T(8,128)(2,1)} %convolution_convert_fusion.11, f32[1024,256,16]{1,0,2:T(8,128)} %fusion.18, f32[16,256,1024]{1,2,0:T(8,128)} %get-tuple-element.84, f32[16,256]{1,0:T(8,128)S(1)} %copy-done.51), kind=kOutput, calls=%fused_computation.111 | convolution fusion | flops 4324856832 | bytes 41959424 | tf_op jit(solution)/shard_map/htk,thc->kc/dot_general | solution.py:759
  1474.9 25.3 %convolution_convert_fusion.8 = bf16[512,16,256]{2,0,1:T(8,128)(2,1)} fusion(bf16[1024,576]{0,1:T(8,128)(2,1)} %all-gather.4.cloned.1.call-done, f32[1024,256,16]{1,0,2:T(8,128)} %fusion.18, f32[16,256,1024]{1,2,0:T(8,128)} %get-tuple-element.84, f32[16,256]{1,0:T(8,128)S(1)} %copy-done.51), kind=kOutput, calls=%fused_computation.80 | convolution fusion | flops 4326429696 | bytes 72384512 | tf_op jit(solution)/shard_map/htk,kc->thc/dot_general | solution.py:759
  1521.9 27.6 %convolution_bitcast_fusion = f32[256,16,64]{0,2,1:T(8,128)} fusion(bf16[1024,576]{0,1:T(8,128)(2,1)} %all-gather.4.cloned.1.call-done, f32[1024,256,16]{1,0,2:T(8,128)} %fusion.18, f32[16,256,1024]{1,2,0:T(8,128)} %get-tuple-element.84, f32[16,256]{1,0:T(8,128)S(1)} %copy-done.51), kind=kOutput, calls=%fused_computation.157 | convolution fusion | flops 566236160 | bytes 68321280 | tf_op jit(solution)/shard_map/htk,kd->thd/dot_general | solution.py:759
  1597.1 43.3 %concatenate.49.grad_ref = bf16[4,4,2,64,6784]{4,3,2,1,0:T(8,128)(2,1)} concatenate(bf16[4,4,2,64,3072]{4,3,2,1,0:T(8,128)(2,1)} %bitcast.430, bf16[4,4,2,64,2048]{4,3,2,1,0:T(8,128)(2,1)} %bitcast.431, bf16[4,4,2,64,1024]{4,3,2,1,0:T(8,128)(2,1)} %convert_element_type.395, bf16[4,4,2,64,576]{4,3,2,1,0:T(8,128)(2,1)} %bitcast.441, ...), dimensions={4} | concatenate | bytes 55574528 | tf_op jit(solution)/shard_map/concatenate | solution.py:1147
  1640.4 125.3 %shard_map.284 = f32[64,6784]{1,0:T(8,128)} custom-call(bf16[4,4,2,64,6784]{4,3,2,1,0:T(8,128)(2,1)} %concatenate.49.grad_ref), custom_call_target="tpu_custom_call" | custom-call | bytes 500000000 | tf_op jit(solution)/shard_map/pallas_call | solution.py:446
  (370 shorter events, 476.2 us)
Async XLA Ops:
  7.2 521.2 %all-gather.4.cloned.1.call-start = ((), (), s32[]{:S(2)}) async-start(), calls=%async_computation.13 | async-start | bytes 1474560 | tf_op jit(solution)/shard_map/all_gather | solution.py:992
  165.2 164.8 %copy-start.40 = (f32[2048,1]{0,1:T(1,128)}, f32[2048,1]{0,1:T(1,128)S(1)}, u32[]{:S(2)}) copy-start(f32[2048,1]{0,1:T(1,128)S(1)} %copy.385) | copy-start | bytes 24580
  169.7 347.4 %copy-start.38 = (f32[256,32]{0,1:T(8,128)}, f32[256,32]{0,1:T(8,128)S(1)}, u32[]{:S(2)}) copy-start(f32[256,32]{0,1:T(8,128)S(1)} %get-tuple-element.79) | copy-start | bytes 98308
  170.5 686.1 %all-gather.6.cloned.1.call-start = ((), (), s32[]{:S(2)}) async-start(), calls=%async_computation.14 | async-start | bytes 6488064 | tf_op jit(solution)/shard_map/all_gather | solution.py:972
  222.7 660.1 %all-gather.8.cloned.1.call-start = ((), (), s32[]{:S(2)}) async-start(), calls=%async_computation.15 | async-start | bytes 3244032 | tf_op jit(solution)/shard_map/all_gather | solution.py:979
  224.4 5.4 collective-permute-start.2
  228.0 296.9 %collective-permute-start = (bf16[2,256,1408]{2,1,0:T(8,128)(2,1)}, bf16[2,256,1408]{2,1,0:T(8,128)(2,1)}, u32[]{:S(2)}, u32[]{:S(2)}) collective-permute-start(bf16[2,256,1408]{2,1,0:T(8,128)(2,1)} %dynamic-slice_bitcast_fusion.7), channel_id=1, source_target_pairs={{0,1},{1,0},{2,3},{3,2},{4,5},{5,4},{6,7},{7,6},{8,9},{9,8},{10,11... | collective-permute-start | bytes 4325384 | tf_op jit(solution)/shard_map/ppermute | solution.py:783
  229.3 121.2 %collective-permute-start.4 = (bf16[2,704,512]{2,1,0:T(8,128)(2,1)}, bf16[2,704,512]{2,1,0:T(8,128)(2,1)}, u32[]{:S(2)}, u32[]{:S(2)}) collective-permute-start(bf16[2,704,512]{2,1,0:T(8,128)(2,1)} %dynamic-slice_bitcast_fusion.5), channel_id=1, source_target_pairs={{0,1},{1,0},{2,3},{3,2},{4,5},{5,4},{6,7},{7,6},{8,9},{9,8},{10,11... | collective-permute-start | bytes 4325384 | tf_op jit(solution)/shard_map/ppermute | solution.py:783
  233.9 120.4 %all-to-all-start.1 = ((bf16[4,256,1408]{2,1,0:T(8,128)(2,1)}), bf16[4,256,1408]{2,1,0:T(8,128)(2,1)}, u32[]{:S(2)}, u32[]{:S(2)}) async-start(bf16[4,256,1408]{2,1,0:T(8,128)(2,1)} %bitcast.39), calls=%async_computation.1 | async-start | bytes 5767168 | tf_op jit(solution)/shard_map/all_to_all | solution.py:811
  343.6 232.9 %copy-start = (bf16[512,16,128]{0,2,1:T(8,128)(2,1)}, bf16[512,16,128]{0,2,1:T(8,128)(2,1)S(1)}, u32[]{:S(2)}) copy-start(bf16[512,16,128]{0,2,1:T(8,128)(2,1)S(1)} %copy.373) | copy-start | bytes 6291460
  345.9 238.8 %copy-start.42 = (f32[2048,1]{0,1:T(1,128)}, f32[2048,1]{0,1:T(1,128)S(1)}, u32[]{:S(2)}) copy-start(f32[2048,1]{0,1:T(1,128)S(1)} %copy.386) | copy-start | bytes 24580
  354.3 197.9 %all-to-all-start.2 = ((bf16[4,704,512]{2,1,0:T(8,128)(2,1)}), bf16[4,704,512]{2,1,0:T(8,128)(2,1)}, u32[]{:S(2)}, u32[]{:S(2)}) async-start(bf16[4,704,512]{2,1,0:T(8,128)(2,1)} %bitcast.440), calls=%async_computation.2 | async-start | bytes 5767168 | tf_op jit(solution)/shard_map/all_to_all | solution.py:811
  552.2 173.8 %all-to-all-start = ((bf16[4,256,1408]{2,1,0:T(8,128)(2,1)}), bf16[4,256,1408]{2,1,0:T(8,128)(2,1)}, u32[]{:S(2)}, u32[]{:S(2)}) async-start(bf16[4,256,1408]{2,1,0:T(8,128)(2,1)} %bitcast.439), calls=%async_computation | async-start | bytes 5767168 | tf_op jit(solution)/shard_map/all_to_all | solution.py:811
  565.5 160.6 %collective-permute-start.3 = (bf16[4,256,1408]{2,1,0:T(8,128)(2,1)}, bf16[4,256,1408]{2,1,0:T(8,128)(2,1)}, u32[]{:S(2)}, u32[]{:S(2)}) collective-permute-start(bf16[4,256,1408]{2,1,0:T(8,128)(2,1)} %all-to-all-done.1), channel_id=1, source_target_pairs={{0,1},{1,0},{2,3},{3,2},{4,5},{5,4},{6,7},{7,6},{8,9},{9,8},{10,11... | collective-permute-start | bytes 8650760 | tf_op jit(solution)/shard_map/ppermute | solution.py:794
  578.5 154.3 %collective-permute-start.5 = (bf16[4,704,512]{2,1,0:T(8,128)(2,1)}, bf16[4,704,512]{2,1,0:T(8,128)(2,1)}, u32[]{:S(2)}, u32[]{:S(2)}) collective-permute-start(bf16[4,704,512]{2,1,0:T(8,128)(2,1)} %all-to-all-done.2), channel_id=1, source_target_pairs={{0,1},{1,0},{2,3},{3,2},{4,5},{5,4},{6,7},{7,6},{8,9},{9,8},{10,11... | collective-permute-start | bytes 8650760 | tf_op jit(solution)/shard_map/ppermute | solution.py:794
  726.0 41.4 %collective-permute-start.1 = (bf16[4,256,1408]{2,1,0:T(8,128)(2,1)}, bf16[4,256,1408]{2,1,0:T(8,128)(2,1)}, u32[]{:S(2)}, u32[]{:S(2)}) collective-permute-start(bf16[4,256,1408]{2,1,0:T(8,128)(2,1)} %all-to-all-done), channel_id=1, source_target_pairs={{0,1},{1,0},{2,3},{3,2},{4,5},{5,4},{6,7},{7,6},{8,9},{9,8},{10,11... | collective-permute-start | bytes 8650760 | tf_op jit(solution)/shard_map/ppermute | solution.py:794
  856.1 37.6 %collective-permute-start.10 = (bf16[4,704,512]{2,1,0:T(8,128)(2,1)}, bf16[4,704,512]{2,1,0:T(8,128)(2,1)}, u32[]{:S(2)}, u32[]{:S(2)}) collective-permute-start(bf16[4,704,512]{2,1,0:T(8,128)(2,1)} %bitcast.421), channel_id=1, source_target_pairs={{0,1},{1,0},{2,3},{3,2},{4,5},{5,4},{6,7},{7,6},{8,9},{9,8},{10,11... | collective-permute-start | bytes 8650760 | tf_op jit(solution)/shard_map/ppermute | solution.py:804
  897.9 68.9 %all-to-all-start.8 = ((bf16[4,704,512]{2,1,0:T(8,128)(2,1)}), bf16[4,704,512]{2,1,0:T(8,128)(2,1)S(1)}, u32[]{:S(2)}, u32[]{:S(2)}) async-start(bf16[4,704,512]{2,1,0:T(8,128)(2,1)} %fusion.13), calls=%async_computation.12 | async-start | bytes 5767168 | tf_op jit(solution)/shard_map/all_to_all | solution.py:811
  901.6 449.8 %reduce-scatter.11.cloned.1.call-start = ((), (), s32[]{:S(2)}) async-start(), calls=%async_computation.19 | async-start | bytes 3244032 | tf_op jit(solution)/shard_map/reduce_scatter | solution.py:1091
  966.8 248.1 %copy-start.8 = (bf16[4,704,512]{2,1,0:T(8,128)(2,1)}, bf16[4,704,512]{2,1,0:T(8,128)(2,1)S(1)}, u32[]{:S(2)}) copy-start(bf16[4,704,512]{2,1,0:T(8,128)(2,1)S(1)} %all-to-all-done.8) | copy-start | bytes 8650756
  966.8 121.4 %all-to-all-start.3 = ((bf16[4,8,64,2048]{3,2,0,1:T(8,128)(2,1)}), bf16[4,8,64,2048]{3,2,0,1:T(8,128)(2,1)}, u32[]{:S(2)}, u32[]{:S(2)}) async-start(bf16[4,8,64,2048]{3,2,0,1:T(8,128)(2,1)} %copy.319), calls=%async_computation.3 | async-start | bytes 16777216 | tf_op jit(solution)/shard_map/all_to_all | solution.py:838
  972.4 396.1 %reduce-scatter.9.cloned.1.call-start = ((), (), s32[]{:S(2)}) async-start(), calls=%async_computation.18 | async-start | bytes 7077888 | tf_op jit(solution)/shard_map/reduce_scatter | solution.py:1086
  1000.0 22.1 %collective-permute-start.8 = (bf16[4,256,1408]{2,1,0:T(8,128)(2,1)S(1)}, bf16[4,256,1408]{2,1,0:T(8,128)(2,1)S(1)}, u32[]{:S(2)}, u32[]{:S(2)}) collective-permute-start(bf16[4,256,1408]{2,1,0:T(8,128)(2,1)S(1)} %dynamic-slice_bitcast_fusion), channel_id=1, source_target_pairs={{0,1},{1,0},{2,3},{3,2},{4,5},{5,4},{6,7},{7,6},{8,9},{9,8},{10,11... | collective-permute-start | bytes 8650760 | tf_op jit(solution)/shard_map/ppermute | solution.py:804
  1021.8 115.3 %collective-permute-start.6 = (bf16[4,256,1408]{2,1,0:T(8,128)(2,1)}, bf16[4,256,1408]{2,1,0:T(8,128)(2,1)}, u32[]{:S(2)}, u32[]{:S(2)}) collective-permute-start(bf16[4,256,1408]{2,1,0:T(8,128)(2,1)} %dynamic-slice_bitcast_fusion.1), channel_id=1, source_target_pairs={{0,1},{1,0},{2,3},{3,2},{4,5},{5,4},{6,7},{7,6},{8,9},{9,8},{10,11... | collective-permute-start | bytes 8650760 | tf_op jit(solution)/shard_map/ppermute | solution.py:804
  1088.2 94.3 %all-to-all-start.7 = ((bf16[4,256,1408]{2,1,0:T(8,128)(2,1)}), bf16[4,256,1408]{2,1,0:T(8,128)(2,1)}, u32[]{:S(2)}, u32[]{:S(2)}) async-start(bf16[4,256,1408]{2,1,0:T(8,128)(2,1)} %fusion.14), calls=%async_computation.11 | async-start | bytes 5767168 | tf_op jit(solution)/shard_map/all_to_all | solution.py:811
  1092.9 283.0 %reduce-scatter.5.cloned.1.call-start = ((), (), s32[]{:S(2)}) async-start(), calls=%async_computation.16 | async-start | bytes 5242880 | tf_op jit(solution)/shard_map/reduce_scatter | solution.py:841
  1182.6 170.7 %all-to-all-start.6 = ((bf16[4,256,1408]{2,1,0:T(8,128)(2,1)}), bf16[4,256,1408]{2,1,0:T(8,128)(2,1)}, u32[]{:S(2)}, u32[]{:S(2)}) async-start(bf16[4,256,1408]{2,1,0:T(8,128)(2,1)} %fusion.15), calls=%async_computation.10 | async-start | bytes 5767168 | tf_op jit(solution)/shard_map/all_to_all | solution.py:811
  1216.0 142.0 %collective-permute-start.11 = (bf16[2,704,512]{2,1,0:T(8,128)(2,1)}, bf16[2,704,512]{2,1,0:T(8,128)(2,1)}, u32[]{:S(2)}, u32[]{:S(2)}) collective-permute-start(bf16[2,704,512]{2,1,0:T(8,128)(2,1)} %dynamic-slice_bitcast_fusion.2), channel_id=1, source_target_pairs={{0,1},{1,0},{2,3},{3,2},{4,5},{5,4},{6,7},{7,6},{8,9},{9,8},{10,11... | collective-permute-start | bytes 4325384 | tf_op jit(solution)/shard_map/ppermute | solution.py:783
  1230.0 133.1 %collective-permute-start.9 = (bf16[2,256,1408]{2,1,0:T(8,128)(2,1)}, bf16[2,256,1408]{2,1,0:T(8,128)(2,1)}, u32[]{:S(2)}, u32[]{:S(2)}) collective-permute-start(bf16[2,256,1408]{2,1,0:T(8,128)(2,1)} %dynamic-slice_bitcast_fusion.3), channel_id=1, source_target_pairs={{0,1},{1,0},{2,3},{3,2},{4,5},{5,4},{6,7},{7,6},{8,9},{9,8},{10,11... | collective-permute-start | bytes 4325384 | tf_op jit(solution)/shard_map/ppermute | solution.py:783
  1355.9 103.4 %collective-permute-start.7 = (bf16[2,256,1408]{2,1,0:T(8,128)(2,1)}, bf16[2,256,1408]{2,1,0:T(8,128)(2,1)}, u32[]{:S(2)}, u32[]{:S(2)}) collective-permute-start(bf16[2,256,1408]{2,1,0:T(8,128)(2,1)} %dynamic-slice_bitcast_fusion.4), channel_id=1, source_target_pairs={{0,1},{1,0},{2,3},{3,2},{4,5},{5,4},{6,7},{7,6},{8,9},{9,8},{10,11... | collective-permute-start | bytes 4325384 | tf_op jit(solution)/shard_map/ppermute | solution.py:783
  1371.5 93.2 %all-to-all-start.5 = ((bf16[2,256,704]{2,0,1:T(2,128)(2,1)}), bf16[2,256,704]{2,0,1:T(2,128)(2,1)}, u32[]{:S(2)}, u32[]{:S(2)}) async-start(bf16[2,256,704]{2,0,1:T(2,128)(2,1)} %copy.346), calls=%async_computation.8 | async-start | bytes 1572864 | tf_op jit(solution)/shard_map/all_to_all | solution.py:1087
  1375.9 184.8 %reduce-scatter.7.cloned.1.call-start = ((), (), s32[]{:S(2)}) async-start(), calls=%async_computation.17 | async-start | bytes 2949120 | tf_op jit(solution)/shard_map/reduce_scatter | solution.py:1112
  (67 other events, 1200.7 us)
Sparse Core Ops, SparseCore 0:
  170.6 44.7 all-gather.3
  222.8 42.2 all-gather.5
  267.0 31.2 all-gather.7
  909.6 45.2 reduce-scatter.10
  982.7 109.5 reduce-scatter.8
  1137.3 123.0 reduce-scatter.4
  1459.4 49.1 reduce-scatter.6

commit v2 on v1

--- a/solution.py
+++ b/solution.py
@@ -119,27 +119,29 @@
     )
 
 
-def greet(z, f, masks, ctx_count):
+def greet(z, f, masks, ctx_count, whole_line=False):
     barrier = pltpu.get_barrier_semaphore()
+
+    def hello(to_z, to_f):
+        pl.semaphore_signal(
+            barrier, inc=1, device_id={"ctx": to_z, "fsdp": to_f}, device_id_type=MESH_ID
+        )
+
     for mask in masks:
-        pl.semaphore_signal(
-            barrier,
-            inc=1,
-            device_id={"ctx": z, "fsdp": toggled(f, mask)},
-            device_id_type=MESH_ID,
-        )
+        hello(z, toggled(f, mask))
+    if whole_line:
+        for step in range(1, ctx_count):
+            hello(lax.rem(z + step, ctx_count), f)
+        pl.semaphore_wait(barrier, len(masks) + ctx_count - 1)
+        return
 
     @pl.when(z > 0)
     def _():
-        pl.semaphore_signal(
-            barrier, inc=1, device_id={"ctx": z - 1, "fsdp": f}, device_id_type=MESH_ID
-        )
+        hello(z - 1, f)
 
     @pl.when(z < ctx_count - 1)
     def _():
-        pl.semaphore_signal(
-            barrier, inc=1, device_id={"ctx": z + 1, "fsdp": f}, device_id_type=MESH_ID
-        )
+        hello(z + 1, f)
 
     along = lax.div(z + ctx_count - 1, ctx_count) + lax.div(2 * ctx_count - 2 - z, ctx_count)
     pl.semaphore_wait(barrier, len(masks) + along)
@@ -155,113 +157,174 @@
         act(1, z - 1)
 
 
-def gather_kernel(
-    ctx_count, shard_ref, out_ref, own_sem, z_send, z_recv, p_send, p_recv, c_send, c_recv
-):
+def halves(rows, width):
+    if rows % 32 == 0:
+        return tuple((pl.ds(start, rows // 2), slice(None)) for start in (0, rows // 2))
+    return tuple((slice(None), pl.ds(start, width // 2)) for start in (0, width // 2))
+
+
+def gather_kernel(ctx_count, kinds, *refs):
+    count = len(kinds)
+    shards, outs = refs[:count], refs[count : 2 * count]
+    own_sem, z_send, z_recv, p_send, p_recv, c_send, c_recv = refs[2 * count :]
     z, f = lax.axis_index("ctx"), lax.axis_index("fsdp")
     core, x_near, y_near = flip(f, 1), flip(f, 2), flip(f, 4)
     far = flip(x_near, 4)
-    half = shard_ref.shape[0] // 2
-    upper, lower = pl.ds(0, half), pl.ds(half, half)
-    greet(z, f, (1, 2, 4), ctx_count)
-    own = pltpu.make_async_copy(shard_ref, out_ref.at[z, f], own_sem)
-    own.start()
-    own.wait()
-
-    def z_copy(block, way, target):
-        at = out_ref.at[block, f]
-        return remote(at, at, z_send.at[block, way], z_recv.at[block], target, f)
-
-    def p_copy(block, which):
+    greet(z, f, (1, 2, 4), ctx_count, True)
+
+    def slot(item, step):
+        return 0 if kinds[item] == "plane" else nearest(z, step)
+
+    def steps(item, step):
+        return step == 0 if kinds[item] == "plane" else 0 <= step < ctx_count
+
+    def z_view(item, block):
+        return outs[item].at[block] if kinds[item] == "column" else outs[item].at[block, f]
+
+    def own(item):
+        source = shards[item].at[z] if kinds[item] == "line" else shards[item]
+        return pltpu.make_async_copy(source, z_view(item, slot(item, 0)), own_sem.at[item])
+
+    def z_copy(item, block, way, target):
+        at = z_view(item, block)
+        return remote(at, at, z_send.at[item, block, way], z_recv.at[item, block], target, f)
+
+    def piece(item, step):
+        target = lax.rem(z + step, ctx_count)
+        return remote(
+            shards[item].at[target],
+            outs[item].at[z, f],
+            z_send.at[item, target, 0],
+            z_recv.at[item, z],
+            target,
+            f,
+        )
+
+    def part(item, block, at, which):
+        rows, columns = halves(*outs[item].shape[2:])[which]
+        return outs[item].at[block, at, rows, columns]
+
+    def p_copy(item, block, which):
         at = (
-            out_ref.at[block, f],
-            out_ref.at[block, f],
-            out_ref.at[block, x_near, upper],
-            out_ref.at[block, y_near, lower],
-        )[which]
+            lambda: outs[item].at[block, f],
+            lambda: outs[item].at[block, f],
+            lambda: part(item, block, x_near, 0),
+            lambda: part(item, block, y_near, 1),
+        )[which]()
         to = (x_near, y_near, y_near, x_near)[which]
-        return remote(at, at, p_send.at[block, which], p_recv.at[block, which], z, to)
-
-    def p_arrived(block, which):
+        sems = (p_send.at[item, block, which], p_recv.at[item, block, which])
+        return remote(at, at, *sems, z, to)
+
+    def p_arrived(item, block, which):
         at = (
-            out_ref.at[block, x_near],
-            out_ref.at[block, y_near],
-            out_ref.at[block, far, upper],
-            out_ref.at[block, far, lower],
-        )[which]
-        remote(at, at, p_send.at[block, which], p_recv.at[block, which], z, x_near).wait_recv()
-
-    def c_copy(block, which):
-        at = out_ref.at[block, (f, x_near, y_near, far)[which]]
-        return remote(at, at, c_send.at[block, which], c_recv.at[block, which], z, core)
-
-    def c_arrived(block, which):
-        at = out_ref.at[block, flip((f, x_near, y_near, far)[which], 1)]
-        remote(at, at, c_send.at[block, which], c_recv.at[block, which], z, core).wait_recv()
-
-    def first(step):
-        block = nearest(z, step)
-        if step > 0:
-            at = out_ref.at[block, f]
-            remote(at, at, z_send.at[block, 0], z_recv.at[block], z, core).wait_recv()
-        both_ways(z, block, ctx_count, lambda way, to: z_copy(block, way, to).start())
-        p_copy(block, 0).start()
-        p_copy(block, 1).start()
-        c_copy(block, 0).start()
-
-    def second(step):
-        block = nearest(z, step)
+            lambda: outs[item].at[block, x_near],
+            lambda: outs[item].at[block, y_near],
+            lambda: part(item, block, far, 0),
+            lambda: part(item, block, far, 1),
+        )[which]()
+        sems = (p_send.at[item, block, which], p_recv.at[item, block, which])
+        remote(at, at, *sems, z, x_near).wait_recv()
+
+    def c_copy(item, block, which):
+        at = outs[item].at[block, (f, x_near, y_near, far)[which]]
+        sems = (c_send.at[item, block, which], c_recv.at[item, block, which])
+        return remote(at, at, *sems, z, core)
+
+    def c_arrived(item, block, which):
+        at = outs[item].at[block, flip((f, x_near, y_near, far)[which], 1)]
+        sems = (c_send.at[item, block, which], c_recv.at[item, block, which])
+        remote(at, at, *sems, z, core).wait_recv()
+
+    def first(item, step):
+        block = slot(item, step)
+        if step == 0:
+            own(item).wait()
+        else:
+            at = z_view(item, block)
+            sems = (z_send.at[item, block, 0], z_recv.at[item, block])
+            remote(at, at, *sems, z, core).wait_recv()
+        if kinds[item] in ("all", "column"):
+            both_ways(z, block, ctx_count, lambda way, to: z_copy(item, block, way, to).start())
+        if kinds[item] != "column":
+            p_copy(item, block, 0).start()
+            p_copy(item, block, 1).start()
+            c_copy(item, block, 0).start()
+
+    def second(item, step):
+        block = slot(item, step)
         for which in (0, 1):
-            p_arrived(block, which)
-            p_copy(block, which + 2).start()
-            c_copy(block, which + 1).start()
-
-    def third(step):
-        block = nearest(z, step)
-        p_arrived(block, 2)
-        p_arrived(block, 3)
-        c_copy(block, 3).start()
-
+            p_arrived(item, block, which)
+            p_copy(item, block, which + 2).start()
+            c_copy(item, block, which + 1).start()
+
+    def third(item, step):
+        block = slot(item, step)
+        p_arrived(item, block, 2)
+        p_arrived(item, block, 3)
+        c_copy(item, block, 3).start()
+
+    for item in range(count):
+        own(item).start()
+        if kinds[item] == "line":
+            for step in range(1, ctx_count):
+                piece(item, step).start()
     for step in range(ctx_count + 2):
-        if step < ctx_count:
-            first(step)
-        if 0 <= step - 1 < ctx_count:
-            second(step - 1)
-        if 0 <= step - 2 < ctx_count:
-            third(step - 2)
-    for step in range(ctx_count):
-        block = nearest(z, step)
-        for which in range(4):
-            c_arrived(block, which)
-    for step in range(ctx_count):
-        block = nearest(z, step)
-        both_ways(z, block, ctx_count, lambda way, to: z_copy(block, way, to).wait_send())
-        for which in range(4):
-            p_copy(block, which).wait_send()
-            c_copy(block, which).wait_send()
-
-
-def gather_dense(shard, ctx_count, fsdp_count):
-    rows, width = shard.shape
+        for lag, stage in ((0, first), (1, second), (2, third)):
+            for item in range(count):
+                if steps(item, step - lag) and (lag == 0 or kinds[item] != "column"):
+                    stage(item, step - lag)
+    for item in range(count):
+        for step in range(ctx_count):
+            if not steps(item, step):
+                continue
+            block = slot(item, step)
+            if kinds[item] != "column":
+                for which in range(4):
+                    c_arrived(item, block, which)
+                    p_copy(item, block, which).wait_send()
+                    c_copy(item, block, which).wait_send()
+            if kinds[item] == "line" and step > 0:
+                piece(item, step).wait_send()
+            if kinds[item] in ("all", "column"):
+                both_ways(
+                    z, block, ctx_count, lambda way, to: z_copy(item, block, way, to).wait_send()
+                )
+
+
+def gather_arrays(items, ctx_count, fsdp_count):
+    kinds = tuple(kind for kind, shard in items)
+    shards = [shard for kind, shard in items]
+    lead = {
+        "all": (ctx_count, fsdp_count),
+        "line": (ctx_count, fsdp_count),
+        "plane": (1, fsdp_count),
+        "column": (ctx_count,),
+    }
+    shapes = [
+        lead[kind] + (shard.shape[1:] if kind == "line" else shard.shape) for kind, shard in items
+    ]
+    count = len(items)
     dma = pltpu.SemaphoreType.DMA
-    out = pl.pallas_call(
-        functools.partial(gather_kernel, ctx_count),
-        out_shape=jax.ShapeDtypeStruct((ctx_count, fsdp_count, rows, width), shard.dtype),
-        in_specs=[pl.BlockSpec(memory_space=pl.ANY)],
-        out_specs=pl.BlockSpec(memory_space=pl.ANY),
+    four = dma((count, ctx_count, 4))
+    return pl.pallas_call(
+        functools.partial(gather_kernel, ctx_count, kinds),
+        out_shape=[
+            jax.ShapeDtypeStruct(shape, shard.dtype) for shape, shard in zip(shapes, shards)
+        ],
+        in_specs=[pl.BlockSpec(memory_space=pl.ANY)] * count,
+        out_specs=[pl.BlockSpec(memory_space=pl.ANY)] * count,
         scratch_shapes=[
-            dma,
-            dma((ctx_count, 2)),
-            dma((ctx_count,)),
-            dma((ctx_count, 4)),
-            dma((ctx_count, 4)),
-            dma((ctx_count, 4)),
-            dma((ctx_count, 4)),
+            dma((count,)),
+            dma((count, ctx_count, 2)),
+            dma((count, ctx_count)),
+            four,
+            four,
+            four,
+            four,
         ],
         compiler_params=pltpu.CompilerParams(collective_id=0, has_side_effects=True),
-        cost_estimate=pl.CostEstimate(flops=0, bytes_accessed=400_000_000, transcendentals=0),
-    )(shard)
-    return out.reshape(ctx_count * fsdp_count * rows, width)
+        cost_estimate=pl.CostEstimate(flops=0, bytes_accessed=500_000_000, transcendentals=0),
+    )(*shards)
 
 
 def add_rows(target, rows, *terms):
@@ -274,201 +337,201 @@
         target[part, :] = total.astype(target.dtype)
 
 
-def scatter_kernel(
-    ctx_count,
-    grad_ref,
-    out_ref,
-    mine,
-    from_core,
-    from_x,
-    from_y,
-    half_x,
-    half_y,
-    from_z,
-    load_sem,
-    c_send,
-    c_recv,
-    p_send,
-    p_recv,
-    z_send,
-    z_recv,
-):
+def scatter_kernel(ctx_count, count, *refs):
+    grads, outs = refs[:count], refs[count : 2 * count]
+    banks = [refs[(2 + kind) * count : (3 + kind) * count] for kind in range(7)]
+    load_sem, c_send, c_recv, p_send, p_recv, z_send, z_recv = refs[9 * count :]
     z, f = lax.axis_index("ctx"), lax.axis_index("fsdp")
     side = lax.rem(f, 2)
     chip = lax.div(f, 2)
     core, x_near, y_near = flip(f, 1), flip(f, 2), flip(f, 4)
     x_chip, y_chip = flip(chip, 1), flip(chip, 2)
     far_chip = flip(x_chip, 2)
-    rows = out_ref.shape[0]
-    half = rows // 2
-    upper, lower = pl.ds(0, half), pl.ds(half, half)
     greet(z, f, (1, 2, 4), ctx_count)
-
-    def load(block):
-        return pltpu.make_async_copy(
-            grad_ref.at[block, :, side], mine.at[block], load_sem.at[block]
-        )
-
-    def c_copy(block):
-        return remote(
-            grad_ref.at[block, :, 1 - side],
-            from_core.at[block],
-            c_send.at[block],
-            c_recv.at[block],
-            z,
-            core,
-        )
-
-    def p_copy(block, which):
-        source, target, to = (
-            (mine.at[block, far_chip, upper], half_y.at[block], y_near),
-            (mine.at[block, far_chip, lower], half_x.at[block], x_near),
-            (mine.at[block, x_chip], from_x.at[block], x_near),
-            (mine.at[block, y_chip], from_y.at[block], y_near),
-        )[which]
-        return remote(source, target, p_send.at[block, which], p_recv.at[block, which], z, to)
-
-    def z_copy(block, way, target):
-        return remote(
-            mine.at[block, chip],
-            from_z.at[way, block],
-            z_send.at[block],
-            z_recv.at[way, block],
-            target,
-            f,
-        )
-
-    def z_arrived(block, way):
-        at = from_z.at[way, block]
-        remote(at, at, z_send.at[block], z_recv.at[way, block], z, core).wait_recv()
-
     order = [nearest(z, ctx_count - 1 - step) for step in range(ctx_count)]
 
-    def first(step):
-        block = order[step]
-        load(block).wait()
-        c_copy(block).wait_recv()
-        add_rows(
-            mine.at[block, far_chip], rows, mine.at[block, far_chip], from_core.at[block, far_chip]
-        )
-        p_copy(block, 0).start()
-        p_copy(block, 1).start()
-
-    def second(step):
-        block = order[step]
-        add_rows(
-            mine.at[block, x_chip], rows, mine.at[block, x_chip], from_core.at[block, x_chip]
-        )
-        add_rows(
-            mine.at[block, y_chip], rows, mine.at[block, y_chip], from_core.at[block, y_chip]
-        )
-        p_copy(block, 0).wait_recv()
-        x_upper = mine.at[block, x_chip, upper]
-        add_rows(x_upper, half, x_upper, half_y.at[block])
-        p_copy(block, 2).start()
-        p_copy(block, 1).wait_recv()
-        y_lower = mine.at[block, y_chip, lower]
-        add_rows(y_lower, half, y_lower, half_x.at[block])
-        p_copy(block, 3).start()
-
-    def third(step):
-        block = order[step]
-        p_copy(block, 2).wait_recv()
-        p_copy(block, 3).wait_recv()
-        own = mine.at[block, chip]
-        terms = (own, from_core.at[block, chip], from_x.at[block], from_y.at[block])
-        if step == ctx_count - 1:
-
-            @pl.when(z > 0)
-            def _():
-                z_arrived(block, 0)
-
-            @pl.when(z < ctx_count - 1)
-            def _():
-                z_arrived(block, 1)
-
-            @pl.when(z == 0)
-            def _():
-                add_rows(out_ref, rows, *terms, from_z.at[1, block])
-
-            @pl.when(z == ctx_count - 1)
-            def _():
-                add_rows(out_ref, rows, *terms, from_z.at[0, block])
-
-            @pl.when((z > 0) & (z < ctx_count - 1))
-            def _():
-                add_rows(out_ref, rows, *terms, from_z.at[0, block], from_z.at[1, block])
-
-            return
-
-        for way, above in ((1, True), (0, False)):
-            heading = (block < z) if above else (block > z)
-            has_more = (z < ctx_count - 1) if above else (z > 0)
-
-            @pl.when(heading & has_more)
-            def _():
-                z_arrived(block, way)
-                add_rows(own, rows, *terms, from_z.at[way, block])
-
-            @pl.when(heading & jnp.logical_not(has_more))
-            def _():
-                add_rows(own, rows, *terms)
-
-            @pl.when(heading)
-            def _():
-                z_copy(block, way, z - 1 if above else z + 1).start()
-
+    def work(item):
+        grad_ref, out_ref = grads[item], outs[item]
+        mine, from_core, from_x, from_y, half_x, half_y, from_z = [bank[item] for bank in banks]
+        rows, width = out_ref.shape
+        left, right = pl.ds(0, width // 2), pl.ds(width // 2, width // 2)
+
+        def load(block):
+            return pltpu.make_async_copy(
+                grad_ref.at[block, :, side], mine.at[block], load_sem.at[item, block]
+            )
+
+        def c_copy(block):
+            return remote(
+                grad_ref.at[block, :, 1 - side],
+                from_core.at[block],
+                c_send.at[item, block],
+                c_recv.at[item, block],
+                z,
+                core,
+            )
+
+        def p_copy(block, which):
+            source, target, to = (
+                (mine.at[block, far_chip, :, left], half_y.at[block], y_near),
+                (mine.at[block, far_chip, :, right], half_x.at[block], x_near),
+                (mine.at[block, x_chip], from_x.at[block], x_near),
+                (mine.at[block, y_chip], from_y.at[block], y_near),
+            )[which]
+            sems = (p_send.at[item, block, which], p_recv.at[item, block, which])
+            return remote(source, target, *sems, z, to)
+
+        def z_copy(block, way, target):
+            return remote(
+                mine.at[block, chip],
+                from_z.at[way, block],
+                z_send.at[item, block],
+                z_recv.at[item, way, block],
+                target,
+                f,
+            )
+
+        def z_arrived(block, way):
+            at = from_z.at[way, block]
+            sems = (z_send.at[item, block], z_recv.at[item, way, block])
+            remote(at, at, *sems, z, core).wait_recv()
+
+        def start(step):
+            c_copy(order[step]).start()
+            load(order[step]).start()
+
+        def first(step):
+            block = order[step]
+            load(block).wait()
+            c_copy(block).wait_recv()
+            far_part = mine.at[block, far_chip]
+            add_rows(far_part, rows, far_part, from_core.at[block, far_chip])
+            p_copy(block, 0).start()
+            p_copy(block, 1).start()
+
+        def second(step):
+            block = order[step]
+            x_part, y_part = mine.at[block, x_chip], mine.at[block, y_chip]
+            add_rows(x_part, rows, x_part, from_core.at[block, x_chip])
+            add_rows(y_part, rows, y_part, from_core.at[block, y_chip])
+            p_copy(block, 0).wait_recv()
+            x_left = mine.at[block, x_chip, :, left]
+            add_rows(x_left, rows, x_left, half_y.at[block])
+            p_copy(block, 2).start()
+            p_copy(block, 1).wait_recv()
+            y_right = mine.at[block, y_chip, :, right]
+            add_rows(y_right, rows, y_right, half_x.at[block])
+            p_copy(block, 3).start()
+
+        def third(step):
+            block = order[step]
+            p_copy(block, 2).wait_recv()
+            p_copy(block, 3).wait_recv()
+            own = mine.at[block, chip]
+            terms = (own, from_core.at[block, chip], from_x.at[block], from_y.at[block])
+            if step == ctx_count - 1:
+
+                @pl.when(z > 0)
+                def _():
+                    z_arrived(block, 0)
+
+                @pl.when(z < ctx_count - 1)
+                def _():
+                    z_arrived(block, 1)
+
+                @pl.when(z == 0)
+                def _():
+                    add_rows(out_ref, rows, *terms, from_z.at[1, block])
+
+                @pl.when(z == ctx_count - 1)
+                def _():
+                    add_rows(out_ref, rows, *terms, from_z.at[0, block])
+
+                @pl.when((z > 0) & (z < ctx_count - 1))
+                def _():
+                    add_rows(out_ref, rows, *terms, from_z.at[0, block], from_z.at[1, block])
+
+                return
+
+            for way, above in ((1, True), (0, False)):
+                heading = (block < z) if above else (block > z)
+                has_more = (z < ctx_count - 1) if above else (z > 0)
+
+                @pl.when(heading & has_more)
+                def _():
+                    z_arrived(block, way)
+                    add_rows(own, rows, *terms, from_z.at[way, block])
+
+                @pl.when(heading & jnp.logical_not(has_more))
+                def _():
+                    add_rows(own, rows, *terms)
+
+                @pl.when(heading)
+                def _():
+                    z_copy(block, way, z - 1 if above else z + 1).start()
+
+        def finish(step):
+            block = order[step]
+            c_copy(block).wait_send()
+            for which in range(4):
+                p_copy(block, which).wait_send()
+            if step < ctx_count - 1:
+                z_copy(block, 0, z).wait_send()
+
+        return start, first, second, third, finish
+
+    stages = list(zip(*[work(item) for item in range(count)]))
     for step in range(ctx_count):
-        c_copy(order[step]).start()
-        load(order[step]).start()
+        for act in stages[0]:
+            act(step)
     for step in range(ctx_count + 2):
-        if step < ctx_count:
-            first(step)
-        if 0 <= step - 1 < ctx_count:
-            second(step - 1)
-        if 0 <= step - 2 < ctx_count:
-            third(step - 2)
+        for lag in (0, 1, 2):
+            if 0 <= step - lag < ctx_count:
+                for act in stages[1 + lag]:
+                    act(step - lag)
     for step in range(ctx_count):
-        block = order[step]
-        c_copy(block).wait_send()
-        for which in range(4):
-            p_copy(block, which).wait_send()
-        if step < ctx_count - 1:
-            z_copy(block, 0, z).wait_send()
-
-
-def scatter_dense(grad, ctx_count, fsdp_count):
-    width = grad.shape[1]
-    rows = grad.shape[0] // (ctx_count * fsdp_count)
+        for act in stages[4]:
+            act(step)
+
+
+def scatter_arrays(grads, ctx_count, fsdp_count):
+    count = len(grads)
+    chips = fsdp_count // 2
+    shapes = [
+        (grad.shape[0] // (ctx_count * fsdp_count), grad.shape[1]) for grad in grads
+    ]
     dma = pltpu.SemaphoreType.DMA
-    chips = fsdp_count // 2
-    vmem = lambda *shape: pltpu.VMEM(shape + (width,), LOW)
+    leads = [(ctx_count, chips), (ctx_count, chips), (ctx_count,), (ctx_count,)]
+    banks = [pltpu.VMEM(lead + shape, LOW) for lead in leads for shape in shapes]
+    banks += [
+        pltpu.VMEM((ctx_count, shape[0], shape[1] // 2), LOW) for _ in range(2) for shape in shapes
+    ]
+    banks += [pltpu.VMEM((2, ctx_count) + shape, LOW) for shape in shapes]
     return pl.pallas_call(
-        functools.partial(scatter_kernel, ctx_count),
-        out_shape=jax.ShapeDtypeStruct((rows, width), FULL),
-        in_specs=[pl.BlockSpec(memory_space=pl.ANY)],
-        out_specs=pl.BlockSpec(memory_space=pltpu.VMEM),
-        scratch_shapes=[
-            vmem(ctx_count, chips, rows),
-            vmem(ctx_count, chips, rows),
-            vmem(ctx_count, rows),
-            vmem(ctx_count, rows),
-            vmem(ctx_count, rows // 2),
-            vmem(ctx_count, rows // 2),
-            vmem(2, ctx_count, rows),
-            dma((ctx_count,)),
-            dma((ctx_count,)),
-            dma((ctx_count,)),
-            dma((ctx_count, 4)),
-            dma((ctx_count, 4)),
-            dma((ctx_count,)),
-            dma((2, ctx_count)),
+        functools.partial(scatter_kernel, ctx_count, count),
+        out_shape=[jax.ShapeDtypeStruct(shape, FULL) for shape in shapes],
+        in_specs=[pl.BlockSpec(memory_space=pl.ANY)] * count,
+        out_specs=[pl.BlockSpec(memory_space=pltpu.VMEM)] * count,
+        scratch_shapes=banks
+        + [
+            dma((count, ctx_count)),
+            dma((count, ctx_count)),
+            dma((count, ctx_count)),
+            dma((count, ctx_count, 4)),
+            dma((count, ctx_count, 4)),
+            dma((count, ctx_count)),
+            dma((count, 2, ctx_count)),
         ],
         compiler_params=pltpu.CompilerParams(
             collective_id=1, has_side_effects=True, vmem_limit_bytes=BIG_VMEM
         ),
         cost_estimate=pl.CostEstimate(flops=0, bytes_accessed=500_000_000, transcendentals=0),
-    )(grad.reshape(ctx_count, chips, 2, rows, width))
+    )(
+        *[
+            grad.reshape((ctx_count, chips, 2) + shape)
+            for grad, shape in zip(grads, shapes)
+        ]
+    )
 
 
 PEERS = (6, 7, 2, 4, 3, 5, 1)
@@ -807,16 +870,6 @@
     return total.astype(LOW)
 
 
-def along_line(array):
-    return lax.all_to_all(array, "ctx", split_axis=0, concat_axis=0, tiled=True)
-
-
-def bring_expert(pieces, members, fsdp_count):
-    swapped = swap_parts(pieces, members, fsdp_count)
-    moved = along_line(swapped.reshape((-1,) + swapped.shape[2:]))
-    return share_parts(moved, members, fsdp_count).swapaxes(0, 1)
-
-
 def return_expert(grad, members, fsdp_count):
     moved = along_line(sum_parts(grad, members, fsdp_count))
     moved = moved.reshape((members, EXP_DEV) + moved.shape[1:])
@@ -841,16 +894,42 @@
     return lax.psum_scatter(total, "ctx", scatter_dimension=0, tiled=False).astype(FULL)
 
 
-def gather_shards(shard, ctx_count, fsdp_count):
+def gather_all(items, ctx_count, fsdp_count):
     if (ctx_count, fsdp_count) == (4, 8):
-        return gather_dense(shard, ctx_count, fsdp_count)
-    return lax.all_gather(shard, ("ctx", "fsdp"), axis=0, tiled=True)
-
-
-def scatter_shards(grad, ctx_count, fsdp_count):
+        return gather_arrays(items, ctx_count, fsdp_count)
+    results = []
+    for kind, shard in items:
+        if kind == "line":
+            shard = lax.all_to_all(shard, "ctx", split_axis=0, concat_axis=0, tiled=True)
+            result = lax.all_gather(shard, "fsdp", axis=1)
+        elif kind == "plane":
+            result = lax.all_gather(shard, "fsdp", axis=0)[None]
+        elif kind == "column":
+            result = lax.all_gather(shard, "ctx", axis=0)
+        else:
+            result = lax.all_gather(shard, ("ctx", "fsdp"), axis=0)
+            result = result.reshape((ctx_count, fsdp_count) + shard.shape)
+        results.append(result)
+    return results
+
+
+def scatter_all(grads, ctx_count, fsdp_count):
+    grads = [grad.astype(LOW) for grad in grads]
     if (ctx_count, fsdp_count) == (4, 8):
-        return scatter_dense(grad, ctx_count, fsdp_count)
-    return lax.psum_scatter(grad, ("ctx", "fsdp"), scatter_dimension=0, tiled=True).astype(FULL)
+        return scatter_arrays(grads, ctx_count, fsdp_count)
+    return [
+        lax.psum_scatter(grad, ("ctx", "fsdp"), scatter_dimension=0, tiled=True).astype(FULL)
+        for grad in grads
+    ]
+
+
+def along_line(array):
+    return lax.all_to_all(array, "ctx", split_axis=0, concat_axis=0, tiled=True)
+
+
+def after(values, *others):
+    tied = lax.optimization_barrier((tuple(values), others))
+    return tied[0]
 
 
 def local(
@@ -900,86 +979,106 @@
     dense_rows = latent_weight.shape[0]
     gain_rows = latent_gain.shape[0]
     rotary_end = LATENT + ROPE
-    query_end = query_weight.shape[1]
-    packed = jnp.concatenate(
+    hidden_units = expert_gate.shape[2]
+    shared_units = shared_gate.shape[1] // ctx_count
+
+    def swapped(weight):
+        weight = weight.reshape((EXP_DEV, members, weight.shape[1] // members) + weight.shape[2:])
+        weight = swap_parts(weight.swapaxes(0, 1), members, fsdp_count)
+        return weight.reshape((ctx_count,) + weight.shape[2:])
+
+    gate_swapped, up_swapped, down_swapped = (
+        swapped(expert_gate),
+        swapped(expert_up),
+        swapped(expert_down),
+    )
+    gate_moved, up_moved, down_moved = (
+        along_line(gate_swapped),
+        along_line(up_swapped),
+        along_line(down_swapped),
+    )
+
+    local_routes = routes[0]
+    expert_index = jnp.arange(experts_total, dtype=jnp.int32)
+    member_of = (local_routes[..., None] == expert_index).astype(FULL)
+    counts = jnp.sum(member_of, axis=1)
+    before = jnp.cumsum(counts, axis=0) - counts
+    within = jnp.sum(member_of * before[:, None, :], axis=-1).astype(jnp.int32)
+    info = jnp.concatenate(
         [
-            query_weight,
-            output_weight,
-            expand_weight.reshape(dense_rows, -1),
+            (local_routes * capacity + within).astype(FULL).T,
+            gate_values[0].T,
+            jnp.zeros((16 - 2 * TOP, row_count), FULL),
+        ]
+    )
+
+    tail = jnp.concatenate(
+        [
             latent_weight,
             attention_gain[:, None],
             feedforward_gain[:, None],
             jnp.pad(latent_gain, (0, dense_rows - gain_rows))[:, None],
-            jnp.zeros((dense_rows, 61), LOW),
+            jnp.zeros((dense_rows, 256 - ROPE - 3), LOW),
         ],
         axis=1,
     )
-    packed = gather_shards(packed, ctx_count, fsdp_count)
-    full_query = packed[:, :query_end]
-    output_end = query_end + output_weight.shape[1]
-    full_output = packed[:, query_end:output_end]
-    expand_end = output_end + expand_weight.shape[1] * gain_rows // dense_rows
-    full_expand = packed[:, output_end:expand_end].reshape(LATENT, -1)
-    tail = packed[:, expand_end:]
-    full_latent = tail[:, :rotary_end]
-    gain_one = tail[:, rotary_end].astype(FULL)
-    gain_two = tail[:, rotary_end + 1].astype(FULL)
+
+    def by_line(weight):
+        return weight.reshape(dense_rows, ctx_count, shared_units).swapaxes(0, 1)
+
+    dense = (
+        info,
+        query_weight,
+        tail,
+        expand_weight,
+        output_weight,
+        by_line(shared_gate),
+        by_line(shared_up),
+        shared_down,
+    )
+    dense = after(dense, gate_swapped, up_swapped, down_swapped)
+    kinds = ("column", "all", "all", "all", "all", "line", "line", "plane")
+    gathered = gather_all(list(zip(kinds, dense)), ctx_count, fsdp_count)
+    all_info = gathered[0]
+    full_query, full_tail, full_expand, full_output, full_sgate, full_sup, full_sdown = [
+        item.reshape(-1, item.shape[-1]) for item in gathered[1:]
+    ]
+    full_latent = full_tail[:, :rotary_end]
+    gain_one = full_tail[:, rotary_end].astype(FULL)
+    gain_two = full_tail[:, rotary_end + 1].astype(FULL)
     gain_latent = (
-        tail[:, rotary_end + 2].reshape(device_count, dense_rows)[:, :gain_rows].reshape(LATENT)
-    ).astype(FULL)
-
-    all_routes = lax.all_gather(routes[0], "ctx", axis=0)
-    all_gates = lax.all_gather(gate_values[0], "ctx", axis=0)
-    expert_index = jnp.arange(experts_total, dtype=jnp.int32)
-    member_of = (all_routes[..., None] == expert_index).astype(FULL)
-    counts = jnp.sum(member_of, axis=2)
-    before = jnp.cumsum(counts, axis=1) - counts
-    within = jnp.sum(member_of * before[:, :, None, :], axis=-1).astype(jnp.int32)
+        full_tail[:, rotary_end + 2].reshape(device_count, dense_rows)[:, :gain_rows]
+    ).reshape(LATENT).astype(FULL)
+
+    flat = all_info[:, :TOP].astype(jnp.int32)
+    all_gates = all_info[:, TOP : 2 * TOP]
+    owner = flat // capacity
     slot = jnp.where(
-        all_routes % ctx_count == z, all_routes // ctx_count * capacity + within, -1
-    )
-    hits = slot[..., None] == jnp.arange(plane_slots, dtype=jnp.int32)
-    chooser = jnp.sum(hits.astype(FULL), axis=2).astype(LOW)
-    mixer = jnp.sum(jnp.where(hits, all_gates[..., None], 0.0), axis=2)
-    mixer = mixer.astype(LOW)
-
-    all_cot, arrived_grad = gather_rows(
-        cot_low, mixer.swapaxes(1, 2), ctx_count, fsdp_count
-    )
+        owner % ctx_count == z, owner // ctx_count * capacity + flat % capacity, -1
+    )
+    slot_index = jnp.arange(plane_slots, dtype=jnp.int32)
+    hits = slot[:, :, :, None] == slot_index
+    chooser = jnp.sum(hits.astype(FULL), axis=1).astype(LOW)
+    mixer = jnp.sum(jnp.where(hits, all_gates[:, :, :, None], 0.0), axis=1).astype(LOW)
+    hits = slot[:, :, None, :] == slot_index[:, None]
+    chooser_turned = jnp.sum(hits.astype(FULL), axis=1).astype(LOW)
+    mixer_turned = jnp.sum(jnp.where(hits, all_gates[:, :, None, :], 0.0), axis=1).astype(LOW)
+
+    (cot_sent,) = after((cot_low,), gate_moved)
+    all_cot, arrived_grad = gather_rows(cot_sent, mixer_turned, ctx_count, fsdp_count)
     all_cot = all_cot.reshape(sequence, model_width)
     arrived_grad = arrived_grad.reshape(-1, model_width)
 
-    hidden_units = expert_gate.shape[2]
-
-    def parts(weight):
-        return weight.reshape(
-            (EXP_DEV, members, weight.shape[1] // members) + weight.shape[2:]
-        ).swapaxes(0, 1)
-
-    gate_all = bring_expert(parts(expert_gate), members, fsdp_count).reshape(
-        model_width, hidden_units
-    )
-    up_all = bring_expert(parts(expert_up), members, fsdp_count).reshape(model_width, hidden_units)
-    down_all = (
-        bring_expert(parts(expert_down), members, fsdp_count)
-        .transpose(1, 2, 0, 3)
-        .reshape(hidden_units, model_width)
-    )
-
-    pair = jnp.stack([shared_gate, shared_up])
-    pair = lax.all_to_all(pair, "ctx", split_axis=2, concat_axis=1, tiled=True)
-    shared_units = pair.shape[2]
-    pair = lax.all_gather(pair, "fsdp", axis=0)
-    pair = (
-        pair.reshape(fsdp_count, 2, ctx_count, dense_rows, shared_units)
-        .transpose(1, 2, 0, 3, 4)
-        .reshape(2, model_width, shared_units)
-    )
-    full_sgate, full_sup = (pair[0], pair[1])
-    full_sdown = lax.all_gather(shared_down, "fsdp", axis=0, tiled=True)
+    def whole(moved):
+        return share_parts(moved, members, fsdp_count).swapaxes(0, 1)
+
+    gate_all = whole(gate_moved).reshape(model_width, hidden_units)
+    up_all = whole(up_moved).reshape(model_width, hidden_units)
+    down_all = whole(down_moved).transpose(1, 2, 0, 3).reshape(hidden_units, model_width)
 
     plain_one, inverse_one = norm_forward(source)
     normed = (plain_one * gain_one).astype(LOW)
+    (normed,) = after((normed,), arrived_grad, up_moved)
     query_raw = jnp.dot(normed, full_query, preferred_element_type=FULL).reshape(
         row_count, HEADS, NOPE + ROPE
     )
@@ -1010,9 +1109,8 @@
     plain_two, inverse_two = norm_forward(middle)
     second = (plain_two * gain_two).astype(LOW)
 
-    all_second, arrived_rows = gather_rows(
-        second, chooser.swapaxes(1, 2), ctx_count, fsdp_count
-    )
+    (second_sent,) = after((second,), down_moved)
+    all_second, arrived_rows = gather_rows(second_sent, chooser_turned, ctx_count, fsdp_count)
     all_second = all_second.reshape(sequence, model_width)
     arrived_rows = arrived_rows.reshape(-1, model_width)
     gate_pre = jnp.dot(arrived_rows, gate_all, preferred_element_type=FULL)
@@ -1025,7 +1123,6 @@
     arrived_back = (mm("sf,df->sd", gate_back, gate_all) + mm("sf,df->sd", up_back, up_all)).astype(
         LOW
     )
-    result = jnp.dot(hidden_act, down_all, preferred_element_type=FULL).astype(LOW)
 
     shared_g = jnp.dot(all_second, full_sgate, preferred_element_type=FULL)
     shared_u = jnp.dot(all_second, full_sup, preferred_element_type=FULL)
@@ -1047,6 +1144,10 @@
         fsdp_count,
         True,
     )
+    hidden_act, gate_back, up_back, shared_hidden, sgate_back, sup_back = after(
+        (hidden_act, gate_back, up_back, shared_hidden, sgate_back, sup_back), second_grad
+    )
+    result = jnp.dot(hidden_act, down_all, preferred_element_type=FULL).astype(LOW)
     shared_out = jnp.dot(shared_hidden, full_sdown, preferred_element_type=FULL)
     out_sum = return_rows(
         result.reshape(slots_shape),
@@ -1143,34 +1244,29 @@
     gain_latent_column = jnp.pad(
         gain_latent_grad.reshape(device_count, gain_rows), ((0, 0), (0, dense_rows - gain_rows))
     ).reshape(model_width)
-    packed_grad = scatter_shards(
-        jnp.concatenate(
-            [
-                query_weight_grad.astype(LOW),
-                output_weight_grad.astype(LOW),
-                expand_grad.astype(LOW).reshape(model_width, -1),
-                latent_weight_grad.astype(LOW),
-                gain_one_grad[:, None].astype(LOW),
-                gain_two_grad[:, None].astype(LOW),
-                gain_latent_column[:, None].astype(LOW),
-                jnp.zeros((model_width, 61), LOW),
-            ],
-            axis=1,
-        ),
-        ctx_count,
-        fsdp_count,
-    )
-    tail_grad = packed_grad[:, expand_end:]
+    tail_grad = jnp.concatenate(
+        [
+            latent_weight_grad,
+            gain_one_grad[:, None],
+            gain_two_grad[:, None],
+            gain_latent_column[:, None],
+            jnp.zeros((model_width, 256 - ROPE - 3), FULL),
+        ],
+        axis=1,
+    )
+    query_sum, tail_sum, expand_sum, output_sum = scatter_all(
+        (query_weight_grad, tail_grad, expand_grad, output_weight_grad), ctx_count, fsdp_count
+    )
     return (
         layer_out,
         tokens_grad,
-        tail_grad[:, rotary_end],
-        packed_grad[:, :query_end],
-        tail_grad[:, :rotary_end],
-        tail_grad[:gain_rows, rotary_end + 2],
-        packed_grad[:, output_end:expand_end].reshape(expand_weight.shape),
-        packed_grad[:, query_end:output_end],
-        tail_grad[:, rotary_end + 1],
+        tail_sum[:, rotary_end],
+        query_sum,
+        tail_sum[:, :rotary_end],
+        tail_sum[:gain_rows, rotary_end + 2],
+        expand_sum,
+        output_sum,
+        tail_sum[:, rotary_end + 1],
         pair_grad[0],
         pair_grad[1],
         sdown_grad,

time: 1800 us -> 1800 us (level)
  waiting for transfers between devices: 128 us -> 314 us
  blocking collectives: 77.2 us -> 0 us
  local copies, waits for them, and re-layouts: 266 us -> 191 us
  Pallas kernels: 682 us -> 658 us
    all_to_all x6, waiting for transfers between devices: 63.7 us -> 265 us  [along_line(): return lax.all_to_all(array, 'ctx', split_axis=0, concat_axis=0, tiled=True)]
    pallas_call x2, Pallas kernels: 290 us -> 231 us  [dispatch_rows(): pl.pallas_call(functools.partial(dispatch_kernel, ctx_count), out_shape=(...]
    pallas_call x2, Pallas kernels: 274 us -> 318 us  [the longest x1 191 us: gather_arrays(): pl.pallas_call(functools.partial(gather_kernel, ctx_count, kinds), out_sh...]
    all_gather x2 -> x0, blocking collectives: 40 us -> none  [the longest x1 29.5 us: local(): all_routes = lax.all_gather(routes[0], 'ctx', axis=0)]
    all_to_all x1 -> x0, blocking collectives: 37.2 us -> none  [local(): pair = lax.all_to_all(pair, 'ctx', split_axis=2, concat_axis=1, tiled=True)]
    concatenate x2 -> x6, local copies, waits for them, and re-layouts: 45.3 us -> 12.8 us  [the longest x4 12 us: local(): jnp.concatenate([latent_weight_grad, gain_one_grad[:, None], gain_two_gra...]
    all_to_all x1, waiting for transfers between devices: 63.7 us -> 42.8 us  [return_rows(): lax.all_to_all(slots, 'fsdp', split_axis=1, concat_axis=1, tiled=True)]
    unnamed x151 -> x199, local copies, waits for them, and re-layouts: 30.2 us -> 40.2 us
  transfers between devices with their start and end apart: 27 -> 25, of which waited for: 3 -> 8; matrix products, arithmetic and copies ran while one was open for 40% -> 32% of each run, Pallas kernels for 23% -> 24%
where the time goes in v2:
time: 1800 us; the launch traced here: 1790 us
  Pallas kernels  658 us (37%)
  matrix products  464 us (26%)
  waiting for transfers between devices  314 us (17%)
  local copies, waits for them, and re-layouts  191 us (11%)
  other arithmetic  94.1 us (5%)
  starting transfers between devices  58 us (3%)
    dot_general x32, matrix products, mm(): return jnp.einsum(subscripts, left, right, preferred_element_type=FULL)  341 us
    all_to_all x6, waiting for transfers between devices, along_line(): return lax.all_to_all(array, 'ctx', split_axis=0, concat_axis=0, tiled=True)  265 us
    pallas_call x2, Pallas kernels, dispatch_rows(): pl.pallas_call(functools.partial(dispatch_kernel, ctx_count), out_shape=(...  231 us
    pallas_call x1, Pallas kernels, gather_arrays(): pl.pallas_call(functools.partial(gather_kernel, ctx_count, kinds), out_sh...  191 us
    pallas_call x1, Pallas kernels, scatter_arrays(): pl.pallas_call(functools.partial(scatter_kernel, ctx_count, count), out_s...  127 us
    pallas_call x1, Pallas kernels, combine_rows(): pl.pallas_call(functools.partial(combine_kernel, ctx_count), out_shape=ja...  109 us
    all_to_all x1, waiting for transfers between devices, return_rows(): lax.all_to_all(slots, 'fsdp', split_axis=1, concat_axis=1, tiled=True)  42.8 us
    unnamed x199, local copies, waits for them, and re-layouts  40.2 us
  transfers between devices with their start and end apart: 25, of which 8 were waited for; matrix products, arithmetic and copies ran while one was open for 32% of the time, Pallas kernels for 24%

profile of v2, /device:TPU:1, one launch (start us, length us, event | category | flops | bytes accessed | tf_op | source)
XLA Modules:
  0.0 1794.3 jit_solution(11731202586348507391)
XLA Ops:
  30.1 57.3 %all-to-all-done = bf16[4,256,1408]{2,1,0:T(8,128)(2,1)S(1)} async-done(((bf16[4,256,1408]{2,1,0:T(8,128)(2,1)}), bf16[4,256,1408]{2,1,0:T(8,128)(2,1)S(1)}, u32[]{:S(2)}, u32[]{:S(2)}) %all-to-all-start) | async-done | bytes 2883616 | tf_op jit(solution)/shard_map/all_to_all | solution.py:927
  105.5 52.7 %all-to-all-done.1 = bf16[4,256,1408]{2,1,0:T(8,128)(2,1)} async-done(((bf16[4,256,1408]{2,1,0:T(8,128)(2,1)}), bf16[4,256,1408]{2,1,0:T(8,128)(2,1)}, u32[]{:S(2)}, u32[]{:S(2)}) %all-to-all-start.1) | async-done | bytes 2883616 | tf_op jit(solution)/shard_map/all_to_all | solution.py:927
  165.1 191.1 %shard_map.280 = (f32[4,16,256]{2,1,0:T(8,128)}, bf16[4,8,64,3072]{3,2,1,0:T(8,128)(2,1)}, bf16[4,8,64,768]{3,2,1,0:T(8,128)(2,1)}, bf16[4,8,16,4096]{3,2,1,0:T(...) custom-call(f32[16,256]{1,0:T(8,128)} %maximum_maximum_fusion.refs_0, ...), custom_call_target="tpu_custom_call" | custom-call | bytes 500000000 | tf_op jit(solution)/shard_map/pallas_call | solution.py:309
  374.1 129.8 %shard_map.281 = (bf16[4,256,2048]{2,1,0:T(8,128)(2,1)}, bf16[4,8,64,2048]{3,2,1,0:T(8,128)(2,1)}) custom-call(bf16[256,2048]{1,0:T(8,128)(2,1)} %bitcast.462, bf16[4,512,256]{2,1,0:T(8,128)(2,1)} %get-tuple-element.92.choose_ref), custom_call_target="tpu_custom_call" | custom-call | flops 2000000000 | bytes 300000000 | tf_op jit(solution)/shard_map/pallas_call | solution.py:627
  516.1 17.3 copy.220
  547.7 13.0 fusion.16
  560.7 11.5 fusion.113
  580.3 10.6 convolution_convert_fusion.10
  601.7 101.5 %shard_map.282 = (bf16[4,256,2048]{2,1,0:T(8,128)(2,1)}, bf16[4,8,64,2048]{3,2,1,0:T(8,128)(2,1)}) custom-call(bf16[256,2048]{1,0:T(8,128)(2,1)} %multiply_convert_fusion.6.rows_ref, bf16[4,512,256]{2,1,0:T(8,128)(2,1)} %get-tuple-element.91.choose_ref), custom_call_target="tpu_custom_call" | custom-call | flops 2000000000 | bytes 300000000 | tf_op jit(solution)/shard_map/pallas_call | solution.py:627
  741.8 19.4 %fusion.115 = f32[2048,1408]{1,0:T(8,128)} fusion(bf16[2048,2048]{1,0:T(8,128)(2,1)} %bitcast.485, bf16[1408,2048]{1,0:T(8,128)(2,1)S(1)} %bitcast.436), kind=kOutput, calls=%fused_computation.280 | convolution fusion | flops 11811160064 | bytes 25690112 | tf_op jit(solution)/shard_map/sd,fd->sf/dot_general | solution.py:822
  770.1 15.8 fusion.114
  791.3 30.0 %multiply_convert_fusion = (bf16[2048,1408]{1,0:T(8,128)(2,1)}, bf16[2048,1408]{1,0:T(8,128)(2,1)}, bf16[2048,1408]{1,0:T(8,128)(2,1)}) fusion(f32[2048,1408]{1,0:T(8,128)} %fusion.115, f32[2048,1408]{1,0:T(8,128)} %fusion.114, bf16[2048,2048]{1,0:T(8,128)(2,1)} %bitcast.487, bf16[2048,1408]{1,0:T(8,128)(2,1)} %bitcast.446), kind=kOutput, calls=%fused_computation.17 | convolution fusion | flops 11854413824 | bytes 54525952 | tf_op jit(solution)/shard_map/dot_general | solution.py:1116
  821.4 19.3 %fusion.118 = f32[2048,2048]{1,0:T(8,128)} fusion(bf16[2048,1408]{1,0:T(8,128)(2,1)} %get-tuple-element.79, bf16[2048,1408]{1,0:T(8,128)(2,1)} %bitcast.447), kind=kOutput, calls=%fused_computation.283 | convolution fusion | flops 11811160064 | bytes 28311552 | tf_op jit(solution)/shard_map/sf,df->sd/dot_general | solution.py:822
  840.7 21.6 %add_convert_fusion = bf16[2048,2048]{1,0:T(8,128)(2,1)} fusion(f32[2048,2048]{1,0:T(8,128)} %fusion.118, bf16[2048,1408]{1,0:T(8,128)(2,1)} %get-tuple-element.80, bf16[2048,1408]{1,0:T(8,128)(2,1)} %bitcast.443), kind=kOutput, calls=%fused_computation.7 | convolution fusion | flops 11819548672 | bytes 36700160 | tf_op jit(solution)/shard_map/sf,df->sd/dot_general | solution.py:822
  862.3 108.8 %shard_map.283 = f32[256,2048]{1,0:T(8,128)} custom-call(bf16[4,8,64,2048]{3,2,1,0:T(8,128)(2,1)} %bitcast.430, bf16[4,256,512]{2,1,0:T(8,128)(2,1)} %get-tuple-element.90.mix_ref, bf16[4,256,2048]{2,1,0:T(8,128)(2,1)} %bitcast.454), custom_call_target="tpu_custom_call" | custom-call | flops 2000000000 | bytes 300000000 | tf_op jit(solution)/shard_map/pallas_call | solution.py:791
  971.0 17.4 convolution_convert_fusion.5
  1017.3 18.8 %convolution_convert_fusion.2 = bf16[2048,2048]{1,0:T(8,128)(2,1)} fusion(bf16[2048,1408]{1,0:T(8,128)(2,1)} %get-tuple-element.71, bf16[1408,2048]{1,0:T(8,128)(2,1)} %bitcast.437), kind=kOutput, calls=%fused_computation.27 | convolution fusion | flops 11815354368 | bytes 19922944 | tf_op jit(solution)/shard_map/dot_general | solution.py:1150
  1052.0 22.9 %all-to-all-done.5 = bf16[4,256,1408]{2,1,0:T(8,128)(2,1)S(1)} async-done(((bf16[4,256,1408]{2,1,0:T(8,128)(2,1)}), bf16[4,256,1408]{2,1,0:T(8,128)(2,1)S(1)}, u32[]{:S(2)}, u32[]{:S(2)}) %all-to-all-start.5) | async-done | bytes 2883616 | tf_op jit(solution)/shard_map/all_to_all | solution.py:927
  1092.5 17.5 convolution_convert_fusion.4
  1114.5 17.0 convolution_convert_fusion.3
  1131.6 10.8 reshape.528
  1155.5 42.8 %all-to-all-done.3 = bf16[4,8,64,2048]{3,2,0,1:T(8,128)(2,1)} async-done(((bf16[4,8,64,2048]{3,2,0,1:T(8,128)(2,1)}), bf16[4,8,64,2048]{3,2,0,1:T(8,128)(2,1)}, u32[]{:S(2)}, u32[]{:S(2)}) %all-to-all-start.3) | async-done | bytes 8388640 | tf_op jit(solution)/shard_map/all_to_all | solution.py:891
  1219.5 10.1 add_convert_fusion.1
  1234.7 73.2 %all-to-all-done.6 = bf16[4,256,1408]{2,1,0:T(8,128)(2,1)S(1)} async-done(((bf16[4,256,1408]{2,1,0:T(8,128)(2,1)}), bf16[4,256,1408]{2,1,0:T(8,128)(2,1)S(1)}, u32[]{:S(2)}, u32[]{:S(2)}) %all-to-all-start.6) | async-done | bytes 2883616 | tf_op jit(solution)/shard_map/all_to_all | solution.py:927
  1317.4 11.8 collective-permute-start.7
  1336.4 58.8 %all-to-all-done.7 = bf16[4,704,512]{2,1,0:T(8,128)(2,1)} async-done(((bf16[4,704,512]{2,1,0:T(8,128)(2,1)}), bf16[4,704,512]{2,1,0:T(8,128)(2,1)}, u32[]{:S(2)}, u32[]{:S(2)}) %all-to-all-start.7) | async-done | bytes 2883616 | tf_op jit(solution)/shard_map/all_to_all | solution.py:927
  1428.9 9.7 fusion.10
  1446.9 28.5 %bitcast_add_fusion.1 = f32[1024,512]{0,1:T(8,128)} fusion(f32[1024,512,1]{0,1,2:T(8,128)} %fusion.10, bf16[16,512,256]{2,1,0:T(8,128)(2,1)} %convolution_convert_fusion.11, f32[1024,256,16]{1,0,2:T(8,128)} %fusion.12, f32[16,256,1024]{1,2,0:T(8,128)} %get-tuple-element.142, f32[16,256]{1,0:T(8,128)S(1)} %copy-done.68), kind=kOutput, calls=%fused_computation.103 | convolution fusion | flops 4324856832 | bytes 41959424 | tf_op jit(solution)/shard_map/htk,thc->kc/dot_general | solution.py:822
  1475.5 22.5 %convolution_bitcast_fusion.1 = f32[1024,64]{0,1:T(8,128)S(1)} fusion(bf16[256,16,32]{0,2,1:T(8,128)(2,1)S(1)} %copy-done.42, bf16[256,16,32]{0,2,1:T(8,128)(2,1)S(1)} %copy-done.40, f32[1024,256,16]{1,0,2:T(8,128)} %fusion.12, f32[16,256,1024]{1,2,0:T(8,128)} %get-tuple-element.142, f32[16,256]{1,0:T(8,128)S(1)} %copy-done.68), kind=kOutput, calls=%fused_computation.153 | convolution fusion | flops 567284736 | bytes 34357248 | tf_op jit(solution)/shard_map/htk,thd->kd/dot_general | solution.py:822
  1525.4 25.2 %convolution_convert_fusion.8 = bf16[512,16,256]{2,0,1:T(8,128)(2,1)} fusion(bf16[1024,576]{0,1:T(8,128)(2,1)} %all-gather.2.cloned.1.call-done, f32[1024,256,16]{1,0,2:T(8,128)} %fusion.12, f32[16,256,1024]{1,2,0:T(8,128)} %get-tuple-element.142, f32[16,256]{1,0:T(8,128)S(1)} %copy-done.68), kind=kOutput, calls=%fused_computation.83 | convolution fusion | flops 4326429696 | bytes 72384512 | tf_op jit(solution)/shard_map/htk,kc->thc/dot_general | solution.py:822
  1572.3 28.2 %convolution_bitcast_fusion = f32[256,16,64]{0,2,1:T(8,128)} fusion(bf16[1024,576]{0,1:T(8,128)(2,1)} %all-gather.2.cloned.1.call-done, f32[1024,256,16]{1,0,2:T(8,128)} %fusion.12, f32[16,256,1024]{1,2,0:T(8,128)} %get-tuple-element.142, f32[16,256]{1,0:T(8,128)S(1)} %copy-done.68), kind=kOutput, calls=%fused_computation.152 | convolution fusion | flops 566236160 | bytes 68321280 | tf_op jit(solution)/shard_map/htk,kd->thd/dot_general | solution.py:822
  1650.3 126.8 %shard_map.284 = (f32[64,3072]{1,0:T(8,128)}, f32[64,768]{1,0:T(8,128)}, f32[16,4096]{1,0:T(8,128)}, f32[64,2048]{1,0:T(8,128)}) custom-call(bf16[4,4,2,64,3072]{4,3,2,1,0:T(8,128)(2,1)} %bitcast.408, bf16[4,4,2,64,768]{4,3,2,1,0:T(8,128)(2,1)} %concatenate.56.refs_1_, bf16[4,4,2,16,4096]{4,3,2,1,0:T(8,128)(2,1)} %convert_element_type.348.refs_2_, ...), custom_call_target="tpu_custom_call" | custom-call | bytes 500000000 | tf_op jit(solution)/shard_map/pallas_call | solution.py:510
  (399 shorter events, 437.4 us)
Async XLA Ops:
  9.9 3.6 collective-permute-start
  17.0 70.3 %all-to-all-start = ((bf16[4,256,1408]{2,1,0:T(8,128)(2,1)}), bf16[4,256,1408]{2,1,0:T(8,128)(2,1)S(1)}, u32[]{:S(2)}, u32[]{:S(2)}) async-start(bf16[4,256,1408]{2,1,0:T(8,128)(2,1)} %bitcast.15), calls=%async_computation | async-start | bytes 5767168 | tf_op jit(solution)/shard_map/all_to_all | solution.py:927
  24.3 3.6 collective-permute-start.1
  88.9 69.2 %all-to-all-start.1 = ((bf16[4,256,1408]{2,1,0:T(8,128)(2,1)}), bf16[4,256,1408]{2,1,0:T(8,128)(2,1)}, u32[]{:S(2)}, u32[]{:S(2)}) async-start(bf16[4,256,1408]{2,1,0:T(8,128)(2,1)} %bitcast.21), calls=%async_computation.1 | async-start | bytes 5767168 | tf_op jit(solution)/shard_map/all_to_all | solution.py:927
  96.2 5.4 collective-permute-start.2
  99.5 407.3 %copy-start.76 = (f32[32]{0:T(128)}, f32[32]{0:T(128)S(1)}, u32[]{:S(2)}) copy-start(f32[32]{0:T(128)S(1)} %multiply_power_fusion) | copy-start | bytes 388
  99.5 407.3 %copy-start.74 = (f32[256]{0:T(256)}, f32[256]{0:T(256)S(1)}, u32[]{:S(2)}) copy-start(f32[256]{0:T(256)S(1)} %fusion.106) | copy-start | bytes 3076
  100.0 273.8 %copy-start.71 = (f32[256]{0:T(256)}, f32[256]{0:T(256)S(1)}, u32[]{:S(2)}) copy-start(f32[256]{0:T(256)S(1)} %add_rsqrt_fusion.2) | copy-start | bytes 3076
  158.1 377.4 %all-to-all-start.2 = ((bf16[4,704,512]{2,1,0:T(8,128)(2,1)}), bf16[4,704,512]{2,1,0:T(8,128)(2,1)}, u32[]{:S(2)}, u32[]{:S(2)}) async-start(bf16[4,704,512]{2,1,0:T(8,128)(2,1)} %bitcast.423), calls=%async_computation.2 | async-start | bytes 5767168 | tf_op jit(solution)/shard_map/all_to_all | solution.py:927
  162.8 384.9 %all-gather.2.cloned.1.call-start = ((), (), s32[]{:S(2)}) async-start(), calls=%async_computation.12 | async-start | bytes 1474560 | tf_op jit(solution)/shard_map/all_gather | solution.py:1091
  364.8 142.3 %copy-start.60 = (f32[512]{0:T(512)}, f32[512]{0:T(512)S(1)}, u32[]{:S(2)}) copy-start(f32[512]{0:T(512)S(1)} %reshape.532) | copy-start | bytes 6148
  374.1 129.8 %copy-start.18 = (bf16[256,2048]{1,0:T(8,128)(2,1)}, bf16[256,2048]{1,0:T(8,128)(2,1)S(1)}, u32[]{:S(2)}) copy-start(bf16[256,2048]{1,0:T(8,128)(2,1)S(1)} %fusion.28) | copy-start | bytes 3145732
  516.0 74.9 %copy-start.2 = (bf16[512,16,128]{0,2,1:T(8,128)(2,1)}, bf16[512,16,128]{0,2,1:T(8,128)(2,1)S(1)}, u32[]{:S(2)}) copy-start(bf16[512,16,128]{0,2,1:T(8,128)(2,1)S(1)} %copy.278) | copy-start | bytes 6291460
  535.0 226.3 %collective-permute-start.4 = (bf16[4,256,1408]{2,1,0:T(8,128)(2,1)}, bf16[4,256,1408]{2,1,0:T(8,128)(2,1)}, u32[]{:S(2)}, u32[]{:S(2)}) collective-permute-start(bf16[4,256,1408]{2,1,0:T(8,128)(2,1)} %all-to-all-done.1), channel_id=1, source_target_pairs={{0,1},{1,0},{2,3},{3,2},{4,5},{5,4},{6,7},{7,6},{8,9},{9,8},{10,11... | collective-permute-start | bytes 8650760 | tf_op jit(solution)/shard_map/ppermute | solution.py:857
  535.2 250.7 %collective-permute-start.3 = (bf16[4,256,1408]{2,1,0:T(8,128)(2,1)}, bf16[4,256,1408]{2,1,0:T(8,128)(2,1)}, u32[]{:S(2)}, u32[]{:S(2)}) collective-permute-start(bf16[4,256,1408]{2,1,0:T(8,128)(2,1)} %copy-done.16), channel_id=1, source_target_pairs={{0,1},{1,0},{2,3},{3,2},{4,5},{5,4},{6,7},{7,6},{8,9},{9,8},{10,11... | collective-permute-start | bytes 8650760 | tf_op jit(solution)/shard_map/ppermute | solution.py:857
  535.5 190.6 %collective-permute-start.5 = (bf16[4,704,512]{2,1,0:T(8,128)(2,1)}, bf16[4,704,512]{2,1,0:T(8,128)(2,1)}, u32[]{:S(2)}, u32[]{:S(2)}) collective-permute-start(bf16[4,704,512]{2,1,0:T(8,128)(2,1)} %all-to-all-done.2), channel_id=1, source_target_pairs={{0,1},{1,0},{2,3},{3,2},{4,5},{5,4},{6,7},{7,6},{8,9},{9,8},{10,11... | collective-permute-start | bytes 8650760 | tf_op jit(solution)/shard_map/ppermute | solution.py:857
  601.7 101.5 %copy-start.81 = (bf16[4,8,64,704]{3,2,1,0:T(8,128)(2,1)S(1)}, bf16[4,8,64,704]{3,2,1,0:T(8,128)(2,1)}, u32[]{:S(2)}) copy-start(bf16[4,8,64,704]{3,2,1,0:T(8,128)(2,1)} %get-tuple-element.67) | copy-start | bytes 8650756
  992.8 8.5 collective-permute-start.6
  1005.5 69.4 %all-to-all-start.5 = ((bf16[4,256,1408]{2,1,0:T(8,128)(2,1)}), bf16[4,256,1408]{2,1,0:T(8,128)(2,1)S(1)}, u32[]{:S(2)}, u32[]{:S(2)}) async-start(bf16[4,256,1408]{2,1,0:T(8,128)(2,1)} %fusion.9), calls=%async_computation.9 | async-start | bytes 5767168 | tf_op jit(solution)/shard_map/all_to_all | solution.py:927
  1009.9 324.6 %reduce-scatter.11.cloned.1.call-start = ((), (), s32[]{:S(2)}) async-start(), calls=%async_computation.16 | async-start | bytes 3244032 | tf_op jit(solution)/shard_map/reduce_scatter | solution.py:1192
  1076.5 121.7 %all-to-all-start.3 = ((bf16[4,8,64,2048]{3,2,0,1:T(8,128)(2,1)}), bf16[4,8,64,2048]{3,2,0,1:T(8,128)(2,1)}, u32[]{:S(2)}, u32[]{:S(2)}) async-start(bf16[4,8,64,2048]{3,2,0,1:T(8,128)(2,1)} %copy.229), calls=%async_computation.3 | async-start | bytes 16777216 | tf_op jit(solution)/shard_map/all_to_all | solution.py:891
  1082.4 317.3 %reduce-scatter.9.cloned.1.call-start = ((), (), s32[]{:S(2)}) async-start(), calls=%async_computation.15 | async-start | bytes 7077888 | tf_op jit(solution)/shard_map/reduce_scatter | solution.py:1187
  1114.3 37.0 %collective-permute-start.8 = (bf16[4,256,1408]{2,1,0:T(8,128)(2,1)}, bf16[4,256,1408]{2,1,0:T(8,128)(2,1)}, u32[]{:S(2)}, u32[]{:S(2)}) collective-permute-start(bf16[4,256,1408]{2,1,0:T(8,128)(2,1)} %dynamic-slice_bitcast_fusion), channel_id=1, source_target_pairs={{0,1},{1,0},{2,3},{3,2},{4,5},{5,4},{6,7},{7,6},{8,9},{9,8},{10,11... | collective-permute-start | bytes 8650760 | tf_op jit(solution)/shard_map/ppermute | solution.py:867
  1150.9 78.7 %collective-permute-start.10 = (bf16[4,704,512]{2,1,0:T(8,128)(2,1)}, bf16[4,704,512]{2,1,0:T(8,128)(2,1)}, u32[]{:S(2)}, u32[]{:S(2)}) collective-permute-start(bf16[4,704,512]{2,1,0:T(8,128)(2,1)} %bitcast.405), channel_id=1, source_target_pairs={{0,1},{1,0},{2,3},{3,2},{4,5},{5,4},{6,7},{7,6},{8,9},{9,8},{10,11... | collective-permute-start | bytes 8650760 | tf_op jit(solution)/shard_map/ppermute | solution.py:867
  1198.2 109.7 %all-to-all-start.6 = ((bf16[4,256,1408]{2,1,0:T(8,128)(2,1)}), bf16[4,256,1408]{2,1,0:T(8,128)(2,1)S(1)}, u32[]{:S(2)}, u32[]{:S(2)}) async-start(bf16[4,256,1408]{2,1,0:T(8,128)(2,1)} %fusion.8), calls=%async_computation.10 | async-start | bytes 5767168 | tf_op jit(solution)/shard_map/all_to_all | solution.py:927
  1201.9 212.2 %reduce-scatter.5.cloned.1.call-start = ((), (), s32[]{:S(2)}) async-start(), calls=%async_computation.13 | async-start | bytes 5242880 | tf_op jit(solution)/shard_map/reduce_scatter | solution.py:894
  1309.5 85.8 %all-to-all-start.7 = ((bf16[4,704,512]{2,1,0:T(8,128)(2,1)}), bf16[4,704,512]{2,1,0:T(8,128)(2,1)}, u32[]{:S(2)}, u32[]{:S(2)}) async-start(bf16[4,704,512]{2,1,0:T(8,128)(2,1)} %fusion.7), calls=%async_computation.11 | async-start | bytes 5767168 | tf_op jit(solution)/shard_map/all_to_all | solution.py:927
  1317.4 89.5 %collective-permute-start.7 = (bf16[2,256,1408]{2,1,0:T(8,128)(2,1)}, bf16[2,256,1408]{2,1,0:T(8,128)(2,1)}, u32[]{:S(2)}, u32[]{:S(2)}) collective-permute-start(bf16[2,256,1408]{2,1,0:T(8,128)(2,1)} %dynamic-slice_bitcast_fusion.4), channel_id=1, source_target_pairs={{0,1},{1,0},{2,3},{3,2},{4,5},{5,4},{6,7},{7,6},{8,9},{9,8},{10,11... | collective-permute-start | bytes 4325384 | tf_op jit(solution)/shard_map/ppermute | solution.py:846
  1330.7 80.0 %collective-permute-start.9 = (bf16[2,256,1408]{2,1,0:T(8,128)(2,1)S(1)}, bf16[2,256,1408]{2,1,0:T(8,128)(2,1)}, u32[]{:S(2)}, u32[]{:S(2)}) collective-permute-start(bf16[2,256,1408]{2,1,0:T(8,128)(2,1)S(1)} %dynamic-slice_bitcast_fusion.3), channel_id=1, source_target_pairs={{0,1},{1,0},{2,3},{3,2},{4,5},{5,4},{6,7},{7,6},{8,9},{9,8},{10,11... | collective-permute-start | bytes 4325384 | tf_op jit(solution)/shard_map/ppermute | solution.py:846
  1397.8 111.5 %collective-permute-start.11 = (bf16[2,704,512]{2,1,0:T(8,128)(2,1)}, bf16[2,704,512]{2,1,0:T(8,128)(2,1)}, u32[]{:S(2)}, u32[]{:S(2)}) collective-permute-start(bf16[2,704,512]{2,1,0:T(8,128)(2,1)} %dynamic-slice_bitcast_fusion.2), channel_id=1, source_target_pairs={{0,1},{1,0},{2,3},{3,2},{4,5},{5,4},{6,7},{7,6},{8,9},{9,8},{10,11... | collective-permute-start | bytes 4325384 | tf_op jit(solution)/shard_map/ppermute | solution.py:846
  1402.6 112.6 %all-to-all-start.4 = ((bf16[2,256,704]{2,0,1:T(2,128)(2,1)}), bf16[2,256,704]{2,0,1:T(2,128)(2,1)}, u32[]{:S(2)}, u32[]{:S(2)}) async-start(bf16[2,256,704]{2,0,1:T(2,128)(2,1)} %copy.250), calls=%async_computation.7 | async-start | bytes 1572864 | tf_op jit(solution)/shard_map/all_to_all | solution.py:1188
  1406.8 204.7 %reduce-scatter.7.cloned.1.call-start = ((), (), s32[]{:S(2)}) async-start(), calls=%async_computation.14 | async-start | bytes 2949120 | tf_op jit(solution)/shard_map/reduce_scatter | solution.py:1213
  (87 other events, 970.9 us)
Sparse Core Ops, SparseCore 0:
  508.1 28.7 all-gather.1
  1017.4 45.7 reduce-scatter.10
  1092.6 109.5 reduce-scatter.8
  1229.8 122.2 reduce-scatter.4
  1501.5 49.8 reduce-scatter.6

commit v3 on v2

--- a/solution.py
+++ b/solution.py
@@ -69,13 +69,6 @@
 def silu_slope(values):
     sigma = jax.nn.sigmoid(values)
     return (values * sigma, sigma * (1.0 + values * (1.0 - sigma)))
-
-
-def score_block(query_latent, query_rope, all_latent, all_keys, allowed, score_scale):
-    raw_scores = jnp.einsum(
-        "thc,kc->htk", query_latent, all_latent, preferred_element_type=jnp.float32
-    ) + jnp.einsum("thd,kd->htk", query_rope, all_keys, preferred_element_type=jnp.float32)
-    return jnp.where(allowed[None], raw_scores * score_scale, masked_score)
 
 
 LOW = jnp.bfloat16
@@ -818,6 +811,178 @@
     )(slots, mixer, extra)
 
 
+HEAD_GROUP = 4
+KEYS = 256
+
+
+def dot_last(left, right):
+    return lax.dot_general(left, right, (((1,), (1,)), ((), ())), preferred_element_type=FULL)
+
+
+def dot_first(left, right):
+    return lax.dot_general(left, right, (((0,), (0,)), ((), ())), preferred_element_type=FULL)
+
+
+def reach(half, rows, ctx_count):
+    ctx = lax.axis_index("ctx")
+    first = jnp.where(half == 0, ctx, 2 * ctx_count - 1 - ctx) * rows
+    return first, lax.div(first + rows + KEYS - 1, KEYS)
+
+
+def block_scores(query, turned, keys_ref, rope_ref, index, first, rows, scale):
+    part = pl.ds(pl.multiple_of(index * KEYS, KEYS), KEYS)
+    keys, rope = keys_ref[part, :], rope_ref[part, :]
+    scores = (dot_last(query, keys) + dot_last(turned, rope)) * scale
+    shape = scores.shape
+    at = first + lax.rem(lax.broadcasted_iota(jnp.int32, shape, 0), rows)
+    key_at = index * KEYS + lax.broadcasted_iota(jnp.int32, shape, 1)
+    return part, keys, rope, scores, at >= key_at
+
+
+def attend_kernel(
+    ctx_count, scale, query_ref, turned_ref, keys_ref, rope_ref, out_ref, log_ref, total, top, norm
+):
+    heads, rows, width = query_ref.shape
+    first, blocks = reach(pl.program_id(0), rows, ctx_count)
+    query = query_ref[...].reshape(heads * rows, width)
+    turned = turned_ref[...].reshape(heads * rows, -1)
+    total[...] = jnp.zeros_like(total)
+    norm[...] = jnp.zeros_like(norm)
+    top[...] = jnp.full_like(top, masked_score)
+
+    @pl.loop(0, blocks)
+    def _(index):
+        part, keys, rope, scores, seen = block_scores(
+            query, turned, keys_ref, rope_ref, index, first, rows, scale
+        )
+        scores = jnp.where(seen, scores, masked_score)
+        old = top[...]
+        new = jnp.maximum(old, jnp.max(scores, axis=1, keepdims=True))
+        weights = jnp.exp(scores - new)
+        shrink = jnp.exp(old - new)
+        top[...] = new
+        norm[...] = norm[...] * shrink + jnp.sum(weights, axis=1, keepdims=True)
+        total[...] = total[...] * shrink + jnp.dot(
+            weights.astype(LOW), keys, preferred_element_type=FULL
+        )
+
+    out_ref[...] = (total[...] / norm[...]).astype(LOW).reshape(out_ref.shape)
+    log_ref[...] = (top[...] + jnp.log(norm[...])).reshape(log_ref.shape)
+
+
+def attend_back_kernel(
+    ctx_count,
+    scale,
+    query_ref,
+    turned_ref,
+    keys_ref,
+    rope_ref,
+    out_ref,
+    log_ref,
+    grad_ref,
+    query_grad_ref,
+    turned_grad_ref,
+    keys_grad_ref,
+    rope_grad_ref,
+    query_total,
+    turned_total,
+):
+    heads, rows, width = query_ref.shape
+    first, blocks = reach(pl.program_id(0), rows, ctx_count)
+    query = query_ref[...].reshape(heads * rows, width)
+    turned = turned_ref[...].reshape(heads * rows, -1)
+    grad = grad_ref[...].reshape(heads * rows, width)
+    out = out_ref[...].reshape(heads * rows, width)
+    logs = log_ref[...].reshape(heads * rows, 1)
+    inner = jnp.sum(grad.astype(FULL) * out.astype(FULL), axis=1, keepdims=True)
+    query_total[...] = jnp.zeros_like(query_total)
+    turned_total[...] = jnp.zeros_like(turned_total)
+
+    @pl.when((pl.program_id(0) == 0) & (pl.program_id(1) == 0))
+    def _():
+        keys_grad_ref[...] = jnp.zeros_like(keys_grad_ref)
+        rope_grad_ref[...] = jnp.zeros_like(rope_grad_ref)
+
+    @pl.loop(0, blocks)
+    def _(index):
+        part, keys, rope, scores, seen = block_scores(
+            query, turned, keys_ref, rope_ref, index, first, rows, scale
+        )
+        weights = jnp.where(seen, jnp.exp(scores - logs), 0.0)
+        change = (weights * (dot_last(grad, keys) - inner) * scale).astype(LOW)
+        query_total[...] += jnp.dot(change, keys, preferred_element_type=FULL)
+        turned_total[...] += jnp.dot(change, rope, preferred_element_type=FULL)
+        keys_grad_ref[part, :] += dot_first(change, query) + dot_first(weights.astype(LOW), grad)
+        rope_grad_ref[part, :] += dot_first(change, turned)
+
+    query_grad_ref[...] = query_total[...].astype(LOW).reshape(query_grad_ref.shape)
+    turned_grad_ref[...] = turned_total[...].reshape(turned_grad_ref.shape)
+
+
+def attend_specs(heads, group, rows, widths):
+    return [pl.BlockSpec((group, rows, width), lambda half, g: (g, half, 0)) for width in widths]
+
+
+def whole_spec(array):
+    return pl.BlockSpec(array.shape, lambda half, g: (0, 0))
+
+
+def attend(query, turned, keys, rope, ctx_count, scale):
+    heads, count, width = query.shape
+    group, rows = HEAD_GROUP, count // 2
+    lanes = turned.shape[2]
+    return pl.pallas_call(
+        functools.partial(attend_kernel, ctx_count, scale),
+        grid=(2, heads // group),
+        out_shape=(
+            jax.ShapeDtypeStruct((heads, count, width), LOW),
+            jax.ShapeDtypeStruct((heads, count, 1), FULL),
+        ),
+        in_specs=attend_specs(heads, group, rows, (width, lanes))
+        + [whole_spec(keys), whole_spec(rope)],
+        out_specs=tuple(attend_specs(heads, group, rows, (width, 1))),
+        scratch_shapes=[
+            pltpu.VMEM((group * rows, width), FULL),
+            pltpu.VMEM((group * rows, 1), FULL),
+            pltpu.VMEM((group * rows, 1), FULL),
+        ],
+        compiler_params=pltpu.CompilerParams(vmem_limit_bytes=BIG_VMEM),
+        cost_estimate=pl.CostEstimate(
+            flops=12_000_000_000, bytes_accessed=12_000_000, transcendentals=3_000_000
+        ),
+    )(query, turned, keys, rope)
+
+
+def attend_back(query, turned, keys, rope, out, logs, grad, ctx_count, scale):
+    heads, count, width = query.shape
+    group, rows = HEAD_GROUP, count // 2
+    lanes = turned.shape[2]
+    return pl.pallas_call(
+        functools.partial(attend_back_kernel, ctx_count, scale),
+        grid=(2, heads // group),
+        out_shape=(
+            jax.ShapeDtypeStruct((heads, count, width), LOW),
+            jax.ShapeDtypeStruct((heads, count, lanes), FULL),
+            jax.ShapeDtypeStruct(keys.shape, FULL),
+            jax.ShapeDtypeStruct(rope.shape, FULL),
+        ),
+        in_specs=attend_specs(heads, group, rows, (width, lanes))
+        + [whole_spec(keys), whole_spec(rope)]
+        + attend_specs(heads, group, rows, (width, 1, width)),
+        out_specs=tuple(
+            attend_specs(heads, group, rows, (width, lanes)) + [whole_spec(keys), whole_spec(rope)]
+        ),
+        scratch_shapes=[
+            pltpu.VMEM((group * rows, width), FULL),
+            pltpu.VMEM((group * rows, lanes), FULL),
+        ],
+        compiler_params=pltpu.CompilerParams(vmem_limit_bytes=BIG_VMEM),
+        cost_estimate=pl.CostEstimate(
+            flops=30_000_000_000, bytes_accessed=30_000_000, transcendentals=3_000_000
+        ),
+    )(query, turned, keys, rope, out, logs, grad)
+
+
 def mm(subscripts, left, right):
     return jnp.einsum(subscripts, left, right, preferred_element_type=FULL)
 
@@ -870,12 +1035,6 @@
     return total.astype(LOW)
 
 
-def return_expert(grad, members, fsdp_count):
-    moved = along_line(sum_parts(grad, members, fsdp_count))
-    moved = moved.reshape((members, EXP_DEV) + moved.shape[1:])
-    return swap_parts(moved, members, fsdp_count).swapaxes(0, 1)
-
-
 def gather_rows(rows, chooser, ctx_count, fsdp_count):
     if (ctx_count, fsdp_count) == (4, 8):
         return dispatch_rows(rows, chooser, ctx_count, fsdp_count)
@@ -885,8 +1044,8 @@
     return every, lax.all_to_all(chosen, "fsdp", split_axis=1, concat_axis=1, tiled=True)
 
 
-def return_rows(slots, mixer, extra, ctx_count, fsdp_count, urgent):
-    if urgent and (ctx_count, fsdp_count) == (4, 8):
+def return_rows(slots, mixer, extra, ctx_count, fsdp_count):
+    if (ctx_count, fsdp_count) == (4, 8):
         return combine_rows(slots, mixer, extra.astype(LOW), ctx_count, fsdp_count)
     back = lax.all_to_all(slots, "fsdp", split_axis=1, concat_axis=1, tiled=True)
     back = back.reshape(ctx_count, mixer.shape[2], -1)
@@ -971,11 +1130,6 @@
     positions = stored_positions(
         z * row_count + jnp.arange(row_count, dtype=jnp.int32), row_count, 2 * ctx_count
     )
-    key_positions = stored_positions(
-        jnp.arange(sequence, dtype=jnp.int32), row_count, 2 * ctx_count
-    )
-    allowed = positions[:, None] >= key_positions[None, :]
-
     dense_rows = latent_weight.shape[0]
     gain_rows = latent_gain.shape[0]
     rotary_end = LATENT + ROPE
@@ -992,11 +1146,7 @@
         swapped(expert_up),
         swapped(expert_down),
     )
-    gate_moved, up_moved, down_moved = (
-        along_line(gate_swapped),
-        along_line(up_swapped),
-        along_line(down_swapped),
-    )
+    gate_moved = along_line(gate_swapped)
 
     local_routes = routes[0]
     expert_index = jnp.arange(experts_total, dtype=jnp.int32)
@@ -1064,8 +1214,12 @@
     chooser_turned = jnp.sum(hits.astype(FULL), axis=1).astype(LOW)
     mixer_turned = jnp.sum(jnp.where(hits, all_gates[:, :, None, :], 0.0), axis=1).astype(LOW)
 
+    (up_swapped,) = after((up_swapped,), all_info)
+    up_moved = along_line(up_swapped)
     (cot_sent,) = after((cot_low,), gate_moved)
     all_cot, arrived_grad = gather_rows(cot_sent, mixer_turned, ctx_count, fsdp_count)
+    (down_swapped,) = after((down_swapped,), arrived_grad)
+    down_moved = along_line(down_swapped)
     all_cot = all_cot.reshape(sequence, model_width)
     arrived_grad = arrived_grad.reshape(-1, model_width)
 
@@ -1079,31 +1233,32 @@
     plain_one, inverse_one = norm_forward(source)
     normed = (plain_one * gain_one).astype(LOW)
     (normed,) = after((normed,), arrived_grad, up_moved)
-    query_raw = jnp.dot(normed, full_query, preferred_element_type=FULL).reshape(
-        row_count, HEADS, NOPE + ROPE
-    )
+    (query_raw,) = after((jnp.dot(normed, full_query, preferred_element_type=FULL),))
+    query_raw = query_raw.reshape(row_count, HEADS, NOPE + ROPE)
     query_nope = query_raw[:, :, :NOPE].astype(LOW)
     query_rope = rotary(query_raw[:, :, NOPE:], positions, 1.0).astype(LOW)
     latent_raw = jnp.dot(normed, full_latent, preferred_element_type=FULL)
     plain_latent, inverse_latent = norm_forward(latent_raw[:, :LATENT])
     latent_norm = (plain_latent * gain_latent).astype(LOW)
     key_rope = rotary(latent_raw[:, LATENT:], positions, 1.0).astype(LOW)
+    half_rows = row_count // 2
+    pad_rope = ((0, 0), (0, 128 - ROPE))
     keys = lax.all_gather(
-        jnp.concatenate([latent_norm, key_rope], axis=1), "ctx", axis=0, tiled=True
-    )
+        jnp.concatenate([latent_norm, jnp.pad(key_rope, pad_rope)], axis=1), "ctx", axis=0
+    )
+    keys = keys.reshape(ctx_count, 2, half_rows, LATENT + 128)
+    keys = jnp.concatenate([keys[:, 0], keys[::-1, 1]]).reshape(sequence, LATENT + 128)
     all_latent, all_keys = (keys[:, :LATENT], keys[:, LATENT:])
     expand = full_expand.reshape(LATENT, HEADS, NOPE + VDIM)
     expand_key = expand[:, :, :NOPE]
     expand_value = expand[:, :, NOPE:]
-    query_latent = mm("thd,chd->thc", query_nope, expand_key).astype(LOW)
-    scores = score_block(query_latent, query_rope, all_latent, all_keys, allowed, score_scale)
-    row_max = jnp.max(scores, axis=-1, keepdims=True)
-    row_sum = jnp.sum(jnp.exp(scores - row_max), axis=-1, keepdims=True)
-    log_total = row_max + jnp.log(row_sum)
-    soft_weights = jnp.exp(scores - log_total)
-    latent_out = mm("htk,kc->thc", soft_weights.astype(LOW), all_latent).astype(LOW)
+    query_latent = mm("thd,chd->htc", query_nope, expand_key).astype(LOW)
+    query_turned = jnp.pad(query_rope.swapaxes(0, 1), ((0, 0),) + pad_rope)
+    latent_out, log_total = attend(
+        query_latent, query_turned, all_latent, all_keys, ctx_count, score_scale
+    )
     values_out = (
-        mm("thc,chv->thv", latent_out, expand_value).astype(LOW).reshape(row_count, HEADS * VDIM)
+        mm("htc,chv->thv", latent_out, expand_value).astype(LOW).reshape(row_count, HEADS * VDIM)
     )
     middle = source + jnp.dot(values_out, full_output, preferred_element_type=FULL)
     plain_two, inverse_two = norm_forward(middle)
@@ -1142,39 +1297,9 @@
         shared_second_grad.reshape(rows_shape),
         ctx_count,
         fsdp_count,
-        True,
-    )
-    hidden_act, gate_back, up_back, shared_hidden, sgate_back, sup_back = after(
-        (hidden_act, gate_back, up_back, shared_hidden, sgate_back, sup_back), second_grad
-    )
-    result = jnp.dot(hidden_act, down_all, preferred_element_type=FULL).astype(LOW)
-    shared_out = jnp.dot(shared_hidden, full_sdown, preferred_element_type=FULL)
-    out_sum = return_rows(
-        result.reshape(slots_shape),
-        mixer,
-        shared_out.reshape(rows_shape),
-        ctx_count,
-        fsdp_count,
-        False,
-    )
-    layer_out = (middle + out_sum).astype(LOW)[None]
-
-    gate_grad = mm("sd,sf->df", arrived_rows, gate_back).astype(LOW)
-    up_grad = mm("sd,sf->df", arrived_rows, up_back).astype(LOW)
-    down_grad = mm("sf,sd->fd", hidden_act, arrived_grad).astype(LOW)
-
-    def give_back(grad, like):
-        return return_expert(grad, members, fsdp_count).reshape(like.shape).astype(FULL)
-
-    part_rows = model_width // ctx_count // members
-    line_shape = (ctx_count, members, part_rows, hidden_units)
-    expert_grads = (
-        give_back(gate_grad.reshape(line_shape).swapaxes(0, 1), expert_gate),
-        give_back(up_grad.reshape(line_shape).swapaxes(0, 1), expert_up),
-        give_back(
-            down_grad.reshape(members, hidden_units // members, ctx_count, -1).swapaxes(1, 2),
-            expert_down,
-        ),
+    )
+    shared_hidden, sgate_back, sup_back = after(
+        (shared_hidden, sgate_back, sup_back), second_grad
     )
     pair_grad = jnp.stack(
         [mm("td,tf->df", all_second, sgate_back), mm("td,tf->df", all_second, sup_back)]
@@ -1184,12 +1309,32 @@
         .transpose(2, 0, 1, 3, 4)
         .reshape(fsdp_count, 2, ctx_count * dense_rows, shared_units)
     )
+    sdown_grad = mm("tf,td->fd", shared_hidden, all_cot).astype(LOW)
+    (hidden_act,) = after((hidden_act,), pair_grad, sdown_grad)
     pair_grad = lax.psum_scatter(pair_grad, "fsdp", scatter_dimension=0, tiled=False)
-    pair_grad = lax.all_to_all(
-        pair_grad, "ctx", split_axis=1, concat_axis=2, tiled=True
-    ).astype(FULL)
-    sdown_grad = mm("tf,td->fd", shared_hidden, all_cot).astype(LOW)
-    sdown_grad = lax.psum_scatter(sdown_grad, "fsdp", scatter_dimension=0, tiled=True).astype(FULL)
+    sdown_grad = lax.psum_scatter(sdown_grad, "fsdp", scatter_dimension=0, tiled=True)
+    result = jnp.dot(hidden_act, down_all, preferred_element_type=FULL).astype(LOW)
+    came_back = lax.all_to_all(
+        result.reshape(slots_shape), "fsdp", split_axis=1, concat_axis=1, tiled=True
+    ).reshape(ctx_count, plane_slots, model_width)
+    hidden_act, gate_back, up_back, shared_hidden = after(
+        (hidden_act, gate_back, up_back, shared_hidden), result
+    )
+    gate_grad = mm("sd,sf->df", arrived_rows, gate_back).astype(LOW)
+    up_grad = mm("sd,sf->df", arrived_rows, up_back).astype(LOW)
+    down_grad = mm("sf,sd->fd", hidden_act, arrived_grad).astype(LOW)
+    line_shape = (ctx_count, members, model_width // ctx_count // members, hidden_units)
+    gate_sum = sum_parts(gate_grad.reshape(line_shape).swapaxes(0, 1), members, fsdp_count)
+    up_sum = sum_parts(up_grad.reshape(line_shape).swapaxes(0, 1), members, fsdp_count)
+    down_sum = sum_parts(
+        down_grad.reshape(members, hidden_units // members, ctx_count, -1).swapaxes(1, 2),
+        members,
+        fsdp_count,
+    )
+    shared_out = jnp.dot(shared_hidden, full_sdown, preferred_element_type=FULL)
+    (second_grad,) = after((second_grad,), gate_sum, up_sum, down_sum, came_back, shared_out)
+    (gate_sum,) = after((gate_sum,), came_back)
+    gate_returned = along_line(gate_sum)
 
     middle_part, gain_two_grad = norm_backward(second_grad, plain_two, inverse_two, gain_two)
     middle_grad = cot_full + middle_part
@@ -1198,27 +1343,50 @@
     values_grad = (
         mm("td,vd->tv", attended_grad, full_output).astype(LOW).reshape(row_count, HEADS, VDIM)
     )
-    latent_out_grad = mm("thv,chv->thc", values_grad, expand_value).astype(LOW)
-    expand_value_grad = mm("thc,thv->chv", latent_out, values_grad)
-    scores = score_block(query_latent, query_rope, all_latent, all_keys, allowed, score_scale)
-    soft_weights = jnp.exp(scores - log_total)
-    soft_grad = mm("thc,kc->htk", latent_out_grad, all_latent)
-    all_latent_grad = mm("htk,thc->kc", soft_weights.astype(LOW), latent_out_grad)
-    row_inner = jnp.sum(soft_weights * soft_grad, axis=-1, keepdims=True)
-    score_grad = (soft_weights * (soft_grad - row_inner) * score_scale).astype(LOW)
-    query_latent_grad = mm("htk,kc->thc", score_grad, all_latent).astype(LOW)
-    all_latent_grad = all_latent_grad + mm("htk,thc->kc", score_grad, query_latent)
-    query_rope_grad = mm("htk,kd->thd", score_grad, all_keys)
-    all_keys_grad = mm("htk,thd->kd", score_grad, query_rope)
+    latent_out_grad = mm("thv,chv->htc", values_grad, expand_value).astype(LOW)
+    query_latent_grad, turned_grad, all_latent_grad, all_keys_grad = attend_back(
+        query_latent,
+        query_turned,
+        all_latent,
+        all_keys,
+        latent_out,
+        log_total,
+        latent_out_grad,
+        ctx_count,
+        score_scale,
+    )
+    query_rope_grad = turned_grad[:, :, :ROPE].swapaxes(0, 1)
+    keys_part = jnp.concatenate([all_latent_grad, all_keys_grad[:, :ROPE]], axis=1)
+    keys_part = keys_part.reshape(2, ctx_count, half_rows, LATENT + ROPE)
+    keys_part = jnp.stack([keys_part[0], keys_part[1, ::-1]], axis=1)
+    (keys_part,) = after((keys_part,), pair_grad, sdown_grad)
     keys_part = lax.psum_scatter(
-        jnp.concatenate([all_latent_grad, all_keys_grad], axis=1),
-        "ctx",
-        scatter_dimension=0,
-        tiled=True,
+        keys_part.reshape(sequence, LATENT + ROPE), "ctx", scatter_dimension=0, tiled=True
     )
     latent_grad, keys_grad = (keys_part[:, :LATENT], keys_part[:, LATENT:])
-    query_nope_grad = mm("thc,chd->thd", query_latent_grad, expand_key)
-    expand_key_grad = mm("thd,thc->chd", query_nope, query_latent_grad)
+    expand_value_grad = mm("htc,thv->chv", latent_out, values_grad)
+
+    (up_sum,) = after((up_sum,), gate_returned, all_latent_grad)
+    up_returned = along_line(up_sum)
+    (out_part,) = after(
+        (
+            (
+                mm("bts,bsd->btd", mixer, came_back)
+                + shared_out.reshape(ctx_count, row_count, model_width)
+            ).astype(LOW),
+        ),
+        keys_part,
+    )
+    out_sum = lax.psum_scatter(out_part, "ctx", scatter_dimension=0, tiled=False).astype(FULL)
+    layer_out = (middle + out_sum).astype(LOW)[None]
+    (pair_grad,) = after((pair_grad,), up_returned)
+    pair_grad = lax.all_to_all(
+        pair_grad, "ctx", split_axis=1, concat_axis=2, tiled=True
+    ).astype(FULL)
+    sdown_grad = sdown_grad.astype(FULL)
+
+    query_nope_grad = mm("htc,chd->thd", query_latent_grad, expand_key)
+    expand_key_grad = mm("thd,htc->chd", query_nope, query_latent_grad)
     expand_grad = jnp.concatenate([expand_key_grad, expand_value_grad], axis=-1).reshape(
         LATENT, HEADS * (NOPE + VDIM)
     )
@@ -1254,8 +1422,24 @@
         ],
         axis=1,
     )
+    (down_sum,) = after((down_sum,), up_returned, normed_grad, pair_grad)
+    down_returned = along_line(down_sum)
+    dense_grads = after(
+        (query_weight_grad, tail_grad, expand_grad, output_weight_grad), up_returned
+    )
     query_sum, tail_sum, expand_sum, output_sum = scatter_all(
-        (query_weight_grad, tail_grad, expand_grad, output_weight_grad), ctx_count, fsdp_count
+        dense_grads, ctx_count, fsdp_count
+    )
+
+    def owned(moved, like):
+        moved = moved.reshape((members, EXP_DEV) + moved.shape[1:])
+        moved = swap_parts(moved, members, fsdp_count).swapaxes(0, 1)
+        return moved.reshape(like.shape).astype(FULL)
+
+    expert_grads = (
+        owned(gate_returned, expert_gate),
+        owned(up_returned, expert_up),
+        owned(down_returned, expert_down),
     )
     return (
         layer_out,

time: 1800 us -> 1560 us (0.87)
  waiting for transfers between devices: 314 us -> 142 us
  matrix products: 464 us -> 314 us
  Pallas kernels: 658 us -> 730 us
    all_to_all x6, waiting for transfers between devices: 265 us -> 102 us  [along_line(): return lax.all_to_all(array, 'ctx', split_axis=0, concat_axis=0, tiled=True)]
    dot_general x32 -> x25, matrix products: 341 us -> 213 us  [mm(): return jnp.einsum(subscripts, left, right, preferred_element_type=FULL)]
    pallas_call x0 -> x2, Pallas kernels: none -> 61.3 us  [the longest x1 32.3 us: attend_back(): pl.pallas_call(functools.partial(attend_back_kernel, ctx_count, scale), g...]
    all_to_all x1, waiting for transfers between devices: 42.8 us -> 0.01 us  [local(): lax.all_to_all(result.reshape(slots_shape), 'fsdp', split_axis=1, concat_...]
    dot_general x2 -> x0, matrix products: 24.4 us -> none  [the longest x1 13 us: score_block(): jnp.einsum('thc,kc->htk', query_latent, all_latent, preferred_element_typ...]
    reduce_scatter x2, waiting for transfers between devices: 0.01 us -> 19.6 us  [the longest x1 19.6 us: local(): lax.psum_scatter(keys_part.reshape(sequence, LATENT + ROPE), 'ctx', scatt...]
    unnamed x199 -> x171, local copies, waits for them, and re-layouts: 40.2 us -> 38.9 us
  transfers between devices with their start and end apart: 25 -> 25, of which waited for: 8 -> 5; matrix products, arithmetic and copies ran while one was open for 32% -> 27% of each run, Pallas kernels for 24% -> 33%
where the time goes in v3:
time: 1560 us; the launch traced here: 1550 us
  Pallas kernels  730 us (47%)
  matrix products  314 us (20%)
  local copies, waits for them, and re-layouts  203 us (13%)
  waiting for transfers between devices  142 us (9%)
  other arithmetic  88.8 us (6%)
  starting transfers between devices  54.5 us (3%)
    pallas_call x2, Pallas kernels, dispatch_rows(): pl.pallas_call(functools.partial(dispatch_kernel, ctx_count), out_shape=(...  247 us
    dot_general x25, matrix products, mm(): return jnp.einsum(subscripts, left, right, preferred_element_type=FULL)  213 us
    pallas_call x1, Pallas kernels, gather_arrays(): pl.pallas_call(functools.partial(gather_kernel, ctx_count, kinds), out_sh...  186 us
    pallas_call x1, Pallas kernels, scatter_arrays(): pl.pallas_call(functools.partial(scatter_kernel, ctx_count, count), out_s...  125 us
    pallas_call x1, Pallas kernels, combine_rows(): pl.pallas_call(functools.partial(combine_kernel, ctx_count), out_shape=ja...  110 us
    all_to_all x6, waiting for transfers between devices, along_line(): return lax.all_to_all(array, 'ctx', split_axis=0, concat_axis=0, tiled=True)  102 us
    all_to_all x6, starting transfers between devices, along_line(): return lax.all_to_all(array, 'ctx', split_axis=0, concat_axis=0, tiled=True)  39.2 us
    unnamed x171, local copies, waits for them, and re-layouts  38.9 us
  transfers between devices with their start and end apart: 25, of which 5 were waited for; matrix products, arithmetic and copies ran while one was open for 27% of the time, Pallas kernels for 33%

profile of v3, /device:TPU:1, one launch (start us, length us, event | category | flops | bytes accessed | tf_op | source)
XLA Modules:
  0.0 1546.9 jit_solution(17020109574637465878)
XLA Ops:
  43.7 186.2 %shard_map.280 = (f32[4,16,256]{2,1,0:T(8,128)}, bf16[4,8,64,3072]{3,2,1,0:T(8,128)(2,1)}, bf16[4,8,64,768]{3,2,1,0:T(8,128)(2,1)}, bf16[4,8,16,4096]{3,2,1,0:T(...) custom-call(f32[16,256]{1,0:T(8,128)} %maximum_maximum_fusion.refs_0, ...), custom_call_target="tpu_custom_call" | custom-call | bytes 500000000 | tf_op jit(solution)/shard_map/pallas_call | solution.py:302
  229.9 14.5 all-to-all-start.1
  265.9 143.2 %shard_map.281 = (bf16[4,256,2048]{2,1,0:T(8,128)(2,1)}, bf16[4,8,64,2048]{3,2,1,0:T(8,128)(2,1)}) custom-call(bf16[256,2048]{1,0:T(8,128)(2,1)} %bitcast.399, bf16[4,512,256]{2,1,0:T(8,128)(2,1)} %get-tuple-element.134.choose_ref), custom_call_target="tpu_custom_call" | custom-call | flops 2000000000 | bytes 300000000 | tf_op jit(solution)/shard_map/pallas_call | solution.py:620
  413.6 9.7 fusion.81
  461.4 29.0 %shard_map.282 = (bf16[16,256,512]{2,1,0:T(8,128)(2,1)}, f32[16,256,1]{2,1,0:T(8,128)}) custom-call(bf16[16,256,512]{2,1,0:T(8,128)(2,1)} %convolution_convert_fusion.6.query_ref, bf16[16,256,128]{2,1,0:T(8,128)(2,1)} %pad.17.turned_ref, bf16[1024,512]{1,0:T(8,128)(2,1)} %slice.176.keys_ref, bf16[1024,128]{1,0:T(8,128)(2,1)} %slice.177.rope_ref), custom_call_target="tpu_custom_call" | custom-call | flops 12000000000 | bytes 12000000 | tf_op jit(solution)/shard_map/pallas_call | solution.py:934
  516.1 104.2 %shard_map.283 = (bf16[4,256,2048]{2,1,0:T(8,128)(2,1)}, bf16[4,8,64,2048]{3,2,1,0:T(8,128)(2,1)}) custom-call(bf16[256,2048]{1,0:T(8,128)(2,1)} %multiply_convert_fusion.6.rows_ref, bf16[4,512,256]{2,1,0:T(8,128)(2,1)} %get-tuple-element.133.choose_ref), custom_call_target="tpu_custom_call" | custom-call | flops 2000000000 | bytes 300000000 | tf_op jit(solution)/shard_map/pallas_call | solution.py:620
  646.8 7.7 add_convert_fusion.2
  654.5 16.2 %fusion.82 = f32[2048,1408]{1,0:T(8,128)} fusion(bf16[2048,2048]{1,0:T(8,128)(2,1)S(1)} %bitcast.433, bf16[2048,1408]{1,0:T(8,128)(2,1)S(1)} %bitcast.367), kind=kOutput, calls=%fused_computation.238 | convolution fusion | flops 11811160064 | bytes 25690112 | tf_op jit(solution)/shard_map/dot_general | solution.py:1272
  673.4 7.0 copy.266
  685.5 19.2 %fusion.85 = f32[2048,1408]{1,0:T(8,128)} fusion(bf16[2048,2048]{1,0:T(8,128)(2,1)} %bitcast.426, bf16[1408,2048]{1,0:T(8,128)(2,1)S(1)} %bitcast.374), kind=kOutput, calls=%fused_computation.241 | convolution fusion | flops 11811160064 | bytes 25690112 | tf_op jit(solution)/shard_map/sd,fd->sf/dot_general | solution.py:987
  704.7 29.9 %multiply_convert_fusion = (bf16[2048,1408]{1,0:T(8,128)(2,1)}, bf16[2048,1408]{1,0:T(8,128)(2,1)}, bf16[2048,1408]{1,0:T(8,128)(2,1)}) fusion(f32[2048,1408]{1,0:T(8,128)} %fusion.85, f32[2048,1408]{1,0:T(8,128)} %fusion.82, bf16[2048,2048]{1,0:T(8,128)(2,1)} %bitcast.428, bf16[2048,1408]{1,0:T(8,128)(2,1)} %bitcast.368), kind=kOutput, calls=%fused_computation.7 | convolution fusion | flops 11854413824 | bytes 54525952 | tf_op jit(solution)/shard_map/dot_general | solution.py:1271
  734.6 19.3 %fusion.86 = f32[2048,2048]{1,0:T(8,128)} fusion(bf16[2048,1408]{1,0:T(8,128)(2,1)} %get-tuple-element.101, bf16[2048,1408]{1,0:T(8,128)(2,1)} %bitcast.369), kind=kOutput, calls=%fused_computation.242 | convolution fusion | flops 11811160064 | bytes 28311552 | tf_op jit(solution)/shard_map/sf,df->sd/dot_general | solution.py:987
  753.9 21.7 %add_convert_fusion = bf16[2048,2048]{1,0:T(8,128)(2,1)} fusion(f32[2048,2048]{1,0:T(8,128)} %fusion.86, bf16[2048,1408]{1,0:T(8,128)(2,1)} %get-tuple-element.102, bf16[2048,1408]{1,0:T(8,128)(2,1)} %bitcast.364), kind=kOutput, calls=%fused_computation | convolution fusion | flops 11819548672 | bytes 36700160 | tf_op jit(solution)/shard_map/sf,df->sd/dot_general | solution.py:987
  775.5 110.4 %shard_map.284 = f32[256,2048]{1,0:T(8,128)} custom-call(bf16[4,8,64,2048]{3,2,1,0:T(8,128)(2,1)} %bitcast.360, bf16[4,256,512]{2,1,0:T(8,128)(2,1)} %get-tuple-element.132.mix_ref, bf16[4,256,2048]{2,1,0:T(8,128)(2,1)} %bitcast.390), custom_call_target="tpu_custom_call" | custom-call | flops 2000000000 | bytes 300000000 | tf_op jit(solution)/shard_map/pallas_call | solution.py:784
  906.0 18.5 %convolution_convert_fusion = bf16[2048,2048]{1,0:T(8,128)(2,1)} fusion(bf16[2048,1408]{1,0:T(8,128)(2,1)} %get-tuple-element.103, bf16[1408,2048]{1,0:T(8,128)(2,1)} %bitcast.375), kind=kOutput, calls=%fused_computation.15 | convolution fusion | flops 11815354368 | bytes 19922944 | tf_op jit(solution)/shard_map/dot_general | solution.py:1316
  924.5 8.4 copy.268
  938.9 17.3 %convolution_convert_fusion.3 = bf16[2048,1408]{1,0:T(8,128)(2,1)S(1)} fusion(bf16[2048,2048]{1,0:T(8,128)(2,1)} %bitcast.429, bf16[2048,1408]{1,0:T(8,128)(2,1)} %get-tuple-element.101), kind=kOutput, calls=%fused_computation.18 | convolution fusion | flops 11814043648 | bytes 19922944 | tf_op jit(solution)/shard_map/sd,sf->df/dot_general | solution.py:987
  959.9 17.9 %convolution_convert_fusion.1 = bf16[1408,2048]{1,0:T(8,128)(2,1)} fusion(bf16[2048,1408]{1,0:T(8,128)(2,1)} %get-tuple-element.103, bf16[2048,2048]{1,0:T(8,128)(2,1)} %bitcast.427), kind=kOutput, calls=%fused_computation.16 | convolution fusion | flops 11814043648 | bytes 19922944 | tf_op jit(solution)/shard_map/sf,sd->fd/dot_general | solution.py:987
  977.8 10.5 reshape.465
  995.3 17.6 %convolution_convert_fusion.2 = bf16[2048,1408]{1,0:T(8,128)(2,1)S(1)} fusion(bf16[2048,2048]{1,0:T(8,128)(2,1)} %bitcast.430, bf16[2048,1408]{1,0:T(8,128)(2,1)} %get-tuple-element.102), kind=kOutput, calls=%fused_computation.17 | convolution fusion | flops 11814043648 | bytes 19922944 | tf_op jit(solution)/shard_map/sd,sf->df/dot_general | solution.py:987
  1016.6 9.5 fusion.88
  1040.4 9.6 copy.269
  1071.1 32.3 %shard_map.285 = (bf16[16,256,512]{2,1,0:T(8,128)(2,1)}, f32[16,256,128]{2,1,0:T(8,128)}, f32[1024,512]{1,0:T(8,128)}, f32[1024,128]{1,0:T(8,128)}) custom-call(bf16[16,256,512]{2,1,0:T(8,128)(2,1)} %convolution_convert_fusion.6.query_ref, bf16[16,256,128]{2,1,0:T(8,128)(2,1)} %pad.17.turned_ref, bf16[1024,512]{1,0:T(8,128)(2,1)} %slice.176.keys_ref, ...), custom_call_target="tpu_custom_call" | custom-call | flops 30000001024 | bytes 30000000 | tf_op jit(solution)/shard_map/pallas_call | solution.py:960
  1116.7 32.3 %all-to-all-done.4 = bf16[4,256,1408]{2,1,0:T(8,128)(2,1)} async-done(((bf16[4,256,1408]{2,1,0:T(8,128)(2,1)}), bf16[4,256,1408]{2,1,0:T(8,128)(2,1)}, u32[]{:S(2)}, u32[]{:S(2)}) %all-to-all-start.4) | async-done | bytes 2883616 | tf_op jit(solution)/shard_map/all_to_all | solution.py:1086
  1164.2 7.9 add_convert_fusion.1
  1176.0 19.6 %reduce-scatter.9.cloned.1.call-done = f32[256,576]{0,1:T(8,128)} async-done(((f32[1024,576]{0,1:T(8,128)}), f32[256,576]{0,1:T(8,128)}) %reduce-scatter.9.cloned.1.call-update) | async-done | bytes 589840 | tf_op jit(solution)/shard_map/reduce_scatter | solution.py:1363
  1207.3 7.8 fusion.89
  1215.2 69.3 %all-to-all-done.5 = bf16[4,256,1408]{2,1,0:T(8,128)(2,1)} async-done(((bf16[4,256,1408]{2,1,0:T(8,128)(2,1)}), bf16[4,256,1408]{2,1,0:T(8,128)(2,1)}, u32[]{:S(2)}, u32[]{:S(2)}) %all-to-all-start.5) | async-done | bytes 2883616 | tf_op jit(solution)/shard_map/all_to_all | solution.py:1086
  1299.4 16.8 %all-to-all-done.6 = bf16[2,256,704]{2,0,1:T(2,128)(2,1)} async-done(((bf16[2,256,704]{2,0,1:T(2,128)(2,1)}), bf16[2,256,704]{2,0,1:T(2,128)(2,1)}, u32[]{:S(2)}, u32[]{:S(2)}) %all-to-all-start.6) | async-done | bytes 720928 | tf_op jit(solution)/shard_map/all_to_all | solution.py:1383
  1341.5 16.5 %concatenate.47 = bf16[2048,768]{0,1:T(8,128)(2,1)} concatenate(bf16[2048,576]{0,1:T(8,128)(2,1)} %fusion.49, f32[2048,1]{0,1:T(1,128)S(1)} %bitcast.415, f32[2048,1]{0,1:T(1,128)S(1)} %bitcast.413, bf16[2048,1]{0,1:T(2,128)(2,1)S(1)} %broadcast_in_dim_reshape.3, bf16[2048,189]{0,1:T(8,128)(2,1)} %broadcast_in_dim.100), dimensions={1} | concatenate | bytes 6299648 | tf_op jit(solution)/shard_map/concatenate | solution.py:1415
  1358.0 10.0 fusion.90
  1384.4 124.8 %shard_map.286 = (f32[64,3072]{1,0:T(8,128)}, f32[64,768]{1,0:T(8,128)}, f32[16,4096]{1,0:T(8,128)}, f32[64,2048]{1,0:T(8,128)}) custom-call(bf16[4,4,2,64,3072]{4,3,2,1,0:T(8,128)(2,1)} %bitcast.336, bf16[4,4,2,64,768]{4,3,2,1,0:T(8,128)(2,1)} %bitcast.353, bf16[4,4,2,16,4096]{4,3,2,1,0:T(8,128)(2,1)} %bitcast.346, bf16[4,4,2,64,2048]{4,3,2,1,0:T(8,128)(2,1)} %bitcast.337), custom_call_target="tpu_custom_call" | custom-call | bytes 500000000 | tf_op jit(solution)/shard_map/pallas_call | solution.py:503
  (378 shorter events, 367.4 us)
Async XLA Ops:
  9.9 3.6 collective-permute-start
  17.0 212.9 %all-to-all-start = ((bf16[4,256,1408]{2,1,0:T(8,128)(2,1)}), bf16[4,256,1408]{2,1,0:T(8,128)(2,1)}, u32[]{:S(2)}, u32[]{:S(2)}) async-start(bf16[4,256,1408]{2,1,0:T(8,128)(2,1)} %bitcast.15), calls=%async_computation | async-start | bytes 5767168 | tf_op jit(solution)/shard_map/all_to_all | solution.py:1086
  25.5 13.6 collective-permute-start.1
  27.4 8.4 collective-permute-start.2
  229.9 179.2 %all-to-all-start.1 = ((bf16[4,256,1408]{2,1,0:T(8,128)(2,1)}), bf16[4,256,1408]{2,1,0:T(8,128)(2,1)}, u32[]{:S(2)}, u32[]{:S(2)}) async-start(bf16[4,256,1408]{2,1,0:T(8,128)(2,1)} %bitcast.355), calls=%async_computation.1 | async-start | bytes 5767168 | tf_op jit(solution)/shard_map/all_to_all | solution.py:1086
  244.4 204.2 %all-gather.3.cloned.1.call-start = ((), (), s32[]{:S(2)}) async-start(), calls=%async_computation.16 | async-start | bytes 1638400 | tf_op jit(solution)/shard_map/all_gather | solution.py:1246
  244.7 167.3 %copy-start.55 = (f32[32]{0:T(128)}, f32[32]{0:T(128)S(1)}, u32[]{:S(2)}) copy-start(f32[32]{0:T(128)S(1)} %multiply_power_fusion) | copy-start | bytes 388
  244.8 167.2 %copy-start.53 = (f32[256]{0:T(256)}, f32[256]{0:T(256)S(1)}, u32[]{:S(2)}) copy-start(f32[256]{0:T(256)S(1)} %fusion.74) | copy-start | bytes 3076
  256.4 155.9 %copy-start.43 = (f32[512]{0:T(512)}, f32[512]{0:T(512)S(1)}, u32[]{:S(2)}) copy-start(f32[512]{0:T(512)S(1)} %reshape.479) | copy-start | bytes 6148
  256.8 243.7 %copy-start.37 = (f32[2048,1]{0,1:T(1,128)}, f32[2048,1]{0,1:T(1,128)S(1)}, u32[]{:S(2)}) copy-start(f32[2048,1]{0,1:T(1,128)S(1)} %copy.314) | copy-start | bytes 24580
  265.9 147.8 %copy-start.17 = (bf16[256,2048]{1,0:T(8,128)(2,1)}, bf16[256,2048]{1,0:T(8,128)(2,1)S(1)}, u32[]{:S(2)}) copy-start(bf16[256,2048]{1,0:T(8,128)(2,1)S(1)} %fusion.12) | copy-start | bytes 3145732
  438.0 78.1 %all-to-all-start.2 = ((bf16[4,704,512]{2,1,0:T(8,128)(2,1)}), bf16[4,704,512]{2,1,0:T(8,128)(2,1)}, u32[]{:S(2)}, u32[]{:S(2)}) async-start(bf16[4,704,512]{2,1,0:T(8,128)(2,1)} %bitcast.354), calls=%async_computation.2 | async-start | bytes 5767168 | tf_op jit(solution)/shard_map/all_to_all | solution.py:1086
  442.6 664.4 %reduce-scatter.7.cloned.1.call-start = ((), (), s32[]{:S(2)}) async-start(), calls=%async_computation.13 | async-start | bytes 3244032 | tf_op jit(solution)/shard_map/reduce_scatter | solution.py:1315
  442.7 60.3 %collective-permute-start.4 = (bf16[4,256,1408]{2,1,0:T(8,128)(2,1)}, bf16[4,256,1408]{2,1,0:T(8,128)(2,1)}, u32[]{:S(2)}, u32[]{:S(2)}) collective-permute-start(bf16[4,256,1408]{2,1,0:T(8,128)(2,1)} %all-to-all-done.1), channel_id=1, source_target_pairs={{0,1},{1,0},{2,3},{3,2},{4,5},{5,4},{6,7},{7,6},{8,9},{9,8},{10,11... | collective-permute-start | bytes 8650760 | tf_op jit(solution)/shard_map/ppermute | solution.py:1022
  443.0 66.7 %collective-permute-start.3 = (bf16[4,256,1408]{2,1,0:T(8,128)(2,1)}, bf16[4,256,1408]{2,1,0:T(8,128)(2,1)}, u32[]{:S(2)}, u32[]{:S(2)}) collective-permute-start(bf16[4,256,1408]{2,1,0:T(8,128)(2,1)} %all-to-all-done), channel_id=1, source_target_pairs={{0,1},{1,0},{2,3},{3,2},{4,5},{5,4},{6,7},{7,6},{8,9},{9,8},{10,11... | collective-permute-start | bytes 8650760 | tf_op jit(solution)/shard_map/ppermute | solution.py:1022
  654.5 16.2 %collective-permute-start.5 = (bf16[4,704,512]{2,1,0:T(8,128)(2,1)}, bf16[4,704,512]{2,1,0:T(8,128)(2,1)S(1)}, u32[]{:S(2)}, u32[]{:S(2)}) collective-permute-start(bf16[4,704,512]{2,1,0:T(8,128)(2,1)} %all-to-all-done.2), channel_id=1, source_target_pairs={{0,1},{1,0},{2,3},{3,2},{4,5},{5,4},{6,7},{7,6},{8,9},{9,8},{10,11... | collective-permute-start | bytes 8650760 | tf_op jit(solution)/shard_map/ppermute | solution.py:1022
  775.5 110.4 %copy-start.69 = (bf16[1024,704]{0,1:T(8,128)(2,1)S(1)}, bf16[1024,704]{0,1:T(8,128)(2,1)}, u32[]{:S(2)}) copy-start(bf16[1024,704]{0,1:T(8,128)(2,1)} %copy-done.68) | copy-start | bytes 4325380
  932.8 107.6 %all-to-all-start.3 = ((bf16[4,8,64,2048]{3,2,0,1:T(8,128)(2,1)}), bf16[4,8,64,2048]{3,2,0,1:T(8,128)(2,1)}, u32[]{:S(2)}, u32[]{:S(2)}) async-start(bf16[4,8,64,2048]{3,2,0,1:T(8,128)(2,1)} %copy.268), calls=%async_computation.3 | async-start | bytes 16777216 | tf_op jit(solution)/shard_map/all_to_all | solution.py:1317
  938.9 168.2 %reduce-scatter.5.cloned.1.call-start = ((), (), s32[]{:S(2)}) async-start(), calls=%async_computation.12 | async-start | bytes 7077888 | tf_op jit(solution)/shard_map/reduce_scatter | solution.py:1314
  959.6 71.2 %collective-permute-start.6 = (bf16[4,256,1408]{2,1,0:T(8,128)(2,1)}, bf16[4,256,1408]{2,1,0:T(8,128)(2,1)}, u32[]{:S(2)}, u32[]{:S(2)}) collective-permute-start(bf16[4,256,1408]{2,1,0:T(8,128)(2,1)} %dynamic-slice_bitcast_fusion.1), channel_id=1, source_target_pairs={{0,1},{1,0},{2,3},{3,2},{4,5},{5,4},{6,7},{7,6},{8,9},{9,8},{10,11... | collective-permute-start | bytes 8650760 | tf_op jit(solution)/shard_map/ppermute | solution.py:1032
  995.1 31.0 %collective-permute-start.8 = (bf16[4,704,512]{2,1,0:T(8,128)(2,1)}, bf16[4,704,512]{2,1,0:T(8,128)(2,1)}, u32[]{:S(2)}, u32[]{:S(2)}) collective-permute-start(bf16[4,704,512]{2,1,0:T(8,128)(2,1)} %bitcast.332), channel_id=1, source_target_pairs={{0,1},{1,0},{2,3},{3,2},{4,5},{5,4},{6,7},{7,6},{8,9},{9,8},{10,11... | collective-permute-start | bytes 8650760 | tf_op jit(solution)/shard_map/ppermute | solution.py:1032
  1016.3 20.1 %collective-permute-start.7 = (bf16[4,256,1408]{2,1,0:T(8,128)(2,1)}, bf16[4,256,1408]{2,1,0:T(8,128)(2,1)}, u32[]{:S(2)}, u32[]{:S(2)}) collective-permute-start(bf16[4,256,1408]{2,1,0:T(8,128)(2,1)} %dynamic-slice_bitcast_fusion), channel_id=1, source_target_pairs={{0,1},{1,0},{2,3},{3,2},{4,5},{5,4},{6,7},{7,6},{8,9},{9,8},{10,11... | collective-permute-start | bytes 8650760 | tf_op jit(solution)/shard_map/ppermute | solution.py:1032
  1061.5 87.4 %all-to-all-start.4 = ((bf16[4,256,1408]{2,1,0:T(8,128)(2,1)}), bf16[4,256,1408]{2,1,0:T(8,128)(2,1)}, u32[]{:S(2)}, u32[]{:S(2)}) async-start(bf16[4,256,1408]{2,1,0:T(8,128)(2,1)} %fusion.3), calls=%async_computation.8 | async-start | bytes 5767168 | tf_op jit(solution)/shard_map/all_to_all | solution.py:1086
  1066.1 129.5 %reduce-scatter.9.cloned.1.call-start = ((), (), s32[]{:S(2)}) async-start(), calls=%async_computation.14 | async-start | bytes 2949120 | tf_op jit(solution)/shard_map/reduce_scatter | solution.py:1363
  1148.9 135.5 %all-to-all-start.5 = ((bf16[4,256,1408]{2,1,0:T(8,128)(2,1)}), bf16[4,256,1408]{2,1,0:T(8,128)(2,1)}, u32[]{:S(2)}, u32[]{:S(2)}) async-start(bf16[4,256,1408]{2,1,0:T(8,128)(2,1)} %fusion.2), calls=%async_computation.9 | async-start | bytes 5767168 | tf_op jit(solution)/shard_map/all_to_all | solution.py:1086
  1153.5 381.7 %reduce-scatter.11.cloned.1.call-start = ((), (), s32[]{:S(2)}) async-start(), calls=%async_computation.15 | async-start | bytes 5242880 | tf_op jit(solution)/shard_map/reduce_scatter | solution.py:1380
  1174.8 156.9 %collective-permute-start.9 = (bf16[2,256,1408]{2,1,0:T(8,128)(2,1)}, bf16[2,256,1408]{2,1,0:T(8,128)(2,1)}, u32[]{:S(2)}, u32[]{:S(2)}) collective-permute-start(bf16[2,256,1408]{2,1,0:T(8,128)(2,1)} %dynamic-slice_bitcast_fusion.4), channel_id=1, source_target_pairs={{0,1},{1,0},{2,3},{3,2},{4,5},{5,4},{6,7},{7,6},{8,9},{9,8},{10,11... | collective-permute-start | bytes 4325384 | tf_op jit(solution)/shard_map/ppermute | solution.py:1011
  1215.1 79.2 %copy-start.51 = (f32[256]{0:T(256)S(1)}, f32[256]{0:T(256)}, u32[]{:S(2)}) copy-start(f32[256]{0:T(256)} %copy-done.50) | copy-start | bytes 3076
  1287.2 28.9 %all-to-all-start.6 = ((bf16[2,256,704]{2,0,1:T(2,128)(2,1)}), bf16[2,256,704]{2,0,1:T(2,128)(2,1)}, u32[]{:S(2)}, u32[]{:S(2)}) async-start(bf16[2,256,704]{2,0,1:T(2,128)(2,1)} %copy.282), calls=%async_computation.10 | async-start | bytes 1572864 | tf_op jit(solution)/shard_map/all_to_all | solution.py:1383
  1316.2 198.8 %all-to-all-start.7 = ((bf16[4,704,512]{2,1,0:T(8,128)(2,1)}), bf16[4,704,512]{2,1,0:T(8,128)(2,1)}, u32[]{:S(2)}, u32[]{:S(2)}) async-start(bf16[4,704,512]{2,1,0:T(8,128)(2,1)} %fusion.1), calls=%async_computation.11 | async-start | bytes 5767168 | tf_op jit(solution)/shard_map/all_to_all | solution.py:1086
  1370.7 153.6 %collective-permute-start.10 = (bf16[2,256,1408]{2,1,0:T(8,128)(2,1)}, bf16[2,256,1408]{2,1,0:T(8,128)(2,1)}, u32[]{:S(2)}, u32[]{:S(2)}) collective-permute-start(bf16[2,256,1408]{2,1,0:T(8,128)(2,1)} %dynamic-slice_bitcast_fusion.3), channel_id=1, source_target_pairs={{0,1},{1,0},{2,3},{3,2},{4,5},{5,4},{6,7},{7,6},{8,9},{9,8},{10,11... | collective-permute-start | bytes 4325384 | tf_op jit(solution)/shard_map/ppermute | solution.py:1011
  1517.5 12.1 collective-permute-start.11
  (71 other events, 813.6 us)
Sparse Core Ops, SparseCore 0:
  413.8 30.8 all-gather.2
  906.1 49.4 reduce-scatter.6
  1016.7 62.9 reduce-scatter.4
  1115.9 79.6 reduce-scatter.8
  1197.7 96.0 reduce-scatter.10

commit v4 on v3

--- a/solution.py
+++ b/solution.py
@@ -527,290 +527,6 @@
     )
 
 
-PEERS = (6, 7, 2, 4, 3, 5, 1)
-
-
-def dispatch_kernel(
-    ctx_count,
-    rows_ref,
-    choose_ref,
-    all_ref,
-    out_ref,
-    blocks,
-    chosen,
-    own_sem,
-    all_sem,
-    keep_sem,
-    z_send,
-    z_recv,
-    p_send,
-    p_recv,
-):
-    z, f = lax.axis_index("ctx"), lax.axis_index("fsdp")
-    width = rows_ref.shape[1]
-    groups, share = chosen.shape[1], chosen.shape[2]
-    greet(z, f, PEERS, ctx_count)
-    own = pltpu.make_async_copy(rows_ref, blocks.at[z], own_sem)
-    own.start()
-    own.wait()
-
-    def z_copy(block, way, target):
-        at = blocks.at[block]
-        return remote(at, at, z_send.at[block, way], z_recv.at[block], target, f)
-
-    def p_copy(block, place):
-        to = toggled(f, PEERS[place])
-        return remote(
-            chosen.at[block, to],
-            out_ref.at[block, f],
-            p_send.at[block, place],
-            p_recv.at[block, place],
-            z,
-            to,
-        )
-
-    def p_arrived(block, place):
-        at = out_ref.at[block, toggled(f, PEERS[place])]
-        remote(at, at, p_send.at[block, place], p_recv.at[block, place], z, flip(f, 1)).wait_recv()
-
-    def keep(block):
-        return pltpu.make_async_copy(
-            chosen.at[block, f], out_ref.at[block, f], keep_sem.at[block]
-        )
-
-    def store(block):
-        return pltpu.make_async_copy(blocks.at[block], all_ref.at[block], all_sem.at[block])
-
-    for step in range(ctx_count):
-        block = nearest(z, step)
-        if step > 0:
-            at = blocks.at[block]
-            remote(at, at, z_send.at[block, 0], z_recv.at[block], z, flip(f, 1)).wait_recv()
-        both_ways(z, block, ctx_count, lambda way, to: z_copy(block, way, to).start())
-        store(block).start()
-
-        @pl.loop(0, width, step=256)
-        def _(start):
-            part = pl.ds(pl.multiple_of(start, 256), 256)
-            tile = jnp.dot(
-                choose_ref[block], blocks[block, :, part], preferred_element_type=FULL
-            ).astype(LOW)
-            chosen[block, :, :, part] = tile.reshape(groups, share, 256)
-
-        for place in range(len(PEERS)):
-            p_copy(block, place).start()
-        keep(block).start()
-    for step in range(ctx_count):
-        block = nearest(z, step)
-        store(block).wait()
-        keep(block).wait()
-        for place in range(len(PEERS)):
-            p_arrived(block, place)
-    for step in range(ctx_count):
-        block = nearest(z, step)
-        both_ways(z, block, ctx_count, lambda way, to: z_copy(block, way, to).wait_send())
-        for place in range(len(PEERS)):
-            p_copy(block, place).wait_send()
-
-
-def dispatch_rows(rows, chooser, ctx_count, fsdp_count):
-    count, width = rows.shape
-    share = chooser.shape[1] // fsdp_count
-    dma = pltpu.SemaphoreType.DMA
-    return pl.pallas_call(
-        functools.partial(dispatch_kernel, ctx_count),
-        out_shape=(
-            jax.ShapeDtypeStruct((ctx_count, count, width), LOW),
-            jax.ShapeDtypeStruct((ctx_count, fsdp_count, share, width), LOW),
-        ),
-        in_specs=[pl.BlockSpec(memory_space=pl.ANY), pl.BlockSpec(memory_space=pltpu.VMEM)],
-        out_specs=(pl.BlockSpec(memory_space=pl.ANY), pl.BlockSpec(memory_space=pl.ANY)),
-        scratch_shapes=[
-            pltpu.VMEM((ctx_count, count, width), LOW),
-            pltpu.VMEM((ctx_count, fsdp_count, share, width), LOW),
-            dma,
-            dma((ctx_count,)),
-            dma((ctx_count,)),
-            dma((ctx_count, 2)),
-            dma((ctx_count,)),
-            dma((ctx_count, len(PEERS))),
-            dma((ctx_count, len(PEERS))),
-        ],
-        compiler_params=pltpu.CompilerParams(
-            collective_id=2, has_side_effects=True, vmem_limit_bytes=BIG_VMEM
-        ),
-        cost_estimate=pl.CostEstimate(
-            flops=2_000_000_000, bytes_accessed=300_000_000, transcendentals=0
-        ),
-    )(rows, chooser)
-
-
-def combine_kernel(
-    ctx_count,
-    slots_ref,
-    mix_ref,
-    extra_ref,
-    out_ref,
-    arrived,
-    extra,
-    parts,
-    from_z,
-    keep_sem,
-    extra_sem,
-    p_send,
-    p_recv,
-    z_send,
-    z_recv,
-):
-    z, f = lax.axis_index("ctx"), lax.axis_index("fsdp")
-    count, width = out_ref.shape
-    slots = mix_ref.shape[2]
-    greet(z, f, PEERS, ctx_count)
-
-    def p_copy(block, place):
-        to = toggled(f, PEERS[place])
-        return remote(
-            slots_ref.at[block, to],
-            arrived.at[block, f],
-            p_send.at[block, place],
-            p_recv.at[block, place],
-            z,
-            to,
-        )
-
-    def p_arrived(block, place):
-        at = arrived.at[block, toggled(f, PEERS[place])]
-        remote(at, at, p_send.at[block, place], p_recv.at[block, place], z, flip(f, 1)).wait_recv()
-
-    def keep(block):
-        return pltpu.make_async_copy(
-            slots_ref.at[block, f], arrived.at[block, f], keep_sem.at[block]
-        )
-
-    def load(block):
-        return pltpu.make_async_copy(extra_ref.at[block], extra.at[block], extra_sem.at[block])
-
-    def z_copy(block, way, target):
-        return remote(
-            parts.at[block],
-            from_z.at[way, block],
-            z_send.at[block],
-            z_recv.at[way, block],
-            target,
-            f,
-        )
-
-    def z_arrived(block, way):
-        at = from_z.at[way, block]
-        remote(at, at, z_send.at[block], z_recv.at[way, block], z, flip(f, 1)).wait_recv()
-
-    def mix(block, target, *ways):
-        @pl.loop(0, width, step=256)
-        def _(start):
-            part = pl.ds(pl.multiple_of(start, 256), 256)
-            total = jnp.dot(
-                mix_ref[block],
-                arrived[block, :, :, part].reshape(slots, 256),
-                preferred_element_type=FULL,
-            ) + extra[block, :, part].astype(FULL)
-            for way in ways:
-                total = total + from_z[way, block, :, part].astype(FULL)
-            target[:, part] = total.astype(target.dtype)
-
-    order = [nearest(z, ctx_count - 1 - step) for step in range(ctx_count)]
-    for block in order:
-        for place in range(len(PEERS)):
-            p_copy(block, place).start()
-        keep(block).start()
-        load(block).start()
-    for step in range(ctx_count):
-        block = order[step]
-        keep(block).wait()
-        load(block).wait()
-        for place in range(len(PEERS)):
-            p_arrived(block, place)
-        if step < ctx_count - 1:
-            for way, above in ((1, True), (0, False)):
-                heading = (block < z) if above else (block > z)
-                has_more = (z < ctx_count - 1) if above else (z > 0)
-
-                @pl.when(heading & has_more)
-                def _():
-                    z_arrived(block, way)
-                    mix(block, parts.at[block], way)
-
-                @pl.when(heading & jnp.logical_not(has_more))
-                def _():
-                    mix(block, parts.at[block])
-
-                @pl.when(heading)
-                def _():
-                    z_copy(block, way, z - 1 if above else z + 1).start()
-
-        else:
-
-            @pl.when(z > 0)
-            def _():
-                z_arrived(block, 0)
-
-            @pl.when(z < ctx_count - 1)
-            def _():
-                z_arrived(block, 1)
-
-            @pl.when(z == 0)
-            def _():
-                mix(block, out_ref, 1)
-
-            @pl.when(z == ctx_count - 1)
-            def _():
-                mix(block, out_ref, 0)
-
-            @pl.when((z > 0) & (z < ctx_count - 1))
-            def _():
-                mix(block, out_ref, 0, 1)
-
-    for step in range(ctx_count):
-        block = order[step]
-        for place in range(len(PEERS)):
-            p_copy(block, place).wait_send()
-        if step < ctx_count - 1:
-            z_copy(block, 0, z).wait_send()
-
-
-def combine_rows(slots, mixer, extra, ctx_count, fsdp_count):
-    share, width = slots.shape[2:]
-    count = mixer.shape[1]
-    dma = pltpu.SemaphoreType.DMA
-    return pl.pallas_call(
-        functools.partial(combine_kernel, ctx_count),
-        out_shape=jax.ShapeDtypeStruct((count, width), FULL),
-        in_specs=[
-            pl.BlockSpec(memory_space=pl.ANY),
-            pl.BlockSpec(memory_space=pltpu.VMEM),
-            pl.BlockSpec(memory_space=pl.ANY),
-        ],
-        out_specs=pl.BlockSpec(memory_space=pltpu.VMEM),
-        scratch_shapes=[
-            pltpu.VMEM((ctx_count, fsdp_count, share, width), LOW),
-            pltpu.VMEM((ctx_count, count, width), LOW),
-            pltpu.VMEM((ctx_count, count, width), LOW),
-            pltpu.VMEM((2, ctx_count, count, width), LOW),
-            dma((ctx_count,)),
-            dma((ctx_count,)),
-            dma((ctx_count, len(PEERS))),
-            dma((ctx_count, len(PEERS))),
-            dma((ctx_count,)),
-            dma((2, ctx_count)),
-        ],
-        compiler_params=pltpu.CompilerParams(
-            collective_id=3, has_side_effects=True, vmem_limit_bytes=BIG_VMEM
-        ),
-        cost_estimate=pl.CostEstimate(
-            flops=2_000_000_000, bytes_accessed=300_000_000, transcendentals=0
-        ),
-    )(slots, mixer, extra)
-
-
 HEAD_GROUP = 4
 KEYS = 256
 
@@ -983,6 +699,567 @@
     )(query, turned, keys, rope, out, logs, grad)
 
 
+PEERS = (6, 7, 2, 4, 3, 5, 1)
+COLUMN_AT, GATE_AT, INFO_ROWS = 8, 16, 24
+
+
+def one_hot(info, z, slots, gated):
+    count = info.shape[1]
+    at = lax.broadcasted_iota(jnp.int32, (slots, count), 0).astype(FULL)
+    plane = z.astype(FULL)
+    total = jnp.zeros((slots, count), FULL)
+    for route in range(TOP):
+        hit = (info[COLUMN_AT + route][None, :] == at) & (info[route][None, :] == plane)
+        value = info[GATE_AT + route][None, :] if gated else 1.0
+        total = total + jnp.where(hit, value, 0.0)
+    return total.astype(LOW)
+
+
+class Dispatch:
+    def __init__(self, ctx_count, gated, rows_ref, info_ref, all_ref, blocks, chosen, arrived, sems):
+        self.own_sem, self.all_sem, self.keep_sem = sems[:3]
+        self.z_send, self.z_recv, self.p_send, self.p_recv = sems[3:]
+        self.ctx_count, self.gated = ctx_count, gated
+        self.rows_ref, self.info_ref, self.all_ref = rows_ref, info_ref, all_ref
+        self.blocks, self.chosen, self.arrived = blocks, chosen, arrived
+        self.z, self.f = lax.axis_index("ctx"), lax.axis_index("fsdp")
+        self.core = flip(self.f, 1)
+
+    def z_copy(self, block, way, target):
+        at = self.blocks.at[block]
+        sems = (self.z_send.at[block, way], self.z_recv.at[block])
+        return remote(at, at, *sems, target, self.f)
+
+    def p_copy(self, block, place):
+        to = toggled(self.f, PEERS[place])
+        sems = (self.p_send.at[block, place], self.p_recv.at[block, place])
+        return remote(
+            self.chosen.at[block, to], self.arrived.at[block, self.f], *sems, self.z, to
+        )
+
+    def keep(self, block):
+        source, target = self.chosen.at[block, self.f], self.arrived.at[block, self.f]
+        return pltpu.make_async_copy(source, target, self.keep_sem.at[block])
+
+    def store(self, block):
+        source, target = self.blocks.at[block], self.all_ref.at[block]
+        return pltpu.make_async_copy(source, target, self.all_sem.at[block])
+
+    def begin(self):
+        greet(self.z, self.f, PEERS, self.ctx_count)
+        own = pltpu.make_async_copy(self.rows_ref, self.blocks.at[self.z], self.own_sem)
+        own.start()
+        own.wait()
+
+    def pass_on(self, block, own):
+        if not own:
+            at = self.blocks.at[block]
+            sems = (self.z_send.at[block, 0], self.z_recv.at[block])
+            remote(at, at, *sems, self.z, self.core).wait_recv()
+        both_ways(
+            self.z, block, self.ctx_count, lambda way, to: self.z_copy(block, way, to).start()
+        )
+        self.store(block).start()
+        groups, share, width = self.chosen.shape[1:]
+        choose = one_hot(self.info_ref[block], self.z, groups * share, self.gated)
+
+        @pl.loop(0, width, step=256)
+        def _(start):
+            part = pl.ds(pl.multiple_of(start, 256), 256)
+            tile = jnp.dot(choose, self.blocks[block, :, part], preferred_element_type=FULL)
+            self.chosen[block, :, :, part] = tile.astype(LOW).reshape(groups, share, 256)
+
+        for place in range(len(PEERS)):
+            self.p_copy(block, place).start()
+        self.keep(block).start()
+
+    def await_slots(self, block):
+        self.keep(block).wait()
+        for place in range(len(PEERS)):
+            at = self.arrived.at[block, toggled(self.f, PEERS[place])]
+            sems = (self.p_send.at[block, place], self.p_recv.at[block, place])
+            remote(at, at, *sems, self.z, self.core).wait_recv()
+
+    def finish(self):
+        for step in range(self.ctx_count):
+            block = nearest(self.z, step)
+            self.store(block).wait()
+            both_ways(
+                self.z,
+                block,
+                self.ctx_count,
+                lambda way, to: self.z_copy(block, way, to).wait_send(),
+            )
+            for place in range(len(PEERS)):
+                self.p_copy(block, place).wait_send()
+
+
+def dispatch_scratch(ctx_count, fsdp_count, count, share, width):
+    dma = pltpu.SemaphoreType.DMA
+    return [
+        pltpu.VMEM((ctx_count, count, width), LOW),
+        pltpu.VMEM((ctx_count, fsdp_count, share, width), LOW),
+    ], [
+        dma,
+        dma((ctx_count,)),
+        dma((ctx_count,)),
+        dma((ctx_count, 2)),
+        dma((ctx_count,)),
+        dma((ctx_count, len(PEERS))),
+        dma((ctx_count, len(PEERS))),
+    ]
+
+
+def dispatch_kernel(ctx_count, rows_ref, info_ref, all_ref, out_ref, blocks, chosen, *sems):
+    move = Dispatch(ctx_count, True, rows_ref, info_ref, all_ref, blocks, chosen, out_ref, sems)
+    move.begin()
+    for step in range(ctx_count):
+        move.pass_on(nearest(move.z, step), step == 0)
+    for step in range(ctx_count):
+        move.await_slots(nearest(move.z, step))
+    move.finish()
+
+
+def dispatch_rows(rows, info, slots, ctx_count, fsdp_count):
+    count, width = rows.shape
+    share = slots // fsdp_count
+    buffers, sems = dispatch_scratch(ctx_count, fsdp_count, count, share, width)
+    return pl.pallas_call(
+        functools.partial(dispatch_kernel, ctx_count),
+        out_shape=(
+            jax.ShapeDtypeStruct((ctx_count, count, width), LOW),
+            jax.ShapeDtypeStruct((ctx_count, fsdp_count, share, width), LOW),
+        ),
+        in_specs=[pl.BlockSpec(memory_space=pl.ANY), pl.BlockSpec(memory_space=pltpu.VMEM)],
+        out_specs=(pl.BlockSpec(memory_space=pl.ANY), pl.BlockSpec(memory_space=pl.ANY)),
+        scratch_shapes=buffers + sems,
+        compiler_params=pltpu.CompilerParams(
+            collective_id=2, has_side_effects=True, vmem_limit_bytes=BIG_VMEM
+        ),
+        cost_estimate=pl.CostEstimate(
+            flops=2_000_000_000, bytes_accessed=300_000_000, transcendentals=0
+        ),
+    )(rows, info)
+
+
+def tiles(width, size=256):
+    return width // size, width % size
+
+
+def each_tile(width, act, size=256):
+    whole, rest = tiles(width, size)
+
+    @pl.loop(0, whole)
+    def _(index):
+        act(pl.ds(pl.multiple_of(index * size, size), size))
+
+    if rest:
+        act(pl.ds(whole * size, rest))
+
+
+def expert_kernel(ctx_count, rows_ref, info_ref, gate_ref, up_ref, down_ref, grads_ref, *refs):
+    all_ref, slots_ref, hidden_ref, gate_back_ref, up_back_ref, back_ref = refs[:6]
+    blocks, chosen, arrived, gate, up, down, grads, hidden, gate_back, up_back, back = refs[6:17]
+    weight_sem, grad_sem, slot_sem, side_sem, back_sem = refs[17:22]
+    move = Dispatch(
+        ctx_count, False, rows_ref, info_ref, all_ref, blocks, chosen, arrived, refs[22:]
+    )
+    slots, width = back.shape
+    units = hidden.shape[1]
+    order = [nearest(move.z, step) for step in range(ctx_count)]
+
+    def block_at(step):
+        block = order[0]
+        for place in range(1, ctx_count):
+            block = jnp.where(step == place, order[place], block)
+        return block
+
+    loads = [
+        pltpu.make_async_copy(source, target, weight_sem.at[place])
+        for place, (source, target) in enumerate(((gate_ref, gate), (up_ref, up), (down_ref, down)))
+    ]
+
+    def load_grads(step):
+        slot = lax.rem(step, 2)
+        return pltpu.make_async_copy(
+            grads_ref.at[block_at(step)], grads.at[slot], grad_sem.at[slot]
+        )
+
+    def store_slots(block):
+        return pltpu.make_async_copy(arrived.at[block], slots_ref.at[block], slot_sem.at[block])
+
+    def store_sides(block):
+        return [
+            pltpu.make_async_copy(source, target.at[block], side_sem.at[place])
+            for place, (source, target) in enumerate(
+                ((hidden, hidden_ref), (gate_back, gate_back_ref), (up_back, up_back_ref))
+            )
+        ]
+
+    def store_back(block):
+        return pltpu.make_async_copy(back, back_ref.at[block], back_sem)
+
+    move.begin()
+    for load in loads:
+        load.start()
+    load_grads(0).start()
+    move.pass_on(order[0], True)
+    move.pass_on(order[1], False)
+    for load in loads:
+        load.wait()
+
+    @pl.loop(0, ctx_count)
+    def _(step):
+        block = block_at(step)
+        slot = lax.rem(step, 2)
+
+        @pl.when(step + 1 < ctx_count)
+        def _():
+            load_grads(step + 1).start()
+
+        load_grads(step).wait()
+        move.await_slots(block)
+        store_slots(block).start()
+
+        @pl.when(step > 0)
+        def _():
+            for copy in store_sides(block):
+                copy.wait()
+
+        rows = arrived[block].reshape(slots, width)
+
+        def hidden_tile(part):
+            pre = jnp.dot(rows, gate[:, part], preferred_element_type=FULL)
+            linear = jnp.dot(rows, up[:, part], preferred_element_type=FULL)
+            grad = dot_last(grads[slot], down[part, :])
+            sigma = jax.nn.sigmoid(pre)
+            act = pre * sigma
+            hidden[:, part] = (act * linear).astype(LOW)
+            up_back[:, part] = (grad * act).astype(LOW)
+            gate_back[:, part] = (
+                grad * linear * (sigma * (1.0 + pre * (1.0 - sigma)))
+            ).astype(LOW)
+
+        each_tile(units, hidden_tile)
+        for copy in store_sides(block):
+            copy.start()
+
+        @pl.when(step > 0)
+        def _():
+            store_back(block).wait()
+
+        def back_tile(part):
+            total = dot_last(gate_back[...], gate[part, :]) + dot_last(up_back[...], up[part, :])
+            back[:, part] = total.astype(LOW)
+
+        each_tile(width, back_tile)
+        store_back(block).start()
+
+        @pl.when(step + 2 < ctx_count)
+        def _():
+            move.pass_on(block_at(step + 2), False)
+
+    for step in range(ctx_count):
+        store_slots(order[step]).wait()
+    for copy in store_sides(order[-1]):
+        copy.wait()
+    store_back(order[-1]).wait()
+    move.finish()
+
+
+def expert_rows(rows, info, gate, up, down, grads, ctx_count, fsdp_count):
+    count, width = rows.shape
+    slots = grads.shape[1]
+    share = slots // fsdp_count
+    units = gate.shape[1]
+    buffers, sems = dispatch_scratch(ctx_count, fsdp_count, count, share, width)
+    dma = pltpu.SemaphoreType.DMA
+    anywhere = pl.BlockSpec(memory_space=pl.ANY)
+    low = lambda *shape: jax.ShapeDtypeStruct((ctx_count,) + shape, LOW)
+    vmem = lambda *shape: pltpu.VMEM(shape, LOW)
+    return pl.pallas_call(
+        functools.partial(expert_kernel, ctx_count),
+        out_shape=(
+            low(count, width),
+            low(fsdp_count, share, width),
+            low(slots, units),
+            low(slots, units),
+            low(slots, units),
+            low(slots, width),
+        ),
+        in_specs=[anywhere, pl.BlockSpec(memory_space=pltpu.VMEM)] + [anywhere] * 4,
+        out_specs=(anywhere,) * 6,
+        scratch_shapes=buffers
+        + [
+            vmem(ctx_count, fsdp_count, share, width),
+            vmem(width, units),
+            vmem(width, units),
+            vmem(units, width),
+            vmem(2, slots, width),
+            vmem(slots, units),
+            vmem(slots, units),
+            vmem(slots, units),
+            vmem(slots, width),
+            dma((3,)),
+            dma((2,)),
+            dma((ctx_count,)),
+            dma((3,)),
+            dma,
+        ]
+        + sems,
+        compiler_params=pltpu.CompilerParams(
+            collective_id=4, has_side_effects=True, vmem_limit_bytes=BIG_VMEM
+        ),
+        cost_estimate=pl.CostEstimate(
+            flops=60_000_000_000, bytes_accessed=400_000_000, transcendentals=3_000_000
+        ),
+    )(rows, info, gate, up, down, grads)
+
+
+def combine_kernel(ctx_count, slots_ref, info_ref, extra_ref, *refs):
+    rows_ref, grads_ref, hidden_ref, gate_back_ref, up_back_ref = refs[:5]
+    out_ref, gate_grad_ref, up_grad_ref, down_grad_ref = refs[5:9]
+    arrived, extra, parts, from_z, wide, left, right, gate_tile, up_tile, down_tile = refs[9:19]
+    keep_sem, extra_sem, p_send, p_recv, z_send, z_recv, load_sem, store_sem = refs[19:]
+    z, f = lax.axis_index("ctx"), lax.axis_index("fsdp")
+    core = flip(f, 1)
+    width = out_ref.shape[1]
+    units = left.shape[1]
+    slots = arrived.shape[1] * arrived.shape[2]
+    greet(z, f, PEERS, ctx_count)
+
+    def p_copy(block, place):
+        to = toggled(f, PEERS[place])
+        sems = (p_send.at[block, place], p_recv.at[block, place])
+        return remote(slots_ref.at[block, to], arrived.at[block, f], *sems, z, to)
+
+    def p_arrived(block, place):
+        at = arrived.at[block, toggled(f, PEERS[place])]
+        sems = (p_send.at[block, place], p_recv.at[block, place])
+        remote(at, at, *sems, z, core).wait_recv()
+
+    def keep(block):
+        return pltpu.make_async_copy(
+            slots_ref.at[block, f], arrived.at[block, f], keep_sem.at[block]
+        )
+
+    def load(block):
+        return pltpu.make_async_copy(extra_ref.at[block], extra.at[block], extra_sem.at[block])
+
+    def z_copy(block, way, target):
+        sems = (z_send.at[block], z_recv.at[way, block])
+        return remote(parts.at[block], from_z.at[way, block], *sems, target, f)
+
+    def z_arrived(block, way):
+        at = from_z.at[way, block]
+        remote(at, at, z_send.at[block], z_recv.at[way, block], z, core).wait_recv()
+
+    def mix(block, target, *ways):
+        choose = one_hot(info_ref[block], z, slots, False)
+
+        @pl.loop(0, width, step=256)
+        def _(start):
+            part = pl.ds(pl.multiple_of(start, 256), 256)
+            total = dot_first(choose, arrived[block, :, :, part].reshape(slots, 256))
+            total = total + extra[block, :, part].astype(FULL)
+            for way in ways:
+                total = total + from_z[way, block, :, part].astype(FULL)
+            target[:, part] = total.astype(target.dtype)
+
+    def inner_step(block):
+        for way, above in ((1, True), (0, False)):
+            heading = (block < z) if above else (block > z)
+            has_more = (z < ctx_count - 1) if above else (z > 0)
+
+            @pl.when(heading & has_more)
+            def _():
+                z_arrived(block, way)
+                mix(block, parts.at[block], way)
+
+            @pl.when(heading & jnp.logical_not(has_more))
+            def _():
+                mix(block, parts.at[block])
+
+            @pl.when(heading)
+            def _():
+                z_copy(block, way, z - 1 if above else z + 1).start()
+
+    def last_step(block):
+        @pl.when(z > 0)
+        def _():
+            z_arrived(block, 0)
+
+        @pl.when(z < ctx_count - 1)
+        def _():
+            z_arrived(block, 1)
+
+        @pl.when(z == 0)
+        def _():
+            mix(block, out_ref, 1)
+
+        @pl.when(z == ctx_count - 1)
+        def _():
+            mix(block, out_ref, 0)
+
+        @pl.when((z > 0) & (z < ctx_count - 1))
+        def _():
+            mix(block, out_ref, 0, 1)
+
+    def fetch(source, target, place):
+        return pltpu.make_async_copy(source, target, load_sem.at[place])
+
+    first_loads = [
+        fetch(rows_ref, wide, 0),
+        fetch(gate_back_ref, left, 1),
+        fetch(up_back_ref, right, 2),
+    ]
+    second_loads = [fetch(grads_ref, wide, 3), fetch(hidden_ref, left, 4)]
+
+    def stores(part):
+        return [
+            pltpu.make_async_copy(gate_tile, gate_grad_ref.at[part, :], store_sem.at[0]),
+            pltpu.make_async_copy(up_tile, up_grad_ref.at[part, :], store_sem.at[1]),
+        ]
+
+    def store_down(start, count):
+        source, target = down_tile, down_grad_ref.at[pl.ds(start, count), :]
+        if count != down_tile.shape[0]:
+            source = down_tile.at[pl.ds(0, count), :]
+        return pltpu.make_async_copy(source, target, store_sem.at[2])
+
+    def outer_tiles(begin, end):
+        @pl.loop(begin, end)
+        def _(index):
+            part = pl.ds(pl.multiple_of(index * 256, 256), 256)
+            turned = wide[:, part]
+            gate_part = dot_first(turned, left[...]).astype(LOW)
+            up_part = dot_first(turned, right[...]).astype(LOW)
+
+            @pl.when(index > 0)
+            def _():
+                for copy in stores(part):
+                    copy.wait()
+
+            gate_tile[...] = gate_part
+            up_tile[...] = up_part
+            for copy in stores(part):
+                copy.start()
+
+    def down_tiles(begin, end):
+        @pl.loop(begin, end)
+        def _(index):
+            start = pl.multiple_of(index * 256, 256)
+            down_part = dot_first(left[:, pl.ds(start, 256)], wide[...]).astype(LOW)
+
+            @pl.when(index > 0)
+            def _():
+                store_down(start, 256).wait()
+
+            down_tile[...] = down_part
+            store_down(start, 256).start()
+
+    order = [nearest(z, ctx_count - 1 - step) for step in range(ctx_count)]
+    for copy in first_loads:
+        copy.start()
+    for block in order:
+        for place in range(len(PEERS)):
+            p_copy(block, place).start()
+        keep(block).start()
+        load(block).start()
+    for copy in first_loads:
+        copy.wait()
+
+    def step_waits(block):
+        keep(block).wait()
+        load(block).wait()
+        for place in range(len(PEERS)):
+            p_arrived(block, place)
+
+    outer = width // 256
+    whole, rest = tiles(units)
+    outer_tiles(0, outer // 2)
+    step_waits(order[0])
+    inner_step(order[0])
+    outer_tiles(outer // 2, outer)
+    for copy in second_loads:
+        copy.start()
+    step_waits(order[1])
+    inner_step(order[1])
+    for copy in second_loads:
+        copy.wait()
+    down_tiles(0, whole // 2)
+    step_waits(order[2])
+    inner_step(order[2])
+    down_tiles(whole // 2, whole)
+    store_down(0, 256).wait()
+    if rest:
+        down_tile[pl.ds(0, rest), :] = dot_first(
+            left[:, pl.ds(whole * 256, rest)], wide[...]
+        ).astype(LOW)
+        store_down(whole * 256, rest).start()
+    step_waits(order[3])
+    last_step(order[3])
+    if rest:
+        store_down(whole * 256, rest).wait()
+    for copy in stores(pl.ds(0, 256)):
+        copy.wait()
+    for step in range(ctx_count):
+        block = order[step]
+        for place in range(len(PEERS)):
+            p_copy(block, place).wait_send()
+        if step < ctx_count - 1:
+            z_copy(block, 0, z).wait_send()
+
+
+def combine_rows(
+    slots, info, extra, rows, grads, hidden, gate_back, up_back, ctx_count, fsdp_count
+):
+    share, width = slots.shape[2:]
+    count = extra.shape[1]
+    units = hidden.shape[1]
+    dma = pltpu.SemaphoreType.DMA
+    anywhere = pl.BlockSpec(memory_space=pl.ANY)
+    resident = pl.BlockSpec(memory_space=pltpu.VMEM)
+    vmem = lambda *shape: pltpu.VMEM(shape, LOW)
+    return pl.pallas_call(
+        functools.partial(combine_kernel, ctx_count),
+        out_shape=(
+            jax.ShapeDtypeStruct((count, width), FULL),
+            jax.ShapeDtypeStruct((width, units), LOW),
+            jax.ShapeDtypeStruct((width, units), LOW),
+            jax.ShapeDtypeStruct((units, width), LOW),
+        ),
+        in_specs=[anywhere, resident] + [anywhere] * 6,
+        out_specs=(resident, anywhere, anywhere, anywhere),
+        scratch_shapes=[
+            vmem(ctx_count, fsdp_count, share, width),
+            vmem(ctx_count, count, width),
+            vmem(ctx_count, count, width),
+            vmem(2, ctx_count, count, width),
+            vmem(rows.shape[0], width),
+            vmem(rows.shape[0], units),
+            vmem(rows.shape[0], units),
+            vmem(256, units),
+            vmem(256, units),
+            vmem(256, width),
+            dma((ctx_count,)),
+            dma((ctx_count,)),
+            dma((ctx_count, len(PEERS))),
+            dma((ctx_count, len(PEERS))),
+            dma((ctx_count,)),
+            dma((2, ctx_count)),
+            dma((5,)),
+            dma((3,)),
+        ],
+        compiler_params=pltpu.CompilerParams(
+            collective_id=3, has_side_effects=True, vmem_limit_bytes=BIG_VMEM
+        ),
+        cost_estimate=pl.CostEstimate(
+            flops=40_000_000_000, bytes_accessed=300_000_000, transcendentals=0
+        ),
+    )(slots, info, extra, rows, grads, hidden, gate_back, up_back)
+
+
 def mm(subscripts, left, right):
     return jnp.einsum(subscripts, left, right, preferred_element_type=FULL)
 
@@ -1035,22 +1312,65 @@
     return total.astype(LOW)
 
 
-def gather_rows(rows, chooser, ctx_count, fsdp_count):
+def routing(info, z, slots, gated):
+    at = jnp.arange(slots, dtype=jnp.int32).astype(FULL)[:, None, None]
+    hit = (info[:, None, COLUMN_AT : COLUMN_AT + TOP].swapaxes(2, 3) == at.reshape(-1, 1, 1)) & (
+        info[:, None, :TOP].swapaxes(2, 3) == z.astype(FULL)
+    )
+    values = info[:, None, GATE_AT : GATE_AT + TOP].swapaxes(2, 3) if gated else 1.0
+    return jnp.sum(jnp.where(hit, values, 0.0), axis=3).astype(LOW)
+
+
+def swap_slots(slots):
+    return lax.all_to_all(slots, "fsdp", split_axis=1, concat_axis=1, tiled=True)
+
+
+def send_rows(rows, info, slots, gated, ctx_count, fsdp_count):
+    every = lax.all_gather(rows, "ctx", axis=0)
+    choose = routing(info, lax.axis_index("ctx"), slots, gated)
+    chosen = mm("bst,btd->bsd", choose, every).astype(LOW)
+    return every, swap_slots(chosen.reshape(ctx_count, fsdp_count, -1, rows.shape[1]))
+
+
+def send_grads(rows, info, slots, ctx_count, fsdp_count):
     if (ctx_count, fsdp_count) == (4, 8):
-        return dispatch_rows(rows, chooser, ctx_count, fsdp_count)
-    every = lax.all_gather(rows, "ctx", axis=0)
-    chosen = mm("bst,btd->bsd", chooser, every).astype(LOW)
-    chosen = chosen.reshape(ctx_count, fsdp_count, -1, rows.shape[1])
-    return every, lax.all_to_all(chosen, "fsdp", split_axis=1, concat_axis=1, tiled=True)
-
-
-def return_rows(slots, mixer, extra, ctx_count, fsdp_count):
+        return dispatch_rows(rows, info, slots, ctx_count, fsdp_count)
+    return send_rows(rows, info, slots, True, ctx_count, fsdp_count)
+
+
+def run_expert(rows, info, gate, up, down, grads, ctx_count, fsdp_count):
     if (ctx_count, fsdp_count) == (4, 8):
-        return combine_rows(slots, mixer, extra.astype(LOW), ctx_count, fsdp_count)
-    back = lax.all_to_all(slots, "fsdp", split_axis=1, concat_axis=1, tiled=True)
-    back = back.reshape(ctx_count, mixer.shape[2], -1)
-    total = (mm("bts,bsd->btd", mixer, back) + extra).astype(LOW)
-    return lax.psum_scatter(total, "ctx", scatter_dimension=0, tiled=False).astype(FULL)
+        return expert_rows(rows, info, gate, up, down, grads, ctx_count, fsdp_count)
+    every, arrived = send_rows(rows, info, grads.shape[1], False, ctx_count, fsdp_count)
+    slots = arrived.reshape(grads.shape)
+    pre = mm("bsd,df->bsf", slots, gate)
+    linear = mm("bsd,df->bsf", slots, up)
+    act, slope = silu_slope(pre)
+    grad = mm("bsd,fd->bsf", grads, down)
+    hidden = (act * linear).astype(LOW)
+    up_back = (grad * act).astype(LOW)
+    gate_back = (grad * linear * slope).astype(LOW)
+    back = (mm("bsf,df->bsd", gate_back, gate) + mm("bsf,df->bsd", up_back, up)).astype(LOW)
+    return every, arrived, hidden, gate_back, up_back, back
+
+
+def return_grads(
+    slots, info, extra, rows, grads, hidden, gate_back, up_back, ctx_count, fsdp_count
+):
+    extra = extra.astype(LOW)
+    if (ctx_count, fsdp_count) == (4, 8):
+        return combine_rows(
+            slots, info, extra, rows, grads, hidden, gate_back, up_back, ctx_count, fsdp_count
+        )
+    back = swap_slots(slots).reshape(ctx_count, -1, slots.shape[3])
+    choose = routing(info, lax.axis_index("ctx"), back.shape[1], False)
+    total = (mm("bst,bsd->btd", choose, back) + extra).astype(LOW)
+    return (
+        lax.psum_scatter(total, "ctx", scatter_dimension=0, tiled=False).astype(FULL),
+        mm("sd,sf->df", rows, gate_back).astype(LOW),
+        mm("sd,sf->df", rows, up_back).astype(LOW),
+        mm("sf,sd->fd", hidden, grads).astype(LOW),
+    )
 
 
 def gather_all(items, ctx_count, fsdp_count):
@@ -1154,13 +1474,12 @@
     counts = jnp.sum(member_of, axis=1)
     before = jnp.cumsum(counts, axis=0) - counts
     within = jnp.sum(member_of * before[:, None, :], axis=-1).astype(jnp.int32)
-    info = jnp.concatenate(
-        [
-            (local_routes * capacity + within).astype(FULL).T,
-            gate_values[0].T,
-            jnp.zeros((16 - 2 * TOP, row_count), FULL),
-        ]
-    )
+    info = jnp.zeros((INFO_ROWS, row_count), FULL)
+    info = info.at[:TOP].set((local_routes % ctx_count).astype(FULL).T)
+    info = info.at[COLUMN_AT : COLUMN_AT + TOP].set(
+        (local_routes // ctx_count * capacity + within).astype(FULL).T
+    )
+    info = info.at[GATE_AT : GATE_AT + TOP].set(gate_values[0].T)
 
     tail = jnp.concatenate(
         [
@@ -1200,28 +1519,14 @@
         full_tail[:, rotary_end + 2].reshape(device_count, dense_rows)[:, :gain_rows]
     ).reshape(LATENT).astype(FULL)
 
-    flat = all_info[:, :TOP].astype(jnp.int32)
-    all_gates = all_info[:, TOP : 2 * TOP]
-    owner = flat // capacity
-    slot = jnp.where(
-        owner % ctx_count == z, owner // ctx_count * capacity + flat % capacity, -1
-    )
-    slot_index = jnp.arange(plane_slots, dtype=jnp.int32)
-    hits = slot[:, :, :, None] == slot_index
-    chooser = jnp.sum(hits.astype(FULL), axis=1).astype(LOW)
-    mixer = jnp.sum(jnp.where(hits, all_gates[:, :, :, None], 0.0), axis=1).astype(LOW)
-    hits = slot[:, :, None, :] == slot_index[:, None]
-    chooser_turned = jnp.sum(hits.astype(FULL), axis=1).astype(LOW)
-    mixer_turned = jnp.sum(jnp.where(hits, all_gates[:, :, None, :], 0.0), axis=1).astype(LOW)
-
     (up_swapped,) = after((up_swapped,), all_info)
     up_moved = along_line(up_swapped)
     (cot_sent,) = after((cot_low,), gate_moved)
-    all_cot, arrived_grad = gather_rows(cot_sent, mixer_turned, ctx_count, fsdp_count)
+    all_cot, arrived_grad = send_grads(cot_sent, all_info, plane_slots, ctx_count, fsdp_count)
     (down_swapped,) = after((down_swapped,), arrived_grad)
     down_moved = along_line(down_swapped)
     all_cot = all_cot.reshape(sequence, model_width)
-    arrived_grad = arrived_grad.reshape(-1, model_width)
+    arrived_grad = arrived_grad.reshape(ctx_count, plane_slots, model_width)
 
     def whole(moved):
         return share_parts(moved, members, fsdp_count).swapaxes(0, 1)
@@ -1265,20 +1570,13 @@
     second = (plain_two * gain_two).astype(LOW)
 
     (second_sent,) = after((second,), down_moved)
-    all_second, arrived_rows = gather_rows(second_sent, chooser_turned, ctx_count, fsdp_count)
+    all_second, arrived_rows, hidden_act, gate_back, up_back, arrived_back = run_expert(
+        second_sent, all_info, gate_all, up_all, down_all, arrived_grad, ctx_count, fsdp_count
+    )
     all_second = all_second.reshape(sequence, model_width)
-    arrived_rows = arrived_rows.reshape(-1, model_width)
-    gate_pre = jnp.dot(arrived_rows, gate_all, preferred_element_type=FULL)
-    up_pre = jnp.dot(arrived_rows, up_all, preferred_element_type=FULL)
-    gate_silu, gate_slope = silu_slope(gate_pre)
-    hidden_act = (gate_silu * up_pre).astype(LOW)
-    hidden_grad = mm("sd,fd->sf", arrived_grad, down_all)
-    up_back = (hidden_grad * gate_silu).astype(LOW)
-    gate_back = (hidden_grad * up_pre * gate_slope).astype(LOW)
-    arrived_back = (mm("sf,df->sd", gate_back, gate_all) + mm("sf,df->sd", up_back, up_all)).astype(
-        LOW
-    )
-
+    hidden_act, gate_back, up_back = [
+        item.reshape(-1, hidden_units) for item in (hidden_act, gate_back, up_back)
+    ]
     shared_g = jnp.dot(all_second, full_sgate, preferred_element_type=FULL)
     shared_u = jnp.dot(all_second, full_sup, preferred_element_type=FULL)
     shared_silu, shared_slope = silu_slope(shared_g)
@@ -1291,16 +1589,31 @@
     )
     slots_shape = (ctx_count, fsdp_count, share, model_width)
     rows_shape = (ctx_count, row_count, model_width)
-    second_grad = return_rows(
+    second_grad, gate_grad, up_grad, down_grad = return_grads(
         arrived_back.reshape(slots_shape),
-        chooser,
+        all_info,
         shared_second_grad.reshape(rows_shape),
+        arrived_rows.reshape(-1, model_width),
+        arrived_grad.reshape(-1, model_width),
+        hidden_act,
+        gate_back,
+        up_back,
         ctx_count,
         fsdp_count,
     )
-    shared_hidden, sgate_back, sup_back = after(
-        (shared_hidden, sgate_back, sup_back), second_grad
-    )
+    line_shape = (ctx_count, members, model_width // ctx_count // members, hidden_units)
+    gate_sum = sum_parts(gate_grad.reshape(line_shape).swapaxes(0, 1), members, fsdp_count)
+    gate_returned = along_line(gate_sum)
+    up_sum = sum_parts(up_grad.reshape(line_shape).swapaxes(0, 1), members, fsdp_count)
+    down_sum = sum_parts(
+        down_grad.reshape(members, hidden_units // members, ctx_count, -1).swapaxes(1, 2),
+        members,
+        fsdp_count,
+    )
+    shared_hidden, sgate_back, sup_back, hidden_act = after(
+        (shared_hidden, sgate_back, sup_back, hidden_act), second_grad
+    )
+    sgate_back, sup_back, hidden_act = after((sgate_back, sup_back, hidden_act), gate_sum)
     pair_grad = jnp.stack(
         [mm("td,tf->df", all_second, sgate_back), mm("td,tf->df", all_second, sup_back)]
     ).astype(LOW)
@@ -1310,32 +1623,14 @@
         .reshape(fsdp_count, 2, ctx_count * dense_rows, shared_units)
     )
     sdown_grad = mm("tf,td->fd", shared_hidden, all_cot).astype(LOW)
-    (hidden_act,) = after((hidden_act,), pair_grad, sdown_grad)
+    pair_sent, sdown_sent = (pair_grad, sdown_grad)
     pair_grad = lax.psum_scatter(pair_grad, "fsdp", scatter_dimension=0, tiled=False)
     sdown_grad = lax.psum_scatter(sdown_grad, "fsdp", scatter_dimension=0, tiled=True)
     result = jnp.dot(hidden_act, down_all, preferred_element_type=FULL).astype(LOW)
-    came_back = lax.all_to_all(
-        result.reshape(slots_shape), "fsdp", split_axis=1, concat_axis=1, tiled=True
-    ).reshape(ctx_count, plane_slots, model_width)
-    hidden_act, gate_back, up_back, shared_hidden = after(
-        (hidden_act, gate_back, up_back, shared_hidden), result
-    )
-    gate_grad = mm("sd,sf->df", arrived_rows, gate_back).astype(LOW)
-    up_grad = mm("sd,sf->df", arrived_rows, up_back).astype(LOW)
-    down_grad = mm("sf,sd->fd", hidden_act, arrived_grad).astype(LOW)
-    line_shape = (ctx_count, members, model_width // ctx_count // members, hidden_units)
-    gate_sum = sum_parts(gate_grad.reshape(line_shape).swapaxes(0, 1), members, fsdp_count)
-    up_sum = sum_parts(up_grad.reshape(line_shape).swapaxes(0, 1), members, fsdp_count)
-    down_sum = sum_parts(
-        down_grad.reshape(members, hidden_units // members, ctx_count, -1).swapaxes(1, 2),
-        members,
-        fsdp_count,
-    )
     shared_out = jnp.dot(shared_hidden, full_sdown, preferred_element_type=FULL)
-    (second_grad,) = after((second_grad,), gate_sum, up_sum, down_sum, came_back, shared_out)
-    (gate_sum,) = after((gate_sum,), came_back)
-    gate_returned = along_line(gate_sum)
-
+    (second_grad,) = after(
+        (second_grad,), gate_sum, up_sum, down_sum, pair_sent, sdown_sent, result, shared_out
+    )
     middle_part, gain_two_grad = norm_backward(second_grad, plain_two, inverse_two, gain_two)
     middle_grad = cot_full + middle_part
     attended_grad = middle_grad.astype(LOW)
@@ -1344,6 +1639,9 @@
         mm("td,vd->tv", attended_grad, full_output).astype(LOW).reshape(row_count, HEADS, VDIM)
     )
     latent_out_grad = mm("thv,chv->htc", values_grad, expand_value).astype(LOW)
+    (latent_out_grad,) = after((latent_out_grad,), gate_returned)
+    (result,) = after((result,), latent_out_grad)
+    came_back = swap_slots(result.reshape(slots_shape)).reshape(ctx_count, plane_slots, model_width)
     query_latent_grad, turned_grad, all_latent_grad, all_keys_grad = attend_back(
         query_latent,
         query_turned,
@@ -1361,28 +1659,21 @@
     keys_part = jnp.stack([keys_part[0], keys_part[1, ::-1]], axis=1)
     (keys_part,) = after((keys_part,), pair_grad, sdown_grad)
     keys_part = lax.psum_scatter(
-        keys_part.reshape(sequence, LATENT + ROPE), "ctx", scatter_dimension=0, tiled=True
-    )
+        keys_part.reshape(sequence, LATENT + ROPE).astype(LOW),
+        "ctx",
+        scatter_dimension=0,
+        tiled=True,
+    ).astype(FULL)
     latent_grad, keys_grad = (keys_part[:, :LATENT], keys_part[:, LATENT:])
     expand_value_grad = mm("htc,thv->chv", latent_out, values_grad)
 
-    (up_sum,) = after((up_sum,), gate_returned, all_latent_grad)
-    up_returned = along_line(up_sum)
-    (out_part,) = after(
-        (
-            (
-                mm("bts,bsd->btd", mixer, came_back)
-                + shared_out.reshape(ctx_count, row_count, model_width)
-            ).astype(LOW),
-        ),
-        keys_part,
-    )
+    out_part = (
+        mm("bst,bsd->btd", routing(all_info, z, plane_slots, True), came_back)
+        + shared_out.reshape(ctx_count, row_count, model_width)
+    ).astype(LOW)
+    (out_part,) = after((out_part,), keys_part)
     out_sum = lax.psum_scatter(out_part, "ctx", scatter_dimension=0, tiled=False).astype(FULL)
     layer_out = (middle + out_sum).astype(LOW)[None]
-    (pair_grad,) = after((pair_grad,), up_returned)
-    pair_grad = lax.all_to_all(
-        pair_grad, "ctx", split_axis=1, concat_axis=2, tiled=True
-    ).astype(FULL)
     sdown_grad = sdown_grad.astype(FULL)
 
     query_nope_grad = mm("htc,chd->thd", query_latent_grad, expand_key)
@@ -1422,6 +1713,12 @@
         ],
         axis=1,
     )
+    (up_sum,) = after((up_sum,), came_back, query_nope_grad)
+    up_returned = along_line(up_sum)
+    (pair_grad,) = after((pair_grad,), up_returned)
+    pair_grad = lax.all_to_all(
+        pair_grad, "ctx", split_axis=1, concat_axis=2, tiled=True
+    ).astype(FULL)
     (down_sum,) = after((down_sum,), up_returned, normed_grad, pair_grad)
     down_returned = along_line(down_sum)
     dense_grads = after(

time: 1560 us -> 1480 us (0.949)
  matrix products: 314 us -> 161 us
  Pallas kernels: 730 us -> 786 us
  starting transfers between devices: 54.5 us -> 72.3 us
    pallas_call x1 -> x2, Pallas kernels: 110 us -> 259 us  [the longest x1 145 us: expert_rows(): pl.pallas_call(functools.partial(expert_kernel, ctx_count), out_shape=(lo...]
    dot_general x25 -> x19, matrix products: 213 us -> 108 us  [mm(): return jnp.einsum(subscripts, left, right, preferred_element_type=FULL)]
    pallas_call x2 -> x1, Pallas kernels: 247 us -> 153 us  [dispatch_rows(): pl.pallas_call(functools.partial(dispatch_kernel, ctx_count), out_shape=(...]
    dot_general x2 -> x0, matrix products: 46.1 us -> none  [the longest x1 29.9 us: local(): gate_pre = jnp.dot(arrived_rows, gate_all, preferred_element_type=FULL)]
    all_to_all x6, waiting for transfers between devices: 102 us -> 55.9 us  [along_line(): return lax.all_to_all(array, 'ctx', split_axis=0, concat_axis=0, tiled=True)]
    reduce_scatter x1, waiting for transfers between devices: 0.01 us -> 31.3 us  [local(): lax.psum_scatter(pair_grad, 'fsdp', scatter_dimension=0, tiled=False)]
    all_to_all x1, waiting for transfers between devices: 0.01 us -> 20.6 us  [swap_slots(): lax.all_to_all(slots, 'fsdp', split_axis=1, concat_axis=1, tiled=True)]
    all_gather x1, waiting for transfers between devices: 0.01 us -> 20.4 us  [local(): lax.all_gather(jnp.concatenate([latent_norm, jnp.pad(key_rope, pad_rope)]...]
  transfers between devices with their start and end apart: 25 -> 25, of which waited for: 5 -> 7; matrix products, arithmetic and copies ran while one was open for 27% -> 25% of each run, Pallas kernels for 33% -> 36%
where the time goes in v4:
time: 1480 us; the launch traced here: 1470 us
  Pallas kernels  786 us (53%)
  local copies, waits for them, and re-layouts  194 us (13%)
  matrix products  161 us (11%)
  waiting for transfers between devices  151 us (10%)
  other arithmetic  87 us (6%)
  starting transfers between devices  72.3 us (5%)
  between operations  15.5 us (1%)
    pallas_call x1, Pallas kernels, gather_arrays(): pl.pallas_call(functools.partial(gather_kernel, ctx_count, kinds), out_sh...  186 us
    pallas_call x1, Pallas kernels, dispatch_rows(): pl.pallas_call(functools.partial(dispatch_kernel, ctx_count), out_shape=(...  153 us
    pallas_call x1, Pallas kernels, expert_rows(): pl.pallas_call(functools.partial(expert_kernel, ctx_count), out_shape=(lo...  145 us
    pallas_call x1, Pallas kernels, scatter_arrays(): pl.pallas_call(functools.partial(scatter_kernel, ctx_count, count), out_s...  126 us
    pallas_call x1, Pallas kernels, combine_rows(): pl.pallas_call(functools.partial(combine_kernel, ctx_count), out_shape=(j...  114 us
    dot_general x19, matrix products, mm(): return jnp.einsum(subscripts, left, right, preferred_element_type=FULL)  108 us
    all_to_all x6, waiting for transfers between devices, along_line(): return lax.all_to_all(array, 'ctx', split_axis=0, concat_axis=0, tiled=True)  55.9 us
    all_to_all x6, starting transfers between devices, along_line(): return lax.all_to_all(array, 'ctx', split_axis=0, concat_axis=0, tiled=True)  46.5 us
  transfers between devices with their start and end apart: 25, of which 7 were waited for; matrix products, arithmetic and copies ran while one was open for 25% of the time, Pallas kernels for 36%

profile of v4, /device:TPU:1, one launch (start us, length us, event | category | flops | bytes accessed | tf_op | source)
XLA Modules:
  0.0 1467.3 jit_solution(1816194506962938110)
XLA Ops:
  43.1 186.4 %shard_map.280 = (f32[4,24,256]{2,1,0:T(8,128)}, bf16[4,8,64,3072]{3,2,1,0:T(8,128)(2,1)}, bf16[4,8,64,768]{3,2,1,0:T(8,128)(2,1)}, bf16[4,8,16,4096]{3,2,1,0:T(...) custom-call(f32[24,256]{1,0:T(8,128)} %copy-done.40, ...), custom_call_target="tpu_custom_call" | custom-call | bytes 500000000 | tf_op jit(solution)/shard_map/pallas_call | solution.py:302
  229.5 15.3 %all-to-all-start.1 = ((bf16[4,256,1408]{2,1,0:T(8,128)(2,1)}), bf16[4,256,1408]{2,1,0:T(8,128)(2,1)}, u32[]{:S(2)}, u32[]{:S(2)}) async-start(bf16[4,256,1408]{2,1,0:T(8,128)(2,1)} %bitcast.364), calls=%async_computation.1 | async-start | bytes 5767168 | tf_op jit(solution)/shard_map/all_to_all | solution.py:1406
  257.1 153.2 %shard_map.281 = (bf16[4,256,2048]{2,1,0:T(8,128)(2,1)}, bf16[4,8,64,2048]{3,2,1,0:T(8,128)(2,1)}) custom-call(bf16[256,2048]{1,0:T(8,128)(2,1)} %bitcast.404, f32[4,24,256]{2,1,0:T(8,128)} %get-tuple-element.124.info_ref), custom_call_target="tpu_custom_call" | custom-call | flops 2000000000 | bytes 300000000 | tf_op jit(solution)/shard_map/pallas_call | solution.py:827
  414.9 9.7 fusion.82
  448.0 20.4 %all-gather.3.cloned.1.call-done = bf16[1024,640]{0,1:T(8,128)(2,1)} async-done(((bf16[256,640]{0,1:T(8,128)(2,1)}), bf16[1024,640]{0,1:T(8,128)(2,1)}) %all-gather.3.cloned.1.call-update) | async-done | bytes 1310736 | tf_op jit(solution)/shard_map/all_gather | solution.py:1551
  481.0 29.2 %shard_map.282 = (bf16[16,256,512]{2,1,0:T(8,128)(2,1)}, f32[16,256,1]{2,1,0:T(8,128)}) custom-call(bf16[16,256,512]{2,1,0:T(8,128)(2,1)} %convolution_convert_fusion.3.query_ref, bf16[16,256,128]{2,1,0:T(8,128)(2,1)} %pad.24.turned_ref, bf16[1024,512]{1,0:T(8,128)(2,1)} %slice.230.keys_ref, bf16[1024,128]{1,0:T(8,128)(2,1)} %slice.231.rope_ref), custom_call_target="tpu_custom_call" | custom-call | flops 12000000000 | bytes 12000000 | tf_op jit(solution)/shard_map/pallas_call | solution.py:650
  514.1 6.2 multiply_reduce_fusion.2
  539.6 7.0 copy.281
  546.6 8.0 copy.330
  554.5 145.2 %shard_map.283 = (bf16[4,256,2048]{2,1,0:T(8,128)(2,1)}, bf16[4,8,64,2048]{3,2,1,0:T(8,128)(2,1)}, bf16[4,512,1408]{2,1,0:T(8,128)(2,1)}, bf16[4,512,1408]{2,1,0...) custom-call(bf16[256,2048]{1,0:T(8,128)(2,1)} %multiply_convert_fusion.3.rows_ref, ...), custom_call_target="tpu_custom_call" | custom-call | flops 60000002048 | bytes 400000000 | tf_op jit(solution)/shard_map/pallas_call | solution.py:980
  722.5 114.2 %shard_map.284 = (f32[256,2048]{1,0:T(8,128)}, bf16[2048,1408]{1,0:T(8,128)(2,1)}, bf16[2048,1408]{1,0:T(8,128)(2,1)}, bf16[1408,2048]{1,0:T(8,128)(2,1)}) custom-call(bf16[4,8,64,2048]{3,2,1,0:T(8,128)(2,1)} %bitcast.433, f32[4,24,256]{2,1,0:T(8,128)} %get-tuple-element.124.info_ref, bf16[4,256,2048]{2,1,0:T(8,128)(2,1)} %bitcast.440, ...), custom_call_target="tpu_custom_call" | custom-call | flops 40000000000 | bytes 300000000 | tf_op jit(solution)/shard_map/pallas_call | solution.py:1224
  844.2 10.6 reshape.545
  861.7 6.4 copy.284
  868.1 7.4 convolution_convert_fusion.1
  875.5 9.1 fusion.86
  889.6 10.5 all-to-all-start.3
  900.0 6.3 convert_bitcast_fusion.2
  925.8 17.1 %convolution_convert_fusion = bf16[2048,2048]{1,0:T(8,128)(2,1)} fusion(bf16[2048,1408]{1,0:T(8,128)(2,1)} %bitcast.435, bf16[1408,2048]{1,0:T(8,128)(2,1)S(1)} %bitcast.375), kind=kOutput, calls=%fused_computation.4 | convolution fusion | flops 11815354368 | bytes 19922944 | tf_op jit(solution)/shard_map/dot_general | solution.py:1629
  948.8 7.3 convolution_convert_fusion.4
  966.6 9.4 copy.288
  985.3 32.2 %shard_map.285 = (bf16[16,256,512]{2,1,0:T(8,128)(2,1)}, f32[16,256,128]{2,1,0:T(8,128)}, f32[1024,512]{1,0:T(8,128)}, f32[1024,128]{1,0:T(8,128)}) custom-call(bf16[16,256,512]{2,1,0:T(8,128)(2,1)} %convolution_convert_fusion.3.query_ref, bf16[16,256,128]{2,1,0:T(8,128)(2,1)} %pad.24.turned_ref, bf16[1024,512]{1,0:T(8,128)(2,1)} %slice.230.keys_ref, ...), custom_call_target="tpu_custom_call" | custom-call | flops 30000001024 | bytes 30000000 | tf_op jit(solution)/shard_map/pallas_call | solution.py:676
  1020.5 31.3 %reduce-scatter.5.cloned.1.call-done = bf16[1,2,256,704]{3,2,1,0:T(8,128)(2,1)} async-done(((bf16[8,2,256,704]{3,2,1,0:T(8,128)(2,1)}), bf16[1,2,256,704]{3,2,1,0:T(8,128)(2,1)}) %reduce-scatter.5.cloned.1.call-update) | async-done | bytes 720912 | tf_op jit(solution)/shard_map/reduce_scatter | solution.py:1627
  1063.2 20.6 %all-to-all-done.4 = bf16[4,8,64,2048]{3,2,0,1:T(8,128)(2,1)} async-done(((bf16[4,8,64,2048]{3,2,0,1:T(8,128)(2,1)}), bf16[4,8,64,2048]{3,2,0,1:T(8,128)(2,1)}, u32[]{:S(2)}, u32[]{:S(2)}) %all-to-all-start.4) | async-done | bytes 8388640 | tf_op jit(solution)/shard_map/all_to_all | solution.py:1325
  1083.8 8.4 copy.289
  1119.8 10.7 add_convert_fusion
  1142.3 7.8 fusion.87
  1150.2 52.8 %all-to-all-done.5 = bf16[4,256,1408]{2,1,0:T(8,128)(2,1)} async-done(((bf16[4,256,1408]{2,1,0:T(8,128)(2,1)}), bf16[4,256,1408]{2,1,0:T(8,128)(2,1)}, u32[]{:S(2)}, u32[]{:S(2)}) %all-to-all-start.5) | async-done | bytes 2883616 | tf_op jit(solution)/shard_map/all_to_all | solution.py:1406
  1218.2 19.6 %all-to-all-done.6 = bf16[2,256,704]{2,0,1:T(2,128)(2,1)} async-done(((bf16[2,256,704]{2,0,1:T(2,128)(2,1)}), bf16[2,256,704]{2,0,1:T(2,128)(2,1)}, u32[]{:S(2)}, u32[]{:S(2)}) %all-to-all-start.6) | async-done | bytes 720928 | tf_op jit(solution)/shard_map/all_to_all | solution.py:1719
  1257.8 16.4 %concatenate.49 = bf16[2048,768]{0,1:T(8,128)(2,1)} concatenate(bf16[2048,576]{0,1:T(8,128)(2,1)} %fusion.48, f32[2048,1]{0,1:T(1,128)S(1)} %bitcast.419, f32[2048,1]{0,1:T(1,128)S(1)} %bitcast.417, bf16[2048,1]{0,1:T(2,128)(2,1)S(1)} %broadcast_in_dim_reshape.3, bf16[2048,189]{0,1:T(8,128)(2,1)} %broadcast_in_dim.88), dimensions={1} | concatenate | bytes 6299648 | tf_op jit(solution)/shard_map/concatenate | solution.py:1706
  1274.3 10.0 fusion.88
  1298.5 6.4 copy.298
  1304.9 125.9 %shard_map.286 = (f32[64,3072]{1,0:T(8,128)}, f32[64,768]{1,0:T(8,128)}, f32[16,4096]{1,0:T(8,128)}, f32[64,2048]{1,0:T(8,128)}) custom-call(bf16[4,4,2,64,3072]{4,3,2,1,0:T(8,128)(2,1)} %bitcast.347, bf16[4,4,2,64,768]{4,3,2,1,0:T(8,128)(2,1)} %bitcast.362, bf16[4,4,2,16,4096]{4,3,2,1,0:T(8,128)(2,1)} %bitcast.355, bf16[4,4,2,64,2048]{4,3,2,1,0:T(8,128)(2,1)} %bitcast.348), custom_call_target="tpu_custom_call" | custom-call | bytes 500000000 | tf_op jit(solution)/shard_map/pallas_call | solution.py:503
  (359 shorter events, 330.9 us)
Async XLA Ops:
  9.9 3.6 collective-permute-start
  17.0 212.5 %all-to-all-start = ((bf16[4,256,1408]{2,1,0:T(8,128)(2,1)}), bf16[4,256,1408]{2,1,0:T(8,128)(2,1)}, u32[]{:S(2)}, u32[]{:S(2)}) async-start(bf16[4,256,1408]{2,1,0:T(8,128)(2,1)} %bitcast.16), calls=%async_computation | async-start | bytes 5767168 | tf_op jit(solution)/shard_map/all_to_all | solution.py:1406
  24.3 10.9 collective-permute-start.2
  26.5 12.0 collective-permute-start.1
  229.5 180.8 %all-to-all-start.1 = ((bf16[4,256,1408]{2,1,0:T(8,128)(2,1)}), bf16[4,256,1408]{2,1,0:T(8,128)(2,1)}, u32[]{:S(2)}, u32[]{:S(2)}) async-start(bf16[4,256,1408]{2,1,0:T(8,128)(2,1)} %bitcast.364), calls=%async_computation.1 | async-start | bytes 5767168 | tf_op jit(solution)/shard_map/all_to_all | solution.py:1406
  244.8 223.5 %all-gather.3.cloned.1.call-start = ((), (), s32[]{:S(2)}) async-start(), calls=%async_computation.16 | async-start | bytes 1638400 | tf_op jit(solution)/shard_map/all_gather | solution.py:1551
  244.9 168.4 %copy-start.57 = (f32[32]{0:T(128)}, f32[32]{0:T(128)S(1)}, u32[]{:S(2)}) copy-start(f32[32]{0:T(128)S(1)} %multiply_power_fusion) | copy-start | bytes 388
  244.9 168.4 %copy-start.55 = (f32[256]{0:T(256)}, f32[256]{0:T(256)S(1)}, u32[]{:S(2)}) copy-start(f32[256]{0:T(256)S(1)} %fusion.75) | copy-start | bytes 3076
  256.2 154.1 %copy-start.43 = (f32[2048,1]{0,1:T(1,128)}, f32[2048,1]{0,1:T(1,128)S(1)}, u32[]{:S(2)}) copy-start(f32[2048,1]{0,1:T(1,128)S(1)} %copy.331) | copy-start | bytes 24580
  256.4 157.1 %copy-start.45 = (f32[512]{0:T(512)}, f32[512]{0:T(512)S(1)}, u32[]{:S(2)}) copy-start(f32[512]{0:T(512)S(1)} %reshape.563) | copy-start | bytes 6148
  256.7 265.8 %copy-start.38 = (f32[2048,1]{0,1:T(1,128)}, f32[2048,1]{0,1:T(1,128)S(1)}, u32[]{:S(2)}) copy-start(f32[2048,1]{0,1:T(1,128)S(1)} %copy.332) | copy-start | bytes 24580
  257.1 157.8 %copy-start.15 = (bf16[256,2048]{1,0:T(8,128)(2,1)}, bf16[256,2048]{1,0:T(8,128)(2,1)S(1)}, u32[]{:S(2)}) copy-start(bf16[256,2048]{1,0:T(8,128)(2,1)S(1)} %fusion.11) | copy-start | bytes 3145732
  426.9 93.4 %all-to-all-start.2 = ((bf16[4,704,512]{2,1,0:T(8,128)(2,1)}), bf16[4,704,512]{2,1,0:T(8,128)(2,1)}, u32[]{:S(2)}, u32[]{:S(2)}) async-start(bf16[4,704,512]{2,1,0:T(8,128)(2,1)} %bitcast.363), calls=%async_computation.2 | async-start | bytes 5767168 | tf_op jit(solution)/shard_map/all_to_all | solution.py:1406
  431.6 588.9 %reduce-scatter.7.cloned.1.call-start = ((), (), s32[]{:S(2)}) async-start(), calls=%async_computation.13 | async-start | bytes 3244032 | tf_op jit(solution)/shard_map/reduce_scatter | solution.py:1628
  444.0 79.8 %collective-permute-start.3 = (bf16[4,256,1408]{2,1,0:T(8,128)(2,1)}, bf16[4,256,1408]{2,1,0:T(8,128)(2,1)}, u32[]{:S(2)}, u32[]{:S(2)}) collective-permute-start(bf16[4,256,1408]{2,1,0:T(8,128)(2,1)} %all-to-all-done), channel_id=1, source_target_pairs={{0,1},{1,0},{2,3},{3,2},{4,5},{5,4},{6,7},{7,6},{8,9},{9,8},{10,11... | collective-permute-start | bytes 8650760 | tf_op jit(solution)/shard_map/ppermute | solution.py:1299
  444.2 86.3 %collective-permute-start.4 = (bf16[4,256,1408]{2,1,0:T(8,128)(2,1)}, bf16[4,256,1408]{2,1,0:T(8,128)(2,1)}, u32[]{:S(2)}, u32[]{:S(2)}) collective-permute-start(bf16[4,256,1408]{2,1,0:T(8,128)(2,1)} %all-to-all-done.1), channel_id=1, source_target_pairs={{0,1},{1,0},{2,3},{3,2},{4,5},{5,4},{6,7},{7,6},{8,9},{9,8},{10,11... | collective-permute-start | bytes 8650760 | tf_op jit(solution)/shard_map/ppermute | solution.py:1299
  520.3 16.5 %collective-permute-start.5 = (bf16[4,704,512]{2,1,0:T(8,128)(2,1)}, bf16[4,704,512]{2,1,0:T(8,128)(2,1)S(1)}, u32[]{:S(2)}, u32[]{:S(2)}) collective-permute-start(bf16[4,704,512]{2,1,0:T(8,128)(2,1)} %all-to-all-done.2), channel_id=1, source_target_pairs={{0,1},{1,0},{2,3},{3,2},{4,5},{5,4},{6,7},{7,6},{8,9},{9,8},{10,11... | collective-permute-start | bytes 8650760 | tf_op jit(solution)/shard_map/ppermute | solution.py:1299
  554.5 145.2 %copy-start.62 = (bf16[4,8,64,704]{3,2,1,0:T(8,128)(2,1)S(1)}, bf16[4,8,64,704]{3,2,1,0:T(8,128)(2,1)}, u32[]{:S(2)}) copy-start(bf16[4,8,64,704]{3,2,1,0:T(8,128)(2,1)} %get-tuple-element.134) | copy-start | bytes 8650756
  840.5 44.1 %collective-permute-start.6 = (bf16[4,256,1408]{2,1,0:T(8,128)(2,1)}, bf16[4,256,1408]{2,1,0:T(8,128)(2,1)}, u32[]{:S(2)}, u32[]{:S(2)}) collective-permute-start(bf16[4,256,1408]{2,1,0:T(8,128)(2,1)} %dynamic-slice_bitcast_fusion.1), channel_id=1, source_target_pairs={{0,1},{1,0},{2,3},{3,2},{4,5},{5,4},{6,7},{7,6},{8,9},{9,8},{10,11... | collective-permute-start | bytes 8650760 | tf_op jit(solution)/shard_map/ppermute | solution.py:1309
  843.6 77.9 %collective-permute-start.7 = (bf16[4,256,1408]{2,1,0:T(8,128)(2,1)}, bf16[4,256,1408]{2,1,0:T(8,128)(2,1)}, u32[]{:S(2)}, u32[]{:S(2)}) collective-permute-start(bf16[4,256,1408]{2,1,0:T(8,128)(2,1)} %dynamic-slice_bitcast_fusion), channel_id=1, source_target_pairs={{0,1},{1,0},{2,3},{3,2},{4,5},{5,4},{6,7},{7,6},{8,9},{9,8},{10,11... | collective-permute-start | bytes 8650760 | tf_op jit(solution)/shard_map/ppermute | solution.py:1309
  861.7 55.4 %collective-permute-start.8 = (bf16[4,704,512]{2,1,0:T(8,128)(2,1)}, bf16[4,704,512]{2,1,0:T(8,128)(2,1)}, u32[]{:S(2)}, u32[]{:S(2)}) collective-permute-start(bf16[4,704,512]{2,1,0:T(8,128)(2,1)} %bitcast.344), channel_id=1, source_target_pairs={{0,1},{1,0},{2,3},{3,2},{4,5},{5,4},{6,7},{7,6},{8,9},{9,8},{10,11... | collective-permute-start | bytes 8650760 | tf_op jit(solution)/shard_map/ppermute | solution.py:1309
  889.6 77.0 %all-to-all-start.3 = ((bf16[4,256,1408]{2,1,0:T(8,128)(2,1)}), bf16[4,256,1408]{2,1,0:T(8,128)(2,1)}, u32[]{:S(2)}, u32[]{:S(2)}) async-start(bf16[4,256,1408]{2,1,0:T(8,128)(2,1)} %fusion.2), calls=%async_computation.3 | async-start | bytes 5767168 | tf_op jit(solution)/shard_map/all_to_all | solution.py:1406
  900.0 151.8 %reduce-scatter.5.cloned.1.call-start = ((), (), s32[]{:S(2)}) async-start(), calls=%async_computation.12 | async-start | bytes 7077888 | tf_op jit(solution)/shard_map/reduce_scatter | solution.py:1627
  976.0 107.8 %all-to-all-start.4 = ((bf16[4,8,64,2048]{3,2,0,1:T(8,128)(2,1)}), bf16[4,8,64,2048]{3,2,0,1:T(8,128)(2,1)}, u32[]{:S(2)}, u32[]{:S(2)}) async-start(bf16[4,8,64,2048]{3,2,0,1:T(8,128)(2,1)} %copy.288), calls=%async_computation.4 | async-start | bytes 16777216 | tf_op jit(solution)/shard_map/all_to_all | solution.py:1325
  981.4 137.4 %reduce-scatter.9.cloned.1.call-start = ((), (), s32[]{:S(2)}) async-start(), calls=%async_computation.14 | async-start | bytes 1474560 | tf_op jit(solution)/shard_map/reduce_scatter | solution.py:1661
  1092.2 110.8 %all-to-all-start.5 = ((bf16[4,256,1408]{2,1,0:T(8,128)(2,1)}), bf16[4,256,1408]{2,1,0:T(8,128)(2,1)}, u32[]{:S(2)}, u32[]{:S(2)}) async-start(bf16[4,256,1408]{2,1,0:T(8,128)(2,1)} %fusion.1), calls=%async_computation.9 | async-start | bytes 5767168 | tf_op jit(solution)/shard_map/all_to_all | solution.py:1406
  1096.9 353.0 %reduce-scatter.11.cloned.1.call-start = ((), (), s32[]{:S(2)}) async-start(), calls=%async_computation.15 | async-start | bytes 5242880 | tf_op jit(solution)/shard_map/reduce_scatter | solution.py:1675
  1111.6 136.2 %collective-permute-start.9 = (bf16[2,256,1408]{2,1,0:T(8,128)(2,1)}, bf16[2,256,1408]{2,1,0:T(8,128)(2,1)}, u32[]{:S(2)}, u32[]{:S(2)}) collective-permute-start(bf16[2,256,1408]{2,1,0:T(8,128)(2,1)} %dynamic-slice_bitcast_fusion.4), channel_id=1, source_target_pairs={{0,1},{1,0},{2,3},{3,2},{4,5},{5,4},{6,7},{7,6},{8,9},{9,8},{10,11... | collective-permute-start | bytes 4325384 | tf_op jit(solution)/shard_map/ppermute | solution.py:1288
  1205.8 31.9 %all-to-all-start.6 = ((bf16[2,256,704]{2,0,1:T(2,128)(2,1)}), bf16[2,256,704]{2,0,1:T(2,128)(2,1)}, u32[]{:S(2)}, u32[]{:S(2)}) async-start(bf16[2,256,704]{2,0,1:T(2,128)(2,1)} %copy.299), calls=%async_computation.10 | async-start | bytes 1572864 | tf_op jit(solution)/shard_map/all_to_all | solution.py:1719
  1237.8 204.9 %all-to-all-start.7 = ((bf16[4,704,512]{2,1,0:T(8,128)(2,1)}), bf16[4,704,512]{2,1,0:T(8,128)(2,1)}, u32[]{:S(2)}, u32[]{:S(2)}) async-start(bf16[4,704,512]{2,1,0:T(8,128)(2,1)} %fusion), calls=%async_computation.11 | async-start | bytes 5767168 | tf_op jit(solution)/shard_map/all_to_all | solution.py:1406
  1287.0 157.9 %collective-permute-start.10 = (bf16[2,256,1408]{2,1,0:T(8,128)(2,1)}, bf16[2,256,1408]{2,1,0:T(8,128)(2,1)}, u32[]{:S(2)}, u32[]{:S(2)}) collective-permute-start(bf16[2,256,1408]{2,1,0:T(8,128)(2,1)} %dynamic-slice_bitcast_fusion.3), channel_id=1, source_target_pairs={{0,1},{1,0},{2,3},{3,2},{4,5},{5,4},{6,7},{7,6},{8,9},{9,8},{10,11... | collective-permute-start | bytes 4325384 | tf_op jit(solution)/shard_map/ppermute | solution.py:1288
  1444.1 8.2 collective-permute-start.11
  (66 other events, 674.8 us)
Sparse Core Ops, SparseCore 0:
  415.0 53.3 all-gather.2
  875.6 50.6 reduce-scatter.6
  943.0 108.7 reduce-scatter.4
  1058.0 43.2 reduce-scatter.8
  1130.7 102.9 reduce-scatter.10

commit v5 on v4

--- a/solution.py
+++ b/solution.py
@@ -156,170 +156,6 @@
     return tuple((slice(None), pl.ds(start, width // 2)) for start in (0, width // 2))
 
 
-def gather_kernel(ctx_count, kinds, *refs):
-    count = len(kinds)
-    shards, outs = refs[:count], refs[count : 2 * count]
-    own_sem, z_send, z_recv, p_send, p_recv, c_send, c_recv = refs[2 * count :]
-    z, f = lax.axis_index("ctx"), lax.axis_index("fsdp")
-    core, x_near, y_near = flip(f, 1), flip(f, 2), flip(f, 4)
-    far = flip(x_near, 4)
-    greet(z, f, (1, 2, 4), ctx_count, True)
-
-    def slot(item, step):
-        return 0 if kinds[item] == "plane" else nearest(z, step)
-
-    def steps(item, step):
-        return step == 0 if kinds[item] == "plane" else 0 <= step < ctx_count
-
-    def z_view(item, block):
-        return outs[item].at[block] if kinds[item] == "column" else outs[item].at[block, f]
-
-    def own(item):
-        source = shards[item].at[z] if kinds[item] == "line" else shards[item]
-        return pltpu.make_async_copy(source, z_view(item, slot(item, 0)), own_sem.at[item])
-
-    def z_copy(item, block, way, target):
-        at = z_view(item, block)
-        return remote(at, at, z_send.at[item, block, way], z_recv.at[item, block], target, f)
-
-    def piece(item, step):
-        target = lax.rem(z + step, ctx_count)
-        return remote(
-            shards[item].at[target],
-            outs[item].at[z, f],
-            z_send.at[item, target, 0],
-            z_recv.at[item, z],
-            target,
-            f,
-        )
-
-    def part(item, block, at, which):
-        rows, columns = halves(*outs[item].shape[2:])[which]
-        return outs[item].at[block, at, rows, columns]
-
-    def p_copy(item, block, which):
-        at = (
-            lambda: outs[item].at[block, f],
-            lambda: outs[item].at[block, f],
-            lambda: part(item, block, x_near, 0),
-            lambda: part(item, block, y_near, 1),
-        )[which]()
-        to = (x_near, y_near, y_near, x_near)[which]
-        sems = (p_send.at[item, block, which], p_recv.at[item, block, which])
-        return remote(at, at, *sems, z, to)
-
-    def p_arrived(item, block, which):
-        at = (
-            lambda: outs[item].at[block, x_near],
-            lambda: outs[item].at[block, y_near],
-            lambda: part(item, block, far, 0),
-            lambda: part(item, block, far, 1),
-        )[which]()
-        sems = (p_send.at[item, block, which], p_recv.at[item, block, which])
-        remote(at, at, *sems, z, x_near).wait_recv()
-
-    def c_copy(item, block, which):
-        at = outs[item].at[block, (f, x_near, y_near, far)[which]]
-        sems = (c_send.at[item, block, which], c_recv.at[item, block, which])
-        return remote(at, at, *sems, z, core)
-
-    def c_arrived(item, block, which):
-        at = outs[item].at[block, flip((f, x_near, y_near, far)[which], 1)]
-        sems = (c_send.at[item, block, which], c_recv.at[item, block, which])
-        remote(at, at, *sems, z, core).wait_recv()
-
-    def first(item, step):
-        block = slot(item, step)
-        if step == 0:
-            own(item).wait()
-        else:
-            at = z_view(item, block)
-            sems = (z_send.at[item, block, 0], z_recv.at[item, block])
-            remote(at, at, *sems, z, core).wait_recv()
-        if kinds[item] in ("all", "column"):
-            both_ways(z, block, ctx_count, lambda way, to: z_copy(item, block, way, to).start())
-        if kinds[item] != "column":
-            p_copy(item, block, 0).start()
-            p_copy(item, block, 1).start()
-            c_copy(item, block, 0).start()
-
-    def second(item, step):
-        block = slot(item, step)
-        for which in (0, 1):
-            p_arrived(item, block, which)
-            p_copy(item, block, which + 2).start()
-            c_copy(item, block, which + 1).start()
-
-    def third(item, step):
-        block = slot(item, step)
-        p_arrived(item, block, 2)
-        p_arrived(item, block, 3)
-        c_copy(item, block, 3).start()
-
-    for item in range(count):
-        own(item).start()
-        if kinds[item] == "line":
-            for step in range(1, ctx_count):
-                piece(item, step).start()
-    for step in range(ctx_count + 2):
-        for lag, stage in ((0, first), (1, second), (2, third)):
-            for item in range(count):
-                if steps(item, step - lag) and (lag == 0 or kinds[item] != "column"):
-                    stage(item, step - lag)
-    for item in range(count):
-        for step in range(ctx_count):
-            if not steps(item, step):
-                continue
-            block = slot(item, step)
-            if kinds[item] != "column":
-                for which in range(4):
-                    c_arrived(item, block, which)
-                    p_copy(item, block, which).wait_send()
-                    c_copy(item, block, which).wait_send()
-            if kinds[item] == "line" and step > 0:
-                piece(item, step).wait_send()
-            if kinds[item] in ("all", "column"):
-                both_ways(
-                    z, block, ctx_count, lambda way, to: z_copy(item, block, way, to).wait_send()
-                )
-
-
-def gather_arrays(items, ctx_count, fsdp_count):
-    kinds = tuple(kind for kind, shard in items)
-    shards = [shard for kind, shard in items]
-    lead = {
-        "all": (ctx_count, fsdp_count),
-        "line": (ctx_count, fsdp_count),
-        "plane": (1, fsdp_count),
-        "column": (ctx_count,),
-    }
-    shapes = [
-        lead[kind] + (shard.shape[1:] if kind == "line" else shard.shape) for kind, shard in items
-    ]
-    count = len(items)
-    dma = pltpu.SemaphoreType.DMA
-    four = dma((count, ctx_count, 4))
-    return pl.pallas_call(
-        functools.partial(gather_kernel, ctx_count, kinds),
-        out_shape=[
-            jax.ShapeDtypeStruct(shape, shard.dtype) for shape, shard in zip(shapes, shards)
-        ],
-        in_specs=[pl.BlockSpec(memory_space=pl.ANY)] * count,
-        out_specs=[pl.BlockSpec(memory_space=pl.ANY)] * count,
-        scratch_shapes=[
-            dma((count,)),
-            dma((count, ctx_count, 2)),
-            dma((count, ctx_count)),
-            four,
-            four,
-            four,
-            four,
-        ],
-        compiler_params=pltpu.CompilerParams(collective_id=0, has_side_effects=True),
-        cost_estimate=pl.CostEstimate(flops=0, bytes_accessed=500_000_000, transcendentals=0),
-    )(*shards)
-
-
 def add_rows(target, rows, *terms):
     @pl.loop(0, rows, step=16)
     def _(start):
@@ -330,7 +166,8 @@
         target[part, :] = total.astype(target.dtype)
 
 
-def scatter_kernel(ctx_count, count, *refs):
+def scatter_kernel(ctx_count, kinds, *refs):
+    count = len(kinds)
     grads, outs = refs[:count], refs[count : 2 * count]
     banks = [refs[(2 + kind) * count : (3 + kind) * count] for kind in range(7)]
     load_sem, c_send, c_recv, p_send, p_recv, z_send, z_recv = refs[9 * count :]
@@ -340,14 +177,15 @@
     core, x_near, y_near = flip(f, 1), flip(f, 2), flip(f, 4)
     x_chip, y_chip = flip(chip, 1), flip(chip, 2)
     far_chip = flip(x_chip, 2)
-    greet(z, f, (1, 2, 4), ctx_count)
+    greet(z, f, (1, 2, 4), ctx_count, True)
     order = [nearest(z, ctx_count - 1 - step) for step in range(ctx_count)]
 
     def work(item):
         grad_ref, out_ref = grads[item], outs[item]
         mine, from_core, from_x, from_y, half_x, half_y, from_z = [bank[item] for bank in banks]
-        rows, width = out_ref.shape
-        left, right = pl.ds(0, width // 2), pl.ds(width // 2, width // 2)
+        rows, width = out_ref.shape[-2:]
+        left, right = halves(rows, width)
+        half_rows = half_x.shape[1]
 
         def load(block):
             return pltpu.make_async_copy(
@@ -366,8 +204,8 @@
 
         def p_copy(block, which):
             source, target, to = (
-                (mine.at[block, far_chip, :, left], half_y.at[block], y_near),
-                (mine.at[block, far_chip, :, right], half_x.at[block], x_near),
+                (mine.at[(block, far_chip) + left], half_y.at[block], y_near),
+                (mine.at[(block, far_chip) + right], half_x.at[block], x_near),
                 (mine.at[block, x_chip], from_x.at[block], x_near),
                 (mine.at[block, y_chip], from_y.at[block], y_near),
             )[which]
@@ -389,6 +227,10 @@
             sems = (z_send.at[item, block], z_recv.at[item, way, block])
             remote(at, at, *sems, z, core).wait_recv()
 
+        def piece(block):
+            sems = (z_send.at[item, block], z_recv.at[item, 0, z])
+            return remote(mine.at[block, chip], out_ref.at[z], *sems, block, f)
+
         def start(step):
             c_copy(order[step]).start()
             load(order[step]).start()
@@ -408,12 +250,12 @@
             add_rows(x_part, rows, x_part, from_core.at[block, x_chip])
             add_rows(y_part, rows, y_part, from_core.at[block, y_chip])
             p_copy(block, 0).wait_recv()
-            x_left = mine.at[block, x_chip, :, left]
-            add_rows(x_left, rows, x_left, half_y.at[block])
+            x_left = mine.at[(block, x_chip) + left]
+            add_rows(x_left, half_rows, x_left, half_y.at[block])
             p_copy(block, 2).start()
             p_copy(block, 1).wait_recv()
-            y_right = mine.at[block, y_chip, :, right]
-            add_rows(y_right, rows, y_right, half_x.at[block])
+            y_right = mine.at[(block, y_chip) + right]
+            add_rows(y_right, half_rows, y_right, half_x.at[block])
             p_copy(block, 3).start()
 
         def third(step):
@@ -422,6 +264,12 @@
             p_copy(block, 3).wait_recv()
             own = mine.at[block, chip]
             terms = (own, from_core.at[block, chip], from_x.at[block], from_y.at[block])
+            if kinds[item] == "line":
+                add_rows(out_ref.at[z] if step == ctx_count - 1 else own, rows, *terms)
+                if step < ctx_count - 1:
+                    piece(block).start()
+                return
+
             if step == ctx_count - 1:
 
                 @pl.when(z > 0)
@@ -468,7 +316,14 @@
             c_copy(block).wait_send()
             for which in range(4):
                 p_copy(block, which).wait_send()
-            if step < ctx_count - 1:
+            if step == ctx_count - 1:
+                return
+            if kinds[item] == "line":
+                piece(block).wait_send()
+                at = out_ref.at[block]
+                sems = (z_send.at[item, block], z_recv.at[item, 0, block])
+                remote(at, at, *sems, z, core).wait_recv()
+            else:
                 z_copy(block, 0, z).wait_send()
 
         return start, first, second, third, finish
@@ -487,22 +342,33 @@
             act(step)
 
 
-def scatter_arrays(grads, ctx_count, fsdp_count):
+def scatter_arrays(items, ctx_count, fsdp_count):
+    kinds = tuple(kind for kind, grad in items)
+    grads = [grad for kind, grad in items]
     count = len(grads)
     chips = fsdp_count // 2
     shapes = [
         (grad.shape[0] // (ctx_count * fsdp_count), grad.shape[1]) for grad in grads
     ]
+    half_shapes = [
+        (rows // 2, width) if rows % 32 == 0 else (rows, width // 2) for rows, width in shapes
+    ]
     dma = pltpu.SemaphoreType.DMA
     leads = [(ctx_count, chips), (ctx_count, chips), (ctx_count,), (ctx_count,)]
     banks = [pltpu.VMEM(lead + shape, LOW) for lead in leads for shape in shapes]
+    banks += [pltpu.VMEM((ctx_count,) + shape, LOW) for _ in range(2) for shape in half_shapes]
     banks += [
-        pltpu.VMEM((ctx_count, shape[0], shape[1] // 2), LOW) for _ in range(2) for shape in shapes
+        pltpu.VMEM((2, ctx_count) + shape if kind == "all" else (1, 1, 16, 128), LOW)
+        for kind, shape in zip(kinds, shapes)
     ]
-    banks += [pltpu.VMEM((2, ctx_count) + shape, LOW) for shape in shapes]
     return pl.pallas_call(
-        functools.partial(scatter_kernel, ctx_count, count),
-        out_shape=[jax.ShapeDtypeStruct(shape, FULL) for shape in shapes],
+        functools.partial(scatter_kernel, ctx_count, kinds),
+        out_shape=[
+            jax.ShapeDtypeStruct(shape, FULL)
+            if kind == "all"
+            else jax.ShapeDtypeStruct((ctx_count,) + shape, LOW)
+            for kind, shape in zip(kinds, shapes)
+        ],
         in_specs=[pl.BlockSpec(memory_space=pl.ANY)] * count,
         out_specs=[pl.BlockSpec(memory_space=pltpu.VMEM)] * count,
         scratch_shapes=banks
@@ -746,7 +612,6 @@
         return pltpu.make_async_copy(source, target, self.all_sem.at[block])
 
     def begin(self):
-        greet(self.z, self.f, PEERS, self.ctx_count)
         own = pltpu.make_async_copy(self.rows_ref, self.blocks.at[self.z], self.own_sem)
         own.start()
         own.wait()
@@ -810,36 +675,192 @@
     ]
 
 
-def dispatch_kernel(ctx_count, rows_ref, info_ref, all_ref, out_ref, blocks, chosen, *sems):
-    move = Dispatch(ctx_count, True, rows_ref, info_ref, all_ref, blocks, chosen, out_ref, sems)
+def gather_kernel(ctx_count, kinds, *refs):
+    count = len(kinds)
+    shards, rows_ref = refs[:count], refs[count]
+    outs, all_ref, slots_ref = refs[count + 1 : 2 * count + 1], refs[2 * count + 1], refs[2 * count + 2]
+    blocks, chosen = refs[2 * count + 3 : 2 * count + 5]
+    own_sem, z_send, z_recv, p_send, p_recv, c_send, c_recv = refs[2 * count + 5 : 2 * count + 12]
+    z, f = lax.axis_index("ctx"), lax.axis_index("fsdp")
+    core, x_near, y_near = flip(f, 1), flip(f, 2), flip(f, 4)
+    far = flip(x_near, 4)
+    move = Dispatch(
+        ctx_count, True, rows_ref, outs[0], all_ref, blocks, chosen, slots_ref, refs[2 * count + 12 :]
+    )
+    greet(z, f, PEERS, ctx_count, True)
+
+    def slot(item, step):
+        return 0 if kinds[item] == "plane" else nearest(z, step)
+
+    def steps(item, step):
+        return step == 0 if kinds[item] == "plane" else 0 <= step < ctx_count
+
+    def z_view(item, block):
+        return outs[item].at[block] if kinds[item] == "column" else outs[item].at[block, f]
+
+    def own(item):
+        source = shards[item].at[z] if kinds[item] == "line" else shards[item]
+        return pltpu.make_async_copy(source, z_view(item, slot(item, 0)), own_sem.at[item])
+
+    def z_copy(item, block, way, target):
+        at = z_view(item, block)
+        return remote(at, at, z_send.at[item, block, way], z_recv.at[item, block], target, f)
+
+    def piece(item, step):
+        target = lax.rem(z + step, ctx_count)
+        return remote(
+            shards[item].at[target],
+            outs[item].at[z, f],
+            z_send.at[item, target, 0],
+            z_recv.at[item, z],
+            target,
+            f,
+        )
+
+    def part(item, block, at, which):
+        rows, columns = halves(*outs[item].shape[2:])[which]
+        return outs[item].at[block, at, rows, columns]
+
+    def p_copy(item, block, which):
+        at = (
+            lambda: outs[item].at[block, f],
+            lambda: outs[item].at[block, f],
+            lambda: part(item, block, x_near, 0),
+            lambda: part(item, block, y_near, 1),
+        )[which]()
+        to = (x_near, y_near, y_near, x_near)[which]
+        sems = (p_send.at[item, block, which], p_recv.at[item, block, which])
+        return remote(at, at, *sems, z, to)
+
+    def p_arrived(item, block, which):
+        at = (
+            lambda: outs[item].at[block, x_near],
+            lambda: outs[item].at[block, y_near],
+            lambda: part(item, block, far, 0),
+            lambda: part(item, block, far, 1),
+        )[which]()
+        sems = (p_send.at[item, block, which], p_recv.at[item, block, which])
+        remote(at, at, *sems, z, x_near).wait_recv()
+
+    def c_copy(item, block, which):
+        at = outs[item].at[block, (f, x_near, y_near, far)[which]]
+        sems = (c_send.at[item, block, which], c_recv.at[item, block, which])
+        return remote(at, at, *sems, z, core)
+
+    def c_arrived(item, block, which):
+        at = outs[item].at[block, flip((f, x_near, y_near, far)[which], 1)]
+        sems = (c_send.at[item, block, which], c_recv.at[item, block, which])
+        remote(at, at, *sems, z, core).wait_recv()
+
+    def first(item, step):
+        block = slot(item, step)
+        if step == 0:
+            own(item).wait()
+        else:
+            at = z_view(item, block)
+            sems = (z_send.at[item, block, 0], z_recv.at[item, block])
+            remote(at, at, *sems, z, core).wait_recv()
+        if kinds[item] in ("all", "column"):
+            both_ways(z, block, ctx_count, lambda way, to: z_copy(item, block, way, to).start())
+        if kinds[item] != "column":
+            p_copy(item, block, 0).start()
+            p_copy(item, block, 1).start()
+            c_copy(item, block, 0).start()
+
+    def second(item, step):
+        block = slot(item, step)
+        for which in (0, 1):
+            p_arrived(item, block, which)
+            p_copy(item, block, which + 2).start()
+            c_copy(item, block, which + 1).start()
+
+    def third(item, step):
+        block = slot(item, step)
+        p_arrived(item, block, 2)
+        p_arrived(item, block, 3)
+        c_copy(item, block, 3).start()
+
+    for item in range(count):
+        own(item).start()
+        if kinds[item] == "line":
+            for step in range(1, ctx_count):
+                piece(item, step).start()
     move.begin()
+    for step in range(ctx_count + 2):
+        for lag, stage in ((0, first), (1, second), (2, third)):
+            for item in range(count):
+                if steps(item, step - lag) and (lag == 0 or kinds[item] != "column"):
+                    stage(item, step - lag)
+            if lag == 0 and step < ctx_count:
+                move.pass_on(nearest(z, step), step == 0)
     for step in range(ctx_count):
-        move.pass_on(nearest(move.z, step), step == 0)
-    for step in range(ctx_count):
-        move.await_slots(nearest(move.z, step))
+        move.await_slots(nearest(z, step))
     move.finish()
-
-
-def dispatch_rows(rows, info, slots, ctx_count, fsdp_count):
-    count, width = rows.shape
+    for item in range(count):
+        for step in range(ctx_count):
+            if not steps(item, step):
+                continue
+            block = slot(item, step)
+            if kinds[item] != "column":
+                for which in range(4):
+                    c_arrived(item, block, which)
+                    p_copy(item, block, which).wait_send()
+                    c_copy(item, block, which).wait_send()
+            if kinds[item] == "line" and step > 0:
+                piece(item, step).wait_send()
+            if kinds[item] in ("all", "column"):
+                both_ways(
+                    z, block, ctx_count, lambda way, to: z_copy(item, block, way, to).wait_send()
+                )
+
+
+def gather_arrays(items, rows, slots, ctx_count, fsdp_count):
+    kinds = tuple(kind for kind, shard in items)
+    shards = [shard for kind, shard in items]
+    lead = {
+        "all": (ctx_count, fsdp_count),
+        "line": (ctx_count, fsdp_count),
+        "plane": (1, fsdp_count),
+        "column": (ctx_count,),
+    }
+    shapes = [
+        lead[kind] + (shard.shape[1:] if kind == "line" else shard.shape) for kind, shard in items
+    ]
+    row_count, width = rows.shape
     share = slots // fsdp_count
-    buffers, sems = dispatch_scratch(ctx_count, fsdp_count, count, share, width)
-    return pl.pallas_call(
-        functools.partial(dispatch_kernel, ctx_count),
-        out_shape=(
-            jax.ShapeDtypeStruct((ctx_count, count, width), LOW),
-            jax.ShapeDtypeStruct((ctx_count, fsdp_count, share, width), LOW),
-        ),
-        in_specs=[pl.BlockSpec(memory_space=pl.ANY), pl.BlockSpec(memory_space=pltpu.VMEM)],
-        out_specs=(pl.BlockSpec(memory_space=pl.ANY), pl.BlockSpec(memory_space=pl.ANY)),
-        scratch_shapes=buffers + sems,
+    shapes += [(ctx_count, row_count, width), (ctx_count, fsdp_count, share, width)]
+    buffers, sems = dispatch_scratch(ctx_count, fsdp_count, row_count, share, width)
+    count = len(items)
+    dma = pltpu.SemaphoreType.DMA
+    four = dma((count, ctx_count, 4))
+    anywhere = pl.BlockSpec(memory_space=pl.ANY)
+    results = pl.pallas_call(
+        functools.partial(gather_kernel, ctx_count, kinds),
+        out_shape=[
+            jax.ShapeDtypeStruct(shape, item.dtype)
+            for shape, item in zip(shapes, shards + [rows, rows])
+        ],
+        in_specs=[anywhere] * (count + 1),
+        out_specs=[pl.BlockSpec(memory_space=pltpu.VMEM)] + [anywhere] * (count + 1),
+        scratch_shapes=buffers
+        + [
+            dma((count,)),
+            dma((count, ctx_count, 2)),
+            dma((count, ctx_count)),
+            four,
+            four,
+            four,
+            four,
+        ]
+        + sems,
         compiler_params=pltpu.CompilerParams(
-            collective_id=2, has_side_effects=True, vmem_limit_bytes=BIG_VMEM
+            collective_id=0, has_side_effects=True, vmem_limit_bytes=BIG_VMEM
         ),
         cost_estimate=pl.CostEstimate(
-            flops=2_000_000_000, bytes_accessed=300_000_000, transcendentals=0
+            flops=2_000_000_000, bytes_accessed=800_000_000, transcendentals=0
         ),
-    )(rows, info)
+    )(*shards, rows)
+    return results[:count], results[count], results[count + 1]
 
 
 def tiles(width, size=256):
@@ -899,6 +920,7 @@
     def store_back(block):
         return pltpu.make_async_copy(back, back_ref.at[block], back_sem)
 
+    greet(move.z, move.f, PEERS, ctx_count)
     move.begin()
     for load in loads:
         load.start()
@@ -1016,248 +1038,265 @@
     )(rows, info, gate, up, down, grads)
 
 
-def combine_kernel(ctx_count, slots_ref, info_ref, extra_ref, *refs):
-    rows_ref, grads_ref, hidden_ref, gate_back_ref, up_back_ref = refs[:5]
-    out_ref, gate_grad_ref, up_grad_ref, down_grad_ref = refs[5:9]
-    arrived, extra, parts, from_z, wide, left, right, gate_tile, up_tile, down_tile = refs[9:19]
-    keep_sem, extra_sem, p_send, p_recv, z_send, z_recv, load_sem, store_sem = refs[19:]
-    z, f = lax.axis_index("ctx"), lax.axis_index("fsdp")
-    core = flip(f, 1)
-    width = out_ref.shape[1]
-    units = left.shape[1]
-    slots = arrived.shape[1] * arrived.shape[2]
-    greet(z, f, PEERS, ctx_count)
-
-    def p_copy(block, place):
-        to = toggled(f, PEERS[place])
-        sems = (p_send.at[block, place], p_recv.at[block, place])
-        return remote(slots_ref.at[block, to], arrived.at[block, f], *sems, z, to)
-
-    def p_arrived(block, place):
-        at = arrived.at[block, toggled(f, PEERS[place])]
-        sems = (p_send.at[block, place], p_recv.at[block, place])
-        remote(at, at, *sems, z, core).wait_recv()
-
-    def keep(block):
+class Combine:
+    def __init__(
+        self, ctx_count, gated, slots_ref, info_ref, extra_ref, out_ref, buffers, sems
+    ):
+        self.ctx_count, self.gated = ctx_count, gated
+        self.slots_ref, self.info_ref = slots_ref, info_ref
+        self.extra_ref, self.out_ref = extra_ref, out_ref
+        self.arrived, self.extra, self.parts, self.from_z = buffers
+        self.keep_sem, self.extra_sem, self.p_send, self.p_recv, self.z_send, self.z_recv = sems
+        self.z, self.f = lax.axis_index("ctx"), lax.axis_index("fsdp")
+        self.core = flip(self.f, 1)
+        self.order = [nearest(self.z, ctx_count - 1 - step) for step in range(ctx_count)]
+
+    def p_copy(self, block, place):
+        to = toggled(self.f, PEERS[place])
+        sems = (self.p_send.at[block, place], self.p_recv.at[block, place])
+        return remote(
+            self.slots_ref.at[block, to], self.arrived.at[block, self.f], *sems, self.z, to
+        )
+
+    def keep(self, block):
+        source, target = self.slots_ref.at[block, self.f], self.arrived.at[block, self.f]
+        return pltpu.make_async_copy(source, target, self.keep_sem.at[block])
+
+    def load(self, step):
         return pltpu.make_async_copy(
-            slots_ref.at[block, f], arrived.at[block, f], keep_sem.at[block]
+            self.extra_ref.at[self.order[step]], self.extra, self.extra_sem
         )
 
-    def load(block):
-        return pltpu.make_async_copy(extra_ref.at[block], extra.at[block], extra_sem.at[block])
-
-    def z_copy(block, way, target):
-        sems = (z_send.at[block], z_recv.at[way, block])
-        return remote(parts.at[block], from_z.at[way, block], *sems, target, f)
-
-    def z_arrived(block, way):
-        at = from_z.at[way, block]
-        remote(at, at, z_send.at[block], z_recv.at[way, block], z, core).wait_recv()
-
-    def mix(block, target, *ways):
-        choose = one_hot(info_ref[block], z, slots, False)
-
-        @pl.loop(0, width, step=256)
+    def place(self, way, block, z):
+        return jnp.where(block == z, self.ctx_count, block) if way == 0 else block
+
+    def send_along(self, step, way, to):
+        block = self.order[step]
+        sems = (self.z_send.at[step], self.z_recv.at[way, block])
+        target = self.from_z.at[self.place(way, block, to)]
+        return remote(self.parts.at[step], target, *sems, to, self.f)
+
+    def z_arrived(self, block, way):
+        at = self.from_z.at[self.place(way, block, self.z)]
+        sems = (self.z_send.at[0], self.z_recv.at[way, block])
+        remote(at, at, *sems, self.z, self.core).wait_recv()
+
+    def start(self):
+        for block in self.order:
+            for place in range(len(PEERS)):
+                self.p_copy(block, place).start()
+            self.keep(block).start()
+        self.load(0).start()
+
+    def mix(self, block, target, *ways):
+        slots = self.arrived.shape[1] * self.arrived.shape[2]
+        choose = one_hot(self.info_ref[block], self.z, slots, self.gated)
+
+        @pl.loop(0, target.shape[1], step=256)
         def _(start):
             part = pl.ds(pl.multiple_of(start, 256), 256)
-            total = dot_first(choose, arrived[block, :, :, part].reshape(slots, 256))
-            total = total + extra[block, :, part].astype(FULL)
+            total = dot_first(choose, self.arrived[block, :, :, part].reshape(slots, 256))
+            total = total + self.extra[:, part].astype(FULL)
             for way in ways:
-                total = total + from_z[way, block, :, part].astype(FULL)
+                total = total + self.from_z[self.place(way, block, self.z), :, part].astype(FULL)
             target[:, part] = total.astype(target.dtype)
 
-    def inner_step(block):
-        for way, above in ((1, True), (0, False)):
-            heading = (block < z) if above else (block > z)
-            has_more = (z < ctx_count - 1) if above else (z > 0)
-
-            @pl.when(heading & has_more)
-            def _():
-                z_arrived(block, way)
-                mix(block, parts.at[block], way)
-
-            @pl.when(heading & jnp.logical_not(has_more))
-            def _():
-                mix(block, parts.at[block])
-
-            @pl.when(heading)
-            def _():
-                z_copy(block, way, z - 1 if above else z + 1).start()
-
-    def last_step(block):
+    def step(self, step):
+        block, z, last = self.order[step], self.z, self.ctx_count - 1
+        self.keep(block).wait()
+        self.load(step).wait()
+        for place in range(len(PEERS)):
+            at = self.arrived.at[block, toggled(self.f, PEERS[place])]
+            sems = (self.p_send.at[block, place], self.p_recv.at[block, place])
+            remote(at, at, *sems, z, self.core).wait_recv()
+        if step < last:
+            target = self.parts.at[step]
+            for way, above in ((1, True), (0, False)):
+                heading = (block < z) if above else (block > z)
+                has_more = (z < last) if above else (z > 0)
+
+                @pl.when(heading & has_more)
+                def _():
+                    self.z_arrived(block, way)
+                    self.mix(block, target, way)
+
+                @pl.when(heading & jnp.logical_not(has_more))
+                def _():
+                    self.mix(block, target)
+
+                @pl.when(heading)
+                def _():
+                    self.send_along(step, way, z - 1 if above else z + 1).start()
+
+            self.load(step + 1).start()
+            return
+
         @pl.when(z > 0)
         def _():
-            z_arrived(block, 0)
-
-        @pl.when(z < ctx_count - 1)
+            self.z_arrived(block, 0)
+
+        @pl.when(z < last)
         def _():
-            z_arrived(block, 1)
+            self.z_arrived(block, 1)
 
         @pl.when(z == 0)
         def _():
-            mix(block, out_ref, 1)
-
-        @pl.when(z == ctx_count - 1)
+            self.mix(block, self.out_ref, 1)
+
+        @pl.when(z == last)
         def _():
-            mix(block, out_ref, 0)
-
-        @pl.when((z > 0) & (z < ctx_count - 1))
+            self.mix(block, self.out_ref, 0)
+
+        @pl.when((z > 0) & (z < last))
         def _():
-            mix(block, out_ref, 0, 1)
-
-    def fetch(source, target, place):
-        return pltpu.make_async_copy(source, target, load_sem.at[place])
-
-    first_loads = [
-        fetch(rows_ref, wide, 0),
-        fetch(gate_back_ref, left, 1),
-        fetch(up_back_ref, right, 2),
+            self.mix(block, self.out_ref, 0, 1)
+
+    def finish(self):
+        for step in range(self.ctx_count):
+            for place in range(len(PEERS)):
+                self.p_copy(self.order[step], place).wait_send()
+            if step < self.ctx_count - 1:
+                self.send_along(step, 0, self.z).wait_send()
+
+
+def combine_kernel(ctx_count, info_ref, *refs):
+    streams = refs[0:4]
+    rows_ref, grads_ref, hidden_ref, gate_back_ref, up_back_ref = refs[4:9]
+    outs = refs[9:11]
+    gate_grad_ref, up_grad_ref, down_grad_ref = refs[11:14]
+    narrow, left, right, gate_tile, up_tile = refs[14:19]
+    side_sem, tile_sem, store_sem = refs[19:22]
+    buffers, sems = refs[22:30], refs[30:42]
+    moves = [
+        Combine(
+            ctx_count,
+            place == 1,
+            streams[2 * place],
+            info_ref,
+            streams[2 * place + 1],
+            outs[place],
+            buffers[4 * place : 4 * place + 4],
+            sems[6 * place : 6 * place + 6],
+        )
+        for place in range(2)
     ]
-    second_loads = [fetch(grads_ref, wide, 3), fetch(hidden_ref, left, 4)]
-
-    def stores(part):
-        return [
-            pltpu.make_async_copy(gate_tile, gate_grad_ref.at[part, :], store_sem.at[0]),
-            pltpu.make_async_copy(up_tile, up_grad_ref.at[part, :], store_sem.at[1]),
-        ]
-
-    def store_down(start, count):
-        source, target = down_tile, down_grad_ref.at[pl.ds(start, count), :]
-        if count != down_tile.shape[0]:
-            source = down_tile.at[pl.ds(0, count), :]
-        return pltpu.make_async_copy(source, target, store_sem.at[2])
-
-    def outer_tiles(begin, end):
+    greet(moves[0].z, moves[0].f, PEERS, ctx_count)
+    tile_count = rows_ref.shape[1] // 256
+
+    def sides(source, target, place):
+        return pltpu.make_async_copy(source, target, side_sem.at[place])
+
+    first_sides = [sides(gate_back_ref, left, 0), sides(up_back_ref, right, 1)]
+    last_side = sides(hidden_ref, left, 2)
+
+    def fetch(source, index):
+        part = pl.ds(pl.multiple_of(index * 256, 256), 256)
+        slot = lax.rem(index, 2)
+        return pltpu.make_async_copy(source.at[:, part], narrow.at[slot], tile_sem.at[slot])
+
+    def store(tile, target, place, index):
+        part = pl.ds(pl.multiple_of(index * 256, 256), 256)
+        return pltpu.make_async_copy(tile, target.at[part, :], store_sem.at[place])
+
+    def products(source, begin, end, pairs):
         @pl.loop(begin, end)
         def _(index):
-            part = pl.ds(pl.multiple_of(index * 256, 256), 256)
-            turned = wide[:, part]
-            gate_part = dot_first(turned, left[...]).astype(LOW)
-            up_part = dot_first(turned, right[...]).astype(LOW)
-
-            @pl.when(index > 0)
+            @pl.when(index + 1 < tile_count)
             def _():
-                for copy in stores(part):
-                    copy.wait()
-
-            gate_tile[...] = gate_part
-            up_tile[...] = up_part
-            for copy in stores(part):
-                copy.start()
-
-    def down_tiles(begin, end):
-        @pl.loop(begin, end)
-        def _(index):
-            start = pl.multiple_of(index * 256, 256)
-            down_part = dot_first(left[:, pl.ds(start, 256)], wide[...]).astype(LOW)
-
-            @pl.when(index > 0)
-            def _():
-                store_down(start, 256).wait()
-
-            down_tile[...] = down_part
-            store_down(start, 256).start()
-
-    order = [nearest(z, ctx_count - 1 - step) for step in range(ctx_count)]
-    for copy in first_loads:
+                fetch(source, index + 1).start()
+
+            fetch(source, index).wait()
+            turned = narrow[lax.rem(index, 2)]
+            for place, (factor, tile, target) in enumerate(pairs):
+                part = dot_first(turned, factor[...]).astype(LOW)
+
+                @pl.when(index > 0)
+                def _():
+                    store(tile, target, place, index).wait()
+
+                tile[...] = part
+                store(tile, target, place, index).start()
+
+    both = ((left, gate_tile, gate_grad_ref), (right, up_tile, up_grad_ref))
+    alone = ((left, gate_tile, down_grad_ref),)
+    half = tile_count // 2
+    for copy in first_sides:
         copy.start()
-    for block in order:
-        for place in range(len(PEERS)):
-            p_copy(block, place).start()
-        keep(block).start()
-        load(block).start()
-    for copy in first_loads:
+    fetch(rows_ref, 0).start()
+    for move in moves:
+        move.start()
+    for copy in first_sides:
         copy.wait()
-
-    def step_waits(block):
-        keep(block).wait()
-        load(block).wait()
-        for place in range(len(PEERS)):
-            p_arrived(block, place)
-
-    outer = width // 256
-    whole, rest = tiles(units)
-    outer_tiles(0, outer // 2)
-    step_waits(order[0])
-    inner_step(order[0])
-    outer_tiles(outer // 2, outer)
-    for copy in second_loads:
-        copy.start()
-    step_waits(order[1])
-    inner_step(order[1])
-    for copy in second_loads:
-        copy.wait()
-    down_tiles(0, whole // 2)
-    step_waits(order[2])
-    inner_step(order[2])
-    down_tiles(whole // 2, whole)
-    store_down(0, 256).wait()
-    if rest:
-        down_tile[pl.ds(0, rest), :] = dot_first(
-            left[:, pl.ds(whole * 256, rest)], wide[...]
-        ).astype(LOW)
-        store_down(whole * 256, rest).start()
-    step_waits(order[3])
-    last_step(order[3])
-    if rest:
-        store_down(whole * 256, rest).wait()
-    for copy in stores(pl.ds(0, 256)):
-        copy.wait()
+    products(rows_ref, 0, half, both)
+    moves[0].step(0)
+    products(rows_ref, half, tile_count, both)
+    for place, (factor, tile, target) in enumerate(both):
+        store(tile, target, place, 0).wait()
+    last_side.start()
+    fetch(grads_ref, 0).start()
+    moves[0].step(1)
+    last_side.wait()
+    products(grads_ref, 0, half, alone)
+    moves[0].step(2)
+    products(grads_ref, half, tile_count, alone)
+    store(gate_tile, down_grad_ref, 0, 0).wait()
+    for step in range(3, ctx_count):
+        moves[0].step(step)
     for step in range(ctx_count):
-        block = order[step]
-        for place in range(len(PEERS)):
-            p_copy(block, place).wait_send()
-        if step < ctx_count - 1:
-            z_copy(block, 0, z).wait_send()
+        moves[1].step(step)
+    for move in moves:
+        move.finish()
 
 
 def combine_rows(
-    slots, info, extra, rows, grads, hidden, gate_back, up_back, ctx_count, fsdp_count
+    slots, extra, out_slots, out_extra, info, sides, ctx_count, fsdp_count
 ):
     share, width = slots.shape[2:]
     count = extra.shape[1]
-    units = hidden.shape[1]
+    total, units = sides[2].shape
     dma = pltpu.SemaphoreType.DMA
     anywhere = pl.BlockSpec(memory_space=pl.ANY)
     resident = pl.BlockSpec(memory_space=pltpu.VMEM)
     vmem = lambda *shape: pltpu.VMEM(shape, LOW)
+    buffers = [
+        vmem(ctx_count, fsdp_count, share, width),
+        vmem(count, width),
+        vmem(ctx_count - 1, count, width),
+        vmem(ctx_count + 1, count, width),
+    ]
+    sems = [
+        dma((ctx_count,)),
+        dma,
+        dma((ctx_count, len(PEERS))),
+        dma((ctx_count, len(PEERS))),
+        dma((ctx_count - 1,)),
+        dma((2, ctx_count)),
+    ]
     return pl.pallas_call(
         functools.partial(combine_kernel, ctx_count),
-        out_shape=(
-            jax.ShapeDtypeStruct((count, width), FULL),
-            jax.ShapeDtypeStruct((width, units), LOW),
-            jax.ShapeDtypeStruct((width, units), LOW),
-            jax.ShapeDtypeStruct((units, width), LOW),
-        ),
-        in_specs=[anywhere, resident] + [anywhere] * 6,
-        out_specs=(resident, anywhere, anywhere, anywhere),
+        out_shape=(jax.ShapeDtypeStruct((count, width), FULL),) * 2
+        + (jax.ShapeDtypeStruct((width, units), LOW),) * 3,
+        in_specs=[resident] + [anywhere] * 9,
+        out_specs=(resident,) * 2 + (anywhere,) * 3,
         scratch_shapes=[
-            vmem(ctx_count, fsdp_count, share, width),
-            vmem(ctx_count, count, width),
-            vmem(ctx_count, count, width),
-            vmem(2, ctx_count, count, width),
-            vmem(rows.shape[0], width),
-            vmem(rows.shape[0], units),
-            vmem(rows.shape[0], units),
+            vmem(2, total, 256),
+            vmem(total, units),
+            vmem(total, units),
             vmem(256, units),
             vmem(256, units),
-            vmem(256, width),
-            dma((ctx_count,)),
-            dma((ctx_count,)),
-            dma((ctx_count, len(PEERS))),
-            dma((ctx_count, len(PEERS))),
-            dma((ctx_count,)),
-            dma((2, ctx_count)),
-            dma((5,)),
             dma((3,)),
-        ],
+            dma((2,)),
+            dma((2,)),
+        ]
+        + buffers * 2
+        + sems * 2,
         compiler_params=pltpu.CompilerParams(
             collective_id=3, has_side_effects=True, vmem_limit_bytes=BIG_VMEM
         ),
         cost_estimate=pl.CostEstimate(
-            flops=40_000_000_000, bytes_accessed=300_000_000, transcendentals=0
+            flops=40_000_000_000, bytes_accessed=600_000_000, transcendentals=0
         ),
-    )(slots, info, extra, rows, grads, hidden, gate_back, up_back)
+    )(info, slots, extra, out_slots, out_extra, *sides)
 
 
 def mm(subscripts, left, right):
@@ -1330,12 +1369,6 @@
     choose = routing(info, lax.axis_index("ctx"), slots, gated)
     chosen = mm("bst,btd->bsd", choose, every).astype(LOW)
     return every, swap_slots(chosen.reshape(ctx_count, fsdp_count, -1, rows.shape[1]))
-
-
-def send_grads(rows, info, slots, ctx_count, fsdp_count):
-    if (ctx_count, fsdp_count) == (4, 8):
-        return dispatch_rows(rows, info, slots, ctx_count, fsdp_count)
-    return send_rows(rows, info, slots, True, ctx_count, fsdp_count)
 
 
 def run_expert(rows, info, gate, up, down, grads, ctx_count, fsdp_count):
@@ -1354,28 +1387,32 @@
     return every, arrived, hidden, gate_back, up_back, back
 
 
-def return_grads(
-    slots, info, extra, rows, grads, hidden, gate_back, up_back, ctx_count, fsdp_count
-):
-    extra = extra.astype(LOW)
+def return_slots(slots, info, extra, gated):
+    back = swap_slots(slots).reshape(slots.shape[0], -1, slots.shape[3])
+    choose = routing(info, lax.axis_index("ctx"), back.shape[1], gated)
+    total = (mm("bst,bsd->btd", choose, back) + extra).astype(LOW)
+    return lax.psum_scatter(total, "ctx", scatter_dimension=0, tiled=False).astype(FULL)
+
+
+def return_both(slots, extra, out_slots, out_extra, info, sides, ctx_count, fsdp_count):
+    extra, out_extra = extra.astype(LOW), out_extra.astype(LOW)
     if (ctx_count, fsdp_count) == (4, 8):
         return combine_rows(
-            slots, info, extra, rows, grads, hidden, gate_back, up_back, ctx_count, fsdp_count
+            slots, extra, out_slots, out_extra, info, sides, ctx_count, fsdp_count
         )
-    back = swap_slots(slots).reshape(ctx_count, -1, slots.shape[3])
-    choose = routing(info, lax.axis_index("ctx"), back.shape[1], False)
-    total = (mm("bst,bsd->btd", choose, back) + extra).astype(LOW)
+    rows, grads, hidden, gate_back, up_back = sides
     return (
-        lax.psum_scatter(total, "ctx", scatter_dimension=0, tiled=False).astype(FULL),
+        return_slots(slots, info, extra, False),
+        return_slots(out_slots, info, out_extra, True),
         mm("sd,sf->df", rows, gate_back).astype(LOW),
         mm("sd,sf->df", rows, up_back).astype(LOW),
-        mm("sf,sd->fd", hidden, grads).astype(LOW),
-    )
-
-
-def gather_all(items, ctx_count, fsdp_count):
+        mm("sd,sf->df", grads, hidden).astype(LOW),
+    )
+
+
+def gather_all(items, rows, slots, ctx_count, fsdp_count):
     if (ctx_count, fsdp_count) == (4, 8):
-        return gather_arrays(items, ctx_count, fsdp_count)
+        return gather_arrays(items, rows, slots, ctx_count, fsdp_count)
     results = []
     for kind, shard in items:
         if kind == "line":
@@ -1389,17 +1426,23 @@
             result = lax.all_gather(shard, ("ctx", "fsdp"), axis=0)
             result = result.reshape((ctx_count, fsdp_count) + shard.shape)
         results.append(result)
+    return (results,) + send_rows(rows, results[0], slots, True, ctx_count, fsdp_count)
+
+
+def scatter_all(items, ctx_count, fsdp_count):
+    items = [(kind, grad.astype(LOW)) for kind, grad in items]
+    if (ctx_count, fsdp_count) == (4, 8):
+        return scatter_arrays(items, ctx_count, fsdp_count)
+    results = []
+    for kind, grad in items:
+        if kind == "line":
+            grad = grad.reshape(ctx_count, fsdp_count, -1, grad.shape[1]).swapaxes(0, 1)
+            grad = lax.psum_scatter(grad, "fsdp", scatter_dimension=0, tiled=False)
+            results.append(along_line(grad))
+        else:
+            total = lax.psum_scatter(grad, ("ctx", "fsdp"), scatter_dimension=0, tiled=True)
+            results.append(total.astype(FULL))
     return results
-
-
-def scatter_all(grads, ctx_count, fsdp_count):
-    grads = [grad.astype(LOW) for grad in grads]
-    if (ctx_count, fsdp_count) == (4, 8):
-        return scatter_arrays(grads, ctx_count, fsdp_count)
-    return [
-        lax.psum_scatter(grad, ("ctx", "fsdp"), scatter_dimension=0, tiled=True).astype(FULL)
-        for grad in grads
-    ]
 
 
 def along_line(array):
@@ -1507,7 +1550,9 @@
     )
     dense = after(dense, gate_swapped, up_swapped, down_swapped)
     kinds = ("column", "all", "all", "all", "all", "line", "line", "plane")
-    gathered = gather_all(list(zip(kinds, dense)), ctx_count, fsdp_count)
+    gathered, all_cot, arrived_grad = gather_all(
+        list(zip(kinds, dense)), cot_low, plane_slots, ctx_count, fsdp_count
+    )
     all_info = gathered[0]
     full_query, full_tail, full_expand, full_output, full_sgate, full_sup, full_sdown = [
         item.reshape(-1, item.shape[-1]) for item in gathered[1:]
@@ -1521,23 +1566,12 @@
 
     (up_swapped,) = after((up_swapped,), all_info)
     up_moved = along_line(up_swapped)
-    (cot_sent,) = after((cot_low,), gate_moved)
-    all_cot, arrived_grad = send_grads(cot_sent, all_info, plane_slots, ctx_count, fsdp_count)
-    (down_swapped,) = after((down_swapped,), arrived_grad)
-    down_moved = along_line(down_swapped)
     all_cot = all_cot.reshape(sequence, model_width)
     arrived_grad = arrived_grad.reshape(ctx_count, plane_slots, model_width)
 
-    def whole(moved):
-        return share_parts(moved, members, fsdp_count).swapaxes(0, 1)
-
-    gate_all = whole(gate_moved).reshape(model_width, hidden_units)
-    up_all = whole(up_moved).reshape(model_width, hidden_units)
-    down_all = whole(down_moved).transpose(1, 2, 0, 3).reshape(hidden_units, model_width)
-
     plain_one, inverse_one = norm_forward(source)
     normed = (plain_one * gain_one).astype(LOW)
-    (normed,) = after((normed,), arrived_grad, up_moved)
+    (normed,) = after((normed,), gate_moved)
     (query_raw,) = after((jnp.dot(normed, full_query, preferred_element_type=FULL),))
     query_raw = query_raw.reshape(row_count, HEADS, NOPE + ROPE)
     query_nope = query_raw[:, :, :NOPE].astype(LOW)
@@ -1558,6 +1592,8 @@
     expand_key = expand[:, :, :NOPE]
     expand_value = expand[:, :, NOPE:]
     query_latent = mm("thd,chd->htc", query_nope, expand_key).astype(LOW)
+    (down_swapped,) = after((down_swapped,), up_moved, query_latent)
+    down_moved = along_line(down_swapped)
     query_turned = jnp.pad(query_rope.swapaxes(0, 1), ((0, 0),) + pad_rope)
     latent_out, log_total = attend(
         query_latent, query_turned, all_latent, all_keys, ctx_count, score_scale
@@ -1569,6 +1605,12 @@
     plain_two, inverse_two = norm_forward(middle)
     second = (plain_two * gain_two).astype(LOW)
 
+    def whole(moved):
+        return share_parts(moved, members, fsdp_count).swapaxes(0, 1)
+
+    gate_all = whole(gate_moved).reshape(model_width, hidden_units)
+    up_all = whole(up_moved).reshape(model_width, hidden_units)
+    down_all = whole(down_moved).transpose(1, 2, 0, 3).reshape(hidden_units, model_width)
     (second_sent,) = after((second,), down_moved)
     all_second, arrived_rows, hidden_act, gate_back, up_back, arrived_back = run_expert(
         second_sent, all_info, gate_all, up_all, down_all, arrived_grad, ctx_count, fsdp_count
@@ -1589,48 +1631,44 @@
     )
     slots_shape = (ctx_count, fsdp_count, share, model_width)
     rows_shape = (ctx_count, row_count, model_width)
-    second_grad, gate_grad, up_grad, down_grad = return_grads(
+    shared_out = jnp.dot(shared_hidden, full_sdown, preferred_element_type=FULL)
+    result = jnp.dot(hidden_act, down_all, preferred_element_type=FULL).astype(LOW)
+    second_grad, out_sum, gate_grad, up_grad, down_grad = return_both(
         arrived_back.reshape(slots_shape),
+        shared_second_grad.reshape(rows_shape),
+        result.reshape(slots_shape),
+        shared_out.reshape(rows_shape),
         all_info,
-        shared_second_grad.reshape(rows_shape),
-        arrived_rows.reshape(-1, model_width),
-        arrived_grad.reshape(-1, model_width),
-        hidden_act,
-        gate_back,
-        up_back,
+        (
+            arrived_rows.reshape(-1, model_width),
+            arrived_grad.reshape(-1, model_width),
+            hidden_act,
+            gate_back,
+            up_back,
+        ),
         ctx_count,
         fsdp_count,
     )
-    line_shape = (ctx_count, members, model_width // ctx_count // members, hidden_units)
-    gate_sum = sum_parts(gate_grad.reshape(line_shape).swapaxes(0, 1), members, fsdp_count)
+    layer_out = (middle + out_sum).astype(LOW)[None]
+
+    def line_sum(grad):
+        grad = grad.reshape(ctx_count, members, -1, hidden_units).swapaxes(0, 1)
+        return sum_parts(grad, members, fsdp_count)
+
+    gate_sum, up_sum, down_sum = (line_sum(gate_grad), line_sum(up_grad), line_sum(down_grad))
     gate_returned = along_line(gate_sum)
-    up_sum = sum_parts(up_grad.reshape(line_shape).swapaxes(0, 1), members, fsdp_count)
-    down_sum = sum_parts(
-        down_grad.reshape(members, hidden_units // members, ctx_count, -1).swapaxes(1, 2),
-        members,
-        fsdp_count,
-    )
-    shared_hidden, sgate_back, sup_back, hidden_act = after(
-        (shared_hidden, sgate_back, sup_back, hidden_act), second_grad
-    )
-    sgate_back, sup_back, hidden_act = after((sgate_back, sup_back, hidden_act), gate_sum)
-    pair_grad = jnp.stack(
-        [mm("td,tf->df", all_second, sgate_back), mm("td,tf->df", all_second, sup_back)]
-    ).astype(LOW)
-    pair_grad = (
-        pair_grad.reshape(2, ctx_count, fsdp_count, dense_rows, shared_units)
-        .transpose(2, 0, 1, 3, 4)
-        .reshape(fsdp_count, 2, ctx_count * dense_rows, shared_units)
-    )
+    sgate_back, sup_back = after((sgate_back, sup_back), gate_sum)
+    shared_hidden, sgate_back, sup_back = after(
+        (shared_hidden, sgate_back, sup_back), second_grad
+    )
+    sgate_grad = mm("td,tf->df", all_second, sgate_back).astype(LOW)
+    sup_grad = mm("td,tf->df", all_second, sup_back).astype(LOW)
     sdown_grad = mm("tf,td->fd", shared_hidden, all_cot).astype(LOW)
-    pair_sent, sdown_sent = (pair_grad, sdown_grad)
-    pair_grad = lax.psum_scatter(pair_grad, "fsdp", scatter_dimension=0, tiled=False)
+    (second_grad,) = after(
+        (second_grad,), gate_sum, up_sum, down_sum, sgate_grad, sup_grad, sdown_grad
+    )
     sdown_grad = lax.psum_scatter(sdown_grad, "fsdp", scatter_dimension=0, tiled=True)
-    result = jnp.dot(hidden_act, down_all, preferred_element_type=FULL).astype(LOW)
-    shared_out = jnp.dot(shared_hidden, full_sdown, preferred_element_type=FULL)
-    (second_grad,) = after(
-        (second_grad,), gate_sum, up_sum, down_sum, pair_sent, sdown_sent, result, shared_out
-    )
+
     middle_part, gain_two_grad = norm_backward(second_grad, plain_two, inverse_two, gain_two)
     middle_grad = cot_full + middle_part
     attended_grad = middle_grad.astype(LOW)
@@ -1640,8 +1678,8 @@
     )
     latent_out_grad = mm("thv,chv->htc", values_grad, expand_value).astype(LOW)
     (latent_out_grad,) = after((latent_out_grad,), gate_returned)
-    (result,) = after((result,), latent_out_grad)
-    came_back = swap_slots(result.reshape(slots_shape)).reshape(ctx_count, plane_slots, model_width)
+    (up_sum,) = after((up_sum,), gate_returned, latent_out_grad)
+    up_returned = along_line(up_sum)
     query_latent_grad, turned_grad, all_latent_grad, all_keys_grad = attend_back(
         query_latent,
         query_turned,
@@ -1657,7 +1695,6 @@
     keys_part = jnp.concatenate([all_latent_grad, all_keys_grad[:, :ROPE]], axis=1)
     keys_part = keys_part.reshape(2, ctx_count, half_rows, LATENT + ROPE)
     keys_part = jnp.stack([keys_part[0], keys_part[1, ::-1]], axis=1)
-    (keys_part,) = after((keys_part,), pair_grad, sdown_grad)
     keys_part = lax.psum_scatter(
         keys_part.reshape(sequence, LATENT + ROPE).astype(LOW),
         "ctx",
@@ -1667,13 +1704,6 @@
     latent_grad, keys_grad = (keys_part[:, :LATENT], keys_part[:, LATENT:])
     expand_value_grad = mm("htc,thv->chv", latent_out, values_grad)
 
-    out_part = (
-        mm("bst,bsd->btd", routing(all_info, z, plane_slots, True), came_back)
-        + shared_out.reshape(ctx_count, row_count, model_width)
-    ).astype(LOW)
-    (out_part,) = after((out_part,), keys_part)
-    out_sum = lax.psum_scatter(out_part, "ctx", scatter_dimension=0, tiled=False).astype(FULL)
-    layer_out = (middle + out_sum).astype(LOW)[None]
     sdown_grad = sdown_grad.astype(FULL)
 
     query_nope_grad = mm("htc,chd->thd", query_latent_grad, expand_key)
@@ -1713,30 +1743,29 @@
         ],
         axis=1,
     )
-    (up_sum,) = after((up_sum,), came_back, query_nope_grad)
-    up_returned = along_line(up_sum)
-    (pair_grad,) = after((pair_grad,), up_returned)
-    pair_grad = lax.all_to_all(
-        pair_grad, "ctx", split_axis=1, concat_axis=2, tiled=True
-    ).astype(FULL)
-    (down_sum,) = after((down_sum,), up_returned, normed_grad, pair_grad)
+    (down_sum,) = after((down_sum,), up_returned, query_nope_grad)
     down_returned = along_line(down_sum)
     dense_grads = after(
-        (query_weight_grad, tail_grad, expand_grad, output_weight_grad), up_returned
-    )
-    query_sum, tail_sum, expand_sum, output_sum = scatter_all(
-        dense_grads, ctx_count, fsdp_count
-    )
-
-    def owned(moved, like):
+        (query_weight_grad, tail_grad, expand_grad, output_weight_grad, sgate_grad, sup_grad),
+        up_returned,
+    )
+    kinds = ("all",) * 4 + ("line",) * 2
+    query_sum, tail_sum, expand_sum, output_sum, sgate_sum, sup_sum = scatter_all(
+        list(zip(kinds, dense_grads)), ctx_count, fsdp_count
+    )
+
+    def joined(pieces):
+        return pieces.swapaxes(0, 1).reshape(dense_rows, -1).astype(FULL)
+
+    def owned(moved):
         moved = moved.reshape((members, EXP_DEV) + moved.shape[1:])
         moved = swap_parts(moved, members, fsdp_count).swapaxes(0, 1)
-        return moved.reshape(like.shape).astype(FULL)
+        return moved.reshape(EXP_DEV, -1, hidden_units).astype(FULL)
 
     expert_grads = (
-        owned(gate_returned, expert_gate),
-        owned(up_returned, expert_up),
-        owned(down_returned, expert_down),
+        owned(gate_returned),
+        owned(up_returned),
+        owned(down_returned).swapaxes(1, 2),
     )
     return (
         layer_out,
@@ -1748,8 +1777,8 @@
         expand_sum,
         output_sum,
         tail_sum[:, rotary_end + 1],
-        pair_grad[0],
-        pair_grad[1],
+        joined(sgate_sum),
+        joined(sup_sum),
         sdown_grad,
         expert_grads[0],
         expert_grads[1],

time: 1480 us -> 1360 us (0.919)
  waiting for transfers between devices: 151 us -> 93.2 us
  Pallas kernels: 786 us -> 840 us
  local copies, waits for them, and re-layouts: 194 us -> 148 us
  starting transfers between devices: 72.3 us -> 47.5 us
  matrix products: 161 us -> 139 us
  other arithmetic: 87 us -> 66.8 us
    pallas_call x2 -> x1, Pallas kernels: 279 us -> 153 us  [scatter_arrays(): pl.pallas_call(functools.partial(scatter_kernel, ctx_count, kinds), out_s...]
    pallas_call x1, Pallas kernels: 186 us -> 277 us  [gather_arrays(): pl.pallas_call(functools.partial(gather_kernel, ctx_count, kinds), out_sh...]
    pallas_call x1, Pallas kernels: 114 us -> 201 us  [combine_rows(): pl.pallas_call(functools.partial(combine_kernel, ctx_count), out_shape=(j...]
    all_to_all x2 -> x0, waiting for transfers between devices: 40.2 us -> none  [the longest x1 20.6 us: swap_slots(): lax.all_to_all(slots, 'fsdp', split_axis=1, concat_axis=1, tiled=True)]
    reduce_scatter x2 -> x0, waiting for transfers between devices: 31.3 us -> none  [the longest x1 31.3 us: local(): lax.psum_scatter(pair_grad, 'fsdp', scatter_dimension=0, tiled=False)]
    dot_general x19 -> x18, matrix products: 108 us -> 85.7 us  [mm(): return jnp.einsum(subscripts, left, right, preferred_element_type=FULL)]
    reduce_scatter x1, waiting for transfers between devices: 0.01 us -> 21.5 us  [local(): lax.psum_scatter(keys_part.reshape(sequence, LATENT + ROPE).astype(LOW),...]
    all_gather x1, waiting for transfers between devices: 20.4 us -> 0.01 us  [local(): lax.all_gather(jnp.concatenate([latent_norm, jnp.pad(key_rope, pad_rope)]...]
  transfers between devices with their start and end apart: 25 -> 21, of which waited for: 7 -> 4; matrix products, arithmetic and copies ran while one was open for 25% -> 19% of each run, Pallas kernels for 36% -> 36%
where the time goes in v5:
time: 1360 us; the launch traced here: 1350 us
  Pallas kernels  840 us (62%)
  local copies, waits for them, and re-layouts  148 us (11%)
  matrix products  139 us (10%)
  waiting for transfers between devices  93.2 us (7%)
  other arithmetic  66.8 us (5%)
  starting transfers between devices  47.5 us (3%)
  between operations  15.3 us (1%)
    pallas_call x1, Pallas kernels, gather_arrays(): pl.pallas_call(functools.partial(gather_kernel, ctx_count, kinds), out_sh...  277 us
    pallas_call x1, Pallas kernels, combine_rows(): pl.pallas_call(functools.partial(combine_kernel, ctx_count), out_shape=(j...  201 us
    pallas_call x1, Pallas kernels, scatter_arrays(): pl.pallas_call(functools.partial(scatter_kernel, ctx_count, kinds), out_s...  153 us
    pallas_call x1, Pallas kernels, expert_rows(): pl.pallas_call(functools.partial(expert_kernel, ctx_count), out_shape=(lo...  147 us
    dot_general x18, matrix products, mm(): return jnp.einsum(subscripts, left, right, preferred_element_type=FULL)  85.7 us
    all_to_all x6, waiting for transfers between devices, along_line(): return lax.all_to_all(array, 'ctx', split_axis=0, concat_axis=0, tiled=True)  68 us
    unnamed x189, local copies, waits for them, and re-layouts  45.6 us
    all_to_all x6, starting transfers between devices, along_line(): return lax.all_to_all(array, 'ctx', split_axis=0, concat_axis=0, tiled=True)  37.4 us
  transfers between devices with their start and end apart: 21, of which 4 were waited for; matrix products, arithmetic and copies ran while one was open for 19% of the time, Pallas kernels for 36%

profile of v5, /device:TPU:1, one launch (start us, length us, event | category | flops | bytes accessed | tf_op | source)
XLA Modules:
  0.0 1349.6 jit_solution(7187228296767960791)
XLA Ops:
  17.0 6.0 all-to-all-start
  40.2 277.0 %shard_map.280 = (f32[4,24,256]{2,1,0:T(8,128)}, bf16[4,8,64,3072]{3,2,1,0:T(8,128)(2,1)}, bf16[4,8,64,768]{3,2,1,0:T(8,128)(2,1)}, bf16[4,8,16,4096]{3,2,1,0:T(...) custom-call(f32[24,256]{1,0:T(8,128)} %copy-done.57, ...), custom_call_target="tpu_custom_call" | custom-call | flops 2000000000 | bytes 800000000 | tf_op jit(solution)/shard_map/pallas_call | solution.py:837
  317.2 8.1 all-to-all-start.1
  328.9 5.6 copy.333
  341.0 9.7 fusion.80
  359.1 5.2 convolution_convert_fusion.6.query_ref
  364.3 48.6 %all-to-all-done.1 = bf16[4,256,1408]{2,1,0:T(8,128)(2,1)} async-done(((bf16[4,256,1408]{2,1,0:T(8,128)(2,1)}), bf16[4,256,1408]{2,1,0:T(8,128)(2,1)}, u32[]{:S(2)}, u32[]{:S(2)}) %all-to-all-start.1) | async-done | bytes 2883616 | tf_op jit(solution)/shard_map/all_to_all | solution.py:1449
  418.0 7.9 fusion.81
  453.8 29.1 %shard_map.281 = (bf16[16,256,512]{2,1,0:T(8,128)(2,1)}, f32[16,256,1]{2,1,0:T(8,128)}) custom-call(bf16[16,256,512]{2,1,0:T(8,128)(2,1)} %convolution_convert_fusion.6.query_ref, bf16[16,256,128]{2,1,0:T(8,128)(2,1)} %pad.24.turned_ref, bf16[1024,512]{1,0:T(8,128)(2,1)} %slice.209.keys_ref, bf16[1024,128]{1,0:T(8,128)(2,1)} %slice.210.rope_ref), custom_call_target="tpu_custom_call" | custom-call | flops 12000000000 | bytes 12000000 | tf_op jit(solution)/shard_map/pallas_call | solution.py:516
  486.8 6.2 multiply_reduce_fusion.2
  510.6 7.0 copy.290
  517.6 7.7 copy.334
  525.3 147.4 %shard_map.282 = (bf16[4,256,2048]{2,1,0:T(8,128)(2,1)}, bf16[4,8,64,2048]{3,2,1,0:T(8,128)(2,1)}, bf16[4,512,1408]{2,1,0:T(8,128)(2,1)}, bf16[4,512,1408]{2,1,0...) custom-call(bf16[256,2048]{1,0:T(8,128)(2,1)} %multiply_convert_fusion.3.rows_ref, ...), custom_call_target="tpu_custom_call" | custom-call | flops 60000002048 | bytes 400000000 | tf_op jit(solution)/shard_map/pallas_call | solution.py:1002
  672.7 18.5 %convolution_convert_fusion = bf16[2048,2048]{1,0:T(8,128)(2,1)} fusion(bf16[2048,1408]{1,0:T(8,128)(2,1)} %bitcast.390, bf16[1408,2048]{1,0:T(8,128)(2,1)} %bitcast.353), kind=kOutput, calls=%fused_computation.2 | convolution fusion | flops 11815354368 | bytes 19922944 | tf_op jit(solution)/shard_map/dot_general | solution.py:1635
  694.6 6.1 multiply_convert_fusion
  700.7 5.5 fusion.83
  706.2 5.1 convolution_convert_fusion.1.refs_3_
  711.4 5.1 add_convert_fusion
  716.5 200.9 %shard_map.283 = (f32[256,2048]{1,0:T(8,128)}, f32[256,2048]{1,0:T(8,128)}, bf16[2048,1408]{1,0:T(8,128)(2,1)}, bf16[2048,1408]{1,0:T(8,128)(2,1)}, bf16[2048,1408]{1,0:T(8,128)(2,1)}) custom-call(f32[4,24,256]{2,1,0:T(8,128)} %get-tuple-element.125.info_ref, bf16[4,8,64,2048]{3,2,1,0:T(8,128)(2,1)} %bitcast.388, bf16[4,256,2048]{2,1,0:T(8,128)(2,1)} %bitcast.400, ...), custom_call_target="tpu_custom_call" | custom-call | flops 40000000000 | bytes 600000000 | tf_op jit(solution)/shard_map/pallas_call | solution.py:1275
  931.4 8.6 all-to-all-start.3
  940.0 7.4 convolution_convert_fusion.4
  979.7 5.6 fusion.43
  985.3 19.4 %all-to-all-done.3 = bf16[4,256,1408]{2,1,0:T(8,128)(2,1)} async-done(((bf16[4,256,1408]{2,1,0:T(8,128)(2,1)}), bf16[4,256,1408]{2,1,0:T(8,128)(2,1)}, u32[]{:S(2)}, u32[]{:S(2)}) %all-to-all-start.3) | async-done | bytes 2883616 | tf_op jit(solution)/shard_map/all_to_all | solution.py:1449
  1009.3 32.4 %shard_map.284 = (bf16[16,256,512]{2,1,0:T(8,128)(2,1)}, f32[16,256,128]{2,1,0:T(8,128)}, f32[1024,512]{1,0:T(8,128)}, f32[1024,128]{1,0:T(8,128)}) custom-call(bf16[16,256,512]{2,1,0:T(8,128)(2,1)} %convolution_convert_fusion.6.query_ref, bf16[16,256,128]{2,1,0:T(8,128)(2,1)} %pad.24.turned_ref, bf16[1024,512]{1,0:T(8,128)(2,1)} %slice.209.keys_ref, ...), custom_call_target="tpu_custom_call" | custom-call | flops 30000001024 | bytes 30000000 | tf_op jit(solution)/shard_map/pallas_call | solution.py:542
  1070.3 21.5 %reduce-scatter.3.cloned.1.call-done = bf16[256,576]{0,1:T(8,128)(2,1)} async-done(((bf16[1024,576]{0,1:T(8,128)(2,1)}), bf16[256,576]{0,1:T(8,128)(2,1)}) %reduce-scatter.3.cloned.1.call-update) | async-done | bytes 294928 | tf_op jit(solution)/shard_map/reduce_scatter | solution.py:1698
  1099.2 5.1 all-to-all-start.5
  1106.8 6.7 fusion.84
  1117.1 12.1 concatenate.47
  1129.3 10.0 fusion.85
  1144.3 6.5 copy.301
  1161.2 153.0 %shard_map.285 = (f32[64,3072]{1,0:T(8,128)}, f32[64,768]{1,0:T(8,128)}, f32[16,4096]{1,0:T(8,128)}, f32[64,2048]{1,0:T(8,128)}, bf16[4,64,704]{2,1,0:T(8,128)(2,1)}, /*index=5*/bf16[4,64,704]{2,1,0:T(8,128)(2,1)}) custom-call(bf16[4,4,2,64,3072]{4,3,2,1,0:T(8,128)(2,1)} %bitcast.315, bf16[4,4,2,64,768]{4,3,2,1,0:T(8,128)(2,1)} %bitcast.331, ...), custom_call_target="tpu_custom_call" | custom-call | bytes 500000000 | tf_op jit(solution)/shard_map/pallas_call | solution.py:364
  1334.1 6.3 copy.309
  (364 shorter events, 232.9 us)
Async XLA Ops:
  9.9 3.6 collective-permute-start
  17.0 300.2 %all-to-all-start = ((bf16[4,256,1408]{2,1,0:T(8,128)(2,1)}), bf16[4,256,1408]{2,1,0:T(8,128)(2,1)}, u32[]{:S(2)}, u32[]{:S(2)}) async-start(bf16[4,256,1408]{2,1,0:T(8,128)(2,1)} %bitcast.16), calls=%async_computation | async-start | bytes 5767168 | tf_op jit(solution)/shard_map/all_to_all | solution.py:1449
  24.2 7.6 collective-permute-start.2
  25.4 10.2 collective-permute-start.1
  30.5 326.8 %copy-start.66 = (f32[256]{0:T(256)}, f32[256]{0:T(256)S(1)}, u32[]{:S(2)}) copy-start(f32[256]{0:T(256)S(1)} %fusion.74) | copy-start | bytes 3076
  30.8 308.9 %copy-start.63 = (f32[256]{0:T(256)}, f32[256]{0:T(256)S(1)}, u32[]{:S(2)}) copy-start(f32[256]{0:T(256)S(1)} %add_rsqrt_fusion.2) | copy-start | bytes 3076
  317.2 95.8 %all-to-all-start.1 = ((bf16[4,256,1408]{2,1,0:T(8,128)(2,1)}), bf16[4,256,1408]{2,1,0:T(8,128)(2,1)}, u32[]{:S(2)}, u32[]{:S(2)}) async-start(bf16[4,256,1408]{2,1,0:T(8,128)(2,1)} %bitcast.335), calls=%async_computation.1 | async-start | bytes 5767168 | tf_op jit(solution)/shard_map/all_to_all | solution.py:1449
  325.3 115.9 %all-gather.3.cloned.1.call-start = ((), (), s32[]{:S(2)}) async-start(), calls=%async_computation.10 | async-start | bytes 1638400 | tf_op jit(solution)/shard_map/all_gather | solution.py:1585
  325.5 31.9 %copy-start.68 = (f32[32]{0:T(128)}, f32[32]{0:T(128)S(1)}, u32[]{:S(2)}) copy-start(f32[32]{0:T(128)S(1)} %multiply_power_fusion) | copy-start | bytes 388
  334.8 23.0 %copy-start.55 = (f32[512]{0:T(512)}, f32[512]{0:T(512)S(1)}, u32[]{:S(2)}) copy-start(f32[512]{0:T(512)S(1)} %reshape.538) | copy-start | bytes 6148
  353.1 78.8 %copy-start.2 = (f32[256,3072]{0,1:T(8,128)}, f32[256,3072]{0,1:T(8,128)S(1)}, u32[]{:S(2)}) copy-start(f32[256,3072]{0,1:T(8,128)S(1)} %copy.277) | copy-start | bytes 9437188
  413.0 80.1 %all-to-all-start.2 = ((bf16[4,704,512]{2,1,0:T(8,128)(2,1)}), bf16[4,704,512]{2,1,0:T(8,128)(2,1)}, u32[]{:S(2)}, u32[]{:S(2)}) async-start(bf16[4,704,512]{2,1,0:T(8,128)(2,1)} %bitcast.334), calls=%async_computation.2 | async-start | bytes 5767168 | tf_op jit(solution)/shard_map/all_to_all | solution.py:1449
  431.7 61.9 %copy-start.49 = (f32[2048,1]{0,1:T(1,128)}, f32[2048,1]{0,1:T(1,128)S(1)}, u32[]{:S(2)}) copy-start(f32[2048,1]{0,1:T(1,128)S(1)} %copy.336) | copy-start | bytes 24580
  440.6 60.9 %collective-permute-start.4 = (bf16[4,256,1408]{2,1,0:T(8,128)(2,1)}, bf16[4,256,1408]{2,1,0:T(8,128)(2,1)}, u32[]{:S(2)}, u32[]{:S(2)}) collective-permute-start(bf16[4,256,1408]{2,1,0:T(8,128)(2,1)} %all-to-all-done.1), channel_id=1, source_target_pairs={{0,1},{1,0},{2,3},{3,2},{4,5},{5,4},{6,7},{7,6},{8,9},{9,8},{10,11... | collective-permute-start | bytes 8650760 | tf_op jit(solution)/shard_map/ppermute | solution.py:1338
  441.1 53.7 %collective-permute-start.3 = (bf16[4,256,1408]{2,1,0:T(8,128)(2,1)}, bf16[4,256,1408]{2,1,0:T(8,128)(2,1)}, u32[]{:S(2)}, u32[]{:S(2)}) collective-permute-start(bf16[4,256,1408]{2,1,0:T(8,128)(2,1)} %all-to-all-done), channel_id=1, source_target_pairs={{0,1},{1,0},{2,3},{3,2},{4,5},{5,4},{6,7},{7,6},{8,9},{9,8},{10,11... | collective-permute-start | bytes 8650760 | tf_op jit(solution)/shard_map/ppermute | solution.py:1338
  453.8 29.2 %copy-start.6 = (bf16[512,16,128]{0,2,1:T(8,128)(2,1)S(1)}, bf16[512,16,128]{0,2,1:T(8,128)(2,1)}, u32[]{:S(2)}) copy-start(bf16[512,16,128]{0,2,1:T(8,128)(2,1)} %copy.319) | copy-start | bytes 6291460
  493.1 14.8 %collective-permute-start.5 = (bf16[4,704,512]{2,1,0:T(8,128)(2,1)}, bf16[4,704,512]{2,1,0:T(8,128)(2,1)S(1)}, u32[]{:S(2)}, u32[]{:S(2)}) collective-permute-start(bf16[4,704,512]{2,1,0:T(8,128)(2,1)} %all-to-all-done.2), channel_id=1, source_target_pairs={{0,1},{1,0},{2,3},{3,2},{4,5},{5,4},{6,7},{7,6},{8,9},{9,8},{10,11... | collective-permute-start | bytes 8650760 | tf_op jit(solution)/shard_map/ppermute | solution.py:1338
  672.7 18.6 %copy-start.73 = (bf16[4,256,2048]{2,1,0:T(8,128)(2,1)S(1)}, bf16[4,256,2048]{2,1,0:T(8,128)(2,1)}, u32[]{:S(2)}) copy-start(bf16[4,256,2048]{2,1,0:T(8,128)(2,1)} %get-tuple-element.133) | copy-start | bytes 12582916
  919.6 8.9 collective-permute-start.6
  923.6 23.9 %collective-permute-start.8 = (bf16[4,256,1408]{2,1,0:T(8,128)(2,1)}, bf16[4,256,1408]{2,1,0:T(8,128)(2,1)}, u32[]{:S(2)}, u32[]{:S(2)}) collective-permute-start(bf16[4,256,1408]{2,1,0:T(8,128)(2,1)} %dynamic-slice_bitcast_fusion), channel_id=1, source_target_pairs={{0,1},{1,0},{2,3},{3,2},{4,5},{5,4},{6,7},{7,6},{8,9},{9,8},{10,11... | collective-permute-start | bytes 8650760 | tf_op jit(solution)/shard_map/ppermute | solution.py:1348
  927.3 30.0 %collective-permute-start.7 = (bf16[4,256,1408]{2,1,0:T(8,128)(2,1)}, bf16[4,256,1408]{2,1,0:T(8,128)(2,1)S(1)}, u32[]{:S(2)}, u32[]{:S(2)}) collective-permute-start(bf16[4,256,1408]{2,1,0:T(8,128)(2,1)} %dynamic-slice_bitcast_fusion.1), channel_id=1, source_target_pairs={{0,1},{1,0},{2,3},{3,2},{4,5},{5,4},{6,7},{7,6},{8,9},{9,8},{10,11... | collective-permute-start | bytes 8650760 | tf_op jit(solution)/shard_map/ppermute | solution.py:1348
  931.4 73.3 %all-to-all-start.3 = ((bf16[4,256,1408]{2,1,0:T(8,128)(2,1)}), bf16[4,256,1408]{2,1,0:T(8,128)(2,1)}, u32[]{:S(2)}, u32[]{:S(2)}) async-start(bf16[4,256,1408]{2,1,0:T(8,128)(2,1)} %fusion.2), calls=%async_computation.3 | async-start | bytes 5767168 | tf_op jit(solution)/shard_map/all_to_all | solution.py:1449
  940.0 112.7 %reduce-scatter.5.cloned.1.call-start = ((), (), s32[]{:S(2)}) async-start(), calls=%async_computation.9 | async-start | bytes 3244032 | tf_op jit(solution)/shard_map/reduce_scatter | solution.py:1670
  1004.7 94.5 %all-to-all-start.4 = ((bf16[4,256,1408]{2,1,0:T(8,128)(2,1)}), bf16[4,256,1408]{2,1,0:T(8,128)(2,1)}, u32[]{:S(2)}, u32[]{:S(2)}) async-start(bf16[4,256,1408]{2,1,0:T(8,128)(2,1)} %fusion.1), calls=%async_computation.5 | async-start | bytes 5767168 | tf_op jit(solution)/shard_map/all_to_all | solution.py:1449
  1009.3 82.6 %reduce-scatter.3.cloned.1.call-start = ((), (), s32[]{:S(2)}) async-start(), calls=%async_computation.8 | async-start | bytes 1474560 | tf_op jit(solution)/shard_map/reduce_scatter | solution.py:1698
  1044.5 20.8 %collective-permute-start.9 = (bf16[2,256,1408]{2,1,0:T(8,128)(2,1)}, bf16[2,256,1408]{2,1,0:T(8,128)(2,1)}, u32[]{:S(2)}, u32[]{:S(2)}) collective-permute-start(bf16[2,256,1408]{2,1,0:T(8,128)(2,1)} %dynamic-slice_bitcast_fusion.5), channel_id=1, source_target_pairs={{0,1},{1,0},{2,3},{3,2},{4,5},{5,4},{6,7},{7,6},{8,9},{9,8},{10,11... | collective-permute-start | bytes 4325384 | tf_op jit(solution)/shard_map/ppermute | solution.py:1327
  1067.4 25.5 %copy-start.67 = (f32[256]{0:T(256)S(1)}, f32[256]{0:T(256)}, u32[]{:S(2)}) copy-start(f32[256]{0:T(256)} %copy-done.66) | copy-start | bytes 3076
  1067.4 25.5 %copy-start.69 = (f32[32]{0:T(128)S(1)}, f32[32]{0:T(128)}, u32[]{:S(2)}) copy-start(f32[32]{0:T(128)} %copy-done.68) | copy-start | bytes 388
  1067.4 25.8 %copy-start.38 = (f32[256,32]{1,0:T(8,128)S(1)}, f32[256,32]{1,0:T(8,128)}, u32[]{:S(2)}) copy-start(f32[256,32]{1,0:T(8,128)} %copy-done.37) | copy-start | bytes 98308
  1099.2 218.0 %all-to-all-start.5 = ((bf16[4,256,1408]{2,1,0:T(8,128)(2,1)}), bf16[4,256,1408]{2,1,0:T(8,128)(2,1)}, u32[]{:S(2)}, u32[]{:S(2)}) async-start(bf16[4,256,1408]{2,1,0:T(8,128)(2,1)} %fusion), calls=%async_computation.7 | async-start | bytes 5767168 | tf_op jit(solution)/shard_map/all_to_all | solution.py:1449
  1142.0 181.5 %collective-permute-start.10 = (bf16[2,256,1408]{2,1,0:T(8,128)(2,1)}, bf16[2,256,1408]{2,1,0:T(8,128)(2,1)}, u32[]{:S(2)}, u32[]{:S(2)}) collective-permute-start(bf16[2,256,1408]{2,1,0:T(8,128)(2,1)} %dynamic-slice_bitcast_fusion.4), channel_id=1, source_target_pairs={{0,1},{1,0},{2,3},{3,2},{4,5},{5,4},{6,7},{7,6},{8,9},{9,8},{10,11... | collective-permute-start | bytes 4325384 | tf_op jit(solution)/shard_map/ppermute | solution.py:1327
  1318.7 10.2 collective-permute-start.11
  (76 other events, 396.2 us)
Sparse Core Ops, SparseCore 0:
  359.3 49.1 all-gather.2
  947.5 45.7 reduce-scatter.4
  1052.8 39.0 reduce-scatter.2

commit v6 on v5

--- a/solution.py
+++ b/solution.py
@@ -99,6 +99,33 @@
     if step == 2:
         return 2 - 2 * lax.rem(z, 2) + upper
     return 3 - 3 * upper
+
+
+def outermost(z, ctx_count):
+    return (z == 0) | (z == ctx_count - 1)
+
+
+def along_order(z, ctx_count, step, take):
+    ends = outermost(z, ctx_count)
+    if step <= 1:
+        take(step)
+    if step == 1:
+
+        @pl.when(jnp.logical_not(ends))
+        def _():
+            take(2)
+
+    if step >= 2:
+
+        @pl.when(ends)
+        def _():
+            take(step)
+
+        if step + 1 < ctx_count:
+
+            @pl.when(jnp.logical_not(ends))
+            def _():
+                take(step + 1)
 
 
 def remote(source, target, send, receive, z, f):
@@ -616,8 +643,9 @@
         own.start()
         own.wait()
 
-    def pass_on(self, block, own):
-        if not own:
+    def take(self, step):
+        block = nearest(self.z, step)
+        if step > 0:
             at = self.blocks.at[block]
             sems = (self.z_send.at[block, 0], self.z_recv.at[block])
             remote(at, at, *sems, self.z, self.core).wait_recv()
@@ -625,6 +653,8 @@
             self.z, block, self.ctx_count, lambda way, to: self.z_copy(block, way, to).start()
         )
         self.store(block).start()
+
+    def choose(self, block):
         groups, share, width = self.chosen.shape[1:]
         choose = one_hot(self.info_ref[block], self.z, groups * share, self.gated)
 
@@ -752,20 +782,28 @@
         sems = (c_send.at[item, block, which], c_recv.at[item, block, which])
         remote(at, at, *sems, z, core).wait_recv()
 
+    def take(step):
+        for item in range(count):
+            if not steps(item, step):
+                continue
+            block = slot(item, step)
+            if step == 0:
+                own(item).wait()
+            else:
+                at = z_view(item, block)
+                sems = (z_send.at[item, block, 0], z_recv.at[item, block])
+                remote(at, at, *sems, z, core).wait_recv()
+            if kinds[item] in ("all", "column"):
+                both_ways(
+                    z, block, ctx_count, lambda way, to: z_copy(item, block, way, to).start()
+                )
+        move.take(step)
+
     def first(item, step):
         block = slot(item, step)
-        if step == 0:
-            own(item).wait()
-        else:
-            at = z_view(item, block)
-            sems = (z_send.at[item, block, 0], z_recv.at[item, block])
-            remote(at, at, *sems, z, core).wait_recv()
-        if kinds[item] in ("all", "column"):
-            both_ways(z, block, ctx_count, lambda way, to: z_copy(item, block, way, to).start())
-        if kinds[item] != "column":
-            p_copy(item, block, 0).start()
-            p_copy(item, block, 1).start()
-            c_copy(item, block, 0).start()
+        p_copy(item, block, 0).start()
+        p_copy(item, block, 1).start()
+        c_copy(item, block, 0).start()
 
     def second(item, step):
         block = slot(item, step)
@@ -787,12 +825,14 @@
                 piece(item, step).start()
     move.begin()
     for step in range(ctx_count + 2):
+        if step < ctx_count:
+            along_order(z, ctx_count, step, take)
         for lag, stage in ((0, first), (1, second), (2, third)):
             for item in range(count):
-                if steps(item, step - lag) and (lag == 0 or kinds[item] != "column"):
+                if steps(item, step - lag) and kinds[item] != "column":
                     stage(item, step - lag)
             if lag == 0 and step < ctx_count:
-                move.pass_on(nearest(z, step), step == 0)
+                move.choose(nearest(z, step))
     for step in range(ctx_count):
         move.await_slots(nearest(z, step))
     move.finish()
@@ -925,8 +965,10 @@
     for load in loads:
         load.start()
     load_grads(0).start()
-    move.pass_on(order[0], True)
-    move.pass_on(order[1], False)
+    along_order(move.z, ctx_count, 0, move.take)
+    move.choose(order[0])
+    along_order(move.z, ctx_count, 1, move.take)
+    move.choose(order[1])
     for load in loads:
         load.wait()
 
@@ -977,9 +1019,15 @@
         each_tile(width, back_tile)
         store_back(block).start()
 
+        for later in range(2, ctx_count):
+
+            @pl.when(step + 2 == later)
+            def _():
+                along_order(move.z, ctx_count, later, move.take)
+
         @pl.when(step + 2 < ctx_count)
         def _():
-            move.pass_on(block_at(step + 2), False)
+            move.choose(block_at(step + 2))
 
     for step in range(ctx_count):
         store_slots(order[step]).wait()
@@ -1499,17 +1547,18 @@
     hidden_units = expert_gate.shape[2]
     shared_units = shared_gate.shape[1] // ctx_count
 
-    def swapped(weight):
-        weight = weight.reshape((EXP_DEV, members, weight.shape[1] // members) + weight.shape[2:])
-        weight = swap_parts(weight.swapaxes(0, 1), members, fsdp_count)
-        return weight.reshape((ctx_count,) + weight.shape[2:])
-
-    gate_swapped, up_swapped, down_swapped = (
-        swapped(expert_gate),
-        swapped(expert_up),
-        swapped(expert_down),
-    )
-    gate_moved = along_line(gate_swapped)
+    def by_part(weight):
+        return weight.reshape(
+            (EXP_DEV, members, weight.shape[1] // members) + weight.shape[2:]
+        ).swapaxes(0, 1)
+
+    def swapped(pieces):
+        pieces = swap_parts(pieces, members, fsdp_count)
+        return pieces.reshape((ctx_count,) + pieces.shape[2:])
+
+    pair_swapped = swapped(jnp.stack([by_part(expert_gate), by_part(expert_up)], axis=2))
+    down_swapped = swapped(by_part(expert_down))
+    pair_moved = along_line(pair_swapped)
 
     local_routes = routes[0]
     expert_index = jnp.arange(experts_total, dtype=jnp.int32)
@@ -1548,7 +1597,7 @@
         by_line(shared_up),
         shared_down,
     )
-    dense = after(dense, gate_swapped, up_swapped, down_swapped)
+    dense = after(dense, pair_swapped)
     kinds = ("column", "all", "all", "all", "all", "line", "line", "plane")
     gathered, all_cot, arrived_grad = gather_all(
         list(zip(kinds, dense)), cot_low, plane_slots, ctx_count, fsdp_count
@@ -1564,14 +1613,12 @@
         full_tail[:, rotary_end + 2].reshape(device_count, dense_rows)[:, :gain_rows]
     ).reshape(LATENT).astype(FULL)
 
-    (up_swapped,) = after((up_swapped,), all_info)
-    up_moved = along_line(up_swapped)
     all_cot = all_cot.reshape(sequence, model_width)
     arrived_grad = arrived_grad.reshape(ctx_count, plane_slots, model_width)
 
     plain_one, inverse_one = norm_forward(source)
     normed = (plain_one * gain_one).astype(LOW)
-    (normed,) = after((normed,), gate_moved)
+    (normed,) = after((normed,), pair_moved)
     (query_raw,) = after((jnp.dot(normed, full_query, preferred_element_type=FULL),))
     query_raw = query_raw.reshape(row_count, HEADS, NOPE + ROPE)
     query_nope = query_raw[:, :, :NOPE].astype(LOW)
@@ -1592,7 +1639,7 @@
     expand_key = expand[:, :, :NOPE]
     expand_value = expand[:, :, NOPE:]
     query_latent = mm("thd,chd->htc", query_nope, expand_key).astype(LOW)
-    (down_swapped,) = after((down_swapped,), up_moved, query_latent)
+    (down_swapped,) = after((down_swapped,), pair_moved, normed)
     down_moved = along_line(down_swapped)
     query_turned = jnp.pad(query_rope.swapaxes(0, 1), ((0, 0),) + pad_rope)
     latent_out, log_total = attend(
@@ -1608,8 +1655,9 @@
     def whole(moved):
         return share_parts(moved, members, fsdp_count).swapaxes(0, 1)
 
-    gate_all = whole(gate_moved).reshape(model_width, hidden_units)
-    up_all = whole(up_moved).reshape(model_width, hidden_units)
+    pair_whole = whole(pair_moved)
+    gate_all = pair_whole[:, :, 0].reshape(model_width, hidden_units)
+    up_all = pair_whole[:, :, 1].reshape(model_width, hidden_units)
     down_all = whole(down_moved).transpose(1, 2, 0, 3).reshape(hidden_units, model_width)
     (second_sent,) = after((second,), down_moved)
     all_second, arrived_rows, hidden_act, gate_back, up_back, arrived_back = run_expert(
@@ -1733,24 +1781,22 @@
     gain_latent_column = jnp.pad(
         gain_latent_grad.reshape(device_count, gain_rows), ((0, 0), (0, dense_rows - gain_rows))
     ).reshape(model_width)
-    tail_grad = jnp.concatenate(
-        [
-            latent_weight_grad,
-            gain_one_grad[:, None],
-            gain_two_grad[:, None],
-            gain_latent_column[:, None],
-            jnp.zeros((model_width, 256 - ROPE - 3), FULL),
-        ],
-        axis=1,
-    )
+    gains_grad = jnp.stack([gain_one_grad, gain_two_grad, gain_latent_column], axis=1)
+    gains_grad = jnp.pad(gains_grad, ((0, 0), (0, 125)))
     (down_sum,) = after((down_sum,), up_returned, query_nope_grad)
     down_returned = along_line(down_sum)
-    dense_grads = after(
-        (query_weight_grad, tail_grad, expand_grad, output_weight_grad, sgate_grad, sup_grad),
-        up_returned,
-    )
-    kinds = ("all",) * 4 + ("line",) * 2
-    query_sum, tail_sum, expand_sum, output_sum, sgate_sum, sup_sum = scatter_all(
+    (gains_grad,) = after((gains_grad,), up_returned)
+    dense_grads = (
+        query_weight_grad,
+        latent_weight_grad,
+        gains_grad,
+        expand_grad,
+        output_weight_grad,
+        sgate_grad,
+        sup_grad,
+    )
+    kinds = ("all",) * 5 + ("line",) * 2
+    query_sum, latent_sum, gains_sum, expand_sum, output_sum, sgate_sum, sup_sum = scatter_all(
         list(zip(kinds, dense_grads)), ctx_count, fsdp_count
     )
 
@@ -1770,13 +1816,13 @@
     return (
         layer_out,
         tokens_grad,
-        tail_sum[:, rotary_end],
+        gains_sum[:, 0],
         query_sum,
-        tail_sum[:, :rotary_end],
-        tail_sum[:gain_rows, rotary_end + 2],
+        latent_sum,
+        gains_sum[:gain_rows, 2],
         expand_sum,
         output_sum,
-        tail_sum[:, rotary_end + 1],
+        gains_sum[:, 1],
         joined(sgate_sum),
         joined(sup_sum),
         sdown_grad,

time: 1360 us -> 1410 us (1.037)
  Pallas kernels: 840 us -> 881 us
  waiting for transfers between devices: 93.2 us -> 58.9 us
  starting transfers between devices: 47.5 us -> 67.3 us
  other arithmetic: 66.8 us -> 86.3 us
    all_to_all x6 -> x5, waiting for transfers between devices: 68 us -> 6.87 us  [along_line(): return lax.all_to_all(array, 'ctx', split_axis=0, concat_axis=0, tiled=True)]
    pallas_call x1, Pallas kernels: 277 us -> 336 us  [gather_arrays(): pl.pallas_call(functools.partial(gather_kernel, ctx_count, kinds), out_sh...]
    all_gather x1, waiting for transfers between devices: 0.01 us -> 42.1 us  [local(): lax.all_gather(jnp.concatenate([latent_norm, jnp.pad(key_rope, pad_rope)]...]
    all_to_all x6 -> x5, starting transfers between devices: 37.4 us -> 59.2 us  [along_line(): return lax.all_to_all(array, 'ctx', split_axis=0, concat_axis=0, tiled=True)]
    pallas_call x1, Pallas kernels: 147 us -> 127 us  [expert_rows(): pl.pallas_call(functools.partial(expert_kernel, ctx_count), out_shape=(lo...]
    slice x3 -> x5, local copies, waits for them, and re-layouts: 2.07 us -> 20.4 us  [the longest x2 16 us: local(): up_all = pair_whole[:, :, 1].reshape(model_width, hidden_units)]
    reduce_scatter x1, waiting for transfers between devices: 21.5 us -> 4.25 us  [local(): lax.psum_scatter(keys_part.reshape(sequence, LATENT + ROPE).astype(LOW),...]
    unnamed x189 -> x168, local copies, waits for them, and re-layouts: 45.6 us -> 38.5 us
  transfers between devices with their start and end apart: 21 -> 18, of which waited for: 4 -> 4; matrix products, arithmetic and copies ran while one was open for 19% -> 20% of each run, Pallas kernels for 36% -> 39%
where the time goes in v6:
time: 1410 us; the launch traced here: 1400 us
  Pallas kernels  881 us (62%)
  local copies, waits for them, and re-layouts  155 us (11%)
  matrix products  137 us (10%)
  other arithmetic  86.3 us (6%)
  starting transfers between devices  67.3 us (5%)
  waiting for transfers between devices  58.9 us (4%)
  between operations  15.4 us (1%)
    pallas_call x1, Pallas kernels, gather_arrays(): pl.pallas_call(functools.partial(gather_kernel, ctx_count, kinds), out_sh...  336 us
    pallas_call x1, Pallas kernels, combine_rows(): pl.pallas_call(functools.partial(combine_kernel, ctx_count), out_shape=(j...  203 us
    pallas_call x1, Pallas kernels, scatter_arrays(): pl.pallas_call(functools.partial(scatter_kernel, ctx_count, kinds), out_s...  153 us
    pallas_call x1, Pallas kernels, expert_rows(): pl.pallas_call(functools.partial(expert_kernel, ctx_count), out_shape=(lo...  127 us
    dot_general x18, matrix products, mm(): return jnp.einsum(subscripts, left, right, preferred_element_type=FULL)  86 us
    all_to_all x5, starting transfers between devices, along_line(): return lax.all_to_all(array, 'ctx', split_axis=0, concat_axis=0, tiled=True)  59.2 us
    all_gather x1, waiting for transfers between devices, local(): lax.all_gather(jnp.concatenate([latent_norm, jnp.pad(key_rope, pad_rope)]...  42.1 us
    unnamed x168, local copies, waits for them, and re-layouts  38.5 us
  transfers between devices with their start and end apart: 18, of which 4 were waited for; matrix products, arithmetic and copies ran while one was open for 20% of the time, Pallas kernels for 39%

profile of v6, /device:TPU:1, one launch (start us, length us, event | category | flops | bytes accessed | tf_op | source)
XLA Modules:
  0.0 1400.9 jit_solution(15382819880267361567)
XLA Ops:
  23.1 5.7 all-to-all-start
  40.7 336.5 %shard_map.280 = (f32[4,24,256]{2,1,0:T(8,128)}, bf16[4,8,64,3072]{3,2,1,0:T(8,128)(2,1)}, bf16[4,8,64,768]{3,2,1,0:T(8,128)(2,1)}, bf16[4,8,16,4096]{3,2,1,0:T(...) custom-call(f32[24,256]{1,0:T(8,128)} %copy-done.47, ...), custom_call_target="tpu_custom_call" | custom-call | flops 2000000000 | bytes 800000000 | tf_op jit(solution)/shard_map/pallas_call | solution.py:877
  389.0 8.2 fusion.80
  400.1 37.7 %all-to-all-start.1 = ((bf16[4,704,512]{2,1,0:T(8,128)(2,1)}), bf16[4,704,512]{2,1,0:T(8,128)(2,1)}, u32[]{:S(2)}, u32[]{:S(2)}) async-start(bf16[4,704,512]{2,1,0:T(8,128)(2,1)} %bitcast.41), calls=%async_computation.1 | async-start | bytes 5767168 | tf_op jit(solution)/shard_map/all_to_all | solution.py:1497
  440.2 9.7 fusion.79
  468.1 42.1 %all-gather.3.cloned.1.call-done = bf16[1024,640]{0,1:T(8,128)(2,1)} async-done(((bf16[256,640]{0,1:T(8,128)(2,1)}), bf16[1024,640]{0,1:T(8,128)(2,1)}) %all-gather.3.cloned.1.call-update) | async-done | bytes 1310736 | tf_op jit(solution)/shard_map/all_gather | solution.py:1632
  522.8 29.2 %shard_map.281 = (bf16[16,256,512]{2,1,0:T(8,128)(2,1)}, f32[16,256,1]{2,1,0:T(8,128)}) custom-call(bf16[16,256,512]{2,1,0:T(8,128)(2,1)} %convolution_convert_fusion.9.query_ref, bf16[16,256,128]{2,1,0:T(8,128)(2,1)} %pad.28.turned_ref, bf16[1024,512]{1,0:T(8,128)(2,1)} %slice.213.keys_ref, bf16[1024,128]{1,0:T(8,128)(2,1)} %slice.214.rope_ref), custom_call_target="tpu_custom_call" | custom-call | flops 12000000000 | bytes 12000000 | tf_op jit(solution)/shard_map/pallas_call | solution.py:543
  555.8 6.2 multiply_reduce_fusion.2
  565.1 9.8 select_bitcast_fusion.1
  574.9 10.0 maximum_bitcast_fusion
  584.8 10.1 fusion.75
  594.9 5.9 copy.273
  606.5 7.0 copy.274
  613.5 7.7 copy.315
  621.2 126.8 %shard_map.282 = (bf16[4,256,2048]{2,1,0:T(8,128)(2,1)}, bf16[4,8,64,2048]{3,2,1,0:T(8,128)(2,1)}, bf16[4,512,1408]{2,1,0:T(8,128)(2,1)}, bf16[4,512,1408]{2,1,0...) custom-call(bf16[256,2048]{1,0:T(8,128)(2,1)} %multiply_convert_fusion.3.rows_ref, ...), custom_call_target="tpu_custom_call" | custom-call | flops 60000002048 | bytes 400000000 | tf_op jit(solution)/shard_map/pallas_call | solution.py:1050
  748.0 18.5 %convolution_convert_fusion.2 = bf16[2048,2048]{1,0:T(8,128)(2,1)} fusion(bf16[2048,1408]{1,0:T(8,128)(2,1)} %bitcast.364, bf16[1408,2048]{1,0:T(8,128)(2,1)} %bitcast.328), kind=kOutput, calls=%fused_computation.4 | convolution fusion | flops 11815354368 | bytes 19922944 | tf_op jit(solution)/shard_map/dot_general | solution.py:1683
  769.9 5.6 multiply_convert_fusion
  775.5 5.9 fusion.82
  791.6 203.0 %shard_map.283 = (f32[256,2048]{1,0:T(8,128)}, f32[256,2048]{1,0:T(8,128)}, bf16[2048,1408]{1,0:T(8,128)(2,1)}, bf16[2048,1408]{1,0:T(8,128)(2,1)}, bf16[2048,1408]{1,0:T(8,128)(2,1)}) custom-call(f32[4,24,256]{2,1,0:T(8,128)} %get-tuple-element.120.info_ref, bf16[4,8,64,2048]{3,2,1,0:T(8,128)(2,1)} %bitcast.362, bf16[4,256,2048]{2,1,0:T(8,128)(2,1)} %bitcast.374, ...), custom_call_target="tpu_custom_call" | custom-call | flops 40000000000 | bytes 600000000 | tf_op jit(solution)/shard_map/pallas_call | solution.py:1323
  1007.7 6.3 all-to-all-start.2
  1014.4 6.7 convolution_convert_fusion.6
  1021.1 5.8 convolution_convert_fusion.4
  1029.8 7.8 convolution_convert_fusion.5
  1068.0 5.6 convolution_convert_fusion.1
  1073.7 6.9 all-to-all-done.2
  1088.3 32.2 %shard_map.284 = (bf16[16,256,512]{2,1,0:T(8,128)(2,1)}, f32[16,256,128]{2,1,0:T(8,128)}, f32[1024,512]{1,0:T(8,128)}, f32[1024,128]{1,0:T(8,128)}) custom-call(bf16[16,256,512]{2,1,0:T(8,128)(2,1)} %convolution_convert_fusion.9.query_ref, bf16[16,256,128]{2,1,0:T(8,128)(2,1)} %pad.28.turned_ref, bf16[1024,512]{1,0:T(8,128)(2,1)} %slice.213.keys_ref, ...), custom_call_target="tpu_custom_call" | custom-call | flops 30000001024 | bytes 30000000 | tf_op jit(solution)/shard_map/pallas_call | solution.py:569
  1138.0 7.9 copy.286
  1145.9 7.4 convert_element_type.307.refs_3_
  1187.6 6.7 fusion.83
  1197.8 6.5 convolution_convert_fusion
  1211.7 153.5 %shard_map.285 = (f32[64,3072]{1,0:T(8,128)}, f32[64,576]{1,0:T(8,128)}, f32[64,128]{1,0:T(8,128)}, f32[16,4096]{1,0:T(8,128)}, f32[64,2048]{1,0:T(8,128)}, /*in...) custom-call(bf16[4,4,2,64,3072]{4,3,2,1,0:T(8,128)(2,1)} %bitcast.293, bf16[4,4,2,64,576]{4,3,2,1,0:T(8,128)(2,1)} %bitcast.310, ...), custom_call_target="tpu_custom_call" | custom-call | bytes 500000000 | tf_op jit(solution)/shard_map/pallas_call | solution.py:391
  1384.5 6.4 copy.294
  (335 shorter events, 240.7 us)
Async XLA Ops:
  12.0 5.6 collective-permute-start
  23.1 374.2 %all-to-all-start = ((bf16[4,2,256,1408]{3,2,1,0:T(8,128)(2,1)}), bf16[4,2,256,1408]{3,2,1,0:T(8,128)(2,1)}, u32[]{:S(2)}, u32[]{:S(2)}) async-start(bf16[4,2,256,1408]{3,2,1,0:T(8,128)(2,1)} %bitcast.295), calls=%async_computation | async-start | bytes 11534336 | tf_op jit(solution)/shard_map/all_to_all | solution.py:1497
  30.4 6.4 collective-permute-start.1
  35.5 402.8 %copy-start.59 = (f32[32]{0:T(128)}, f32[32]{0:T(128)S(1)}, u32[]{:S(2)}) copy-start(f32[32]{0:T(128)S(1)} %multiply_power_fusion) | copy-start | bytes 388
  35.5 402.8 %copy-start.56 = (f32[256]{0:T(256)}, f32[256]{0:T(256)S(1)}, u32[]{:S(2)}) copy-start(f32[256]{0:T(256)S(1)} %fusion.72) | copy-start | bytes 3076
  35.9 352.8 %copy-start.53 = (f32[256]{0:T(256)}, f32[256]{0:T(256)S(1)}, u32[]{:S(2)}) copy-start(f32[256]{0:T(256)S(1)} %add_rsqrt_fusion.2) | copy-start | bytes 3076
  388.2 173.9 %copy-start.37 = (f32[2048,1]{0,1:T(1,128)}, f32[2048,1]{0,1:T(1,128)S(1)}, u32[]{:S(2)}) copy-start(f32[2048,1]{0,1:T(1,128)S(1)} %copy.317) | copy-start | bytes 24580
  388.3 50.5 %copy-start.44 = (f32[512]{0:T(512)}, f32[512]{0:T(512)S(1)}, u32[]{:S(2)}) copy-start(f32[512]{0:T(512)S(1)} %reshape.518) | copy-start | bytes 6148
  389.0 51.2 %copy-start.16 = (bf16[256,2048]{1,0:T(8,128)(2,1)}, bf16[256,2048]{1,0:T(8,128)(2,1)S(1)}, u32[]{:S(2)}) copy-start(bf16[256,2048]{1,0:T(8,128)(2,1)S(1)} %fusion.15) | copy-start | bytes 3145732
  400.1 38.7 %copy-start.20 = (f32[256,576]{0,1:T(8,128)}, f32[256,576]{0,1:T(8,128)S(1)}, u32[]{:S(2)}) copy-start(f32[256,576]{0,1:T(8,128)S(1)} %fusion.13) | copy-start | bytes 1769476
  400.1 164.5 %all-to-all-start.1 = ((bf16[4,704,512]{2,1,0:T(8,128)(2,1)}), bf16[4,704,512]{2,1,0:T(8,128)(2,1)}, u32[]{:S(2)}, u32[]{:S(2)}) async-start(bf16[4,704,512]{2,1,0:T(8,128)(2,1)} %bitcast.41), calls=%async_computation.1 | async-start | bytes 5767168 | tf_op jit(solution)/shard_map/all_to_all | solution.py:1497
  437.8 72.4 %all-gather.3.cloned.1.call-start = ((), (), s32[]{:S(2)}) async-start(), calls=%async_computation.9 | async-start | bytes 1638400 | tf_op jit(solution)/shard_map/all_gather | solution.py:1632
  438.7 21.0 %copy-start.26 = (f32[256,32]{1,0:T(8,128)}, f32[256,32]{1,0:T(8,128)S(1)}, u32[]{:S(2)}) copy-start(f32[256,32]{1,0:T(8,128)S(1)} %copy.265) | copy-start | bytes 98308
  439.7 125.4 %collective-permute-start.2 = (bf16[4,2,256,1408]{3,2,1,0:T(8,128)(2,1)}, bf16[4,2,256,1408]{3,2,1,0:T(8,128)(2,1)}, u32[]{:S(2)}, u32[]{:S(2)}) collective-permute-start(bf16[4,2,256,1408]{3,2,1,0:T(8,128)(2,1)} %all-to-all-done), channel_id=1, source_target_pairs={{0,1},{1,0},{2,3},{3,2},{4,5},{5,4},{6,7},{7,6},{8,9},{9,8},{10,11... | collective-permute-start | bytes 17301512 | tf_op jit(solution)/shard_map/ppermute | solution.py:1386
  452.3 12.1 copy-start.3
  522.8 29.2 %copy-start.7 = (bf16[512,16,128]{0,2,1:T(8,128)(2,1)S(1)}, bf16[512,16,128]{0,2,1:T(8,128)(2,1)}, u32[]{:S(2)}) copy-start(bf16[512,16,128]{0,2,1:T(8,128)(2,1)} %copy.300) | copy-start | bytes 6291460
  564.6 39.2 %collective-permute-start.3 = (bf16[4,704,512]{2,1,0:T(8,128)(2,1)}, bf16[4,704,512]{2,1,0:T(8,128)(2,1)S(1)}, u32[]{:S(2)}, u32[]{:S(2)}) collective-permute-start(bf16[4,704,512]{2,1,0:T(8,128)(2,1)} %all-to-all-done.1), channel_id=1, source_target_pairs={{0,1},{1,0},{2,3},{3,2},{4,5},{5,4},{6,7},{7,6},{8,9},{9,8},{10,11... | collective-permute-start | bytes 8650760 | tf_op jit(solution)/shard_map/ppermute | solution.py:1386
  748.0 18.6 %copy-start.64 = (bf16[4,256,2048]{2,1,0:T(8,128)(2,1)S(1)}, bf16[4,256,2048]{2,1,0:T(8,128)(2,1)}, u32[]{:S(2)}) copy-start(bf16[4,256,2048]{2,1,0:T(8,128)(2,1)} %get-tuple-element.127) | copy-start | bytes 12582916
  748.0 18.6 %copy-start.66 = (bf16[4,8,64,704]{3,2,1,0:T(8,128)(2,1)S(1)}, bf16[4,8,64,704]{3,2,1,0:T(8,128)(2,1)}, u32[]{:S(2)}) copy-start(bf16[4,8,64,704]{3,2,1,0:T(8,128)(2,1)} %get-tuple-element.129) | copy-start | bytes 8650756
  996.8 8.0 collective-permute-start.4
  999.9 42.4 %collective-permute-start.6 = (bf16[4,256,1408]{2,1,0:T(8,128)(2,1)}, bf16[4,256,1408]{2,1,0:T(8,128)(2,1)}, u32[]{:S(2)}, u32[]{:S(2)}) collective-permute-start(bf16[4,256,1408]{2,1,0:T(8,128)(2,1)} %dynamic-slice_bitcast_fusion), channel_id=1, source_target_pairs={{0,1},{1,0},{2,3},{3,2},{4,5},{5,4},{6,7},{7,6},{8,9},{9,8},{10,11... | collective-permute-start | bytes 8650760 | tf_op jit(solution)/shard_map/ppermute | solution.py:1396
  1003.6 44.2 %collective-permute-start.5 = (bf16[4,256,1408]{2,1,0:T(8,128)(2,1)}, bf16[4,256,1408]{2,1,0:T(8,128)(2,1)}, u32[]{:S(2)}, u32[]{:S(2)}) collective-permute-start(bf16[4,256,1408]{2,1,0:T(8,128)(2,1)} %dynamic-slice_bitcast_fusion.1), channel_id=1, source_target_pairs={{0,1},{1,0},{2,3},{3,2},{4,5},{5,4},{6,7},{7,6},{8,9},{9,8},{10,11... | collective-permute-start | bytes 8650760 | tf_op jit(solution)/shard_map/ppermute | solution.py:1396
  1007.7 72.8 %all-to-all-start.2 = ((bf16[4,256,1408]{2,1,0:T(8,128)(2,1)}), bf16[4,256,1408]{2,1,0:T(8,128)(2,1)}, u32[]{:S(2)}, u32[]{:S(2)}) async-start(bf16[4,256,1408]{2,1,0:T(8,128)(2,1)} %fusion.2), calls=%async_computation.2 | async-start | bytes 5767168 | tf_op jit(solution)/shard_map/all_to_all | solution.py:1497
  1014.0 139.3 %reduce-scatter.5.cloned.1.call-start = ((), (), s32[]{:S(2)}) async-start(), calls=%async_computation.8 | async-start | bytes 3244032 | tf_op jit(solution)/shard_map/reduce_scatter | solution.py:1718
  1055.0 13.0 copy-start.5
  1083.1 78.7 %collective-permute-start.7 = (bf16[2,256,1408]{2,1,0:T(8,128)(2,1)}, bf16[2,256,1408]{2,1,0:T(8,128)(2,1)}, u32[]{:S(2)}, u32[]{:S(2)}) collective-permute-start(bf16[2,256,1408]{2,1,0:T(8,128)(2,1)} %dynamic-slice_bitcast_fusion.5), channel_id=1, source_target_pairs={{0,1},{1,0},{2,3},{3,2},{4,5},{5,4},{6,7},{7,6},{8,9},{9,8},{10,11... | collective-permute-start | bytes 4325384 | tf_op jit(solution)/shard_map/ppermute | solution.py:1375
  1083.6 99.1 %all-to-all-start.3 = ((bf16[4,256,1408]{2,1,0:T(8,128)(2,1)}), bf16[4,256,1408]{2,1,0:T(8,128)(2,1)}, u32[]{:S(2)}, u32[]{:S(2)}) async-start(bf16[4,256,1408]{2,1,0:T(8,128)(2,1)} %fusion.1), calls=%async_computation.4 | async-start | bytes 5767168 | tf_op jit(solution)/shard_map/all_to_all | solution.py:1497
  1088.3 82.8 %reduce-scatter.3.cloned.1.call-start = ((), (), s32[]{:S(2)}) async-start(), calls=%async_computation.7 | async-start | bytes 1474560 | tf_op jit(solution)/shard_map/reduce_scatter | solution.py:1746
  1163.9 11.4 copy-start.27
  1182.7 185.5 %all-to-all-start.4 = ((bf16[4,256,1408]{2,1,0:T(8,128)(2,1)}), bf16[4,256,1408]{2,1,0:T(8,128)(2,1)}, u32[]{:S(2)}, u32[]{:S(2)}) async-start(bf16[4,256,1408]{2,1,0:T(8,128)(2,1)} %fusion), calls=%async_computation.6 | async-start | bytes 5767168 | tf_op jit(solution)/shard_map/all_to_all | solution.py:1497
  1206.9 166.9 %collective-permute-start.8 = (bf16[2,256,1408]{2,1,0:T(8,128)(2,1)}, bf16[2,256,1408]{2,1,0:T(8,128)(2,1)}, u32[]{:S(2)}, u32[]{:S(2)}) collective-permute-start(bf16[2,256,1408]{2,1,0:T(8,128)(2,1)} %dynamic-slice_bitcast_fusion.4), channel_id=1, source_target_pairs={{0,1},{1,0},{2,3},{3,2},{4,5},{5,4},{6,7},{7,6},{8,9},{9,8},{10,11... | collective-permute-start | bytes 4325384 | tf_op jit(solution)/shard_map/ppermute | solution.py:1375
  1369.7 9.5 collective-permute-start.9
  (62 other events, 311.2 us)
Sparse Core Ops, SparseCore 0:
  440.7 69.3 all-gather.2
  1021.2 46.2 reduce-scatter.4
  1132.6 38.4 reduce-scatter.2

commit v7 on v6

--- a/solution.py
+++ b/solution.py
@@ -152,7 +152,8 @@
     if whole_line:
         for step in range(1, ctx_count):
             hello(lax.rem(z + step, ctx_count), f)
-        pl.semaphore_wait(barrier, len(masks) + ctx_count - 1)
+            hello(lax.rem(z + step, ctx_count), flip(f, 1))
+        pl.semaphore_wait(barrier, len(masks) + 2 * (ctx_count - 1))
         return
 
     @pl.when(z > 0)
@@ -723,7 +724,39 @@
         return 0 if kinds[item] == "plane" else nearest(z, step)
 
     def steps(item, step):
+        if kinds[item] == "expert":
+            return False
         return step == 0 if kinds[item] == "plane" else 0 <= step < ctx_count
+
+    side = lax.rem(f, 2)
+
+    def expert_pieces(item, act):
+        half = shards[item].shape[1] // 2
+        for which in range(2):
+            for part in range(2):
+                source = shards[item].at[which, pl.ds(part * half, half)]
+                target = outs[item].at[z]
+                to_z = 2 * side + which
+                here = (to_z == z) & (side == part)
+
+                @pl.when(here)
+                def _():
+                    act(pltpu.make_async_copy(source, target, own_sem.at[item]), True)
+
+                @pl.when(jnp.logical_not(here))
+                def _():
+                    sems = (z_send.at[item, 2 * which + part, 0], z_recv.at[item, z])
+                    act(remote(source, target, *sems, to_z, f - side + part), False)
+
+    def expert_arrived(item):
+        for origin in range(ctx_count):
+            at = outs[item].at[origin]
+            mine = (origin == z) & (lax.div(z, 2) == side)
+
+            @pl.when(jnp.logical_not(mine))
+            def _():
+                sems = (z_send.at[item, 0, 0], z_recv.at[item, origin])
+                remote(at, at, *sems, z, core).wait_recv()
 
     def z_view(item, block):
         return outs[item].at[block] if kinds[item] == "column" else outs[item].at[block, f]
@@ -818,7 +851,10 @@
         p_arrived(item, block, 3)
         c_copy(item, block, 3).start()
 
+    experts = [item for item in range(count) if kinds[item] == "expert"]
     for item in range(count):
+        if kinds[item] == "expert":
+            continue
         own(item).start()
         if kinds[item] == "line":
             for step in range(1, ctx_count):
@@ -827,6 +863,9 @@
     for step in range(ctx_count + 2):
         if step < ctx_count:
             along_order(z, ctx_count, step, take)
+        if step in (1, 3):
+            for item in experts[step // 2 :: 2]:
+                expert_pieces(item, lambda copy, local: copy.start())
         for lag, stage in ((0, first), (1, second), (2, third)):
             for item in range(count):
                 if steps(item, step - lag) and kinds[item] != "column":
@@ -836,6 +875,9 @@
     for step in range(ctx_count):
         move.await_slots(nearest(z, step))
     move.finish()
+    for item in experts:
+        expert_arrived(item)
+        expert_pieces(item, lambda copy, local: copy.wait() if local else copy.wait_send())
     for item in range(count):
         for step in range(ctx_count):
             if not steps(item, step):
@@ -864,7 +906,10 @@
         "column": (ctx_count,),
     }
     shapes = [
-        lead[kind] + (shard.shape[1:] if kind == "line" else shard.shape) for kind, shard in items
+        (ctx_count, shard.shape[1] // 2, shard.shape[2])
+        if kind == "expert"
+        else lead[kind] + (shard.shape[1:] if kind == "line" else shard.shape)
+        for kind, shard in items
     ]
     row_count, width = rows.shape
     share = slots // fsdp_count
@@ -918,12 +963,14 @@
         act(pl.ds(whole * size, rest))
 
 
-def expert_kernel(ctx_count, rows_ref, info_ref, gate_ref, up_ref, down_ref, grads_ref, *refs):
-    all_ref, slots_ref, hidden_ref, gate_back_ref, up_back_ref, back_ref = refs[:6]
-    blocks, chosen, arrived, gate, up, down, grads, hidden, gate_back, up_back, back = refs[6:17]
-    weight_sem, grad_sem, slot_sem, side_sem, back_sem = refs[17:22]
+def expert_kernel(ctx_count, rows_ref, info_ref, *refs):
+    weight_refs, grads_ref = (refs[0:2], refs[2:4], refs[4:6]), refs[6]
+    all_ref, slots_ref, hidden_ref, gate_back_ref, up_back_ref, back_ref, result_ref = refs[7:14]
+    blocks, chosen, arrived, gate, up, down, grads = refs[14:21]
+    hidden, gate_back, up_back, back, result = refs[21:26]
+    weight_sem, grad_sem, slot_sem, side_sem, back_sem = refs[26:31]
     move = Dispatch(
-        ctx_count, False, rows_ref, info_ref, all_ref, blocks, chosen, arrived, refs[22:]
+        ctx_count, False, rows_ref, info_ref, all_ref, blocks, chosen, arrived, refs[31:]
     )
     slots, width = back.shape
     units = hidden.shape[1]
@@ -935,10 +982,21 @@
             block = jnp.where(step == place, order[place], block)
         return block
 
-    loads = [
-        pltpu.make_async_copy(source, target, weight_sem.at[place])
-        for place, (source, target) in enumerate(((gate_ref, gate), (up_ref, up), (down_ref, down)))
-    ]
+    loads = []
+    for which, target in enumerate((gate, up, down)):
+        for place, source in enumerate(weight_refs[which]):
+            side = lax.rem(move.f, 2)
+            member = 1 - side if place else side
+            half, piece_width = source.shape[1:]
+            for origin in range(ctx_count):
+                if which < 2:
+                    start = pl.multiple_of((2 * origin + member) * half, half)
+                    at = target.at[pl.ds(start, half)]
+                else:
+                    start = pl.multiple_of(member * half, half)
+                    at = target.at[pl.ds(start, half), pl.ds(origin * piece_width, piece_width)]
+                sem = weight_sem.at[which, place, origin]
+                loads.append(pltpu.make_async_copy(source.at[origin], at, sem))
 
     def load_grads(step):
         slot = lax.rem(step, 2)
@@ -958,7 +1016,10 @@
         ]
 
     def store_back(block):
-        return pltpu.make_async_copy(back, back_ref.at[block], back_sem)
+        return pltpu.make_async_copy(back, back_ref.at[block], back_sem.at[0])
+
+    def store_result(block):
+        return pltpu.make_async_copy(result, result_ref.at[block], back_sem.at[1])
 
     greet(move.z, move.f, PEERS, ctx_count)
     move.begin()
@@ -1011,6 +1072,14 @@
         @pl.when(step > 0)
         def _():
             store_back(block).wait()
+            store_result(block).wait()
+
+        def result_tile(part):
+            total = jnp.dot(hidden[...], down[:, part], preferred_element_type=FULL)
+            result[:, part] = total.astype(LOW)
+
+        each_tile(width, result_tile)
+        store_result(block).start()
 
         def back_tile(part):
             total = dot_last(gate_back[...], gate[part, :]) + dot_last(up_back[...], up[part, :])
@@ -1034,14 +1103,15 @@
     for copy in store_sides(order[-1]):
         copy.wait()
     store_back(order[-1]).wait()
+    store_result(order[-1]).wait()
     move.finish()
 
 
-def expert_rows(rows, info, gate, up, down, grads, ctx_count, fsdp_count):
+def expert_rows(rows, info, weights, grads, ctx_count, fsdp_count):
     count, width = rows.shape
     slots = grads.shape[1]
     share = slots // fsdp_count
-    units = gate.shape[1]
+    units = weights[0].shape[2]
     buffers, sems = dispatch_scratch(ctx_count, fsdp_count, count, share, width)
     dma = pltpu.SemaphoreType.DMA
     anywhere = pl.BlockSpec(memory_space=pl.ANY)
@@ -1056,9 +1126,10 @@
             low(slots, units),
             low(slots, units),
             low(slots, width),
+            low(slots, width),
         ),
-        in_specs=[anywhere, pl.BlockSpec(memory_space=pltpu.VMEM)] + [anywhere] * 4,
-        out_specs=(anywhere,) * 6,
+        in_specs=[anywhere, pl.BlockSpec(memory_space=pltpu.VMEM)] + [anywhere] * 7,
+        out_specs=(anywhere,) * 7,
         scratch_shapes=buffers
         + [
             vmem(ctx_count, fsdp_count, share, width),
@@ -1070,11 +1141,12 @@
             vmem(slots, units),
             vmem(slots, units),
             vmem(slots, width),
-            dma((3,)),
+            vmem(slots, width),
+            dma((3, 2, ctx_count)),
             dma((2,)),
             dma((ctx_count,)),
             dma((3,)),
-            dma,
+            dma((2,)),
         ]
         + sems,
         compiler_params=pltpu.CompilerParams(
@@ -1083,7 +1155,7 @@
         cost_estimate=pl.CostEstimate(
             flops=60_000_000_000, bytes_accessed=400_000_000, transcendentals=3_000_000
         ),
-    )(rows, info, gate, up, down, grads)
+    )(rows, info, *weights, grads)
 
 
 class Combine:
@@ -1419,9 +1491,18 @@
     return every, swap_slots(chosen.reshape(ctx_count, fsdp_count, -1, rows.shape[1]))
 
 
-def run_expert(rows, info, gate, up, down, grads, ctx_count, fsdp_count):
+def run_expert(rows, info, pieces, grads, ctx_count, fsdp_count):
+    members = ctx_count // EXP_DEV
     if (ctx_count, fsdp_count) == (4, 8):
-        return expert_rows(rows, info, gate, up, down, grads, ctx_count, fsdp_count)
+        pairs = member_pairs(fsdp_count, members, 1)
+        weights = []
+        for piece in pieces:
+            weights += [piece, lax.ppermute(piece, "fsdp", pairs)]
+        return expert_rows(rows, info, weights, grads, ctx_count, fsdp_count)
+    whole = [share_parts(piece, members, fsdp_count).swapaxes(0, 1) for piece in pieces]
+    units = whole[0].shape[3]
+    gate, up = [item.reshape(-1, units) for item in whole[:2]]
+    down = whole[2].transpose(1, 2, 0, 3).reshape(units, -1)
     every, arrived = send_rows(rows, info, grads.shape[1], False, ctx_count, fsdp_count)
     slots = arrived.reshape(grads.shape)
     pre = mm("bsd,df->bsf", slots, gate)
@@ -1432,7 +1513,8 @@
     up_back = (grad * act).astype(LOW)
     gate_back = (grad * linear * slope).astype(LOW)
     back = (mm("bsf,df->bsd", gate_back, gate) + mm("bsf,df->bsd", up_back, up)).astype(LOW)
-    return every, arrived, hidden, gate_back, up_back, back
+    result = mm("bsf,fd->bsd", hidden, down).astype(LOW)
+    return every, arrived, hidden, gate_back, up_back, back, result
 
 
 def return_slots(slots, info, extra, gated):
@@ -1458,6 +1540,12 @@
     )
 
 
+def swap_experts(weight, members, fsdp_count):
+    pieces = weight.reshape((EXP_DEV, members, weight.shape[1] // members) + weight.shape[2:])
+    pieces = swap_parts(pieces.swapaxes(0, 1), members, fsdp_count)
+    return pieces.reshape((-1,) + pieces.shape[2:])
+
+
 def gather_all(items, rows, slots, ctx_count, fsdp_count):
     if (ctx_count, fsdp_count) == (4, 8):
         return gather_arrays(items, rows, slots, ctx_count, fsdp_count)
@@ -1470,6 +1558,8 @@
             result = lax.all_gather(shard, "fsdp", axis=0)[None]
         elif kind == "column":
             result = lax.all_gather(shard, "ctx", axis=0)
+        elif kind == "expert":
+            result = along_line(swap_experts(shard, ctx_count // EXP_DEV, fsdp_count))
         else:
             result = lax.all_gather(shard, ("ctx", "fsdp"), axis=0)
             result = result.reshape((ctx_count, fsdp_count) + shard.shape)
@@ -1547,18 +1637,7 @@
     hidden_units = expert_gate.shape[2]
     shared_units = shared_gate.shape[1] // ctx_count
 
-    def by_part(weight):
-        return weight.reshape(
-            (EXP_DEV, members, weight.shape[1] // members) + weight.shape[2:]
-        ).swapaxes(0, 1)
-
-    def swapped(pieces):
-        pieces = swap_parts(pieces, members, fsdp_count)
-        return pieces.reshape((ctx_count,) + pieces.shape[2:])
-
-    pair_swapped = swapped(jnp.stack([by_part(expert_gate), by_part(expert_up)], axis=2))
-    down_swapped = swapped(by_part(expert_down))
-    pair_moved = along_line(pair_swapped)
+    down_swapped = swap_experts(expert_down, members, fsdp_count)
 
     local_routes = routes[0]
     expert_index = jnp.arange(experts_total, dtype=jnp.int32)
@@ -1596,16 +1675,18 @@
         by_line(shared_gate),
         by_line(shared_up),
         shared_down,
-    )
-    dense = after(dense, pair_swapped)
-    kinds = ("column", "all", "all", "all", "all", "line", "line", "plane")
+        expert_gate,
+        expert_up,
+    )
+    kinds = ("column", "all", "all", "all", "all", "line", "line", "plane", "expert", "expert")
     gathered, all_cot, arrived_grad = gather_all(
         list(zip(kinds, dense)), cot_low, plane_slots, ctx_count, fsdp_count
     )
     all_info = gathered[0]
     full_query, full_tail, full_expand, full_output, full_sgate, full_sup, full_sdown = [
-        item.reshape(-1, item.shape[-1]) for item in gathered[1:]
+        item.reshape(-1, item.shape[-1]) for item in gathered[1:-2]
     ]
+    gate_moved, up_moved = gathered[-2:]
     full_latent = full_tail[:, :rotary_end]
     gain_one = full_tail[:, rotary_end].astype(FULL)
     gain_two = full_tail[:, rotary_end + 1].astype(FULL)
@@ -1618,7 +1699,6 @@
 
     plain_one, inverse_one = norm_forward(source)
     normed = (plain_one * gain_one).astype(LOW)
-    (normed,) = after((normed,), pair_moved)
     (query_raw,) = after((jnp.dot(normed, full_query, preferred_element_type=FULL),))
     query_raw = query_raw.reshape(row_count, HEADS, NOPE + ROPE)
     query_nope = query_raw[:, :, :NOPE].astype(LOW)
@@ -1639,7 +1719,7 @@
     expand_key = expand[:, :, :NOPE]
     expand_value = expand[:, :, NOPE:]
     query_latent = mm("thd,chd->htc", query_nope, expand_key).astype(LOW)
-    (down_swapped,) = after((down_swapped,), pair_moved, normed)
+    (down_swapped,) = after((down_swapped,), normed)
     down_moved = along_line(down_swapped)
     query_turned = jnp.pad(query_rope.swapaxes(0, 1), ((0, 0),) + pad_rope)
     latent_out, log_total = attend(
@@ -1652,16 +1732,15 @@
     plain_two, inverse_two = norm_forward(middle)
     second = (plain_two * gain_two).astype(LOW)
 
-    def whole(moved):
-        return share_parts(moved, members, fsdp_count).swapaxes(0, 1)
-
-    pair_whole = whole(pair_moved)
-    gate_all = pair_whole[:, :, 0].reshape(model_width, hidden_units)
-    up_all = pair_whole[:, :, 1].reshape(model_width, hidden_units)
-    down_all = whole(down_moved).transpose(1, 2, 0, 3).reshape(hidden_units, model_width)
+    (down_moved,) = after((down_moved,), latent_out)
     (second_sent,) = after((second,), down_moved)
-    all_second, arrived_rows, hidden_act, gate_back, up_back, arrived_back = run_expert(
-        second_sent, all_info, gate_all, up_all, down_all, arrived_grad, ctx_count, fsdp_count
+    all_second, arrived_rows, hidden_act, gate_back, up_back, arrived_back, result = run_expert(
+        second_sent,
+        all_info,
+        (gate_moved, up_moved, down_moved),
+        arrived_grad,
+        ctx_count,
+        fsdp_count,
     )
     all_second = all_second.reshape(sequence, model_width)
     hidden_act, gate_back, up_back = [
@@ -1680,7 +1759,6 @@
     slots_shape = (ctx_count, fsdp_count, share, model_width)
     rows_shape = (ctx_count, row_count, model_width)
     shared_out = jnp.dot(shared_hidden, full_sdown, preferred_element_type=FULL)
-    result = jnp.dot(hidden_act, down_all, preferred_element_type=FULL).astype(LOW)
     second_grad, out_sum, gate_grad, up_grad, down_grad = return_both(
         arrived_back.reshape(slots_shape),
         shared_second_grad.reshape(rows_shape),

time: 1410 us -> 1260 us (0.89)
  starting transfers between devices: 67.3 us -> 28.9 us
  waiting for transfers between devices: 58.9 us -> 22.3 us
  local copies, waits for them, and re-layouts: 155 us -> 127 us
  other arithmetic: 86.3 us -> 58.4 us
  matrix products: 137 us -> 115 us
    all_to_all x5 -> x4, starting transfers between devices: 59.2 us -> 20.7 us  [along_line(): return lax.all_to_all(array, 'ctx', split_axis=0, concat_axis=0, tiled=True)]
    pallas_call x1, Pallas kernels: 336 us -> 303 us  [gather_arrays(): pl.pallas_call(functools.partial(gather_kernel, ctx_count, kinds), out_sh...]
    all_gather x1, waiting for transfers between devices: 42.1 us -> 10.8 us  [local(): lax.all_gather(jnp.concatenate([latent_norm, jnp.pad(key_rope, pad_rope)]...]
    pallas_call x1, Pallas kernels: 127 us -> 154 us  [expert_rows(): pl.pallas_call(functools.partial(expert_kernel, ctx_count), out_shape=(lo...]
    slice x3 -> x0, local copies, waits for them, and re-layouts: 19 us -> none  [the longest x2 16 us: local(): up_all = pair_whole[:, :, 1].reshape(model_width, hidden_units)]
    dot_general x1 -> x0, matrix products: 18.5 us -> none  [local(): jnp.dot(hidden_act, down_all, preferred_element_type=FULL).astype(LOW)]
    another operation x9 -> x5, other arithmetic: 27.4 us -> 9.98 us  [by_member(): jnp.stack([jnp.where(first, own, others[0]), jnp.where(first, others[0],...]
    unnamed x168 -> x181, local copies, waits for them, and re-layouts: 38.5 us -> 34.3 us
  transfers between devices with their start and end apart: 18 -> 17, of which waited for: 4 -> 3; matrix products, arithmetic and copies ran while one was open for 20% -> 20% of each run, Pallas kernels for 39% -> 42%
where the time goes in v7:
time: 1260 us; the launch traced here: 1240 us
  Pallas kernels  878 us (70%)
  local copies, waits for them, and re-layouts  127 us (10%)
  matrix products  115 us (9%)
  other arithmetic  58.4 us (5%)
  starting transfers between devices  28.9 us (2%)
  waiting for transfers between devices  22.3 us (2%)
  between operations  15.5 us (1%)
    pallas_call x1, Pallas kernels, gather_arrays(): pl.pallas_call(functools.partial(gather_kernel, ctx_count, kinds), out_sh...  303 us
    pallas_call x1, Pallas kernels, combine_rows(): pl.pallas_call(functools.partial(combine_kernel, ctx_count), out_shape=(j...  206 us
    pallas_call x1, Pallas kernels, expert_rows(): pl.pallas_call(functools.partial(expert_kernel, ctx_count), out_shape=(lo...  154 us
    pallas_call x1, Pallas kernels, scatter_arrays(): pl.pallas_call(functools.partial(scatter_kernel, ctx_count, kinds), out_s...  154 us
    dot_general x18, matrix products, mm(): return jnp.einsum(subscripts, left, right, preferred_element_type=FULL)  83.6 us
    unnamed x181, local copies, waits for them, and re-layouts  34.3 us
    pallas_call x1, Pallas kernels, attend_back(): pl.pallas_call(functools.partial(attend_back_kernel, ctx_count, scale), g...  32.2 us
    pallas_call x1, Pallas kernels, attend(): pl.pallas_call(functools.partial(attend_kernel, ctx_count, scale), grid=(...  28.9 us
  transfers between devices with their start and end apart: 17, of which 3 were waited for; matrix products, arithmetic and copies ran while one was open for 20% of the time, Pallas kernels for 42%

profile of v7, /device:TPU:1, one launch (start us, length us, event | category | flops | bytes accessed | tf_op | source)
XLA Modules:
  0.0 1244.9 jit_solution(8587524278861297293)
XLA Ops:
  15.2 302.8 %shard_map.280 = (f32[4,24,256]{2,1,0:T(8,128)}, bf16[4,8,64,3072]{3,2,1,0:T(8,128)(2,1)}, bf16[4,8,64,768]{3,2,1,0:T(8,128)(2,1)}, bf16[4,8,16,4096]{3,2,1,0:T(...) custom-call(f32[24,256]{1,0:T(8,128)} %copy-done.45, ...), custom_call_target="tpu_custom_call" | custom-call | flops 2000000000 | bytes 800000000 | tf_op jit(solution)/shard_map/pallas_call | solution.py:922
  333.6 4.8 all-to-all-start
  338.4 9.9 fusion.48
  374.2 10.8 all-gather.3.cloned.1.call-done
  400.6 28.9 %shard_map.281 = (bf16[16,256,512]{2,1,0:T(8,128)(2,1)}, f32[16,256,1]{2,1,0:T(8,128)}) custom-call(bf16[16,256,512]{2,1,0:T(8,128)(2,1)} %convolution_convert_fusion.8.query_ref, bf16[16,256,128]{2,1,0:T(8,128)(2,1)} %pad.28.turned_ref, bf16[1024,512]{1,0:T(8,128)(2,1)} %slice.205.keys_ref, bf16[1024,128]{1,0:T(8,128)(2,1)} %slice.206.rope_ref), custom_call_target="tpu_custom_call" | custom-call | flops 12000000000 | bytes 12000000 | tf_op jit(solution)/shard_map/pallas_call | solution.py:544
  436.5 8.0 fusion.83
  451.1 154.2 %shard_map.282 = (bf16[4,256,2048]{2,1,0:T(8,128)(2,1)}, bf16[4,8,64,2048]{3,2,1,0:T(8,128)(2,1)}, bf16[4,512,1408]{2,1,0:T(8,128)(2,1)}, bf16[4,512,1408]{2,1,0...) custom-call(bf16[256,2048]{1,0:T(8,128)(2,1)} %multiply_convert_fusion.3, ...), custom_call_target="tpu_custom_call" | custom-call | flops 60000002048 | bytes 400000000 | tf_op jit(solution)/shard_map/pallas_call | solution.py:1120
  605.3 5.2 fusion.84
  610.5 5.4 multiply_convert_fusion
  615.9 5.8 fusion.85
  621.8 5.4 convolution_convert_fusion.2.refs_3_
  627.1 5.1 add_convert_fusion
  632.2 205.8 %shard_map.283 = (f32[256,2048]{1,0:T(8,128)}, f32[256,2048]{1,0:T(8,128)}, bf16[2048,1408]{1,0:T(8,128)(2,1)}, bf16[2048,1408]{1,0:T(8,128)(2,1)}, bf16[2048,1408]{1,0:T(8,128)(2,1)}) custom-call(f32[4,24,256]{2,1,0:T(8,128)} %get-tuple-element.106.info_ref, bf16[4,8,64,2048]{3,2,1,0:T(8,128)(2,1)} %bitcast.349, bf16[4,256,2048]{2,1,0:T(8,128)(2,1)} %bitcast.358, ...), custom_call_target="tpu_custom_call" | custom-call | flops 40000000000 | bytes 600000000 | tf_op jit(solution)/shard_map/pallas_call | solution.py:1395
  851.2 6.4 all-to-all-start.1
  858.0 6.7 convolution_convert_fusion.5
  864.7 5.8 convolution_convert_fusion.3
  873.3 7.7 convolution_convert_fusion.4
  881.0 4.7 copy.220
  885.7 5.4 fusion
  904.3 5.1 convolution_convert_fusion.7.grad_ref
  911.5 5.6 convolution_convert_fusion.1
  917.1 7.0 all-to-all-done.1
  927.2 4.6 all-to-all-start.2
  931.8 32.2 %shard_map.284 = (bf16[16,256,512]{2,1,0:T(8,128)(2,1)}, f32[16,256,128]{2,1,0:T(8,128)}, f32[1024,512]{1,0:T(8,128)}, f32[1024,128]{1,0:T(8,128)}) custom-call(bf16[16,256,512]{2,1,0:T(8,128)(2,1)} %convolution_convert_fusion.8.query_ref, bf16[16,256,128]{2,1,0:T(8,128)(2,1)} %pad.28.turned_ref, bf16[1024,512]{1,0:T(8,128)(2,1)} %slice.205.keys_ref, ...), custom_call_target="tpu_custom_call" | custom-call | flops 30000001024 | bytes 30000000 | tf_op jit(solution)/shard_map/pallas_call | solution.py:570
  981.5 7.9 copy.219
  989.3 7.4 convert_element_type.316.refs_3_
  1000.5 4.7 fusion.27
  1026.2 4.8 all-to-all-start.3
  1031.2 6.7 fusion.86
  1041.4 6.6 convolution_convert_fusion
  1055.6 153.7 %shard_map.285 = (f32[64,3072]{1,0:T(8,128)}, f32[64,576]{1,0:T(8,128)}, f32[64,128]{1,0:T(8,128)}, f32[16,4096]{1,0:T(8,128)}, f32[64,2048]{1,0:T(8,128)}, /*in...) custom-call(bf16[4,4,2,64,3072]{4,3,2,1,0:T(8,128)(2,1)} %bitcast.275, bf16[4,4,2,64,576]{4,3,2,1,0:T(8,128)(2,1)} %bitcast.293, ...), custom_call_target="tpu_custom_call" | custom-call | bytes 500000000 | tf_op jit(solution)/shard_map/pallas_call | solution.py:392
  1228.5 6.3 copy.227
  (334 shorter events, 188.1 us)
Async XLA Ops:
  7.3 377.8 %all-gather.3.cloned.1.call-start = ((), (), s32[]{:S(2)}) async-start(), calls=%async_computation.8 | async-start | bytes 1638400 | tf_op jit(solution)/shard_map/all_gather | solution.py:1712
  8.9 320.8 %collective-permute-start = (bf16[2,704,512]{2,1,0:T(8,128)(2,1)S(1)}, bf16[2,704,512]{2,1,0:T(8,128)(2,1)}, u32[]{:S(2)}, u32[]{:S(2)}) collective-permute-start(bf16[2,704,512]{2,1,0:T(8,128)(2,1)S(1)} %dynamic-slice_bitcast_fusion.6), channel_id=1, source_target_pairs={{0,1},{1,0},{2,3},{3,2},{4,5},{5,4},{6,7},{7,6},{8,9},{9,8},{10,11... | collective-permute-start | bytes 4325384 | tf_op jit(solution)/shard_map/ppermute | solution.py:1447
  9.9 328.4 %copy-start.52 = (f32[256]{0:T(256)}, f32[256]{0:T(256)S(1)}, u32[]{:S(2)}) copy-start(f32[256]{0:T(256)S(1)} %add_rsqrt_fusion.2) | copy-start | bytes 3076
  322.0 16.4 %copy-start.36 = (f32[2048,1]{0,1:T(1,128)}, f32[2048,1]{0,1:T(1,128)S(1)}, u32[]{:S(2)}) copy-start(f32[2048,1]{0,1:T(1,128)S(1)} %copy.248) | copy-start | bytes 24580
  329.1 121.9 %collective-permute-start.1 = (bf16[4,256,1408]{2,1,0:T(8,128)(2,1)}, bf16[4,256,1408]{2,1,0:T(8,128)(2,1)}, u32[]{:S(2)}, u32[]{:S(2)}) collective-permute-start(bf16[4,256,1408]{2,1,0:T(8,128)(2,1)} %get-tuple-element.110.refs_0_), channel_id=1, source_target_pairs={{0,1},{1,0},{2,3},{3,2},{4,5},{5,4},{6,7},{7,6},{8,9},{9,8},{10,11... | collective-permute-start | bytes 8650760 | tf_op jit(solution)/shard_map/ppermute | solution.py:1500
  329.4 121.7 %collective-permute-start.2 = (bf16[4,256,1408]{2,1,0:T(8,128)(2,1)}, bf16[4,256,1408]{2,1,0:T(8,128)(2,1)}, u32[]{:S(2)}, u32[]{:S(2)}) collective-permute-start(bf16[4,256,1408]{2,1,0:T(8,128)(2,1)} %get-tuple-element.111.refs_2_), channel_id=1, source_target_pairs={{0,1},{1,0},{2,3},{3,2},{4,5},{5,4},{6,7},{7,6},{8,9},{9,8},{10,11... | collective-permute-start | bytes 8650760 | tf_op jit(solution)/shard_map/ppermute | solution.py:1500
  333.6 95.9 %all-to-all-start = ((bf16[4,704,512]{2,1,0:T(8,128)(2,1)}), bf16[4,704,512]{2,1,0:T(8,128)(2,1)}, u32[]{:S(2)}, u32[]{:S(2)}) async-start(bf16[4,704,512]{2,1,0:T(8,128)(2,1)} %bitcast.292), calls=%async_computation | async-start | bytes 5767168 | tf_op jit(solution)/shard_map/all_to_all | solution.py:1587
  338.4 10.0 copy-start.25
  351.9 10.6 copy-start.29
  429.5 21.6 %collective-permute-start.3 = (bf16[4,704,512]{2,1,0:T(8,128)(2,1)}, bf16[4,704,512]{2,1,0:T(8,128)(2,1)}, u32[]{:S(2)}, u32[]{:S(2)}) collective-permute-start(bf16[4,704,512]{2,1,0:T(8,128)(2,1)} %all-to-all-done.refs_4_), channel_id=1, source_target_pairs={{0,1},{1,0},{2,3},{3,2},{4,5},{5,4},{6,7},{7,6},{8,9},{9,8},{10,11... | collective-permute-start | bytes 8650760 | tf_op jit(solution)/shard_map/ppermute | solution.py:1500
  434.1 10.3 copy-start.8
  436.5 12.1 copy-start.41
  436.5 9.5 slice-start
  436.5 9.5 slice-start.1
  451.0 154.2 %copy-start.67 = (bf16[4,8,64,704]{3,2,1,0:T(8,128)(2,1)S(1)}, bf16[4,8,64,704]{3,2,1,0:T(8,128)(2,1)}, u32[]{:S(2)}) copy-start(bf16[4,8,64,704]{3,2,1,0:T(8,128)(2,1)} %get-tuple-element.118) | copy-start | bytes 8650756
  840.3 8.0 collective-permute-start.4
  843.4 42.4 %collective-permute-start.6 = (bf16[4,256,1408]{2,1,0:T(8,128)(2,1)}, bf16[4,256,1408]{2,1,0:T(8,128)(2,1)}, u32[]{:S(2)}, u32[]{:S(2)}) collective-permute-start(bf16[4,256,1408]{2,1,0:T(8,128)(2,1)} %dynamic-slice_bitcast_fusion), channel_id=1, source_target_pairs={{0,1},{1,0},{2,3},{3,2},{4,5},{5,4},{6,7},{7,6},{8,9},{9,8},{10,11... | collective-permute-start | bytes 8650760 | tf_op jit(solution)/shard_map/ppermute | solution.py:1468
  847.0 44.1 %collective-permute-start.5 = (bf16[4,256,1408]{2,1,0:T(8,128)(2,1)}, bf16[4,256,1408]{2,1,0:T(8,128)(2,1)}, u32[]{:S(2)}, u32[]{:S(2)}) collective-permute-start(bf16[4,256,1408]{2,1,0:T(8,128)(2,1)} %dynamic-slice_bitcast_fusion.1), channel_id=1, source_target_pairs={{0,1},{1,0},{2,3},{3,2},{4,5},{5,4},{6,7},{7,6},{8,9},{9,8},{10,11... | collective-permute-start | bytes 8650760 | tf_op jit(solution)/shard_map/ppermute | solution.py:1468
  851.2 72.9 %all-to-all-start.1 = ((bf16[4,256,1408]{2,1,0:T(8,128)(2,1)}), bf16[4,256,1408]{2,1,0:T(8,128)(2,1)}, u32[]{:S(2)}, u32[]{:S(2)}) async-start(bf16[4,256,1408]{2,1,0:T(8,128)(2,1)} %fusion.2), calls=%async_computation.1 | async-start | bytes 5767168 | tf_op jit(solution)/shard_map/all_to_all | solution.py:1587
  857.6 139.1 %reduce-scatter.5.cloned.1.call-start = ((), (), s32[]{:S(2)}) async-start(), calls=%async_computation.7 | async-start | bytes 3244032 | tf_op jit(solution)/shard_map/reduce_scatter | solution.py:1796
  881.0 10.1 slice-start.4
  898.3 13.1 %copy-start.6 = (f32[256,2048]{1,0:T(8,128)}, f32[256,2048]{1,0:T(8,128)S(1)}, u32[]{:S(2)}) copy-start(f32[256,2048]{1,0:T(8,128)S(1)} %get-tuple-element.228) | copy-start | bytes 6291460
  926.7 78.6 %collective-permute-start.7 = (bf16[2,256,1408]{2,1,0:T(8,128)(2,1)}, bf16[2,256,1408]{2,1,0:T(8,128)(2,1)}, u32[]{:S(2)}, u32[]{:S(2)}) collective-permute-start(bf16[2,256,1408]{2,1,0:T(8,128)(2,1)} %dynamic-slice_bitcast_fusion.5), channel_id=1, source_target_pairs={{0,1},{1,0},{2,3},{3,2},{4,5},{5,4},{6,7},{7,6},{8,9},{9,8},{10,11... | collective-permute-start | bytes 4325384 | tf_op jit(solution)/shard_map/ppermute | solution.py:1447
  927.2 99.1 %all-to-all-start.2 = ((bf16[4,256,1408]{2,1,0:T(8,128)(2,1)}), bf16[4,256,1408]{2,1,0:T(8,128)(2,1)}, u32[]{:S(2)}, u32[]{:S(2)}) async-start(bf16[4,256,1408]{2,1,0:T(8,128)(2,1)} %fusion.1), calls=%async_computation.3 | async-start | bytes 5767168 | tf_op jit(solution)/shard_map/all_to_all | solution.py:1587
  931.8 82.9 %reduce-scatter.3.cloned.1.call-start = ((), (), s32[]{:S(2)}) async-start(), calls=%async_computation.6 | async-start | bytes 1474560 | tf_op jit(solution)/shard_map/reduce_scatter | solution.py:1824
  1007.3 8.4 copy-start.19
  1007.3 9.8 copy-start.60
  1007.3 9.8 copy-start.63
  1007.3 11.5 copy-start.30
  1026.2 186.0 %all-to-all-start.3 = ((bf16[4,256,1408]{2,1,0:T(8,128)(2,1)}), bf16[4,256,1408]{2,1,0:T(8,128)(2,1)}, u32[]{:S(2)}, u32[]{:S(2)}) async-start(bf16[4,256,1408]{2,1,0:T(8,128)(2,1)} %fusion), calls=%async_computation.5 | async-start | bytes 5767168 | tf_op jit(solution)/shard_map/all_to_all | solution.py:1587
  1050.7 167.1 %collective-permute-start.8 = (bf16[2,256,1408]{2,1,0:T(8,128)(2,1)}, bf16[2,256,1408]{2,1,0:T(8,128)(2,1)}, u32[]{:S(2)}, u32[]{:S(2)}) collective-permute-start(bf16[2,256,1408]{2,1,0:T(8,128)(2,1)} %dynamic-slice_bitcast_fusion.4), channel_id=1, source_target_pairs={{0,1},{1,0},{2,3},{3,2},{4,5},{5,4},{6,7},{7,6},{8,9},{9,8},{10,11... | collective-permute-start | bytes 4325384 | tf_op jit(solution)/shard_map/ppermute | solution.py:1447
  1213.8 9.4 collective-permute-start.9
  (68 other events, 301.3 us)
Sparse Core Ops, SparseCore 0:
  329.3 55.7 all-gather.2
  864.8 46.2 reduce-scatter.4
  976.1 38.5 reduce-scatter.2

commit v8 on v7

--- a/solution.py
+++ b/solution.py
@@ -1069,6 +1069,16 @@
         for copy in store_sides(block):
             copy.start()
 
+        for later in range(2, ctx_count):
+
+            @pl.when(step + 2 == later)
+            def _():
+                along_order(move.z, ctx_count, later, move.take)
+
+        @pl.when(step + 2 < ctx_count)
+        def _():
+            move.choose(block_at(step + 2))
+
         @pl.when(step > 0)
         def _():
             store_back(block).wait()
@@ -1087,16 +1097,6 @@
 
         each_tile(width, back_tile)
         store_back(block).start()
-
-        for later in range(2, ctx_count):
-
-            @pl.when(step + 2 == later)
-            def _():
-                along_order(move.z, ctx_count, later, move.take)
-
-        @pl.when(step + 2 < ctx_count)
-        def _():
-            move.choose(block_at(step + 2))
 
     for step in range(ctx_count):
         store_slots(order[step]).wait()
@@ -1833,7 +1833,7 @@
     sdown_grad = sdown_grad.astype(FULL)
 
     query_nope_grad = mm("htc,chd->thd", query_latent_grad, expand_key)
-    expand_key_grad = mm("thd,htc->chd", query_nope, query_latent_grad)
+    expand_key_grad = mm("htc,thd->chd", query_latent_grad, query_nope)
     expand_grad = jnp.concatenate([expand_key_grad, expand_value_grad], axis=-1).reshape(
         LATENT, HEADS * (NOPE + VDIM)
     )

time: 1260 us -> 1260 us (level)
  transfers between devices with their start and end apart: 17 -> 17, of which waited for: 3 -> 3; matrix products, arithmetic and copies ran while one was open for 20% -> 20% of each run, Pallas kernels for 42% -> 41%
where the time goes in v8:
time: 1260 us; the launch traced here: 1250 us
  Pallas kernels  881 us (70%)
  local copies, waits for them, and re-layouts  131 us (10%)
  matrix products  115 us (9%)
  other arithmetic  58.5 us (5%)
  starting transfers between devices  31.5 us (2%)
  waiting for transfers between devices  21.1 us (2%)
  between operations  15.5 us (1%)
    pallas_call x1, Pallas kernels, gather_arrays(): pl.pallas_call(functools.partial(gather_kernel, ctx_count, kinds), out_sh...  303 us
    pallas_call x1, Pallas kernels, combine_rows(): pl.pallas_call(functools.partial(combine_kernel, ctx_count), out_shape=(j...  200 us
    pallas_call x1, Pallas kernels, expert_rows(): pl.pallas_call(functools.partial(expert_kernel, ctx_count), out_shape=(lo...  164 us
    pallas_call x1, Pallas kernels, scatter_arrays(): pl.pallas_call(functools.partial(scatter_kernel, ctx_count, kinds), out_s...  154 us
    dot_general x18, matrix products, mm(): return jnp.einsum(subscripts, left, right, preferred_element_type=FULL)  83.7 us
    unnamed x181, local copies, waits for them, and re-layouts  37.9 us
    pallas_call x1, Pallas kernels, attend_back(): pl.pallas_call(functools.partial(attend_back_kernel, ctx_count, scale), g...  32.2 us
    pallas_call x1, Pallas kernels, attend(): pl.pallas_call(functools.partial(attend_kernel, ctx_count, scale), grid=(...  28.9 us
  transfers between devices with their start and end apart: 17, of which 3 were waited for; matrix products, arithmetic and copies ran while one was open for 20% of the time, Pallas kernels for 41%

profile of v8, /device:TPU:1, one launch (start us, length us, event | category | flops | bytes accessed | tf_op | source)
XLA Modules:
  0.0 1253.9 jit_solution(11552103587712562249)
XLA Ops:
  15.2 302.8 %shard_map.280 = (f32[4,24,256]{2,1,0:T(8,128)}, bf16[4,8,64,3072]{3,2,1,0:T(8,128)(2,1)}, bf16[4,8,64,768]{3,2,1,0:T(8,128)(2,1)}, bf16[4,8,16,4096]{3,2,1,0:T(...) custom-call(f32[24,256]{1,0:T(8,128)} %copy-done.45, ...), custom_call_target="tpu_custom_call" | custom-call | flops 2000000000 | bytes 800000000 | tf_op jit(solution)/shard_map/pallas_call | solution.py:922
  333.6 4.8 all-to-all-start
  338.4 9.9 fusion.48
  374.2 10.8 all-gather.3.cloned.1.call-done
  400.6 28.9 %shard_map.281 = (bf16[16,256,512]{2,1,0:T(8,128)(2,1)}, f32[16,256,1]{2,1,0:T(8,128)}) custom-call(bf16[16,256,512]{2,1,0:T(8,128)(2,1)} %convolution_convert_fusion.8.query_ref, bf16[16,256,128]{2,1,0:T(8,128)(2,1)} %pad.28.turned_ref, bf16[1024,512]{1,0:T(8,128)(2,1)} %slice.205.keys_ref, bf16[1024,128]{1,0:T(8,128)(2,1)} %slice.206.rope_ref), custom_call_target="tpu_custom_call" | custom-call | flops 12000000000 | bytes 12000000 | tf_op jit(solution)/shard_map/pallas_call | solution.py:544
  436.5 8.0 fusion.83
  451.1 164.3 %shard_map.282 = (bf16[4,256,2048]{2,1,0:T(8,128)(2,1)}, bf16[4,8,64,2048]{3,2,1,0:T(8,128)(2,1)}, bf16[4,512,1408]{2,1,0:T(8,128)(2,1)}, bf16[4,512,1408]{2,1,0...) custom-call(bf16[256,2048]{1,0:T(8,128)(2,1)} %multiply_convert_fusion.3, ...), custom_call_target="tpu_custom_call" | custom-call | flops 60000002048 | bytes 400000000 | tf_op jit(solution)/shard_map/pallas_call | solution.py:1120
  615.4 5.2 fusion.84
  620.6 5.4 multiply_convert_fusion
  626.0 5.8 fusion.85
  631.9 5.4 convolution_convert_fusion.2.refs_3_
  637.3 5.1 add_convert_fusion
  642.4 199.5 %shard_map.283 = (f32[256,2048]{1,0:T(8,128)}, f32[256,2048]{1,0:T(8,128)}, bf16[2048,1408]{1,0:T(8,128)(2,1)}, bf16[2048,1408]{1,0:T(8,128)(2,1)}, bf16[2048,1408]{1,0:T(8,128)(2,1)}) custom-call(f32[4,24,256]{2,1,0:T(8,128)} %get-tuple-element.106.info_ref, bf16[4,8,64,2048]{3,2,1,0:T(8,128)(2,1)} %bitcast.349, bf16[4,256,2048]{2,1,0:T(8,128)(2,1)} %bitcast.358, ...), custom_call_target="tpu_custom_call" | custom-call | flops 40000000000 | bytes 600000000 | tf_op jit(solution)/shard_map/pallas_call | solution.py:1395
  855.0 11.7 all-to-all-start.1
  867.1 6.7 convolution_convert_fusion.5
  873.9 5.8 convolution_convert_fusion.3
  882.4 7.8 convolution_convert_fusion.4
  890.2 4.7 copy.220
  894.9 5.5 fusion
  913.7 5.0 convolution_convert_fusion.7.grad_ref
  920.8 5.6 convolution_convert_fusion.1
  926.4 5.0 all-to-all-done.1
  940.1 32.2 %shard_map.284 = (bf16[16,256,512]{2,1,0:T(8,128)(2,1)}, f32[16,256,128]{2,1,0:T(8,128)}, f32[1024,512]{1,0:T(8,128)}, f32[1024,128]{1,0:T(8,128)}) custom-call(bf16[16,256,512]{2,1,0:T(8,128)(2,1)} %convolution_convert_fusion.8.query_ref, bf16[16,256,128]{2,1,0:T(8,128)(2,1)} %pad.28.turned_ref, bf16[1024,512]{1,0:T(8,128)(2,1)} %slice.205.keys_ref, ...), custom_call_target="tpu_custom_call" | custom-call | flops 30000001024 | bytes 30000000 | tf_op jit(solution)/shard_map/pallas_call | solution.py:570
  989.7 7.8 copy.219
  997.6 7.4 convert_element_type.316.refs_3_
  1008.7 4.7 fusion.27
  1018.5 5.2 reduce-scatter.3.cloned.1.call-done
  1035.3 4.8 all-to-all-start.3
  1040.2 6.7 fusion.86
  1050.4 6.6 convolution_convert_fusion
  1064.6 153.7 %shard_map.285 = (f32[64,3072]{1,0:T(8,128)}, f32[64,576]{1,0:T(8,128)}, f32[64,128]{1,0:T(8,128)}, f32[16,4096]{1,0:T(8,128)}, f32[64,2048]{1,0:T(8,128)}, /*in...) custom-call(bf16[4,4,2,64,3072]{4,3,2,1,0:T(8,128)(2,1)} %bitcast.275, bf16[4,4,2,64,576]{4,3,2,1,0:T(8,128)(2,1)} %bitcast.293, ...), custom_call_target="tpu_custom_call" | custom-call | bytes 500000000 | tf_op jit(solution)/shard_map/pallas_call | solution.py:392
  1237.6 6.3 copy.227
  (334 shorter events, 189.2 us)
Async XLA Ops:
  7.3 377.8 %all-gather.3.cloned.1.call-start = ((), (), s32[]{:S(2)}) async-start(), calls=%async_computation.8 | async-start | bytes 1638400 | tf_op jit(solution)/shard_map/all_gather | solution.py:1712
  8.9 320.8 %collective-permute-start = (bf16[2,704,512]{2,1,0:T(8,128)(2,1)S(1)}, bf16[2,704,512]{2,1,0:T(8,128)(2,1)}, u32[]{:S(2)}, u32[]{:S(2)}) collective-permute-start(bf16[2,704,512]{2,1,0:T(8,128)(2,1)S(1)} %dynamic-slice_bitcast_fusion.6), channel_id=1, source_target_pairs={{0,1},{1,0},{2,3},{3,2},{4,5},{5,4},{6,7},{7,6},{8,9},{9,8},{10,11... | collective-permute-start | bytes 4325384 | tf_op jit(solution)/shard_map/ppermute | solution.py:1447
  9.9 328.4 %copy-start.52 = (f32[256]{0:T(256)}, f32[256]{0:T(256)S(1)}, u32[]{:S(2)}) copy-start(f32[256]{0:T(256)S(1)} %add_rsqrt_fusion.2) | copy-start | bytes 3076
  322.0 16.4 %copy-start.36 = (f32[2048,1]{0,1:T(1,128)}, f32[2048,1]{0,1:T(1,128)S(1)}, u32[]{:S(2)}) copy-start(f32[2048,1]{0,1:T(1,128)S(1)} %copy.248) | copy-start | bytes 24580
  329.1 121.9 %collective-permute-start.1 = (bf16[4,256,1408]{2,1,0:T(8,128)(2,1)}, bf16[4,256,1408]{2,1,0:T(8,128)(2,1)}, u32[]{:S(2)}, u32[]{:S(2)}) collective-permute-start(bf16[4,256,1408]{2,1,0:T(8,128)(2,1)} %get-tuple-element.110.refs_0_), channel_id=1, source_target_pairs={{0,1},{1,0},{2,3},{3,2},{4,5},{5,4},{6,7},{7,6},{8,9},{9,8},{10,11... | collective-permute-start | bytes 8650760 | tf_op jit(solution)/shard_map/ppermute | solution.py:1500
  329.4 121.7 %collective-permute-start.2 = (bf16[4,256,1408]{2,1,0:T(8,128)(2,1)}, bf16[4,256,1408]{2,1,0:T(8,128)(2,1)}, u32[]{:S(2)}, u32[]{:S(2)}) collective-permute-start(bf16[4,256,1408]{2,1,0:T(8,128)(2,1)} %get-tuple-element.111.refs_2_), channel_id=1, source_target_pairs={{0,1},{1,0},{2,3},{3,2},{4,5},{5,4},{6,7},{7,6},{8,9},{9,8},{10,11... | collective-permute-start | bytes 8650760 | tf_op jit(solution)/shard_map/ppermute | solution.py:1500
  333.6 95.9 %all-to-all-start = ((bf16[4,704,512]{2,1,0:T(8,128)(2,1)}), bf16[4,704,512]{2,1,0:T(8,128)(2,1)}, u32[]{:S(2)}, u32[]{:S(2)}) async-start(bf16[4,704,512]{2,1,0:T(8,128)(2,1)} %bitcast.292), calls=%async_computation | async-start | bytes 5767168 | tf_op jit(solution)/shard_map/all_to_all | solution.py:1587
  338.4 10.0 copy-start.25
  351.9 10.6 copy-start.29
  429.5 21.6 %collective-permute-start.3 = (bf16[4,704,512]{2,1,0:T(8,128)(2,1)}, bf16[4,704,512]{2,1,0:T(8,128)(2,1)}, u32[]{:S(2)}, u32[]{:S(2)}) collective-permute-start(bf16[4,704,512]{2,1,0:T(8,128)(2,1)} %all-to-all-done.refs_4_), channel_id=1, source_target_pairs={{0,1},{1,0},{2,3},{3,2},{4,5},{5,4},{6,7},{7,6},{8,9},{9,8},{10,11... | collective-permute-start | bytes 8650760 | tf_op jit(solution)/shard_map/ppermute | solution.py:1500
  434.1 10.3 copy-start.8
  436.5 12.1 copy-start.41
  436.5 9.5 slice-start
  436.5 9.5 slice-start.1
  451.0 164.3 %copy-start.67 = (bf16[4,8,64,704]{3,2,1,0:T(8,128)(2,1)S(1)}, bf16[4,8,64,704]{3,2,1,0:T(8,128)(2,1)}, u32[]{:S(2)}) copy-start(bf16[4,8,64,704]{3,2,1,0:T(8,128)(2,1)} %get-tuple-element.118) | copy-start | bytes 8650756
  844.1 6.7 collective-permute-start.4
  847.2 47.7 %collective-permute-start.6 = (bf16[4,256,1408]{2,1,0:T(8,128)(2,1)}, bf16[4,256,1408]{2,1,0:T(8,128)(2,1)}, u32[]{:S(2)}, u32[]{:S(2)}) collective-permute-start(bf16[4,256,1408]{2,1,0:T(8,128)(2,1)} %dynamic-slice_bitcast_fusion), channel_id=1, source_target_pairs={{0,1},{1,0},{2,3},{3,2},{4,5},{5,4},{6,7},{7,6},{8,9},{9,8},{10,11... | collective-permute-start | bytes 8650760 | tf_op jit(solution)/shard_map/ppermute | solution.py:1468
  850.9 49.6 %collective-permute-start.5 = (bf16[4,256,1408]{2,1,0:T(8,128)(2,1)}, bf16[4,256,1408]{2,1,0:T(8,128)(2,1)}, u32[]{:S(2)}, u32[]{:S(2)}) collective-permute-start(bf16[4,256,1408]{2,1,0:T(8,128)(2,1)} %dynamic-slice_bitcast_fusion.1), channel_id=1, source_target_pairs={{0,1},{1,0},{2,3},{3,2},{4,5},{5,4},{6,7},{7,6},{8,9},{9,8},{10,11... | collective-permute-start | bytes 8650760 | tf_op jit(solution)/shard_map/ppermute | solution.py:1468
  855.0 12.1 copy-start.72
  855.0 76.4 %all-to-all-start.1 = ((bf16[4,256,1408]{2,1,0:T(8,128)(2,1)}), bf16[4,256,1408]{2,1,0:T(8,128)(2,1)}, u32[]{:S(2)}, u32[]{:S(2)}) async-start(bf16[4,256,1408]{2,1,0:T(8,128)(2,1)} %fusion.2), calls=%async_computation.1 | async-start | bytes 5767168 | tf_op jit(solution)/shard_map/all_to_all | solution.py:1587
  866.7 138.2 %reduce-scatter.5.cloned.1.call-start = ((), (), s32[]{:S(2)}) async-start(), calls=%async_computation.7 | async-start | bytes 3244032 | tf_op jit(solution)/shard_map/reduce_scatter | solution.py:1796
  890.2 10.2 slice-start.4
  907.7 13.1 %copy-start.6 = (f32[256,2048]{1,0:T(8,128)}, f32[256,2048]{1,0:T(8,128)S(1)}, u32[]{:S(2)}) copy-start(f32[256,2048]{1,0:T(8,128)S(1)} %get-tuple-element.228) | copy-start | bytes 6291460
  933.9 79.5 %collective-permute-start.7 = (bf16[2,256,1408]{2,1,0:T(8,128)(2,1)}, bf16[2,256,1408]{2,1,0:T(8,128)(2,1)}, u32[]{:S(2)}, u32[]{:S(2)}) collective-permute-start(bf16[2,256,1408]{2,1,0:T(8,128)(2,1)} %dynamic-slice_bitcast_fusion.5), channel_id=1, source_target_pairs={{0,1},{1,0},{2,3},{3,2},{4,5},{5,4},{6,7},{7,6},{8,9},{9,8},{10,11... | collective-permute-start | bytes 4325384 | tf_op jit(solution)/shard_map/ppermute | solution.py:1447
  935.4 99.9 %all-to-all-start.2 = ((bf16[4,256,1408]{2,1,0:T(8,128)(2,1)}), bf16[4,256,1408]{2,1,0:T(8,128)(2,1)}, u32[]{:S(2)}, u32[]{:S(2)}) async-start(bf16[4,256,1408]{2,1,0:T(8,128)(2,1)} %fusion.1), calls=%async_computation.3 | async-start | bytes 5767168 | tf_op jit(solution)/shard_map/all_to_all | solution.py:1587
  940.0 83.7 %reduce-scatter.3.cloned.1.call-start = ((), (), s32[]{:S(2)}) async-start(), calls=%async_computation.6 | async-start | bytes 1474560 | tf_op jit(solution)/shard_map/reduce_scatter | solution.py:1824
  1015.6 10.7 copy-start.60
  1015.6 10.7 copy-start.63
  1015.6 12.3 copy-start.30
  1035.3 186.0 %all-to-all-start.3 = ((bf16[4,256,1408]{2,1,0:T(8,128)(2,1)}), bf16[4,256,1408]{2,1,0:T(8,128)(2,1)}, u32[]{:S(2)}, u32[]{:S(2)}) async-start(bf16[4,256,1408]{2,1,0:T(8,128)(2,1)} %fusion), calls=%async_computation.5 | async-start | bytes 5767168 | tf_op jit(solution)/shard_map/all_to_all | solution.py:1587
  1059.8 167.1 %collective-permute-start.8 = (bf16[2,256,1408]{2,1,0:T(8,128)(2,1)}, bf16[2,256,1408]{2,1,0:T(8,128)(2,1)}, u32[]{:S(2)}, u32[]{:S(2)}) collective-permute-start(bf16[2,256,1408]{2,1,0:T(8,128)(2,1)} %dynamic-slice_bitcast_fusion.4), channel_id=1, source_target_pairs={{0,1},{1,0},{2,3},{3,2},{4,5},{5,4},{6,7},{7,6},{8,9},{9,8},{10,11... | collective-permute-start | bytes 4325384 | tf_op jit(solution)/shard_map/ppermute | solution.py:1447
  1222.8 9.4 collective-permute-start.9
  (68 other events, 305.5 us)
Sparse Core Ops, SparseCore 0:
  329.3 55.7 all-gather.2
  874.0 46.2 reduce-scatter.4
  984.4 39.3 reduce-scatter.2
